TPU v7x, 32 devices: a whole 2x2x4 slice. The times are simulated.
32 devices in a mesh: dp: 16 (over z, x, core), seq: 2 (over y).
Axes of the slice: x: 2, y: 2, z: 4, core: 2. Of those that a mesh axis runs over, the one named last changes fastest.
Arguments:
- inputs: float32 [32, 1024, 1024], P('dp', 'seq'), may hold values from -6 to 6
- grad_out: float32 [32, 1024, 1024], P('dp', 'seq'), may hold values from -6 to 6
- random_blocks: int32 [32, 16, 16, 3], P('dp', None, 'seq'), may hold values from 1 to 14, as said below
- w_query: bfloat16 [1024, 1024], P(('dp', 'seq')), may hold values from -0.1875 to 0.1875
- w_key: bfloat16 [1024, 1024], P(('dp', 'seq')), may hold values from -0.1875 to 0.1875
- w_value: bfloat16 [1024, 1024], P(('dp', 'seq')), may hold values from -0.1875 to 0.1875
- w_out: bfloat16 [1024, 1024], P(('dp', 'seq')), may hold values from -3 to 3
- w_up: bfloat16 [1024, 4096], P(('dp', 'seq')), may hold values from -0.1875 to 0.1875
- w_down: bfloat16 [4096, 1024], P(('dp', 'seq')), may hold values from -0.125 to 0.125
- ln1_gain: bfloat16 [1024], P(('dp', 'seq')), may hold values from 0.5 to 1.5
- ln1_bias: bfloat16 [1024], P(('dp', 'seq')), may hold values from -4 to 4
- query_bias: bfloat16 [1024], P(('dp', 'seq')), may hold values from -6 to 6
- value_bias: bfloat16 [1024], P(('dp', 'seq')), may hold values from -1.5 to 1.5
- out_bias: bfloat16 [1024], P(('dp', 'seq')), may hold values from -4 to 4
- ln2_gain: bfloat16 [1024], P(('dp', 'seq')), may hold values from 0.5 to 1.5
- ln2_bias: bfloat16 [1024], P(('dp', 'seq')), may hold values from -4 to 4
- up_bias: bfloat16 [4096], P(('dp', 'seq')), may hold values from -6 to 6
- down_bias: bfloat16 [1024], P(('dp', 'seq')), may hold values from -4 to 4
Outputs:
- outputs: float32 [32, 1024, 1024], P('dp', 'seq')
- grad_inputs: float32 [32, 1024, 1024], P('dp', 'seq')
- grad_w_query: float32 [1024, 1024], P(('dp', 'seq'))
- grad_w_key: float32 [1024, 1024], P(('dp', 'seq'))
- grad_w_value: float32 [1024, 1024], P(('dp', 'seq'))
- grad_w_out: float32 [1024, 1024], P(('dp', 'seq'))
- grad_w_up: float32 [1024, 4096], P(('dp', 'seq'))
- grad_w_down: float32 [4096, 1024], P(('dp', 'seq'))
- grad_ln1_gain: float32 [1024], P(('dp', 'seq'))
- grad_ln1_bias: float32 [1024], P(('dp', 'seq'))
- grad_query_bias: float32 [1024], P(('dp', 'seq'))
- grad_value_bias: float32 [1024], P(('dp', 'seq'))
- grad_out_bias: float32 [1024], P(('dp', 'seq'))
- grad_ln2_gain: float32 [1024], P(('dp', 'seq'))
- grad_ln2_bias: float32 [1024], P(('dp', 'seq'))
- grad_up_bias: float32 [4096], P(('dp', 'seq'))
- grad_down_bias: float32 [1024], P(('dp', 'seq'))
Inputs may be any that keep to these rules, and one draw needn't show every extreme that they name: `random_blocks`: for each sequence, head and query block: 3 different key blocks, none equal to the query block or to a block beside it, and none equal to 0 or 15.
All inputs are finite; a program needn't handle non-finite values.
Results may differ from a plain program's by a relative error of at most 0.013.
Values may be sent and summed in bfloat16 or wider, within the bound.
No kernel may reach another device: no remote copies, remote signals or barrier semaphores. Data moves between devices by JAX's collectives and lax.ppermute only.
A program may use at most 384 MiB of HBM per device.

v0:
```python
import jax
import jax.numpy as jnp
from jax import lax
from jax.sharding import PartitionSpec as P

HEADS = 16
BLOCK = 64


eps_norm = 1e-05
neg_fill = -1e30


def layer_norm(values, norm_gain, norm_shift):
    centre = values - jnp.mean(values, axis=-1, keepdims=True)
    spread = jnp.mean(centre * centre, axis=-1, keepdims=True)
    return centre * lax.rsqrt(spread + eps_norm) * norm_gain + norm_shift


def gelu_tanh(values):
    return jax.nn.gelu(values, approximate=True)


def project(left, right):
    return jnp.dot(left, right, preferred_element_type=jnp.float32)


def project_back(grad_rows, weight):
    return lax.dot_general(
        grad_rows, weight, (((1,), (1,)), ((), ())), preferred_element_type=jnp.float32
    )


def weight_grad(left, grad_rows):
    return lax.dot_general(
        left, grad_rows, (((0,), (0,)), ((), ())), preferred_element_type=jnp.float32
    )


def column_sum(grad_rows):
    return jnp.sum(grad_rows, axis=0, dtype=jnp.float32)


def to_table(block_rows):
    block_count = block_rows.shape[0] // BLOCK
    head_dim = block_rows.shape[1] // HEADS
    shaped = block_rows.reshape(block_count, BLOCK, HEADS, head_dim)
    return shaped.transpose(2, 0, 1, 3).reshape(HEADS, block_count, BLOCK * head_dim)


def from_table(table):
    block_count = table.shape[1]
    head_dim = table.shape[2] // BLOCK
    shaped = table.reshape(HEADS, block_count, BLOCK, head_dim)
    return shaped.transpose(1, 2, 0, 3).reshape(block_count * BLOCK, HEADS * head_dim)


def key_layout(first_block, local_blocks, all_blocks, random_ids):
    query_ids = first_block + jnp.arange(local_blocks, dtype=jnp.int32)
    window = jnp.stack([query_ids - 1, query_ids, query_ids + 1], axis=1)
    inside = (window >= 1) & (window <= all_blocks - 2)
    window = jnp.clip(window, 0, all_blocks - 1)
    end_blocks = jnp.broadcast_to(jnp.array([0, all_blocks - 1], jnp.int32), (local_blocks, 2))
    fixed_slots = jnp.concatenate([end_blocks, window], axis=1)
    key_slots = jnp.concatenate(
        [jnp.broadcast_to(fixed_slots[None], (HEADS, local_blocks, 5)), random_ids], axis=2
    )
    key_valid = jnp.concatenate(
        [
            jnp.ones((local_blocks, 2), jnp.bool_),
            inside,
            jnp.ones((local_blocks, random_ids.shape[2]), jnp.bool_),
        ],
        axis=1,
    )
    return (key_slots, jnp.repeat(key_valid, BLOCK, axis=1))


def pick_blocks(table, key_slots):
    head_index = jnp.arange(HEADS)[:, None, None]
    picked = table[head_index, key_slots]
    head_dim = table.shape[2] // BLOCK
    return picked.reshape(HEADS, key_slots.shape[1], key_slots.shape[2] * BLOCK, head_dim)


def sparse_scores(query_heads, key_picked, key_valid, score_scale):
    raw_scores = jnp.einsum(
        "hqid,hqkd->hqik", query_heads, key_picked, preferred_element_type=jnp.float32
    )
    return jnp.where(key_valid[None, :, None, :], raw_scores * score_scale, neg_fill)


def dense_scores(query_block, key_flat, score_scale):
    return (
        jnp.einsum("hid,hkd->hik", query_block, key_flat, preferred_element_type=jnp.float32)
        * score_scale
    )


def dense_forward(query_block, key_flat, value_flat, score_scale):
    scores = dense_scores(query_block, key_flat, score_scale)
    top_score = jnp.max(scores, axis=-1, keepdims=True)
    expos = jnp.exp(scores - top_score)
    totals = jnp.sum(expos, axis=-1, keepdims=True)
    attn_prob = (expos / totals).astype(jnp.bfloat16)
    result = jnp.einsum("hik,hkd->ihd", attn_prob, value_flat, preferred_element_type=jnp.float32)
    return (result, (top_score + jnp.log(totals))[..., 0])


def softmax_back(attn_prob, grad_prob, score_scale):
    inner = jnp.sum(attn_prob * grad_prob, axis=-1, keepdims=True)
    return (attn_prob * (grad_prob - inner) * score_scale).astype(jnp.bfloat16)


def dense_backward(query_block, key_flat, value_flat, grad_block, log_total, score_scale):
    attn_prob = jnp.exp(dense_scores(query_block, key_flat, score_scale) - log_total[..., None])
    grad_prob = jnp.einsum(
        "ihd,hkd->hik", grad_block, value_flat, preferred_element_type=jnp.float32
    )
    grad_value = jnp.einsum(
        "hik,ihd->hkd",
        attn_prob.astype(jnp.bfloat16),
        grad_block,
        preferred_element_type=jnp.float32,
    )
    grad_scores = softmax_back(attn_prob, grad_prob, score_scale)
    grad_query = jnp.einsum(
        "hik,hkd->ihd", grad_scores, key_flat, preferred_element_type=jnp.float32
    )
    grad_key = jnp.einsum(
        "hik,hid->hkd", grad_scores, query_block, preferred_element_type=jnp.float32
    )
    return (grad_query, grad_key, grad_value)


def run_forward(weights, in_rows, random_ids):
    (
        w_query,
        w_key,
        w_value,
        w_out,
        w_up,
        w_down,
        ln1_gain,
        ln1_bias,
        query_bias,
        value_bias,
        out_bias,
        ln2_gain,
        ln2_bias,
        up_bias,
        down_bias,
    ) = weights
    normed, pull_first = jax.vjp(
        layer_norm, in_rows, ln1_gain.astype(jnp.float32), ln1_bias.astype(jnp.float32)
    )
    normed_low = normed.astype(jnp.bfloat16)
    queries = (project(normed_low, w_query) + query_bias.astype(jnp.float32)).astype(jnp.bfloat16)
    key_rows = project(normed_low, w_key).astype(jnp.bfloat16)
    value_rows = (project(normed_low, w_value) + value_bias.astype(jnp.float32)).astype(
        jnp.bfloat16
    )
    key_all, value_all = (
        lax.all_gather(key_rows, "seq", axis=0, tiled=True),
        lax.all_gather(value_rows, "seq", axis=0, tiled=True),
    )
    place = lax.axis_index("seq")
    ranks = lax.axis_size("seq")
    local_blocks = in_rows.shape[0] // BLOCK
    all_blocks = key_all.shape[0] // BLOCK
    head_dim = queries.shape[1] // HEADS
    score_scale = head_dim ** (-0.5)
    key_slots, key_valid = key_layout(place * local_blocks, local_blocks, all_blocks, random_ids)
    key_table = to_table(key_all)
    value_table = to_table(value_all)
    key_picked = pick_blocks(key_table, key_slots)
    value_picked = pick_blocks(value_table, key_slots)
    query_heads = to_table(queries).reshape(HEADS, local_blocks, BLOCK, head_dim)
    scores = sparse_scores(query_heads, key_picked, key_valid, score_scale)
    top_score = jnp.max(scores, axis=-1, keepdims=True)
    expos = jnp.exp(scores - top_score)
    totals = jnp.sum(expos, axis=-1, keepdims=True)
    prob_low = (expos / totals).astype(jnp.bfloat16)
    log_sparse = (top_score + jnp.log(totals))[..., 0]
    sparse_out = jnp.einsum(
        "hqik,hqkd->qihd", prob_low, value_picked, preferred_element_type=jnp.float32
    )
    is_edge = (place == 0) | (place == ranks - 1)
    edge_slot = jnp.where(place == 0, 0, local_blocks - 1)
    key_flat = key_table.reshape(HEADS, all_blocks * BLOCK, head_dim)
    value_flat = value_table.reshape(HEADS, all_blocks * BLOCK, head_dim)
    query_edge = lax.dynamic_index_in_dim(query_heads, edge_slot, 1, keepdims=False)
    edge_out, log_edge = lax.cond(
        is_edge,
        lambda: dense_forward(query_edge, key_flat, value_flat, score_scale),
        lambda: (
            jnp.zeros((BLOCK, HEADS, head_dim), jnp.float32),
            jnp.zeros((HEADS, BLOCK), jnp.float32),
        ),
    )
    current = lax.dynamic_index_in_dim(sparse_out, edge_slot, 0, keepdims=False)
    mixed_heads = lax.dynamic_update_index_in_dim(
        sparse_out, jnp.where(is_edge, edge_out, current), edge_slot, 0
    )
    mixed_low = mixed_heads.reshape(in_rows.shape[0], queries.shape[1]).astype(jnp.bfloat16)
    middle = in_rows + (project(mixed_low, w_out) + out_bias.astype(jnp.float32))
    normed_two, pull_second = jax.vjp(
        layer_norm, middle, ln2_gain.astype(jnp.float32), ln2_bias.astype(jnp.float32)
    )
    normed_two_low = normed_two.astype(jnp.bfloat16)
    hidden_pre = project(normed_two_low, w_up) + up_bias.astype(jnp.float32)
    hidden, pull_gelu = jax.vjp(gelu_tanh, hidden_pre)
    hidden_low = hidden.astype(jnp.bfloat16)
    result = middle + (project(hidden_low, w_down) + down_bias.astype(jnp.float32))
    saved = {
        "pull_first": pull_first,
        "pull_second": pull_second,
        "pull_gelu": pull_gelu,
        "normed_low": normed_low,
        "normed_two_low": normed_two_low,
        "hidden_low": hidden_low,
        "mixed_low": mixed_low,
        "query_heads": query_heads,
        "query_edge": query_edge,
        "key_picked": key_picked,
        "value_picked": value_picked,
        "key_flat": key_flat,
        "value_flat": value_flat,
        "key_slots": key_slots,
        "key_valid": key_valid,
        "log_sparse": log_sparse,
        "log_edge": log_edge,
        "is_edge": is_edge,
        "edge_slot": edge_slot,
    }
    return (saved, result)


def run_backward(weights, saved, grad_rows):
    (
        w_query,
        w_key,
        w_value,
        w_out,
        w_up,
        w_down,
        ln1_gain,
        ln1_bias,
        query_bias,
        value_bias,
        out_bias,
        ln2_gain,
        ln2_bias,
        up_bias,
        down_bias,
    ) = weights
    query_heads = saved["query_heads"]
    key_picked = saved["key_picked"]
    value_picked = saved["value_picked"]
    key_slots = saved["key_slots"]
    is_edge = saved["is_edge"]
    edge_slot = saved["edge_slot"]
    local_blocks = query_heads.shape[1]
    head_dim = query_heads.shape[3]
    all_blocks = saved["key_flat"].shape[1] // BLOCK
    score_scale = head_dim ** (-0.5)
    token_count = grad_rows.shape[0]
    grad_ff_low = grad_rows.astype(jnp.bfloat16)
    grad_w_down = weight_grad(saved["hidden_low"], grad_ff_low)
    grad_down_bias = column_sum(grad_ff_low)
    (grad_pre,) = saved["pull_gelu"](project_back(grad_ff_low, w_down))
    grad_pre_low = grad_pre.astype(jnp.bfloat16)
    grad_w_up = weight_grad(saved["normed_two_low"], grad_pre_low)
    grad_up_bias = column_sum(grad_pre_low)
    grad_normed_two = project_back(grad_pre_low, w_up)
    grad_middle, grad_ln2_gain, grad_ln2_bias = saved["pull_second"](grad_normed_two)
    grad_middle = grad_middle + grad_rows
    grad_attn_low = grad_middle.astype(jnp.bfloat16)
    grad_w_out = weight_grad(saved["mixed_low"], grad_attn_low)
    grad_out_bias = column_sum(grad_attn_low)
    grad_mixed = (
        project_back(grad_attn_low, w_out)
        .astype(jnp.bfloat16)
        .reshape(local_blocks, BLOCK, HEADS, head_dim)
    )
    block_ids = jnp.arange(local_blocks, dtype=jnp.int32)
    keep_sparse = jnp.where(is_edge & (block_ids == edge_slot), 0.0, 1.0).astype(jnp.bfloat16)
    grad_sparse = grad_mixed * keep_sparse[:, None, None, None]
    scores = sparse_scores(query_heads, key_picked, saved["key_valid"], score_scale)
    attn_prob = jnp.exp(scores - saved["log_sparse"][..., None])
    grad_prob = jnp.einsum(
        "qihd,hqkd->hqik", grad_sparse, value_picked, preferred_element_type=jnp.float32
    )
    grad_value_picked = jnp.einsum(
        "hqik,qihd->hqkd",
        attn_prob.astype(jnp.bfloat16),
        grad_sparse,
        preferred_element_type=jnp.float32,
    )
    grad_scores = softmax_back(attn_prob, grad_prob, score_scale)
    grad_query_sparse = jnp.einsum(
        "hqik,hqkd->qihd", grad_scores, key_picked, preferred_element_type=jnp.float32
    )
    grad_key_picked = jnp.einsum(
        "hqik,hqid->hqkd", grad_scores, query_heads, preferred_element_type=jnp.float32
    )
    head_index = jnp.arange(HEADS)[:, None, None]
    slot_count = key_slots.shape[2]
    table_shape = (HEADS, all_blocks, BLOCK * head_dim)
    grad_key_table = (
        jnp.zeros(table_shape, jnp.float32)
        .at[head_index, key_slots]
        .add(grad_key_picked.reshape(HEADS, local_blocks, slot_count, BLOCK * head_dim))
    )
    grad_value_table = (
        jnp.zeros(table_shape, jnp.float32)
        .at[head_index, key_slots]
        .add(grad_value_picked.reshape(HEADS, local_blocks, slot_count, BLOCK * head_dim))
    )
    grad_edge_block = lax.dynamic_index_in_dim(grad_mixed, edge_slot, 0, keepdims=False)
    flat_shape = (HEADS, all_blocks * BLOCK, head_dim)
    grad_query_edge, grad_key_edge, grad_value_edge = lax.cond(
        is_edge,
        lambda: dense_backward(
            saved["query_edge"],
            saved["key_flat"],
            saved["value_flat"],
            grad_edge_block,
            saved["log_edge"],
            score_scale,
        ),
        lambda: (
            jnp.zeros((BLOCK, HEADS, head_dim), jnp.float32),
            jnp.zeros(flat_shape, jnp.float32),
            jnp.zeros(flat_shape, jnp.float32),
        ),
    )
    grad_key_table = grad_key_table + grad_key_edge.reshape(table_shape)
    grad_value_table = grad_value_table + grad_value_edge.reshape(table_shape)
    grad_key_own, grad_value_own = (
        lax.psum_scatter(
            from_table(grad_key_table).astype(jnp.bfloat16), "seq", scatter_dimension=0, tiled=True
        ).astype(jnp.float32),
        lax.psum_scatter(
            from_table(grad_value_table).astype(jnp.bfloat16),
            "seq",
            scatter_dimension=0,
            tiled=True,
        ).astype(jnp.float32),
    )
    current = lax.dynamic_index_in_dim(grad_query_sparse, edge_slot, 0, keepdims=False)
    grad_query_all = lax.dynamic_update_index_in_dim(
        grad_query_sparse, current + grad_query_edge, edge_slot, 0
    )
    grad_query_low = grad_query_all.reshape(token_count, HEADS * head_dim).astype(jnp.bfloat16)
    grad_key_low = grad_key_own.astype(jnp.bfloat16)
    grad_value_low = grad_value_own.astype(jnp.bfloat16)
    normed_low = saved["normed_low"]
    grad_w_query = weight_grad(normed_low, grad_query_low)
    grad_w_key = weight_grad(normed_low, grad_key_low)
    grad_w_value = weight_grad(normed_low, grad_value_low)
    grad_query_bias = column_sum(grad_query_low)
    grad_value_bias = column_sum(grad_value_low)
    grad_normed = (
        project_back(grad_query_low, w_query)
        + project_back(grad_key_low, w_key)
        + project_back(grad_value_low, w_value)
    )
    grad_inputs, grad_ln1_gain, grad_ln1_bias = saved["pull_first"](grad_normed)
    grad_inputs = grad_inputs + grad_middle
    grads = (
        grad_w_query,
        grad_w_key,
        grad_w_value,
        grad_w_out,
        grad_w_up,
        grad_w_down,
        grad_ln1_gain,
        grad_ln1_bias,
        grad_query_bias,
        grad_value_bias,
        grad_out_bias,
        grad_ln2_gain,
        grad_ln2_bias,
        grad_up_bias,
        grad_down_bias,
    )
    return (grad_inputs, grads)


def on_device(
    inputs,
    grad_out,
    random_blocks,
    w_query,
    w_key,
    w_value,
    w_out,
    w_up,
    w_down,
    ln1_gain,
    ln1_bias,
    query_bias,
    value_bias,
    out_bias,
    ln2_gain,
    ln2_bias,
    up_bias,
    down_bias,
):
    shards = (
        w_query,
        w_key,
        w_value,
        w_out,
        w_up,
        w_down,
        ln1_gain,
        ln1_bias,
        query_bias,
        value_bias,
        out_bias,
        ln2_gain,
        ln2_bias,
        up_bias,
        down_bias,
    )

    def micro_step(carried, sequence):
        in_rows, grad_rows, random_ids = sequence
        forward_weights = (
            lax.all_gather(w_query, ("dp", "seq"), axis=0, tiled=True),
            lax.all_gather(w_key, ("dp", "seq"), axis=0, tiled=True),
            lax.all_gather(w_value, ("dp", "seq"), axis=0, tiled=True),
            lax.all_gather(w_out, ("dp", "seq"), axis=0, tiled=True),
            lax.all_gather(w_up, ("dp", "seq"), axis=0, tiled=True),
            lax.all_gather(w_down, ("dp", "seq"), axis=0, tiled=True),
            lax.all_gather(ln1_gain, ("dp", "seq"), axis=0, tiled=True),
            lax.all_gather(ln1_bias, ("dp", "seq"), axis=0, tiled=True),
            lax.all_gather(query_bias, ("dp", "seq"), axis=0, tiled=True),
            lax.all_gather(value_bias, ("dp", "seq"), axis=0, tiled=True),
            lax.all_gather(out_bias, ("dp", "seq"), axis=0, tiled=True),
            lax.all_gather(ln2_gain, ("dp", "seq"), axis=0, tiled=True),
            lax.all_gather(ln2_bias, ("dp", "seq"), axis=0, tiled=True),
            lax.all_gather(up_bias, ("dp", "seq"), axis=0, tiled=True),
            lax.all_gather(down_bias, ("dp", "seq"), axis=0, tiled=True),
        )
        saved, result = run_forward(forward_weights, in_rows, random_ids)
        backward_weights = (
            lax.all_gather(w_query, ("dp", "seq"), axis=0, tiled=True),
            lax.all_gather(w_key, ("dp", "seq"), axis=0, tiled=True),
            lax.all_gather(w_value, ("dp", "seq"), axis=0, tiled=True),
            lax.all_gather(w_out, ("dp", "seq"), axis=0, tiled=True),
            lax.all_gather(w_up, ("dp", "seq"), axis=0, tiled=True),
            lax.all_gather(w_down, ("dp", "seq"), axis=0, tiled=True),
            lax.all_gather(ln1_gain, ("dp", "seq"), axis=0, tiled=True),
            lax.all_gather(ln1_bias, ("dp", "seq"), axis=0, tiled=True),
            lax.all_gather(query_bias, ("dp", "seq"), axis=0, tiled=True),
            lax.all_gather(value_bias, ("dp", "seq"), axis=0, tiled=True),
            lax.all_gather(out_bias, ("dp", "seq"), axis=0, tiled=True),
            lax.all_gather(ln2_gain, ("dp", "seq"), axis=0, tiled=True),
            lax.all_gather(ln2_bias, ("dp", "seq"), axis=0, tiled=True),
            lax.all_gather(up_bias, ("dp", "seq"), axis=0, tiled=True),
            lax.all_gather(down_bias, ("dp", "seq"), axis=0, tiled=True),
        )
        grad_in, grads = run_backward(backward_weights, saved, grad_rows)
        summed = (
            lax.psum_scatter(grads[0], ("dp", "seq"), scatter_dimension=0, tiled=True),
            lax.psum_scatter(grads[1], ("dp", "seq"), scatter_dimension=0, tiled=True),
            lax.psum_scatter(grads[2], ("dp", "seq"), scatter_dimension=0, tiled=True),
            lax.psum_scatter(grads[3], ("dp", "seq"), scatter_dimension=0, tiled=True),
            lax.psum_scatter(grads[4], ("dp", "seq"), scatter_dimension=0, tiled=True),
            lax.psum_scatter(grads[5], ("dp", "seq"), scatter_dimension=0, tiled=True),
            lax.psum_scatter(grads[6], ("dp", "seq"), scatter_dimension=0, tiled=True),
            lax.psum_scatter(grads[7], ("dp", "seq"), scatter_dimension=0, tiled=True),
            lax.psum_scatter(grads[8], ("dp", "seq"), scatter_dimension=0, tiled=True),
            lax.psum_scatter(grads[9], ("dp", "seq"), scatter_dimension=0, tiled=True),
            lax.psum_scatter(grads[10], ("dp", "seq"), scatter_dimension=0, tiled=True),
            lax.psum_scatter(grads[11], ("dp", "seq"), scatter_dimension=0, tiled=True),
            lax.psum_scatter(grads[12], ("dp", "seq"), scatter_dimension=0, tiled=True),
            lax.psum_scatter(grads[13], ("dp", "seq"), scatter_dimension=0, tiled=True),
            lax.psum_scatter(grads[14], ("dp", "seq"), scatter_dimension=0, tiled=True),
        )
        carried = tuple((left + right for left, right in zip(carried, summed)))
        return (carried, (result, grad_in))

    initial = tuple((jnp.zeros(shard_part.shape, jnp.float32) for shard_part in shards))
    carried, (results, grads_in) = lax.scan(micro_step, initial, (inputs, grad_out, random_blocks))
    return (results, grads_in) + tuple(carried)


def solution(mesh):
    in_specs = (
        P("dp", "seq", None),
        P("dp", "seq", None),
        P("dp", None, "seq", None),
        P(("dp", "seq"), None),
        P(("dp", "seq"), None),
        P(("dp", "seq"), None),
        P(("dp", "seq"), None),
        P(("dp", "seq"), None),
        P(("dp", "seq"), None),
        P(("dp", "seq")),
        P(("dp", "seq")),
        P(("dp", "seq")),
        P(("dp", "seq")),
        P(("dp", "seq")),
        P(("dp", "seq")),
        P(("dp", "seq")),
        P(("dp", "seq")),
        P(("dp", "seq")),
    )
    out_specs = (
        P("dp", "seq", None),
        P("dp", "seq", None),
        P(("dp", "seq"), None),
        P(("dp", "seq"), None),
        P(("dp", "seq"), None),
        P(("dp", "seq"), None),
        P(("dp", "seq"), None),
        P(("dp", "seq"), None),
        P(("dp", "seq")),
        P(("dp", "seq")),
        P(("dp", "seq")),
        P(("dp", "seq")),
        P(("dp", "seq")),
        P(("dp", "seq")),
        P(("dp", "seq")),
        P(("dp", "seq")),
        P(("dp", "seq")),
    )
    return jax.shard_map(
        on_device, mesh=mesh, in_specs=in_specs, out_specs=out_specs, check_vma=False
    )
```

profile of v0, /device:TPU:8, one launch (start us, length us, event | category | flops | bytes accessed | tf_op | source)
XLA Modules:
  0.0 4311.1 jit_solution(2451414137044691808)
XLA Ops:
  7.3 4296.9 %while.45 = (s32[]{:T(128)}, f32[32,1024]{1,0:T(8,128)}, f32[32,1024]{1,0:T(8,128)}, f32[32,1024]{1,0:T(8,128)}, f32[32,1024]{1,0:T(8,128)}, /*index=5*/f32[32,4...) while((s32[]{:T(128)}, f32[32,1024]{1,0:T(8,128)}, ...), condition=%wide.region_47.48_spmd.clone, body=%wide.region_0.47_spmd.clone.sunk | while | flops 43095355392 | bytes 1486486528 | solution.py:488
  16.6 40.9 all-reduce.29
  72.3 54.7 %all-gather.17.cloned.1.call-done = bf16[1024,1024]{1,0:T(8,128)(2,1)} async-done(((bf16[32,1024]{1,0:T(8,128)(2,1)}), bf16[1024,1024]{1,0:T(8,128)(2,1)}) %all-gather.17.cloned.1.call-update) | async-done | bytes 2097168 | tf_op jit(solution)/shard_map/while/body/eval_jaxpr/all_gather | solution.py:434
  135.3 54.1 %all-gather.3 = bf16[32,1,128]{2,1,0:T(2,128)(2,1)S(1)} all-gather(bf16[1,1,128]{2,1,0:T(2,128)(2,1)S(1)} %bitcast.281), channel_id=1, replica_groups=mesh['dp'=16,'seq'=2] {'dp','seq'}, dimensions={0}, use_global_device_ids=true | all-gather | bytes 8448 | tf_op jit(solution)/shard_map/while/body/eval_jaxpr/all_gather | solution.py:445
  203.9 15.9 all-gather.15.cloned.1.call-done
  231.8 22.6 all-gather.19.cloned.1.call-done
  289.3 40.8 gather_fusion
  330.1 35.9 gather_fusion.1
  366.0 23.6 reshape.508
  389.6 23.7 reshape.505
  523.0 67.5 %fusion.299 = f32[16,8,512,64]{3,2,1,0:T(8,128)} fusion(bf16[8,64,16,64]{1,3,0,2:T(8,128)(2,1)} %copy.206, f32[16,8,64,512]{3,2,1,0:T(8,128)} %fusion.295, f32[16,8,64,512]{3,2,1,0:T(8,128)} %get-tuple-element.1112, f32[16,8,64]{2,1,0:T(8,128)S(1)} %log_add_fusion.3), kind=kOutput, calls=%fused_computation.79.clone.1 | convolution fusion | flops 566239744 | bytes 51412992 | tf_op jit(solution)/shard_map/while/body/eval_jaxpr/hqik,hqid->hqkd/dot_general | solution.py:304
  590.4 27.9 reshape.512
  618.4 58.4 %conditional.7 = (f32[64,16,64]{2,0,1:T(8,128)S(1)}, f32[16,16,4096]{2,1,0:T(8,128)}, f32[16,16,4096]{2,1,0:T(8,128)}) conditional(s32[]{:T(128)} %convert_element_type.416, () %tuple.126, (bf16[16,64,64]{1,2,0:T(8,128)(2,1)S(1)}, bf16[16,1024,64]{1,2,0:T(8,128)(2,1)}, f32[16,64]{1,0:T(8,128)S(1)}, bf16[8,64,16,64]{3,2,1,0:T(8,128)(2,1)}, ...), branch_computations={%region_14.14_spmd, %region_15.16_spmd} | conditional | flops 693112832 | bytes 84947568 | solution.py:322
  676.8 31.1 scatter_fusion
  732.8 18.7 fusion.301
  751.5 28.0 reshape.513
  779.5 31.4 scatter_fusion.1
  836.9 59.5 %multiply_convert_fusion.10 = bf16[16,8,64,512]{3,2,1,0:T(8,128)(2,1)} fusion(f32[16,8,64,512]{3,2,1,0:T(8,128)} %fusion.295, f32[16,8,64,512]{3,2,1,0:T(8,128)} %get-tuple-element.1112, f32[16,8,64]{2,1,0:T(8,128)S(1)} %log_add_fusion.3), kind=kOutput, calls=%fused_computation.46.clone.2 | output fusion | flops 29368832 | bytes 41975808 | tf_op jit(solution)/shard_map/while/body/eval_jaxpr/sub | solution.py:112
  982.5 41.6 all-reduce.30
  1030.7 107.7 %reduce-scatter.9.cloned.1.call-done = f32[32,1024]{1,0:T(8,128)} async-done(((f32[1024,1024]{1,0:T(8,128)}), f32[32,1024]{1,0:T(8,128)}) %reduce-scatter.9.cloned.1.call-update) | async-done | bytes 131088 | tf_op jit(solution)/shard_map/while/body/eval_jaxpr/reduce_scatter | solution.py:468
  1139.9 138.9 %reduce-scatter.13.cloned.1.call-done = f32[32,1024]{1,0:T(8,128)} async-done(((f32[1024,1024]{1,0:T(8,128)}), f32[32,1024]{1,0:T(8,128)}) %reduce-scatter.13.cloned.1.call-update) | async-done | bytes 131088 | tf_op jit(solution)/shard_map/while/body/eval_jaxpr/reduce_scatter | solution.py:469
  1279.7 139.3 %reduce-scatter.17.cloned.1.call-done = f32[32,1024]{1,0:T(8,128)} async-done(((f32[1024,1024]{1,0:T(8,128)}), f32[32,1024]{1,0:T(8,128)}) %reduce-scatter.17.cloned.1.call-update) | async-done | bytes 131088 | tf_op jit(solution)/shard_map/while/body/eval_jaxpr/reduce_scatter | solution.py:470
  1420.0 368.0 %reduce-scatter.23.cloned.1.call-done = f32[128,1024]{1,0:T(8,128)} async-done(((f32[4096,1024]{1,0:T(8,128)}), f32[128,1024]{1,0:T(8,128)}) %reduce-scatter.23.cloned.1.call-update) | async-done | bytes 524304 | tf_op jit(solution)/shard_map/while/body/eval_jaxpr/reduce_scatter | solution.py:473
  1789.2 359.4 %reduce-scatter.21.cloned.1.call-done = f32[32,4096]{1,0:T(8,128)} async-done(((f32[1024,4096]{1,0:T(8,128)}), f32[32,4096]{1,0:T(8,128)}) %reduce-scatter.21.cloned.1.call-update) | async-done | bytes 524304 | tf_op jit(solution)/shard_map/while/body/eval_jaxpr/reduce_scatter | solution.py:472
  2159.5 40.9 all-reduce.29
  2215.3 54.5 %all-gather.17.cloned.1.call-done = bf16[1024,1024]{1,0:T(8,128)(2,1)} async-done(((bf16[32,1024]{1,0:T(8,128)(2,1)}), bf16[1024,1024]{1,0:T(8,128)(2,1)}) %all-gather.17.cloned.1.call-update) | async-done | bytes 2097168 | tf_op jit(solution)/shard_map/while/body/eval_jaxpr/all_gather | solution.py:434
  2278.1 54.1 %all-gather.3 = bf16[32,1,128]{2,1,0:T(2,128)(2,1)S(1)} all-gather(bf16[1,1,128]{2,1,0:T(2,128)(2,1)S(1)} %bitcast.281), channel_id=1, replica_groups=mesh['dp'=16,'seq'=2] {'dp','seq'}, dimensions={0}, use_global_device_ids=true | all-gather | bytes 8448 | tf_op jit(solution)/shard_map/while/body/eval_jaxpr/all_gather | solution.py:445
  2346.8 15.9 all-gather.15.cloned.1.call-done
  2374.6 22.8 all-gather.19.cloned.1.call-done
  2432.3 41.3 gather_fusion
  2473.7 45.5 %gather_fusion.1 = bf16[1024,4096]{1,0:T(8,128)(2,1)} fusion(bf16[16,16,4096]{2,1,0:T(8,128)(2,1)S(1)} %reshape.507, s32[1024]{0:T(1024)S(1)} %reshape.504), kind=kCustom, calls=%fused_computation.1.clone.clone.1 | custom fusion | bytes 16785408 | tf_op jit(solution)/shard_map/while/body/eval_jaxpr/gather | solution.py:81
  2519.2 23.6 reshape.508
  2542.8 23.7 reshape.505
  2675.4 67.2 %fusion.299 = f32[16,8,512,64]{3,2,1,0:T(8,128)} fusion(bf16[8,64,16,64]{1,3,0,2:T(8,128)(2,1)} %copy.206, f32[16,8,64,512]{3,2,1,0:T(8,128)} %fusion.295, f32[16,8,64,512]{3,2,1,0:T(8,128)} %get-tuple-element.1112, f32[16,8,64]{2,1,0:T(8,128)S(1)} %log_add_fusion.3), kind=kOutput, calls=%fused_computation.79.clone.1 | convolution fusion | flops 566239744 | bytes 51412992 | tf_op jit(solution)/shard_map/while/body/eval_jaxpr/hqik,hqid->hqkd/dot_general | solution.py:304
  2742.6 27.9 reshape.512
  2770.5 58.6 %conditional.7 = (f32[64,16,64]{2,0,1:T(8,128)S(1)}, f32[16,16,4096]{2,1,0:T(8,128)}, f32[16,16,4096]{2,1,0:T(8,128)}) conditional(s32[]{:T(128)} %convert_element_type.416, () %tuple.126, (bf16[16,64,64]{1,2,0:T(8,128)(2,1)S(1)}, bf16[16,1024,64]{1,2,0:T(8,128)(2,1)}, f32[16,64]{1,0:T(8,128)S(1)}, bf16[8,64,16,64]{3,2,1,0:T(8,128)(2,1)}, ...), branch_computations={%region_14.14_spmd, %region_15.16_spmd} | conditional | flops 693112832 | bytes 84947568 | solution.py:322
  2829.1 31.1 scatter_fusion
  2885.1 18.7 fusion.301
  2903.8 28.0 reshape.513
  2931.8 31.4 scatter_fusion.1
  2989.2 59.4 %multiply_convert_fusion.10 = bf16[16,8,64,512]{3,2,1,0:T(8,128)(2,1)} fusion(f32[16,8,64,512]{3,2,1,0:T(8,128)} %fusion.295, f32[16,8,64,512]{3,2,1,0:T(8,128)} %get-tuple-element.1112, f32[16,8,64]{2,1,0:T(8,128)S(1)} %log_add_fusion.3), kind=kOutput, calls=%fused_computation.46.clone.2 | output fusion | flops 29368832 | bytes 41975808 | tf_op jit(solution)/shard_map/while/body/eval_jaxpr/sub | solution.py:112
  3084.9 15.5 fusion.305
  3134.7 41.7 all-reduce.30
  3183.0 107.2 %reduce-scatter.9.cloned.1.call-done = f32[32,1024]{1,0:T(8,128)} async-done(((f32[1024,1024]{1,0:T(8,128)}), f32[32,1024]{1,0:T(8,128)}) %reduce-scatter.9.cloned.1.call-update) | async-done | bytes 131088 | tf_op jit(solution)/shard_map/while/body/eval_jaxpr/reduce_scatter | solution.py:468
  3291.8 139.2 %reduce-scatter.13.cloned.1.call-done = f32[32,1024]{1,0:T(8,128)} async-done(((f32[1024,1024]{1,0:T(8,128)}), f32[32,1024]{1,0:T(8,128)}) %reduce-scatter.13.cloned.1.call-update) | async-done | bytes 131088 | tf_op jit(solution)/shard_map/while/body/eval_jaxpr/reduce_scatter | solution.py:469
  3432.0 139.6 %reduce-scatter.17.cloned.1.call-done = f32[32,1024]{1,0:T(8,128)} async-done(((f32[1024,1024]{1,0:T(8,128)}), f32[32,1024]{1,0:T(8,128)}) %reduce-scatter.17.cloned.1.call-update) | async-done | bytes 131088 | tf_op jit(solution)/shard_map/while/body/eval_jaxpr/reduce_scatter | solution.py:470
  3572.6 367.9 %reduce-scatter.23.cloned.1.call-done = f32[128,1024]{1,0:T(8,128)} async-done(((f32[4096,1024]{1,0:T(8,128)}), f32[128,1024]{1,0:T(8,128)}) %reduce-scatter.23.cloned.1.call-update) | async-done | bytes 524304 | tf_op jit(solution)/shard_map/while/body/eval_jaxpr/reduce_scatter | solution.py:473
  3941.7 359.6 %reduce-scatter.21.cloned.1.call-done = f32[32,4096]{1,0:T(8,128)} async-done(((f32[1024,4096]{1,0:T(8,128)}), f32[32,4096]{1,0:T(8,128)}) %reduce-scatter.21.cloned.1.call-update) | async-done | bytes 524304 | tf_op jit(solution)/shard_map/while/body/eval_jaxpr/reduce_scatter | solution.py:472
  (776 shorter events, 810.1 us)
Async XLA Ops:
  7.6 60.8 %all-gather.13.cloned.1.call-start = ((), (), s32[]{:S(2)}) async-start(), calls=%async_computation.8 | async-start | bytes 2162688 | tf_op jit(solution)/shard_map/while/body/eval_jaxpr/all_gather | solution.py:433
  8.3 118.7 %all-gather.17.cloned.1.call-start = ((), (), s32[]{:S(2)}) async-start(), calls=%async_computation.10 | async-start | bytes 2162688 | tf_op jit(solution)/shard_map/while/body/eval_jaxpr/all_gather | solution.py:434
  9.1 186.4 %all-gather.21.cloned.1.call-start = ((), (), s32[]{:S(2)}) async-start(), calls=%async_computation.12 | async-start | bytes 2162688 | tf_op jit(solution)/shard_map/while/body/eval_jaxpr/all_gather | solution.py:432
  9.8 210.0 %all-gather.15.cloned.1.call-start = ((), (), s32[]{:S(2)}) async-start(), calls=%async_computation.9 | async-start | bytes 3145728 | tf_op jit(solution)/shard_map/while/body/eval_jaxpr/all_gather | solution.py:164
  72.2 182.2 %all-gather.19.cloned.1.call-start = ((), (), s32[]{:S(2)}) async-start(), calls=%async_computation.11 | async-start | bytes 3145728 | tf_op jit(solution)/shard_map/while/body/eval_jaxpr/all_gather | solution.py:165
  130.9 331.9 %all-gather.23.cloned.1.call-start = ((), (), s32[]{:S(2)}) async-start(), calls=%async_computation.13 | async-start | bytes 2162688 | tf_op jit(solution)/shard_map/while/body/eval_jaxpr/all_gather | solution.py:435
  131.5 335.7 %all-gather.25.cloned.1.call-start = ((), (), s32[]{:S(2)}) async-start(), calls=%async_computation.14 | async-start | bytes 8650752 | tf_op jit(solution)/shard_map/while/body/eval_jaxpr/all_gather | solution.py:436
  132.2 345.7 %all-gather.27.cloned.1.call-start = ((), (), s32[]{:S(2)}) async-start(), calls=%async_computation.15 | async-start | bytes 8650752 | tf_op jit(solution)/shard_map/while/body/eval_jaxpr/all_gather | solution.py:455
  133.0 789.0 %reduce-scatter.11.cloned.1.call-start = ((), (), s32[]{:S(2)}) async-start(), calls=%async_computation.17 | async-start | bytes 3145728 | tf_op jit(solution)/shard_map/while/body/eval_jaxpr/reduce_scatter | solution.py:341
  732.8 195.3 %reduce-scatter.15.cloned.1.call-start = ((), (), s32[]{:S(2)}) async-start(), calls=%async_computation.19 | async-start | bytes 3145728 | tf_op jit(solution)/shard_map/while/body/eval_jaxpr/reduce_scatter | solution.py:344
  833.4 196.3 %reduce-scatter.19.cloned.1.call-start = ((), (), s32[]{:S(2)}) async-start(), calls=%async_computation.21 | async-start | bytes 4325376 | tf_op jit(solution)/shard_map/while/body/eval_jaxpr/reduce_scatter | solution.py:471
  836.8 301.5 %reduce-scatter.9.cloned.1.call-start = ((), (), s32[]{:S(2)}) async-start(), calls=%async_computation.16 | async-start | bytes 4325376 | tf_op jit(solution)/shard_map/while/body/eval_jaxpr/reduce_scatter | solution.py:468
  921.8 356.9 %reduce-scatter.13.cloned.1.call-start = ((), (), s32[]{:S(2)}) async-start(), calls=%async_computation.18 | async-start | bytes 4325376 | tf_op jit(solution)/shard_map/while/body/eval_jaxpr/reduce_scatter | solution.py:469
  927.7 491.3 %reduce-scatter.17.cloned.1.call-start = ((), (), s32[]{:S(2)}) async-start(), calls=%async_computation.20 | async-start | bytes 4325376 | tf_op jit(solution)/shard_map/while/body/eval_jaxpr/reduce_scatter | solution.py:470
  932.6 855.4 %reduce-scatter.23.cloned.1.call-start = ((), (), s32[]{:S(2)}) async-start(), calls=%async_computation.23 | async-start | bytes 17301504 | tf_op jit(solution)/shard_map/while/body/eval_jaxpr/reduce_scatter | solution.py:473
  948.1 1200.5 %reduce-scatter.21.cloned.1.call-start = ((), (), s32[]{:S(2)}) async-start(), calls=%async_computation.22 | async-start | bytes 17301504 | tf_op jit(solution)/shard_map/while/body/eval_jaxpr/reduce_scatter | solution.py:472
  1027.9 250.9 %copy-start.37 = (f32[32,1024]{1,0:T(8,128)S(1)}, f32[32,1024]{1,0:T(8,128)}, u32[]{:S(2)}) copy-start(f32[32,1024]{1,0:T(8,128)} %get-tuple-element.1222) | copy-start | bytes 393220 | tf_op jit(solution)/shard_map/while
  1027.9 391.1 %copy-start.35 = (f32[32,1024]{1,0:T(8,128)S(1)}, f32[32,1024]{1,0:T(8,128)}, u32[]{:S(2)}) copy-start(f32[32,1024]{1,0:T(8,128)} %get-tuple-element.1223) | copy-start | bytes 393220 | tf_op jit(solution)/shard_map/while
  1027.9 760.0 %copy-start.29 = (f32[128,1024]{1,0:T(8,128)S(1)}, f32[128,1024]{1,0:T(8,128)}, u32[]{:S(2)}) copy-start(f32[128,1024]{1,0:T(8,128)} %get-tuple-element.1226) | copy-start | bytes 1572868 | tf_op jit(solution)/shard_map/while
  1027.9 1120.7 %copy-start.31 = (f32[32,4096]{1,0:T(8,128)S(1)}, f32[32,4096]{1,0:T(8,128)}, u32[]{:S(2)}) copy-start(f32[32,4096]{1,0:T(8,128)} %get-tuple-element.1225) | copy-start | bytes 1572868 | tf_op jit(solution)/shard_map/while
  1030.7 1119.1 %copy-start.34 = (f32[32,1024]{1,0:T(8,128)}, f32[32,1024]{1,0:T(8,128)S(1)}, u32[]{:S(2)}) copy-start(f32[32,1024]{1,0:T(8,128)S(1)} %select_add_fusion.15) | copy-start | bytes 393220 | tf_op jit(solution)/shard_map/while
  1279.7 870.1 %copy-start.38 = (f32[32,1024]{1,0:T(8,128)}, f32[32,1024]{1,0:T(8,128)S(1)}, u32[]{:S(2)}) copy-start(f32[32,1024]{1,0:T(8,128)S(1)} %select_add_fusion.13) | copy-start | bytes 393220 | tf_op jit(solution)/shard_map/while
  1419.9 729.9 %copy-start.36 = (f32[32,1024]{1,0:T(8,128)}, f32[32,1024]{1,0:T(8,128)S(1)}, u32[]{:S(2)}) copy-start(f32[32,1024]{1,0:T(8,128)S(1)} %select_add_fusion.14) | copy-start | bytes 393220 | tf_op jit(solution)/shard_map/while
  1789.2 360.7 %copy-start.30 = (f32[128,1024]{1,0:T(8,128)}, f32[128,1024]{1,0:T(8,128)S(1)}, u32[]{:S(2)}) copy-start(f32[128,1024]{1,0:T(8,128)S(1)} %select_add_fusion.17) | copy-start | bytes 1572868 | tf_op jit(solution)/shard_map/while
  2150.8 60.6 %all-gather.13.cloned.1.call-start = ((), (), s32[]{:S(2)}) async-start(), calls=%async_computation.8 | async-start | bytes 2162688 | tf_op jit(solution)/shard_map/while/body/eval_jaxpr/all_gather | solution.py:433
  2151.4 118.5 %all-gather.17.cloned.1.call-start = ((), (), s32[]{:S(2)}) async-start(), calls=%async_computation.10 | async-start | bytes 2162688 | tf_op jit(solution)/shard_map/while/body/eval_jaxpr/all_gather | solution.py:434
  2152.0 186.3 %all-gather.21.cloned.1.call-start = ((), (), s32[]{:S(2)}) async-start(), calls=%async_computation.12 | async-start | bytes 2162688 | tf_op jit(solution)/shard_map/while/body/eval_jaxpr/all_gather | solution.py:432
  2152.7 210.0 %all-gather.15.cloned.1.call-start = ((), (), s32[]{:S(2)}) async-start(), calls=%async_computation.9 | async-start | bytes 3145728 | tf_op jit(solution)/shard_map/while/body/eval_jaxpr/all_gather | solution.py:164
  2215.2 182.2 %all-gather.19.cloned.1.call-start = ((), (), s32[]{:S(2)}) async-start(), calls=%async_computation.11 | async-start | bytes 3145728 | tf_op jit(solution)/shard_map/while/body/eval_jaxpr/all_gather | solution.py:165
  2273.7 341.4 %all-gather.23.cloned.1.call-start = ((), (), s32[]{:S(2)}) async-start(), calls=%async_computation.13 | async-start | bytes 2162688 | tf_op jit(solution)/shard_map/while/body/eval_jaxpr/all_gather | solution.py:435
  2274.5 345.1 %all-gather.25.cloned.1.call-start = ((), (), s32[]{:S(2)}) async-start(), calls=%async_computation.14 | async-start | bytes 8650752 | tf_op jit(solution)/shard_map/while/body/eval_jaxpr/all_gather | solution.py:436
  2275.2 354.9 %all-gather.27.cloned.1.call-start = ((), (), s32[]{:S(2)}) async-start(), calls=%async_computation.15 | async-start | bytes 8650752 | tf_op jit(solution)/shard_map/while/body/eval_jaxpr/all_gather | solution.py:455
  2275.8 798.4 %reduce-scatter.11.cloned.1.call-start = ((), (), s32[]{:S(2)}) async-start(), calls=%async_computation.17 | async-start | bytes 3145728 | tf_op jit(solution)/shard_map/while/body/eval_jaxpr/reduce_scatter | solution.py:341
  2885.1 195.2 %reduce-scatter.15.cloned.1.call-start = ((), (), s32[]{:S(2)}) async-start(), calls=%async_computation.19 | async-start | bytes 3145728 | tf_op jit(solution)/shard_map/while/body/eval_jaxpr/reduce_scatter | solution.py:344
  2985.7 196.3 %reduce-scatter.19.cloned.1.call-start = ((), (), s32[]{:S(2)}) async-start(), calls=%async_computation.21 | async-start | bytes 4325376 | tf_op jit(solution)/shard_map/while/body/eval_jaxpr/reduce_scatter | solution.py:471
  2989.1 301.1 %reduce-scatter.9.cloned.1.call-start = ((), (), s32[]{:S(2)}) async-start(), calls=%async_computation.16 | async-start | bytes 4325376 | tf_op jit(solution)/shard_map/while/body/eval_jaxpr/reduce_scatter | solution.py:468
  3074.1 356.9 %reduce-scatter.13.cloned.1.call-start = ((), (), s32[]{:S(2)}) async-start(), calls=%async_computation.18 | async-start | bytes 4325376 | tf_op jit(solution)/shard_map/while/body/eval_jaxpr/reduce_scatter | solution.py:469
  3079.9 491.7 %reduce-scatter.17.cloned.1.call-start = ((), (), s32[]{:S(2)}) async-start(), calls=%async_computation.20 | async-start | bytes 4325376 | tf_op jit(solution)/shard_map/while/body/eval_jaxpr/reduce_scatter | solution.py:470
  3084.8 855.7 %reduce-scatter.23.cloned.1.call-start = ((), (), s32[]{:S(2)}) async-start(), calls=%async_computation.23 | async-start | bytes 17301504 | tf_op jit(solution)/shard_map/while/body/eval_jaxpr/reduce_scatter | solution.py:473
  3100.4 1200.9 %reduce-scatter.21.cloned.1.call-start = ((), (), s32[]{:S(2)}) async-start(), calls=%async_computation.22 | async-start | bytes 17301504 | tf_op jit(solution)/shard_map/while/body/eval_jaxpr/reduce_scatter | solution.py:472
  3180.2 250.8 %copy-start.37 = (f32[32,1024]{1,0:T(8,128)S(1)}, f32[32,1024]{1,0:T(8,128)}, u32[]{:S(2)}) copy-start(f32[32,1024]{1,0:T(8,128)} %get-tuple-element.1222) | copy-start | bytes 393220 | tf_op jit(solution)/shard_map/while
  3180.2 391.4 %copy-start.35 = (f32[32,1024]{1,0:T(8,128)S(1)}, f32[32,1024]{1,0:T(8,128)}, u32[]{:S(2)}) copy-start(f32[32,1024]{1,0:T(8,128)} %get-tuple-element.1223) | copy-start | bytes 393220 | tf_op jit(solution)/shard_map/while
  3180.2 760.2 %copy-start.29 = (f32[128,1024]{1,0:T(8,128)S(1)}, f32[128,1024]{1,0:T(8,128)}, u32[]{:S(2)}) copy-start(f32[128,1024]{1,0:T(8,128)} %get-tuple-element.1226) | copy-start | bytes 1572868 | tf_op jit(solution)/shard_map/while
  3180.2 1121.0 %copy-start.31 = (f32[32,4096]{1,0:T(8,128)S(1)}, f32[32,4096]{1,0:T(8,128)}, u32[]{:S(2)}) copy-start(f32[32,4096]{1,0:T(8,128)} %get-tuple-element.1225) | copy-start | bytes 1572868 | tf_op jit(solution)/shard_map/while
  3183.0 1119.5 %copy-start.34 = (f32[32,1024]{1,0:T(8,128)}, f32[32,1024]{1,0:T(8,128)S(1)}, u32[]{:S(2)}) copy-start(f32[32,1024]{1,0:T(8,128)S(1)} %select_add_fusion.15) | copy-start | bytes 393220 | tf_op jit(solution)/shard_map/while
  3432.0 870.5 %copy-start.38 = (f32[32,1024]{1,0:T(8,128)}, f32[32,1024]{1,0:T(8,128)S(1)}, u32[]{:S(2)}) copy-start(f32[32,1024]{1,0:T(8,128)S(1)} %select_add_fusion.13) | copy-start | bytes 393220 | tf_op jit(solution)/shard_map/while
  3572.6 729.9 %copy-start.36 = (f32[32,1024]{1,0:T(8,128)}, f32[32,1024]{1,0:T(8,128)S(1)}, u32[]{:S(2)}) copy-start(f32[32,1024]{1,0:T(8,128)S(1)} %select_add_fusion.14) | copy-start | bytes 393220 | tf_op jit(solution)/shard_map/while
  3941.7 360.8 %copy-start.30 = (f32[128,1024]{1,0:T(8,128)}, f32[128,1024]{1,0:T(8,128)S(1)}, u32[]{:S(2)}) copy-start(f32[128,1024]{1,0:T(8,128)S(1)} %select_add_fusion.17) | copy-start | bytes 1572868 | tf_op jit(solution)/shard_map/while
  (174 other events, 2919.1 us)
Sparse Core Ops, SparseCore 0:
  11.5 56.8 all-gather.12
  71.5 55.4 all-gather.16
  130.1 55.4 all-gather.20
  186.9 32.8 all-gather.14
  221.2 33.1 all-gather.18
  257.3 55.5 all-gather.22
  316.1 77.1 all-gather.24
  396.4 76.0 all-gather.26
  732.9 32.2 reduce-scatter.10
  833.5 32.1 reduce-scatter.14
  868.0 129.6 reduce-scatter.18
  999.8 138.4 reduce-scatter.8
  1140.7 138.0 reduce-scatter.12
  1280.9 138.0 reduce-scatter.16
  1421.1 366.7 reduce-scatter.22
  1790.1 358.4 reduce-scatter.20
  2154.4 56.8 all-gather.12
  2214.3 55.4 all-gather.16
  2272.9 55.4 all-gather.20
  2329.8 32.8 all-gather.14
  2364.2 33.1 all-gather.18
  2400.5 55.5 all-gather.22
  2459.2 77.1 all-gather.24
  2539.4 75.9 all-gather.26
  2885.2 31.9 reduce-scatter.10
  2985.8 31.9 reduce-scatter.14
  3019.9 129.5 reduce-scatter.18
  3151.8 138.3 reduce-scatter.8
  3292.6 138.4 reduce-scatter.12
  3433.1 138.4 reduce-scatter.16
  3573.9 366.5 reduce-scatter.22
  3942.8 358.4 reduce-scatter.20
where the time goes:
time: 4330 us; the launch traced here: 4310 us
  waiting for transfers between devices  2430 us (56%)
  local copies, waits for them, and re-layouts  673 us (16%)
  matrix products  579 us (13%)
  other arithmetic  332 us (8%)
  blocking collectives  273 us (6%)
    reduce_scatter x2, waiting for transfers between devices, micro_step(): lax.psum_scatter(grads[5], ('dp', 'seq'), scatter_dimension=0, tiled=True)  736 us
    reduce_scatter x2, waiting for transfers between devices, micro_step(): lax.psum_scatter(grads[4], ('dp', 'seq'), scatter_dimension=0, tiled=True)  719 us
    reduce_scatter x2, waiting for transfers between devices, micro_step(): lax.psum_scatter(grads[2], ('dp', 'seq'), scatter_dimension=0, tiled=True)  279 us
    reduce_scatter x2, waiting for transfers between devices, micro_step(): lax.psum_scatter(grads[1], ('dp', 'seq'), scatter_dimension=0, tiled=True)  278 us
    reduce_scatter x2, waiting for transfers between devices, micro_step(): lax.psum_scatter(grads[0], ('dp', 'seq'), scatter_dimension=0, tiled=True)  215 us
    while x4, blocking collectives  165 us
    gather x4, local copies, waits for them, and re-layouts, pick_blocks(): picked = table[head_index, key_slots]  164 us
    dot_general x2, matrix products, run_backward(): jnp.einsum('hqik,hqid->hqkd', grad_scores, query_heads, preferred_element...  135 us
  transfers between devices with their start and end apart: 32, of which 18 were waited for; matrix products, arithmetic and copies ran while one was open for 24% of the time, Pallas kernels for 0%

commit v1 on v0

--- a/solution.py
+++ b/solution.py
@@ -1,10 +1,13 @@
 import jax
 import jax.numpy as jnp
 from jax import lax
+from jax.experimental import pallas as pl
+from jax.experimental.pallas import tpu as pltpu
 from jax.sharding import PartitionSpec as P
 
 HEADS = 16
 BLOCK = 64
+BOTH = ("dp", "seq")
 
 
 eps_norm = 1e-05
@@ -388,33 +391,1207 @@
     return (grad_inputs, grads)
 
 
-def on_device(
-    inputs,
-    grad_out,
-    random_blocks,
-    w_query,
-    w_key,
-    w_value,
-    w_out,
-    w_up,
-    w_down,
-    ln1_gain,
-    ln1_bias,
-    query_bias,
-    value_bias,
-    out_bias,
-    ln2_gain,
-    ln2_bias,
-    up_bias,
-    down_bias,
-):
-    shards = (
-        w_query,
-        w_key,
-        w_value,
-        w_out,
-        w_up,
-        w_down,
+def on_device(inputs, grad_out, random_blocks, *shards):
+    weights = tuple(lax.all_gather(part, BOTH, axis=0, tiled=True) for part in shards)
+
+    def micro_step(totals, sequence):
+        in_rows, grad_rows, random_ids = sequence
+        saved, result = run_forward(weights, in_rows, random_ids)
+        grad_in, grads = run_backward(weights, saved, grad_rows)
+        return (tuple(left + right for left, right in zip(totals, grads)), (result, grad_in))
+
+    initial = tuple(jnp.zeros(weight.shape, jnp.float32) for weight in weights)
+    totals, (results, grads_in) = lax.scan(micro_step, initial, (inputs, grad_out, random_blocks))
+    summed = tuple(
+        lax.psum_scatter(total, BOTH, scatter_dimension=0, tiled=True) for total in totals
+    )
+    return (results, grads_in) + summed
+
+
+F32, BF16 = jnp.float32, jnp.bfloat16
+PAIR = 128
+TIMES = dict(
+    cast_far=1,
+    join_first=2,
+    join_up=2,
+    join_plane=2,
+    small_vectors=2,
+    norm_project=2.2,
+    attn_forward=5,
+    out_norm=2,
+    join_low=2.5,
+    feed_forward=9,
+    split_add=0.6,
+    merge_add=3,
+    middle_back=12,
+    grad_wide=1.8,
+    attn_backward=5,
+    split_depth=1.5,
+    input_back=4,
+    pack_vectors=3,
+    fill_far=1.5,
+    last_add=1.5,
+)
+COST = 0.3 * 1e9
+NEAR = tuple((dx, dc, dy) for dx in range(2) for dc in range(2) for dy in range(2))
+
+
+def contract(left, right, left_dim, right_dim):
+    return lax.dot_general(
+        left, right, (((left_dim,), (right_dim,)), ((), ())), preferred_element_type=F32
+    )
+
+
+def held(*shape):
+    zeros = (0,) * len(shape)
+    return pl.BlockSpec(shape, lambda *_: zeros, pipeline_mode=pl.Buffered(1))
+
+
+def whole_ref():
+    return pl.BlockSpec(memory_space=pltpu.HBM)
+
+
+def call(body, name, grid, in_specs, out_specs, out_shape, args, scratch=(), vmem=24, alias=None):
+    spec = pltpu.PrefetchScalarGridSpec(
+        num_scalar_prefetch=1,
+        grid=grid,
+        in_specs=in_specs,
+        out_specs=out_specs,
+        scratch_shapes=scratch,
+    )
+    return pl.pallas_call(
+        body,
+        grid_spec=spec,
+        out_shape=out_shape,
+        name=name,
+        input_output_aliases=alias or {},
+        compiler_params=pltpu.CompilerParams(vmem_limit_bytes=vmem << 20),
+        cost_estimate=pl.CostEstimate(
+            flops=int(TIMES[name] * grid[0] * COST), bytes_accessed=1, transcendentals=1
+        ),
+    )(*args)
+
+
+def shape_of(kind, *shape):
+    return jax.ShapeDtypeStruct(shape, kind)
+
+
+def norm_parts(values):
+    mean = jnp.mean(values, axis=-1, keepdims=True)
+    centre = values - mean
+    spread = jnp.mean(centre * centre, axis=-1, keepdims=True)
+    scale = lax.rsqrt(spread + eps_norm)
+    return centre * scale, scale
+
+
+def norm_back(unit, scale, gain, grad):
+    inner = grad * gain
+    first = jnp.mean(inner, axis=-1, keepdims=True)
+    second = jnp.mean(inner * unit, axis=-1, keepdims=True)
+    return scale * (inner - first - unit * second)
+
+
+def column(values):
+    return jnp.sum(values, axis=0, keepdims=True)
+
+
+def gelu_both(values):
+    root = 2 * 0.7978845608028654
+    cubic = root * 0.044715
+    turn = -1.4426950408889634
+    square = values * values
+    power = jnp.exp2(jnp.minimum(values * (turn * root + (turn * cubic) * square), 126.0))
+    part = pl.reciprocal(1.0 + power, approx=True)
+    hidden = values * part
+    return hidden, part + (hidden - hidden * part) * (root + (3 * cubic) * square)
+
+
+def flip(value, bit):
+    return 1 - value if bit else value
+
+
+def parts_copies(place_ref, part_refs, weight, sems, start, size, into, chunk):
+    copies = []
+    for at, (dx, dc, dy) in enumerate(NEAR):
+        spot = (slice(None), flip(place_ref[1], dx), flip(place_ref[2], dc), flip(place_ref[3], dy))
+        copies.append(
+            pltpu.make_async_copy(
+                part_refs[at].at[:, :, pl.ds(start, size)],
+                weight.at[spot + (slice(None), pl.ds(into, size))],
+                sems.at[chunk, at],
+            )
+        )
+    return copies
+
+
+def weight_scratch(part, columns):
+    depth, rows, _ = part.shape
+    return pltpu.VMEM((depth, 2, 2, 2, rows, columns), BF16)
+
+
+def flat(value):
+    return value.reshape(-1, value.shape[-1])
+
+
+def depth_copies(place_ref, part_refs, weight, sems):
+    depth = weight.shape[0]
+    copies = []
+    for step in range(depth):
+        there = lax.rem(place_ref[0] + depth - step, depth)
+        for dc in range(2):
+            core = flip(place_ref[2], dc)
+            copies.append(
+                pltpu.make_async_copy(
+                    part_refs[2 * step + dc], weight.at[there, :, core], sems.at[there, dc]
+                )
+            )
+    return copies
+
+
+def depth_wait(place_ref, part_refs, weight, sems, at):
+    for dc in range(2):
+        core = flip(place_ref[2], dc)
+        pltpu.make_async_copy(part_refs[dc], weight.at[at, :, core], sems.at[at, dc]).wait()
+
+
+def own_spec(step, width, parts):
+    return pl.BlockSpec((1, step, width), lambda i, p: (p[3], jnp.minimum(i, parts - 1), 0))
+
+
+def far_spec(step, width, parts):
+    return pl.BlockSpec((step, width), lambda i, _: (jnp.maximum(i - parts, 0), 0))
+
+
+def join(place, blocks, moves, shapes, name):
+    def body(place_ref, *refs):
+        ins, outs = refs[: len(blocks)], refs[len(blocks) :]
+        for i, cut, j, spot in moves:
+            outs[j][spot(place_ref)] = ins[i][cut]
+
+    return call(
+        body,
+        name,
+        (1,),
+        [held(*block.shape) for block in blocks],
+        [held(*shape) for shape in shapes],
+        [shape_of(BF16, *shape) for shape in shapes],
+        (place,) + tuple(blocks),
+        vmem=10,
+    )
+
+
+def join_low(place, grad_out, far):
+    half, width = far.shape
+
+    def body(place_ref, own_ref, far_ref, low_ref, sum_ref):
+        low = own_ref[0].astype(BF16)
+        low_ref[:half] = low
+        low_ref[half:] = far_ref[...]
+        sum_ref[...] = column(low.astype(F32)) + column(far_ref[...].astype(F32))
+
+    return call(
+        body,
+        "join_low",
+        (1,),
+        [
+            pl.BlockSpec((1, half, width), lambda i, p: (p[3], 0, 0), pipeline_mode=pl.Buffered(1)),
+            held(half, width),
+        ],
+        [held(2 * half, width), held(1, width)],
+        [shape_of(BF16, 2 * half, width), shape_of(F32, 1, width)],
+        (place, grad_out, far),
+        vmem=12,
+    )
+
+
+def cast_far(place, values):
+    _, half, width = values.shape
+    step = half // 2
+
+    def body(place_ref, values_ref, out_ref):
+        out_ref[...] = values_ref[0].astype(BF16)
+
+    return call(
+        body,
+        "cast_far",
+        (half // step,),
+        [pl.BlockSpec((1, step, width), lambda i, p: (1 - p[3], i, 0))],
+        pl.BlockSpec((step, width), lambda i, _: (i, 0)),
+        shape_of(BF16, half, width),
+        (place, values),
+        vmem=6,
+    )
+
+
+def norm_project(place, inputs, far, gain, shift, left, right, bias):
+    half, width = far.shape
+    columns = bias.shape[1]
+    step = 512
+    left_steps = left[0].shape[-1] // step
+    steps = columns // step
+    sub = 256
+
+    def body(place_ref, own_ref, far_ref, gain_ref, shift_ref, bias_ref, *refs):
+        left_refs, right_refs = refs[:8], refs[8:16]
+        normed_ref, out_ref, weight, sems = refs[16:]
+        at = pl.program_id(0)
+
+        def copies(chunk):
+            refs, start = (left_refs, chunk) if chunk < left_steps else (right_refs, chunk - left_steps)
+            return parts_copies(place_ref, refs, weight, sems, start * step, step, chunk * step, chunk)
+
+        @pl.when(at == 0)
+        def _():
+            for chunk in range(steps):
+                for copy in copies(chunk):
+                    copy.start()
+            for start, rows in ((0, own_ref[0]), (half, far_ref[...])):
+                unit, _ = norm_parts(rows.astype(F32))
+                normed_ref[start : start + half, :] = (
+                    unit * gain_ref[...] + shift_ref[...]
+                ).astype(BF16)
+
+        for chunk in range(steps):
+            @pl.when(at == chunk)
+            def _():
+                for copy in copies(chunk):
+                    copy.wait()
+
+        cut = pl.ds(pl.multiple_of(at * step, step), step)
+        part = flat(weight[:, :, :, :, :, cut])
+        for start in range(0, 2 * half, sub):
+            result = contract(normed_ref[start : start + sub], part, 1, 0) + bias_ref[...]
+            out_ref[start : start + sub] = result.astype(BF16)
+
+    return call(
+        body,
+        "norm_project",
+        (steps,),
+        [
+            pl.BlockSpec((1, half, width), lambda i, p: (p[3], 0, 0), pipeline_mode=pl.Buffered(1)),
+            held(half, width),
+            held(1, width),
+            held(1, width),
+            pl.BlockSpec((1, step), lambda i, _: (0, i)),
+        ]
+        + [whole_ref()] * 16,
+        [
+            pl.BlockSpec((2 * half, width), lambda i, _: (0, 0)),
+            pl.BlockSpec((2 * half, step), lambda i, _: (0, i)),
+        ],
+        [shape_of(BF16, 2 * half, width), shape_of(BF16, 2 * half, columns)],
+        (place, inputs, far, gain, shift, bias) + tuple(left) + tuple(right),
+        scratch=[weight_scratch(left[0], columns), pltpu.SemaphoreType.DMA((steps, 8))],
+        vmem=56,
+    )
+
+
+def out_norm(place, mixed, right, bias, inputs, far, gain, shift, down_bias):
+    half, width = far.shape
+    step = 256
+    parts = half // step
+
+    def body(place_ref, mixed_ref, bias_ref, own_ref, far_ref, gain_ref, shift_ref, down_ref, *refs):
+        right_refs = refs[:8]
+        middle_ref, normed_ref, start_ref, weight, sems = refs[8:]
+
+        @pl.when(pl.program_id(0) == 0)
+        def _():
+            copies = parts_copies(place_ref, right_refs, weight, sems, width, width, 0, 0)
+            for copy in copies:
+                copy.start()
+            for copy in copies:
+                copy.wait()
+
+        near = pl.program_id(0) < parts
+        rows = jnp.where(near, own_ref[0], far_ref[...].astype(F32))
+        middle = rows + (contract(mixed_ref[...], flat(weight[...]), 1, 0) + bias_ref[...])
+        middle_ref[...] = middle
+        start_ref[...] = middle + down_ref[...]
+        unit, _ = norm_parts(middle)
+        normed_ref[...] = (unit * gain_ref[...] + shift_ref[...]).astype(BF16)
+
+    here = pl.BlockSpec((step, width), lambda i, _: (i, 0))
+    return call(
+        body,
+        "out_norm",
+        (2 * parts,),
+        [
+            here,
+            held(1, width),
+            own_spec(step, width, parts),
+            far_spec(step, width, parts),
+            held(1, width),
+            held(1, width),
+            held(1, width),
+        ]
+        + [whole_ref()] * 8,
+        [here, here, here],
+        [shape_of(F32, 2 * half, width), shape_of(BF16, 2 * half, width), shape_of(F32, 2 * half, width)],
+        (place, mixed, bias, inputs, far, gain, shift, down_bias) + tuple(right),
+        scratch=[weight_scratch(right[0], width), pltpu.SemaphoreType.DMA((1, 8))],
+        vmem=56,
+    )
+
+
+def fill_far(place, partial, base, delta):
+    _, half, width = base.shape
+    step = 256
+
+    def body(place_ref, partial_ref, base_ref, delta_ref, out_ref):
+        out_ref[0] = base_ref[0] + delta_ref[...].astype(F32)
+
+    there = pl.BlockSpec((1, step, width), lambda i, p: (1 - p[3], i, 0))
+    return call(
+        body,
+        "fill_far",
+        (half // step,),
+        [whole_ref(), there, pl.BlockSpec((step, width), lambda i, _: (i, 0))],
+        there,
+        shape_of(F32, 2, half, width),
+        (place, partial, base, delta),
+        alias={1: 0},
+        vmem=8,
+    )
+
+
+def grad_wide(place, left, rights, rows, pieces, before=()):
+    tokens, tall = left.shape
+    width = rights[0].shape[1]
+    step = 512
+    each = width // step
+    steps = each * len(rights)
+    group = 4 * rows
+    per = steps // pieces
+    total = width * len(rights)
+
+    def body(place_ref, left_ref, *refs):
+        right_refs = refs[: len(rights)]
+        outs = refs[len(rights) + len(before) : -1]
+        sums = refs[-1]
+        at = pl.program_id(0)
+        for which, right_ref in enumerate(right_refs):
+            @pl.when(at // each == which)
+            def _():
+                result = contract(left_ref[...], right_ref[...], 0, 0)
+                sums[...] = result.reshape(tall // group, 2, group // 2, step)
+
+        for piece in range(pieces):
+            @pl.when(at // per == piece)
+            def _():
+                outs[2 * piece][...] = sums[:, place_ref[2]].astype(BF16)
+                outs[2 * piece + 1][...] = sums[:, 1 - place_ref[2]].astype(BF16)
+
+    def right_at(which):
+        return lambda i, _: (0, jnp.clip(i - which * each, 0, each - 1))
+
+    wide_total = before[0].shape[-1] if before else total // pieces
+    start = (wide_total - total // pieces) // step
+
+    def out_at(piece):
+        return lambda i, _: (0, 0, start + jnp.clip(i - piece * per, 0, per - 1))
+
+    return call(
+        body,
+        "grad_wide",
+        (steps,),
+        [held(tokens, tall)]
+        + [pl.BlockSpec((tokens, step), right_at(i)) for i in range(len(rights))]
+        + [whole_ref()] * len(before),
+        [
+            pl.BlockSpec((tall // group, group // 2, step), out_at(piece))
+            for piece in range(pieces)
+            for _ in range(2)
+        ],
+        [shape_of(BF16, tall // group, group // 2, wide_total)] * (2 * pieces),
+        (place, left) + tuple(rights) + tuple(before),
+        scratch=[pltpu.VMEM((tall // group, 2, group // 2, step), F32)],
+        vmem=20,
+        alias={2 + len(rights) + i: i for i in range(len(before))},
+    )
+
+
+def feed_forward(place, first, count, depth, normed, grad_low, up_parts, down_parts, up_bias, far, state, wide):
+    tokens, width = normed.shape
+    half = tokens // 2
+    hidden_width = up_bias.shape[1]
+    step = hidden_width // (2 * depth)
+    steps = 2 * count
+    rows = down_parts[0].shape[-2]
+    group = width // (2 * depth)
+    last = first + count == depth
+    sub = 256
+    columns, offset, before = wide
+    offset = offset // step
+
+    def body(place_ref, normed_ref, grad_ref, bias_ref, far_ref, out_in, back_in, *refs):
+        up_refs, down_refs = refs[:8], refs[8 : 8 + 2 * depth]
+        refs = refs[8 + 2 * depth + len(before) :]
+        tall_mine, tall_other, wide_mine, wide_other, sum_ref, back_ref = refs[:6]
+        if last:
+            out_ref, delta_ref = refs[6:8]
+            total, refs = refs[8], refs[9:]
+        else:
+            total, refs = refs[6], refs[7:]
+        up, down, up_sems, down_sems, hidden, before_low, tall_sums, wide_sums = refs
+        at = pl.program_id(0)
+        slot = lax.rem(at, 2)
+
+        def up_copies(index, into):
+            start = pl.multiple_of((2 * first + index) * step, step)
+            copies = []
+            for which, (dx, dc, dy) in enumerate(NEAR):
+                x, c, y = flip(place_ref[1], dx), flip(place_ref[2], dc), flip(place_ref[3], dy)
+                copies.append(
+                    pltpu.make_async_copy(
+                        up_refs[which].at[:, :, pl.ds(start, step)],
+                        up.at[into, :, x, c, y],
+                        up_sems.at[into, which],
+                    )
+                )
+            return copies
+
+        def down_copies(index, into, turn):
+            x = lax.rem(index, 2)
+            return [
+                pltpu.make_async_copy(
+                    down_refs[2 * turn + dc].at[x],
+                    down.at[into, flip(place_ref[2], dc)],
+                    down_sems.at[into, dc],
+                )
+                for dc in range(2)
+            ]
+
+        def begin(index, into):
+            for copy in up_copies(index, into):
+                copy.start()
+            away = lax.rem(place_ref[0] + depth - first - index // 2, depth)
+            for turn in range(depth):
+                @pl.when(away == turn)
+                def _():
+                    for copy in down_copies(index, into, turn):
+                        copy.start()
+
+        @pl.when(at == 0)
+        def _():
+            begin(0, 0)
+            total[...] = out_in[...]
+            back_ref[...] = back_in[...] if first else jnp.zeros((tokens, width), F32)
+
+        @pl.when(at + 1 < steps)
+        def _():
+            begin(at + 1, 1 - slot)
+
+        for copy in up_copies(at, slot) + down_copies(at, slot, 0):
+            copy.wait()
+        up_part, down_part = flat(up[slot]), flat(down[slot])
+        bias_sum = jnp.zeros((1, step), F32)
+        for start in range(0, tokens, sub):
+            cut = slice(start, start + sub)
+            hidden_part, slope = gelu_both(contract(normed_ref[cut], up_part, 1, 0) + bias_ref[...])
+            hidden_low = hidden_part.astype(BF16)
+            hidden[cut] = hidden_low
+            total[cut] += contract(hidden_low, down_part, 1, 0)
+            low = (contract(grad_ref[cut], down_part, 1, 1) * slope).astype(BF16)
+            before_low[cut] = low
+            bias_sum += column(low.astype(F32))
+            back_ref[cut] += contract(low, up_part, 1, 1)
+        sum_ref[...] = bias_sum
+        tall_sums[...] = contract(hidden[...], grad_ref[...], 0, 0).reshape(tall_sums.shape)
+        tall_mine[0] = tall_sums[place_ref[2]].astype(BF16)
+        tall_other[0] = tall_sums[1 - place_ref[2]].astype(BF16)
+        wide_sums[...] = contract(normed_ref[...], before_low[...], 0, 0).reshape(wide_sums.shape)
+        wide_mine[...] = wide_sums[:, place_ref[2]].astype(BF16)
+        wide_other[...] = wide_sums[:, 1 - place_ref[2]].astype(BF16)
+
+        if last:
+            @pl.when(at == steps - 1)
+            def _():
+                out_ref[0] = total[:half]
+                delta_ref[...] = (total[half:] - far_ref[...].astype(F32)).astype(BF16)
+
+    full = held(tokens, width)
+    tall = pl.BlockSpec((1, 2 * rows, width), lambda i, _: (i, 0, 0))
+    broad = pl.BlockSpec((2 * depth, group // 2, step), lambda i, _: (0, 0, offset + i))
+    bias_spec = pl.BlockSpec((1, step), lambda i, _: (0, 2 * first + i))
+    out_specs = [tall, tall, broad, broad, pl.BlockSpec((1, step), lambda i, _: (0, i)), full]
+    out_shape = [shape_of(BF16, steps, 2 * rows, width)] * 2
+    out_shape += [shape_of(BF16, 2 * depth, group // 2, columns)] * 2
+    out_shape += [shape_of(F32, 1, steps * step), shape_of(F32, tokens, width)]
+    scratch = [
+        pltpu.VMEM((2, depth, 2, 2, 2, group // 4, step), BF16),
+        pltpu.VMEM((2, 2, 2, rows, width), BF16),
+        pltpu.SemaphoreType.DMA((2, 8)),
+        pltpu.SemaphoreType.DMA((2, 2)),
+        pltpu.VMEM((tokens, step), BF16),
+        pltpu.VMEM((tokens, step), BF16),
+        pltpu.VMEM((2, 2 * rows, width), F32),
+        pltpu.VMEM((2 * depth, 2, group // 2, step), F32),
+    ]
+    if last:
+        out_specs += [
+            pl.BlockSpec((1, half, width), lambda i, p: (p[3], 0, 0), pipeline_mode=pl.Buffered(1)),
+            held(half, width),
+        ]
+        out_shape += [shape_of(F32, 2, half, width), shape_of(BF16, half, width)]
+        scratch = [pltpu.VMEM((tokens, width), F32)] + scratch
+    else:
+        out_specs += [full]
+        out_shape += [shape_of(F32, tokens, width)]
+    args = (place, normed, grad_low, up_bias, far) + tuple(state) + tuple(up_parts) + tuple(down_parts)
+    alias = {len(args) + i: 2 + i for i in range(len(before))}
+    return call(
+        body,
+        "feed_forward",
+        (steps,),
+        [full, full, bias_spec, held(half, width), full, full]
+        + [whole_ref()] * (8 + 2 * depth + len(before)),
+        out_specs,
+        out_shape,
+        args + tuple(before),
+        scratch=scratch,
+        vmem=50,
+        alias=alias,
+    )
+
+
+def middle_back(place, grad_normed, middle, gain, grad_out, far, right):
+    half, width = far.shape
+    step = 256
+    parts = half // step
+
+    def body(place_ref, grad_ref, middle_ref, gain_ref, own_ref, far_ref, *refs):
+        right_refs = refs[:8]
+        total_ref, low_ref, mixed_ref = refs[8:11]
+        sums = refs[11:14]
+        weight, sems = refs[14:]
+        at = pl.program_id(0)
+
+        def copies():
+            return parts_copies(place_ref, right_refs, weight, sems, width, width, 0, 0)
+
+        @pl.when(at == 0)
+        def _():
+            for copy in copies():
+                copy.start()
+            for ref in sums:
+                ref[...] = jnp.zeros_like(ref)
+
+        grad_normed = grad_ref[...]
+        unit, scale = norm_parts(middle_ref[...])
+        out_grad = jnp.where(at < parts, own_ref[0], far_ref[...].astype(F32))
+        total = out_grad + norm_back(unit, scale, gain_ref[...], grad_normed)
+        total_ref[...] = total
+        low = total.astype(BF16)
+        low_ref[...] = low
+        sums[0][...] += column(grad_normed * unit)
+        sums[1][...] += column(grad_normed)
+        sums[2][...] += column(low.astype(F32))
+
+        @pl.when(at == 0)
+        def _():
+            for copy in copies():
+                copy.wait()
+
+        mixed_ref[...] = contract(low, flat(weight[...]), 1, 1).astype(BF16)
+
+    here = pl.BlockSpec((step, width), lambda i, _: (i, 0))
+    vector = pl.BlockSpec((1, width), lambda i, _: (0, 0))
+    tokens = 2 * half
+    return call(
+        body,
+        "middle_back",
+        (2 * parts,),
+        [here, here, held(1, width), own_spec(step, width, parts), far_spec(step, width, parts)]
+        + [whole_ref()] * 8,
+        [here, here, here, vector, vector, vector],
+        [shape_of(F32, tokens, width), shape_of(BF16, tokens, width), shape_of(BF16, tokens, width)]
+        + [shape_of(F32, 1, width)] * 3,
+        (place, grad_normed, middle, gain, grad_out, far) + tuple(right),
+        scratch=[weight_scratch(right[0], width), pltpu.SemaphoreType.DMA((1, 8))],
+        vmem=24,
+    )
+
+
+def input_back(place, grads, left, right, inputs, far, gain, middle_grad, far_grad):
+    half, width = far.shape
+    step = 256
+    parts = half // step
+
+    def body(
+        place_ref, query_ref, key_ref, value_ref, own_ref, far_ref, gain_ref, middle_ref, far_grad_ref, *refs
+    ):
+        left_refs, right_refs = refs[:8], refs[8:16]
+        out_ref, delta_ref = refs[16:18]
+        sums = refs[18:22]
+        gain_sum_ref, shift_sum_ref, query_sum_ref, value_sum_ref = sums
+        weight, sems = refs[22:]
+        at = pl.program_id(0)
+
+        def copies():
+            result = []
+            for chunk, part_refs in enumerate((left_refs, left_refs, right_refs)):
+                result += parts_copies(
+                    place_ref, part_refs, weight, sems, (chunk % 2) * width, width, chunk * width, chunk
+                )
+            return result
+
+        @pl.when(at == 0)
+        def _():
+            for copy in copies():
+                copy.start()
+            for ref in sums:
+                ref[...] = jnp.zeros_like(ref)
+
+        @pl.when(at == 0)
+        def _():
+            for copy in copies():
+                copy.wait()
+
+        def part(chunk):
+            return flat(weight[:, :, :, :, :, chunk * width : (chunk + 1) * width])
+
+        grad_normed = contract(query_ref[...], part(0), 1, 1)
+        grad_normed += contract(key_ref[...], part(1), 1, 1)
+        grad_normed += contract(value_ref[...], part(2), 1, 1)
+        rows = jnp.where(at < parts, own_ref[0], far_ref[...].astype(F32))
+        unit, scale = norm_parts(rows)
+        gain_sum_ref[...] += column(grad_normed * unit)
+        shift_sum_ref[...] += column(grad_normed)
+        query_sum_ref[...] += column(query_ref[...].astype(F32))
+        value_sum_ref[...] += column(value_ref[...].astype(F32))
+        result = middle_ref[...] + norm_back(unit, scale, gain_ref[...], grad_normed)
+
+        @pl.when(at < parts)
+        def _():
+            out_ref[0] = result
+
+        @pl.when(at >= parts)
+        def _():
+            delta_ref[...] = (result - far_grad_ref[...].astype(F32)).astype(BF16)
+
+    here = pl.BlockSpec((step, width), lambda i, _: (i, 0))
+    vector = pl.BlockSpec((1, width), lambda i, _: (0, 0))
+    return call(
+        body,
+        "input_back",
+        (2 * parts,),
+        [
+            here,
+            here,
+            here,
+            own_spec(step, width, parts),
+            far_spec(step, width, parts),
+            held(1, width),
+            here,
+            far_spec(step, width, parts),
+        ]
+        + [whole_ref()] * 16,
+        [own_spec(step, width, parts), far_spec(step, width, parts), vector, vector, vector, vector],
+        [shape_of(F32, 2, half, width), shape_of(BF16, half, width)] + [shape_of(F32, 1, width)] * 4,
+        (place,) + tuple(grads) + (inputs, far, gain, middle_grad, far_grad) + tuple(left) + tuple(right),
+        scratch=[weight_scratch(left[0], 3 * width), pltpu.SemaphoreType.DMA((3, 8))],
+        vmem=56,
+    )
+
+
+def split_add(place, mine, came, spot):
+    groups, _, rows, columns = mine.shape
+
+    def body(place_ref, mine_ref, came_ref, sent_ref, kept_ref):
+        for ref, at in ((sent_ref, 1 - place_ref[spot]), (kept_ref, place_ref[spot])):
+            ref[0] = (mine_ref[0, at].astype(F32) + came_ref[0, at].astype(F32)).astype(BF16)
+
+    block = pl.BlockSpec((1, 2, rows, columns), lambda i, _: (i, 0, 0, 0))
+    out = pl.BlockSpec((1, rows, columns), lambda i, _: (i, 0, 0))
+    return call(
+        body,
+        "split_add",
+        (groups,),
+        [block, block],
+        [out, out],
+        [shape_of(BF16, groups, rows, columns)] * 2,
+        (place, mine, came),
+        vmem=8,
+    )
+
+
+def split_depth(place, pairs):
+    depth, rows = pairs[0][0].shape[:2]
+    widths = [mine.shape[2] for mine, _ in pairs]
+    total = sum(widths)
+
+    def body(place_ref, *refs):
+        outs = refs[2 * len(pairs) :]
+        for step, ref in enumerate(outs):
+            at = lax.rem(place_ref[0] + step, depth)
+            start = 0
+            for which, width in enumerate(widths):
+                value = refs[2 * which][at].astype(F32) + refs[2 * which + 1][at].astype(F32)
+                ref[:, start : start + width] = value.astype(ref.dtype)
+                start += width
+
+    return call(
+        body,
+        "split_depth",
+        (1,),
+        [held(depth, rows, width) for width in widths for _ in range(2)],
+        [held(rows, total)] * depth,
+        [shape_of(F32, rows, total)] + [shape_of(BF16, rows, total)] * (depth - 1),
+        (place,) + tuple(value for pair in pairs for value in pair),
+        vmem=8,
+    )
+
+
+def last_add(place, own, came, cuts):
+    rows, total = own.shape
+
+    def body(place_ref, own_ref, *refs):
+        value = own_ref[...]
+        for ref in refs[: len(came)]:
+            value = value + ref[...].astype(F32)
+        for ref, (start, stop) in zip(refs[len(came) :], cuts):
+            ref[...] = value[:, start:stop]
+
+    return call(
+        body,
+        "last_add",
+        (1,),
+        [held(rows, total)] * (1 + len(came)),
+        [held(rows, stop - start) for start, stop in cuts],
+        [shape_of(F32, rows, stop - start) for start, stop in cuts],
+        (place, own) + tuple(came),
+        vmem=6,
+    )
+
+
+def spread_rows(count, per, size, row):
+    span = size * per
+    lane = lax.broadcasted_iota(jnp.int32, (per, count * span), 1)
+    line = lax.broadcasted_iota(jnp.int32, (per, count * span), 0)
+    return jnp.where(lane % span == row * per + line, 1.0, 0.0)
+
+
+def chosen_rows(count, span):
+    lane = lax.broadcasted_iota(jnp.int32, (count, count * span), 1)
+    line = lax.broadcasted_iota(jnp.int32, (count, count * span), 0)
+    return lane // span == line
+
+
+def small_vectors(place, right, start, sizes, per):
+    depth, rows, _ = right[0].shape
+    count = depth * 8
+
+    def body(place_ref, *refs):
+        part_refs, outs, held_rows = refs[:8], refs[8:-1], refs[-1]
+        for at, (dx, dc, dy) in enumerate(NEAR):
+            x, c, y = flip(place_ref[1], dx), flip(place_ref[2], dc), flip(place_ref[3], dy)
+            held_rows[:, x, c, y] = part_refs[at][...].astype(F32)
+        table = held_rows[...].reshape(count, rows, PAIR)
+        at = 0
+        for ref, size in zip(outs, sizes):
+            chosen = chosen_rows(count, size * per)
+            line = jnp.zeros((1, count * size * per), F32)
+            for row in range(size):
+                spread = spread_rows(count, per, size, row).astype(BF16)
+                wide = contract(table[:, at + row, :per].astype(BF16), spread, 1, 0)
+                line += column(jnp.where(chosen, wide, 0.0))
+            at += size
+            ref[...] = line
+
+    return call(
+        body,
+        "small_vectors",
+        (1,),
+        [pl.BlockSpec((depth, rows, PAIR), lambda i, _: (0, 0, start // PAIR))] * 8,
+        [held(1, count * size * per) for size in sizes],
+        [shape_of(F32, 1, count * size * per) for size in sizes],
+        (place,) + tuple(right),
+        scratch=[pltpu.VMEM((depth, 2, 2, 2, rows, PAIR), F32)],
+        vmem=12,
+    )
+
+
+def pack_vectors(place, vectors, sizes, per):
+    count = vectors[0].shape[1] // (sizes[0] * per)
+
+    def body(place_ref, *refs):
+        out = refs[-1]
+        at = 0
+        for ref, size in zip(refs[:-1], sizes):
+            chosen = chosen_rows(count, size * per)
+            wide = jnp.where(chosen, jnp.broadcast_to(ref[...], (count, count * size * per)), 0.0)
+            for row in range(size):
+                out[at + row] = lax.dot_general(
+                    wide,
+                    spread_rows(count, per, size, row),
+                    (((1,), (1,)), ((), ())),
+                    precision=lax.Precision.HIGHEST,
+                    preferred_element_type=F32,
+                )
+            at += size
+
+    return call(
+        body,
+        "pack_vectors",
+        (1,),
+        [held(*vector.shape) for vector in vectors],
+        held(sum(sizes), count, per),
+        shape_of(F32, sum(sizes), count, per),
+        (place,) + tuple(vectors),
+        vmem=12,
+    )
+
+
+def merge_add(place, mine, came, spot):
+    counts = [part.shape[0] for part in mine]
+    _, _, rows, columns = mine[0].shape
+
+    def body(place_ref, *refs):
+        sent_ref, kept_ref = refs[2 * len(mine) :]
+        start = 0
+        for which, count in enumerate(counts):
+            for ref, at in ((sent_ref, 1 - place_ref[spot]), (kept_ref, place_ref[spot])):
+                total = refs[which][:, at].astype(F32) + refs[len(mine) + which][:, at].astype(F32)
+                ref[start : start + count] = total.astype(BF16)
+            start += count
+
+    shape = (sum(counts), rows, columns)
+    return call(
+        body,
+        "merge_add",
+        (1,),
+        [held(*part.shape) for part in mine + came],
+        [held(*shape)] * 2,
+        [shape_of(BF16, *shape)] * 2,
+        (place,) + tuple(mine) + tuple(came),
+        vmem=12,
+    )
+
+
+def attn_forward_kernel(q_ref, k_ref, v_ref, bias_ref, prob_ref, mixed_ref, total_ref):
+    tokens, lanes = q_ref.shape
+    half = lanes // 2
+    lane = lax.broadcasted_iota(jnp.int32, (tokens, lanes), 1)
+    block = lax.broadcasted_iota(jnp.int32, (tokens, lanes), 0) // BLOCK
+    scale = half ** -0.5
+    q = q_ref[...].astype(jnp.float32) * scale
+    k = k_ref[...].astype(jnp.float32)
+    v = v_ref[...].astype(jnp.float32)
+    sides = []
+    for head in range(2):
+        own = (lane >= half) if head else (lane < half)
+        first = 0 if head else half
+        bias = jnp.broadcast_to(bias_ref[head][:, None, :], (tokens // BLOCK, BLOCK, lanes)).reshape(tokens, lanes)
+        q_ext = jnp.where(own, q, jnp.where(lane - first == block, 1.0, 0.0)).astype(jnp.bfloat16)
+        k_ext = jnp.where(own, k, bias).astype(jnp.bfloat16)
+        v_ext = jnp.where(own, v, 1.0).astype(jnp.bfloat16)
+        sides.append((q_ext, k_ext, v_ext))
+    rows = 256
+    low_lane = lax.broadcasted_iota(jnp.int32, (rows, lanes), 1) < half
+    for start in range(0, tokens, rows):
+        sums = []
+        for head, (q_ext, k_ext, v_ext) in enumerate(sides):
+            scores = contract(q_ext[start:start + rows], k_ext, 1, 1)
+            top = jnp.max(scores, axis=1, keepdims=True)
+            prob = jnp.exp(scores - top).astype(jnp.bfloat16)
+            prob_ref[head, start:start + rows, :] = prob
+            sums.append(contract(prob, v_ext, 1, 0))
+        result = jnp.where(low_lane, sums[0], sums[1])
+        totals = pltpu.roll(jnp.where(low_lane, sums[1], sums[0]), half, 1)
+        mixed_ref[start:start + rows, :] = (result / totals).astype(jnp.bfloat16)
+        total_ref[start:start + rows, :] = totals
+
+def attn_backward_kernel(q_ref, k_ref, v_ref, prob_ref, mixed_ref, total_ref, grad_ref, dq_ref, dk_ref, dv_ref):
+    tokens, lanes = q_ref.shape
+    half = lanes // 2
+    scale = half ** -0.5
+    lane = lax.broadcasted_iota(jnp.int32, (tokens, lanes), 1)
+    grad = grad_ref[...].astype(jnp.float32) / total_ref[...]
+    inner = grad * mixed_ref[...].astype(jnp.float32)
+    grad_low = grad.astype(jnp.bfloat16)
+    q_turned = q_ref[...].T
+    grad_turned = grad_low.T
+    v = v_ref[...].astype(jnp.float32)
+    k = k_ref[...]
+    rows = 256
+    low_lane = lax.broadcasted_iota(jnp.int32, (rows, lanes), 1) < half
+    dq = [[None, None] for _ in range(tokens // rows)]
+    dk, dv = [], []
+    for head in range(2):
+        own = (lane >= half) if head else (lane < half)
+        first = 0 if head else half
+        minus = -jnp.sum(jnp.where(own, inner, 0.0), axis=1, keepdims=True)
+        high = minus.astype(jnp.bfloat16).astype(jnp.float32)
+        grad_ext = jnp.where(own, grad, jnp.where(lane == first, high, jnp.where(lane == first + 1, minus - high, 0.0))).astype(jnp.bfloat16)
+        v_ext = jnp.where(own, v, jnp.where(lane - first < 2, 1.0, 0.0)).astype(jnp.bfloat16)
+        dk_sum = dv_sum = None
+        for index in range(tokens // rows):
+            part = slice(index * rows, (index + 1) * rows)
+            prob = prob_ref[head, part, :]
+            spread = contract(grad_ext[part], v_ext, 1, 1)
+            grad_scores = (prob.astype(jnp.float32) * spread).astype(jnp.bfloat16)
+            dq[index][head] = contract(grad_scores, k, 1, 0)
+            rows_of = slice(head * half, (head + 1) * half)
+            dk_part = contract(q_turned[rows_of, part], grad_scores, 1, 0)
+            dv_part = contract(grad_turned[rows_of, part], prob, 1, 0)
+            dk_sum = dk_part if dk_sum is None else dk_sum + dk_part
+            dv_sum = dv_part if dv_sum is None else dv_sum + dv_part
+        dk.append(dk_sum)
+        dv.append(dv_sum)
+    for index, pair in enumerate(dq):
+        dq_ref[index * rows:(index + 1) * rows, :] = (jnp.where(low_lane, pair[0], pair[1]) * scale).astype(jnp.bfloat16)
+    dk_ref[...] = (jnp.concatenate(dk, axis=0) * scale).T.astype(jnp.bfloat16)
+    dv_ref[...] = jnp.concatenate(dv, axis=0).T.astype(jnp.bfloat16)
+
+
+def attn_forward(place, qkv, bias, first, count, before=()):
+    tokens, width = qkv.shape[0], qkv.shape[1] // 3
+    pairs = width // PAIR
+
+    def at(part):
+        return pl.BlockSpec((tokens, PAIR), lambda i, _: (0, part * pairs + first + i))
+
+    def body(place_ref, *refs):
+        attn_forward_kernel(*refs[:4], *refs[4 + len(before) :])
+
+    return call(
+        body,
+        "attn_forward",
+        (count,),
+        [at(0), at(1), at(2), pl.BlockSpec((2, tokens // BLOCK, PAIR), lambda i, _: (first + i, 0, 0))]
+        + [whole_ref()] * len(before),
+        [pl.BlockSpec((2, tokens, tokens), lambda i, _: (first + i, 0, 0)), at(0), at(0)],
+        [
+            shape_of(BF16, 2 * pairs, tokens, tokens),
+            shape_of(BF16, tokens, width),
+            shape_of(F32, tokens, width),
+        ],
+        (place, qkv, qkv, qkv, bias) + tuple(before),
+        vmem=28,
+        alias={5 + i: i for i in range(len(before))},
+    )
+
+
+def attn_backward(place, qkv, prob, mixed, total, grad, first, count, before=()):
+    tokens, width = qkv.shape[0], qkv.shape[1] // 3
+    pairs = width // PAIR
+
+    def at(part):
+        return pl.BlockSpec((tokens, PAIR), lambda i, _: (0, part * pairs + first + i))
+
+    def body(place_ref, *refs):
+        attn_backward_kernel(*refs[:7], *refs[7 + len(before) :])
+
+    return call(
+        body,
+        "attn_backward",
+        (count,),
+        [at(0), at(1), at(2), pl.BlockSpec((2, tokens, tokens), lambda i, _: (first + i, 0, 0))]
+        + [at(0)] * 3
+        + [whole_ref()] * len(before),
+        [at(0)] * 3,
+        [shape_of(BF16, tokens, width)] * 3,
+        (place, qkv, qkv, qkv, prob, mixed, total, grad) + tuple(before),
+        vmem=28,
+        alias={8 + i: i for i in range(len(before))},
+    )
+
+
+def key_bias(random_ids, block_ids):
+    heads, blocks, _ = random_ids.shape
+    row, col = block_ids[:, None], block_ids[None, :]
+    last = blocks - 1
+    fixed = (row == 0) | (row == last) | (col == 0) | (col == last) | (jnp.abs(row - col) <= 1)
+    drawn = jnp.any(random_ids[:, :, :, None] == block_ids, axis=2)
+    bias = jnp.where(fixed[None] | drawn, 0.0, -1e30)
+    bias = bias.transpose(0, 2, 1).reshape(heads // 2, 2, blocks, blocks)
+    lanes = 128
+    even = jnp.pad(bias[:, 0], ((0, 0), (0, 0), (lanes // 2, lanes // 2 - blocks)))
+    odd = jnp.pad(bias[:, 1], ((0, 0), (0, 0), (0, lanes - blocks)))
+    return jnp.stack([even, odd], axis=1).reshape(heads, blocks, lanes)
+
+
+def pair_swap(value, axis, bit):
+    size = lax.axis_size(axis)
+    return lax.ppermute(value, axis, [(i, i ^ bit) for i in range(size)])
+
+
+def pick(value, index, axis):
+    return lax.dynamic_index_in_dim(value, index, axis, keepdims=False)
+
+
+def swap_x(value):
+    return pair_swap(value, "dp", 2)
+
+
+def swap_core(value):
+    return pair_swap(value, "dp", 1)
+
+
+def swap_y(value):
+    return pair_swap(value, "seq", 1)
+
+
+def ring_z(value, step):
+    size = lax.axis_size("dp")
+    return lax.ppermute(value, "dp", [(i, (i + 4 * step) % size) for i in range(size)])
+
+
+def tie(*values):
+    return lax.optimization_barrier(values)
+
+
+def sum_all(values):
+    depth = lax.axis_size("dp") // 4
+    for swap in (swap_core, swap_x, swap_y):
+        values = values + swap(values)
+    total = values
+    for step in range(1, depth):
+        total = total + ring_z(values, step)
+    return total
+
+
+class Reduce:
+    def __init__(self, place, rows, x_first):
+        self.place, self.rows, self.x_first = place, rows, x_first
+
+    def begin(self, mine, other):
+        self.mine, self.came = mine, swap_core(other)
+
+    def first(self):
+        groups, tall, columns = self.mine.shape
+        if self.x_first:
+            shape = (groups // 2, 2, tall, columns)
+        else:
+            shape = (groups, 2, self.rows, columns)
+        spot, swap = (1, swap_x) if self.x_first else (3, swap_y)
+        sent, kept = split_add(self.place, self.mine.reshape(shape), self.came.reshape(shape), spot)
+        self.mine, self.came = kept, swap(sent)
+
+    def second(self, *others):
+        spot, swap = (3, swap_y) if self.x_first else (1, swap_x)
+        mine, came = [], []
+        for part in (self,) + others:
+            shape = (-1, 2, self.rows, part.mine.shape[-1])
+            mine.append(part.mine.reshape(shape))
+            came.append(part.came.reshape(shape))
+        if others:
+            sent, kept = merge_add(self.place, mine, came, spot)
+        else:
+            sent, kept = split_add(self.place, mine[0], came[0], spot)
+        self.mine, self.came = kept, swap(sent)
+
+    def third(self, *others):
+        pairs = [(self.mine, self.came)] + [(other.mine, other.came) for other in others]
+        own, *sent = split_depth(self.place, pairs)
+        self.mine = own
+        self.came = [ring_z(block, step + 1) for step, block in enumerate(sent)]
+
+    def last(self, cuts=None):
+        return last_add(self.place, self.mine, self.came, cuts or [(0, self.mine.shape[1])])
+
+    def hold(self, *others):
+        self.mine, self.came, others = tie(self.mine, self.came, others)
+        return others
+
+
+def split_depth_spot(place_ref, step, depth):
+    return lax.rem(place_ref[0] + depth - step, depth)
+
+
+def join_depth(place, blocks, cuts, name):
+    depth = len(blocks)
+    rows = blocks[0].shape[0]
+    moves = []
+    for step in range(depth):
+        for j, (start, stop) in enumerate(cuts):
+            cut = (slice(None), slice(start, stop))
+            moves.append((step, cut, j, lambda p, step=step: split_depth_spot(p, step, depth)))
+    return join(place, blocks, moves, [(depth, rows, stop - start) for start, stop in cuts], name)
+
+
+def join_plane(place, blocks):
+    moves = []
+    for at, (dx, dy) in enumerate(((0, 0), (1, 0), (0, 1), (1, 1))):
+        moves.append(
+            (at, (), 0, lambda p, dx=dx, dy=dy: (flip(p[1], dx), flip(p[3], dy)))
+        )
+    return join(place, blocks, moves, [(2, 2) + blocks[0].shape], "join_plane")[0]
+
+
+def near_parts(own, by_x, by_y, by_xy, cores):
+    blocks = {(0, 0): own, (1, 0): by_x, (0, 1): by_y, (1, 1): by_xy}
+    return [cores[dx, dy] if dc else blocks[dx, dy] for dx, dc, dy in NEAR]
+
+
+def paired(inputs, grad_out, random_blocks, *shards):
+    depth = lax.axis_size("dp") // 4
+    dp, y = lax.axis_index("dp"), lax.axis_index("seq")
+    z, x, c = dp // 4, (dp // 2) % 2, dp % 2
+    spots = (z, x, c, y)
+    place = jnp.stack(spots).astype(jnp.int32)
+    w_query, w_key, w_value, w_out, w_up, w_down = shards[:6]
+    vectors = shards[6:]
+    half, width = inputs.shape[1:]
+    rows, tall_rows, hidden_width = w_up.shape[0], w_down.shape[0], w_up.shape[1]
+    pairs = width // PAIR
+    ring = range(1, depth)
+
+    small = jnp.concatenate([vector.reshape(-1, rows) for vector in vectors])
+    small = jnp.pad(small, ((0, rows - small.shape[0]), (0, PAIR - rows)))
+    shard = jnp.concatenate([w_query, w_key, w_value, w_out, small], axis=1)
+    turned = [shard] + [ring_z(shard, step) for step in ring]
+    down_x = swap_x(w_down)
+    far_rows = swap_y(cast_far(place, inputs))
+    far_grad_low = cast_far(place, grad_out)
+    turned, down_x, far_rows, w_up, w_down, random_blocks = tie(
+        turned, down_x, far_rows, w_up, w_down, random_blocks
+    )
+    cut = 2 * width
+    left, right = join_depth(place, turned, [(0, cut), (cut, shard.shape[1])], "join_first")
+    left_y, right_x = swap_y(left), swap_x(right)
+    up_turned = {1: ring_z(w_up, 1), depth - 1: ring_z(w_up, depth - 1)}
+    down_y, down_xy = swap_y(w_down), swap_y(down_x)
+    left_y, right_x, up_turned, down_y, down_xy, down_x = tie(
+        left_y, right_x, up_turned, down_y, down_xy, down_x
+    )
+    left_x, left_xy = swap_x(left), swap_x(left_y)
+    right_y, right_xy = swap_y(right), swap_y(right_x)
+    for step in ring:
+        if step not in up_turned:
+            up_turned[step] = ring_z(w_up, step)
+    left_x, left_xy, right_y, right_xy, up_turned, left_y, right_x, down_x, random_blocks = tie(
+        left_x, left_xy, right_y, right_xy, up_turned, left_y, right_x, down_x, random_blocks
+    )
+    (up_own,) = join_depth(place, [w_up] + [up_turned[step] for step in ring], [(0, hidden_width)], "join_up")
+    plane = join_plane(place, [w_down, down_x, down_y, down_xy])
+    up_own, plane, left, left_x, left_y, left_xy, right, right_x, right_y, right_xy = tie(
+        up_own, plane, left, left_x, left_y, left_xy, right, right_x, right_y, right_xy
+    )
+    up_y = swap_y(up_own)
+    left_core = {
+        (0, 0): swap_core(left), (0, 1): swap_core(left_y),
+        (1, 0): swap_core(left_x), (1, 1): swap_core(left_xy),
+    }
+    right_core = {
+        (0, 0): swap_core(right), (0, 1): swap_core(right_y),
+        (1, 0): swap_core(right_x), (1, 1): swap_core(right_xy),
+    }
+    random_far = swap_y(pick(random_blocks, 1 - y, 0))
+    left_parts = near_parts(left, left_x, left_y, left_xy, left_core)
+    right_parts = near_parts(right, right_x, right_y, right_xy, right_core)
+    sizes = [vector.shape[0] // rows for vector in vectors]
+    local_blocks = half // BLOCK
+    ids = jnp.arange(2 * local_blocks, dtype=jnp.int32)
+    block_ids = (ids + y * local_blocks) % (2 * local_blocks)
+    random_ids = jnp.concatenate([pick(random_blocks, y, 0), random_far], axis=1)
+    bias = key_bias(random_ids, block_ids)
+    left_parts, right_parts, plane, bias = tie(left_parts, right_parts, plane, bias)
+
+    planes = {0: plane, 1: ring_z(plane, 1), depth - 1: ring_z(plane, depth - 1)}
+    spans = small_vectors(place, right_parts, cut, sizes, rows)
+    (
         ln1_gain,
         ln1_bias,
         query_bias,
@@ -424,111 +1601,186 @@
         ln2_bias,
         up_bias,
         down_bias,
-    )
-
-    def micro_step(carried, sequence):
-        in_rows, grad_rows, random_ids = sequence
-        forward_weights = (
-            lax.all_gather(w_query, ("dp", "seq"), axis=0, tiled=True),
-            lax.all_gather(w_key, ("dp", "seq"), axis=0, tiled=True),
-            lax.all_gather(w_value, ("dp", "seq"), axis=0, tiled=True),
-            lax.all_gather(w_out, ("dp", "seq"), axis=0, tiled=True),
-            lax.all_gather(w_up, ("dp", "seq"), axis=0, tiled=True),
-            lax.all_gather(w_down, ("dp", "seq"), axis=0, tiled=True),
-            lax.all_gather(ln1_gain, ("dp", "seq"), axis=0, tiled=True),
-            lax.all_gather(ln1_bias, ("dp", "seq"), axis=0, tiled=True),
-            lax.all_gather(query_bias, ("dp", "seq"), axis=0, tiled=True),
-            lax.all_gather(value_bias, ("dp", "seq"), axis=0, tiled=True),
-            lax.all_gather(out_bias, ("dp", "seq"), axis=0, tiled=True),
-            lax.all_gather(ln2_gain, ("dp", "seq"), axis=0, tiled=True),
-            lax.all_gather(ln2_bias, ("dp", "seq"), axis=0, tiled=True),
-            lax.all_gather(up_bias, ("dp", "seq"), axis=0, tiled=True),
-            lax.all_gather(down_bias, ("dp", "seq"), axis=0, tiled=True),
+    ) = spans
+    qkv_bias = jnp.concatenate([query_bias, jnp.zeros_like(query_bias), value_bias], axis=1)
+    normed_low, qkv = norm_project(
+        place, inputs, far_rows, ln1_gain, ln1_bias, left_parts, right_parts, qkv_bias
+    )
+    qkv, up_y = tie(qkv, up_y)
+    up_x, up_xy = swap_x(up_own), swap_x(up_y)
+    attended = attn_forward(place, qkv, bias, 0, pairs // 2)
+    attended, planes, far_grad_low = tie(attended, planes, far_grad_low)
+    for step in ring:
+        if step not in planes:
+            planes[step] = ring_z(planes[0], step)
+    far_grad = swap_y(far_grad_low)
+    prob, mixed_low, totals = attn_forward(place, qkv, bias, pairs // 2, pairs - pairs // 2, attended)
+    middle, normed_two_low, start_out = out_norm(
+        place, mixed_low, right_parts, out_bias, inputs, far_rows, ln2_gain, ln2_bias, down_bias
+    )
+    normed_two_low, up_x, up_xy, far_grad = tie(normed_two_low, up_x, up_xy, far_grad)
+    up_core = {
+        (0, 0): swap_core(up_own), (0, 1): swap_core(up_y),
+        (1, 0): swap_core(up_x), (1, 1): swap_core(up_xy),
+    }
+    up_parts = near_parts(up_own, up_x, up_y, up_xy, up_core)
+    down_parts = [part for step in range(depth) for part in (planes[step], swap_core(planes[step]))]
+    grad_ff_low, grad_down_bias = join_low(place, grad_out, far_grad)
+
+    down_sums = [Reduce(place, tall_rows, True) for _ in range(3)]
+    near_sum = Reduce(place, rows, False)
+    wide_sum = Reduce(place, rows, True)
+    out_sum = Reduce(place, rows, True)
+    left_sum = Reduce(place, rows, True)
+    right_sum = Reduce(place, rows, False)
+
+    def feed(first, count, state, wide):
+        return feed_forward(
+            place, first, count, depth, normed_two_low, grad_ff_low, up_parts, down_parts, up_bias,
+            far_rows, state, wide,
         )
-        saved, result = run_forward(forward_weights, in_rows, random_ids)
-        backward_weights = (
-            lax.all_gather(w_query, ("dp", "seq"), axis=0, tiled=True),
-            lax.all_gather(w_key, ("dp", "seq"), axis=0, tiled=True),
-            lax.all_gather(w_value, ("dp", "seq"), axis=0, tiled=True),
-            lax.all_gather(w_out, ("dp", "seq"), axis=0, tiled=True),
-            lax.all_gather(w_up, ("dp", "seq"), axis=0, tiled=True),
-            lax.all_gather(w_down, ("dp", "seq"), axis=0, tiled=True),
-            lax.all_gather(ln1_gain, ("dp", "seq"), axis=0, tiled=True),
-            lax.all_gather(ln1_bias, ("dp", "seq"), axis=0, tiled=True),
-            lax.all_gather(query_bias, ("dp", "seq"), axis=0, tiled=True),
-            lax.all_gather(value_bias, ("dp", "seq"), axis=0, tiled=True),
-            lax.all_gather(out_bias, ("dp", "seq"), axis=0, tiled=True),
-            lax.all_gather(ln2_gain, ("dp", "seq"), axis=0, tiled=True),
-            lax.all_gather(ln2_bias, ("dp", "seq"), axis=0, tiled=True),
-            lax.all_gather(up_bias, ("dp", "seq"), axis=0, tiled=True),
-            lax.all_gather(down_bias, ("dp", "seq"), axis=0, tiled=True),
-        )
-        grad_in, grads = run_backward(backward_weights, saved, grad_rows)
-        summed = (
-            lax.psum_scatter(grads[0], ("dp", "seq"), scatter_dimension=0, tiled=True),
-            lax.psum_scatter(grads[1], ("dp", "seq"), scatter_dimension=0, tiled=True),
-            lax.psum_scatter(grads[2], ("dp", "seq"), scatter_dimension=0, tiled=True),
-            lax.psum_scatter(grads[3], ("dp", "seq"), scatter_dimension=0, tiled=True),
-            lax.psum_scatter(grads[4], ("dp", "seq"), scatter_dimension=0, tiled=True),
-            lax.psum_scatter(grads[5], ("dp", "seq"), scatter_dimension=0, tiled=True),
-            lax.psum_scatter(grads[6], ("dp", "seq"), scatter_dimension=0, tiled=True),
-            lax.psum_scatter(grads[7], ("dp", "seq"), scatter_dimension=0, tiled=True),
-            lax.psum_scatter(grads[8], ("dp", "seq"), scatter_dimension=0, tiled=True),
-            lax.psum_scatter(grads[9], ("dp", "seq"), scatter_dimension=0, tiled=True),
-            lax.psum_scatter(grads[10], ("dp", "seq"), scatter_dimension=0, tiled=True),
-            lax.psum_scatter(grads[11], ("dp", "seq"), scatter_dimension=0, tiled=True),
-            lax.psum_scatter(grads[12], ("dp", "seq"), scatter_dimension=0, tiled=True),
-            lax.psum_scatter(grads[13], ("dp", "seq"), scatter_dimension=0, tiled=True),
-            lax.psum_scatter(grads[14], ("dp", "seq"), scatter_dimension=0, tiled=True),
-        )
-        carried = tuple((left + right for left, right in zip(carried, summed)))
-        return (carried, (result, grad_in))
-
-    initial = tuple((jnp.zeros(shard_part.shape, jnp.float32) for shard_part in shards))
-    carried, (results, grads_in) = lax.scan(micro_step, initial, (inputs, grad_out, random_blocks))
-    return (results, grads_in) + tuple(carried)
+
+    near = depth // 2
+    near_width = hidden_width // 2
+    each = hidden_width // depth
+    mine, other, up_mine, up_other, bias_0, back, total = feed(
+        0, near, (start_out, start_out), (near_width, 0, ())
+    )
+    down_sums[0].begin(mine, other)
+    near_sum.begin(up_mine, up_other)
+    mine, other, up_mine, up_other, bias_1, back, total = feed(
+        near, depth - 1 - near, (total, back), (near_width, 0, ())
+    )
+    (back,) = down_sums[0].hold(back)
+    (back,) = near_sum.hold(back)
+    down_sums[1].begin(mine, other)
+    down_sums[0].first()
+    near_sum.first()
+    down_sums[0].mine, near_sum.mine, back = tie(down_sums[0].mine, near_sum.mine, back)
+    mine, other, up_mine, up_other, bias_2, back, out_part, out_delta = feed(
+        depth - 1, 1, (total, back), (near_width, (depth - 1 - near) * each, (up_mine, up_other))
+    )
+    (back,) = down_sums[0].hold(back)
+    (back,) = near_sum.hold(back)
+    (back,) = down_sums[1].hold(back)
+    down_sums[2].begin(mine, other)
+    wide_sum.begin(up_mine, up_other)
+    down_sums[1].first()
+    down_sums[1].mine, back = tie(down_sums[1].mine, back)
+    grad_up_bias = jnp.concatenate([bias_0, bias_1, bias_2], axis=1)
+    grad_middle, grad_attn_low, grad_mixed_low, grad_ln2_gain, grad_ln2_bias, grad_out_bias = middle_back(
+        place, back, middle, ln2_gain, grad_out, far_grad, right_parts
+    )
+    out_sum.begin(*grad_wide(place, mixed_low, (grad_attn_low,), rows, 1))
+    out_sum.mine, grad_mixed_low = tie(out_sum.mine, grad_mixed_low)
+    (grad_mixed_low,) = down_sums[1].hold(grad_mixed_low)
+    (grad_mixed_low,) = down_sums[2].hold(grad_mixed_low)
+    (grad_mixed_low,) = wide_sum.hold(grad_mixed_low)
+    down_sums[2].first()
+    near_sum.second()
+    down_sums[2].mine, near_sum.mine, grad_mixed_low, out_delta = tie(
+        down_sums[2].mine, near_sum.mine, grad_mixed_low, out_delta
+    )
+    out_far = swap_y(out_delta)
+    grads = attn_backward(place, qkv, prob, mixed_low, totals, grad_mixed_low, 0, pairs // 2)
+    grads, out_far = tie(grads, out_far)
+    (grads,) = near_sum.hold(grads)
+    (grads,) = down_sums[2].hold(grads)
+    (grads,) = out_sum.hold(grads)
+    wide_sum.first()
+    near_sum.third()
+    down_sums[0].second(*down_sums[1:])
+    down_sum = down_sums[0]
+    down_sum.mine, near_sum.mine, wide_sum.mine, out_sum.mine, grads = tie(
+        down_sum.mine, near_sum.mine, wide_sum.mine, out_sum.mine, grads
+    )
+    grads = attn_backward(
+        place, qkv, prob, mixed_low, totals, grad_mixed_low, pairs // 2, pairs - pairs // 2, grads
+    )
+    (grads,) = near_sum.hold(grads)
+    (grads,) = wide_sum.hold(grads)
+    (grads,) = down_sum.hold(grads)
+    out_sum.first()
+    wide_sum.second()
+    down_sum.third()
+    out_sum.mine, wide_sum.mine, down_sum.mine, grads = tie(
+        out_sum.mine, wide_sum.mine, down_sum.mine, grads
+    )
+    wide = grad_wide(place, normed_low, grads, rows, 2)
+    (wide,) = out_sum.hold(wide)
+    (wide,) = wide_sum.hold(wide)
+    left_sum.begin(*wide[:2])
+    right_sum.begin(*wide[2:])
+    out_sum.second()
+    (grad_up_near,) = near_sum.last()
+    left_sum.mine, grads, grad_up_near, out_sum.mine = tie(left_sum.mine, grads, grad_up_near, out_sum.mine)
+    (grads,) = left_sum.hold(grads)
+    left_sum.first()
+    (grads,) = right_sum.hold(grads)
+    right_sum.first()
+    left_sum.mine, right_sum.mine, grads = tie(left_sum.mine, right_sum.mine, grads)
+    in_part, in_delta, grad_ln1_gain, grad_ln1_bias, grad_query_bias, grad_value_bias = input_back(
+        place, grads, left_parts, right_parts, inputs, far_rows, ln1_gain, grad_middle, far_grad
+    )
+    (in_delta,) = left_sum.hold(in_delta)
+    left_sum.second()
+    (in_delta,) = right_sum.hold(in_delta)
+    right_sum.second()
+    left_sum.mine, right_sum.mine, in_delta, grad_ln1_gain, wide_sum.mine = tie(
+        left_sum.mine, right_sum.mine, in_delta, grad_ln1_gain, wide_sum.mine
+    )
+    (grad_ln1_gain,) = out_sum.hold(grad_ln1_gain)
+    (grad_ln1_gain,) = down_sum.hold(grad_ln1_gain)
+    wide_sum.third(out_sum)
+    (grad_w_down,) = down_sum.last()
+    wide_sum.mine, in_delta, grad_ln1_gain, grad_w_down = tie(
+        wide_sum.mine, in_delta, grad_ln1_gain, grad_w_down
+    )
+    in_delta, grad_ln1_gain = left_sum.hold(in_delta, grad_ln1_gain)
+    in_delta, grad_ln1_gain = right_sum.hold(in_delta, grad_ln1_gain)
+    left_sum.third(right_sum)
+    left_sum.mine, in_delta, grad_ln1_gain = tie(left_sum.mine, in_delta, grad_ln1_gain)
+    grad_vectors = (
+        grad_ln1_gain,
+        grad_ln1_bias,
+        grad_query_bias,
+        grad_value_bias,
+        grad_out_bias,
+        grad_ln2_gain,
+        grad_ln2_bias,
+        grad_up_bias,
+        grad_down_bias,
+    )
+    in_far = swap_y(in_delta)
+    packed = pick(sum_all(pack_vectors(place, grad_vectors, sizes, rows)), dp * 2 + y, 1)
+    result = fill_far(place, out_part, inputs, out_far)
+    grad_up_far, grad_w_out = wide_sum.last([(0, near_width), (near_width, near_width + width)])
+    grad_w_up = jnp.concatenate([grad_up_near, grad_up_far], axis=1)
+    grad_in = fill_far(place, in_part, grad_out, in_far)
+    out_vectors = []
+    at = 0
+    for size in sizes:
+        out_vectors.append(packed[at : at + size].reshape(-1))
+        at += size
+    qkv_cuts = [(part * width, (part + 1) * width) for part in range(3)]
+    return (
+        (result, grad_in)
+        + tuple(left_sum.last(qkv_cuts))
+        + (grad_w_out, grad_w_up, grad_w_down)
+        + tuple(out_vectors)
+    )
 
 
 def solution(mesh):
-    in_specs = (
-        P("dp", "seq", None),
-        P("dp", "seq", None),
-        P("dp", None, "seq", None),
-        P(("dp", "seq"), None),
-        P(("dp", "seq"), None),
-        P(("dp", "seq"), None),
-        P(("dp", "seq"), None),
-        P(("dp", "seq"), None),
-        P(("dp", "seq"), None),
-        P(("dp", "seq")),
-        P(("dp", "seq")),
-        P(("dp", "seq")),
-        P(("dp", "seq")),
-        P(("dp", "seq")),
-        P(("dp", "seq")),
-        P(("dp", "seq")),
-        P(("dp", "seq")),
-        P(("dp", "seq")),
-    )
-    out_specs = (
-        P("dp", "seq", None),
-        P("dp", "seq", None),
-        P(("dp", "seq"), None),
-        P(("dp", "seq"), None),
-        P(("dp", "seq"), None),
-        P(("dp", "seq"), None),
-        P(("dp", "seq"), None),
-        P(("dp", "seq"), None),
-        P(("dp", "seq")),
-        P(("dp", "seq")),
-        P(("dp", "seq")),
-        P(("dp", "seq")),
-        P(("dp", "seq")),
-        P(("dp", "seq")),
-        P(("dp", "seq")),
-        P(("dp", "seq")),
-        P(("dp", "seq")),
-    )
+    tokens, table, matrix, vector = P("dp", "seq", None), P("dp", None, "seq", None), P(BOTH, None), P(BOTH)
+    in_specs = (tokens, tokens, table) + (matrix,) * 6 + (vector,) * 9
+    out_specs = (tokens, tokens) + (matrix,) * 6 + (vector,) * 9
+    paired_fits = mesh.shape["seq"] == 2 and mesh.shape["dp"] % 4 == 0
+
+    def body(inputs, *rest):
+        whole = paired if paired_fits and inputs.shape[0] == 2 else on_device
+        return whole(inputs, *rest)
+
     return jax.shard_map(
-        on_device, mesh=mesh, in_specs=in_specs, out_specs=out_specs, check_vma=False
-    )
+        body, mesh=mesh, in_specs=in_specs, out_specs=out_specs, check_vma=False
+    )

time: 4330 us -> 538 us (0.12)
  waiting for transfers between devices: 2430 us -> 111 us
  local copies, waits for them, and re-layouts: 673 us -> 41.2 us
  matrix products: 579 us -> 0 us
  other arithmetic: 332 us -> 2.64 us
  Pallas kernels: 0 us -> 297 us
  blocking collectives: 273 us -> 0 us
  starting transfers between devices: 2.47 us -> 75.4 us
    reduce_scatter x16 -> x0, waiting for transfers between devices: 2230 us -> none  [the longest x2 736 us: micro_step(): lax.psum_scatter(grads[5], ('dp', 'seq'), scatter_dimension=0, tiled=True)]
    dot_general x62 -> x0, matrix products: 579 us -> none  [the longest x2 135 us: run_backward(): jnp.einsum('hqik,hqid->hqkd', grad_scores, query_heads, preferred_element...]
    reshape x32 -> x3, local copies, waits for them, and re-layouts: 333 us -> 1.22 us  [the longest x2 1.14 us: paired(): out_vectors.append(packed[at:at + size].reshape(-1))]
    pallas_call x0 -> x45, Pallas kernels: none -> 297 us  [call(): pl.pallas_call(body, grid_spec=spec, out_shape=out_shape, name=name, inpu...]
    all_gather x16 -> x0, waiting for transfers between devices: 197 us -> none  [the longest x2 109 us: micro_step(): lax.all_gather(w_value, ('dp', 'seq'), axis=0, tiled=True)]
    while x4 -> x0, blocking collectives: 165 us -> none
    gather x4 -> x0, local copies, waits for them, and re-layouts: 164 us -> none  [pick_blocks(): picked = table[head_index, key_slots]]
    while x10 -> x0, other arithmetic: 125 us -> none
  transfers between devices with their start and end apart: 32 -> 82, of which waited for: 18 -> 21; matrix products, arithmetic and copies ran while one was open for 24% -> 1% of each run, Pallas kernels for 0% -> 47%
where the time goes in v1:
time: 538 us; the launch traced here: 531 us
  Pallas kernels  297 us (55%)
  waiting for transfers between devices  111 us (21%)
  starting transfers between devices  75.4 us (14%)
  local copies, waits for them, and re-layouts  41.2 us (8%)
    pallas_call x45, Pallas kernels, call(): pl.pallas_call(body, grid_spec=spec, out_shape=out_shape, name=name, inpu...  297 us
    ppermute x58, waiting for transfers between devices, pair_swap(): return lax.ppermute(value, axis, [(i, i ^ bit) for i in range(size)])  60.7 us
    ppermute x24, waiting for transfers between devices, ring_z(): lax.ppermute(value, 'dp', [(i, (i + 4 * step) % size) for i in range(size)])  50.7 us
    ppermute x58, starting transfers between devices, pair_swap(): return lax.ppermute(value, axis, [(i, i ^ bit) for i in range(size)])  42.6 us
    unnamed x241, local copies, waits for them, and re-layouts  38.9 us
    ppermute x24, starting transfers between devices, ring_z(): lax.ppermute(value, 'dp', [(i, (i + 4 * step) % size) for i in range(size)])  32.8 us
  transfers between devices with their start and end apart: 82, of which 21 were waited for; matrix products, arithmetic and copies ran while one was open for 1% of the time, Pallas kernels for 47%

profile of v1, /device:TPU:8, one launch (start us, length us, event | category | flops | bytes accessed | tf_op | source)
XLA Modules:
  0.0 530.8 jit_solution(11987509494245431978)
XLA Ops:
  0.8 2.2 copy-done.1
  6.3 2.6 collective-permute-start.1
  8.9 2.5 collective-permute-start
  12.9 5.4 %collective-permute-done.3.refs_1_ = bf16[128,1024]{1,0:T(8,128)(2,1)S(1)} collective-permute-done((bf16[128,1024]{1,0:T(8,128)(2,1)S(1)}, bf16[128,1024]{1,0:T(8,128)(2,1)S(1)}, u32[]{:S(2)}, u32[]{:S(2)}) %collective-permute-start.3) | collective-permute-done | bytes 262176 | tf_op jit(solution)/shard_map/ppermute | solution.py:1417
  18.3 8.5 %collective-permute-done.2.refs_3_ = bf16[32,4224]{1,0:T(8,128)(2,1)S(1)} collective-permute-done((bf16[32,4224]{1,0:T(8,128)(2,1)S(1)}, bf16[32,4224]{1,0:T(8,128)(2,1)S(1)}, u32[]{:S(2)}, u32[]{:S(2)}) %collective-permute-start.2) | collective-permute-done | bytes 270368 | tf_op jit(solution)/shard_map/ppermute | solution.py:1438
  26.9 4.6 collective-permute-done.refs_1_
  38.1 5.6 %collective-permute-done.10.refs_2_ = bf16[128,1024]{1,0:T(8,128)(2,1)S(1)} collective-permute-done((bf16[128,1024]{1,0:T(8,128)(2,1)S(1)}, bf16[128,1024]{1,0:T(8,128)(2,1)S(1)}, u32[]{:S(2)}, u32[]{:S(2)}) %collective-permute-start.10) | collective-permute-done | bytes 262176 | tf_op jit(solution)/shard_map/ppermute | solution.py:1417
  44.4 2.5 collective-permute-start.8
  46.9 11.6 %collective-permute-done.11.refs_3_ = bf16[128,1024]{1,0:T(8,128)(2,1)S(1)} collective-permute-done((bf16[128,1024]{1,0:T(8,128)(2,1)S(1)}, bf16[128,1024]{1,0:T(8,128)(2,1)S(1)}, u32[]{:S(2)}, u32[]{:S(2)}) %collective-permute-start.11) | collective-permute-done | bytes 262176 | tf_op jit(solution)/shard_map/ppermute | solution.py:1417
  64.8 8.7 %collective-permute-done.15.refs_2_ = bf16[32,4096]{1,0:T(8,128)(2,1)} collective-permute-done((bf16[32,4096]{1,0:T(8,128)(2,1)S(1)}, bf16[32,4096]{1,0:T(8,128)(2,1)}, u32[]{:S(2)}, u32[]{:S(2)}) %collective-permute-start.15) | collective-permute-done | bytes 262176 | tf_op jit(solution)/shard_map/ppermute | solution.py:1438
  73.5 4.3 collective-permute-done.5.refs_4_
  77.8 7.7 %collective-permute-done.12.refs_5_ = bf16[4,32,2048]{2,1,0:T(8,128)(2,1)} collective-permute-done((bf16[4,32,2048]{2,1,0:T(8,128)(2,1)}, bf16[4,32,2048]{2,1,0:T(8,128)(2,1)}, u32[]{:S(2)}, u32[]{:S(2)}) %collective-permute-start.12) | collective-permute-done | bytes 524320 | tf_op jit(solution)/shard_map/ppermute | solution.py:1417
  88.0 2.5 join_up.1.refs_0_
  99.9 2.5 collective-permute-start.26
  105.2 14.4 %norm_project.1 = (bf16[1024,1024]{1,0:T(8,128)(2,1)}, bf16[1024,3072]{1,0:T(8,128)(2,1)}) custom-call(s32[4]{0:T(128)} %copy-done.48, f32[2,512,1024]{2,1,0:T(8,128)} %own_ref.9, bf16[512,1024]{1,0:T(8,128)(2,1)} %copy-done.9, f32[1,1024]{1,0:T(1,128)} %copy-done.52, f32[1,1024]{1,0:T(1,128)} %copy-done.77, f32[1,3072]{1,0:T(1,128)} %pad_maximum_fusion.3.bias_ref, ...), custom_call_target="tpu_custom_call" | custom-call | flops 3960000000 | bytes 1 | tf_op jit(solution)/shard_map/norm_project/pallas_call | solution.py:462
  119.6 3.5 collective-permute-done.25.refs_1_
  126.3 2.8 copy-done
  129.1 19.6 %attn_forward.2 = (bf16[16,1024,1024]{2,1,0:T(8,128)(2,1)}, bf16[1024,1024]{1,0:T(8,128)(2,1)S(1)}, f32[1024,1024]{1,0:T(8,128)S(1)}) custom-call(s32[4]{0:T(128)S(1)} %copy-done.49, bf16[1024,3072]{1,0:T(8,128)(2,1)S(1)} %copy-done, bf16[1024,3072]{1,0:T(8,128)(2,1)S(1)} %copy-done, bf16[1024,3072]{1,0:T(8,128)(2,1)S(1)} %copy-done, f32[16,16,128]{2,1,0:T(8,128)S(1)} %bitcast.90), custom_call_target="tpu_custom_call" | custom-call | flops 6000000000 | bytes 1 | tf_op jit(solution)/shard_map/attn_forward/pallas_call | solution.py:462
  151.7 19.7 %attn_forward.3 = (bf16[16,1024,1024]{2,1,0:T(8,128)(2,1)}, bf16[1024,1024]{1,0:T(8,128)(2,1)S(1)}, f32[1024,1024]{1,0:T(8,128)S(1)}) custom-call(s32[4]{0:T(128)S(1)} %copy-done.49, bf16[1024,3072]{1,0:T(8,128)(2,1)S(1)} %copy-done, bf16[1024,3072]{1,0:T(8,128)(2,1)S(1)} %copy-done, ...), custom_call_target="tpu_custom_call", output_to_operand_aliasing={{0}: (5, {}), {1}: (6, {}), {2}: (7, {})} | custom-call | flops 6000000000 | bytes 1 | tf_op jit(solution)/shard_map/attn_forward/pallas_call | solution.py:462
  172.7 10.6 %out_norm.1 = (f32[1024,1024]{1,0:T(8,128)}, bf16[1024,1024]{1,0:T(8,128)(2,1)}, f32[1024,1024]{1,0:T(8,128)}) custom-call(s32[4]{0:T(128)} %copy-done.48, bf16[1024,1024]{1,0:T(8,128)(2,1)} %copy-done.3, f32[1,1024]{1,0:T(1,128)} %copy-done.55, f32[2,512,1024]{2,1,0:T(8,128)} %own_ref.9, bf16[512,1024]{1,0:T(8,128)(2,1)} %copy-done.9, ...), custom_call_target="tpu_custom_call" | custom-call | flops 2400000000 | bytes 1 | tf_op jit(solution)/shard_map/out_norm/pallas_call | solution.py:462
  184.4 12.6 %collective-permute-done.37.refs_12_ = bf16[2,2,128,1024]{3,2,1,0:T(8,128)(2,1)} collective-permute-done((bf16[2,2,128,1024]{3,2,1,0:T(8,128)(2,1)}, bf16[2,2,128,1024]{3,2,1,0:T(8,128)(2,1)}, u32[]{:S(2)}, u32[]{:S(2)}) %collective-permute-start.37) | collective-permute-done | bytes 1048608 | tf_op jit(solution)/shard_map/ppermute | solution.py:1438
  197.6 2.2 copy-done.6
  204.5 42.1 %feed_forward.3 = (bf16[4,256,1024]{2,1,0:T(8,128)(2,1)}, bf16[4,256,1024]{2,1,0:T(8,128)(2,1)}, bf16[8,64,2048]{2,1,0:T(8,128)(2,1)}, bf16[8,64,2048]{2,1,0:T(8...) custom-call(s32[4]{0:T(128)S(1)} %copy-done.50, ...), custom_call_target="tpu_custom_call" | custom-call | flops 10800000000 | bytes 1 | tf_op jit(solution)/shard_map/feed_forward/pallas_call | solution.py:462
  247.2 27.1 %feed_forward.4 = (bf16[2,256,1024]{2,1,0:T(8,128)(2,1)S(1)}, bf16[2,256,1024]{2,1,0:T(8,128)(2,1)}, bf16[8,64,2048]{2,1,0:T(8,128)(2,1)}, bf16[8,64,2048]{2,1,0...) custom-call(s32[4]{0:T(128)S(1)} %copy-done.50, ...), custom_call_target="tpu_custom_call" | custom-call | flops 5400000000 | bytes 1 | tf_op jit(solution)/shard_map/feed_forward/pallas_call | solution.py:462
  274.4 3.3 split_add.13
  278.8 6.0 %split_add.14 = (bf16[8,32,2048]{2,1,0:T(8,128)(2,1)}, bf16[8,32,2048]{2,1,0:T(8,128)(2,1)S(1)}) custom-call(s32[4]{0:T(128)S(1)} %copy-done.50, bf16[8,2,32,2048]{3,2,1,0:T(8,128)(2,1)S(1)} %bitcast.106, bf16[8,2,32,2048]{3,2,1,0:T(8,128)(2,1)} %bitcast.25.came_ref), custom_call_target="tpu_custom_call" | custom-call | flops 1440000000 | bytes 1 | tf_op jit(solution)/shard_map/split_add/pallas_call | solution.py:462
  287.6 27.3 %feed_forward.5 = (bf16[2,256,1024]{2,1,0:T(8,128)(2,1)S(1)}, bf16[2,256,1024]{2,1,0:T(8,128)(2,1)S(1)}, bf16[8,64,2048]{2,1,0:T(8,128)(2,1)}, bf16[8,64,2048]{2...) custom-call(s32[4]{0:T(128)S(1)} %copy-done.50, ...), custom_call_target="tpu_custom_call", output_to_operand_aliasing={{2}: (23, {}), {3}: (24, {})} | custom-call | flops 5400000000 | bytes 1 | tf_op jit(solution)/shard_map/feed_forward/pallas_call | solution.py:462
  320.9 2.2 copy-done.7
  324.3 2.2 copy-done.58
  326.5 2.2 copy-done.59
  328.7 7.7 %middle_back.1 = (f32[1024,1024]{1,0:T(8,128)S(1)}, bf16[1024,1024]{1,0:T(8,128)(2,1)S(1)}, bf16[1024,1024]{1,0:T(8,128)(2,1)S(1)}, f32[1,1024]{1,0:T(1,128)S(1)...) custom-call(s32[4]{0:T(128)S(1)} %copy-done.50, f32[1024,1024]{1,0:T(8,128)S(1)} %copy-done.59, ...), custom_call_target="tpu_custom_call" | custom-call | flops 14400000000 | bytes 1 | tf_op jit(solution)/shard_map/middle_back/pallas_call | solution.py:462
  337.8 3.7 grad_wide.2
  347.9 3.4 split_add.18
  351.9 20.8 %attn_backward.2 = (bf16[1024,1024]{1,0:T(8,128)(2,1)S(1)}, bf16[1024,1024]{1,0:T(8,128)(2,1)S(1)}, bf16[1024,1024]{1,0:T(8,128)(2,1)S(1)}) custom-call(s32[4]{0:T(128)S(1)} %copy-done.50, bf16[1024,3072]{1,0:T(8,128)(2,1)S(1)} %bitcast.80, bf16[1024,3072]{1,0:T(8,128)(2,1)S(1)} %bitcast.80, bf16[1024,3072]{1,0:T(8,128)(2,1)S(1)} %bitcast.80, ...), custom_call_target="tpu_custom_call" | custom-call | flops 6000000000 | bytes 1 | tf_op jit(solution)/shard_map/attn_backward/pallas_call | solution.py:462
  377.2 4.3 collective-permute-start.54
  381.5 20.7 %attn_backward.3 = (bf16[1024,1024]{1,0:T(8,128)(2,1)S(1)}, bf16[1024,1024]{1,0:T(8,128)(2,1)S(1)}, bf16[1024,1024]{1,0:T(8,128)(2,1)S(1)}) custom-call(s32[4]{0:T(128)S(1)} %copy-done.50, bf16[1024,3072]{1,0:T(8,128)(2,1)S(1)} %bitcast.80, bf16[1024,3072]{1,0:T(8,128)(2,1)S(1)} %bitcast.80, ...), custom_call_target="tpu_custom_call", output_to_operand_aliasing={{0}: (8, {}), {1}: (9, {}), {2}: (10, {})} | custom-call | flops 6000000000 | bytes 1 | tf_op jit(solution)/shard_map/attn_backward/pallas_call | solution.py:462
  408.6 10.3 %grad_wide.3 = (bf16[8,64,1536]{2,1,0:T(8,128)(2,1)S(1)}, bf16[8,64,1536]{2,1,0:T(8,128)(2,1)S(1)}, bf16[8,64,1536]{2,1,0:T(8,128)(2,1)S(1)}, bf16[8,64,1536]{2,1,0:T(8,128)(2,1)S(1)}) custom-call(s32[4]{0:T(128)S(1)} %copy-done.50, bf16[1024,1024]{1,0:T(8,128)(2,1)S(1)} %copy-done.89, bf16[1024,1024]{1,0:T(8,128)(2,1)S(1)} %get-tuple-element.612.refs_0_.query_ref, ...), custom_call_target="tpu_custom_call" | custom-call | flops 3240000000 | bytes 1 | tf_op jit(solution)/shard_map/grad_wide/pallas_call | solution.py:462
  432.1 18.6 %input_back.1 = (f32[2,512,1024]{2,1,0:T(8,128)}, bf16[512,1024]{1,0:T(8,128)(2,1)}, f32[1,1024]{1,0:T(1,128)}, f32[1,1024]{1,0:T(1,128)}, f32[1,1024]{1,0:T(1,128)}, /*index=5*/f32[1,1024]{1,0:T(1,128)}) custom-call(s32[4]{0:T(128)} %copy-done.48, bf16[1024,1024]{1,0:T(8,128)(2,1)} %copy-done.13, bf16[1024,1024]{1,0:T(8,128)(2,1)} %copy-done.14, ...), custom_call_target="tpu_custom_call" | custom-call | flops 4800000000 | bytes 1 | tf_op jit(solution)/shard_map/input_back/pallas_call | solution.py:462
  460.2 3.0 collective-permute-start.74
  465.4 3.1 pack_vectors.1
  473.6 3.4 collective-permute-done.77
  479.3 2.2 copy-done.2
  483.4 3.8 collective-permute-done.75.refs_2_
  489.4 16.7 %collective-permute-done.78 = f32[12,32,32]{2,1,0:T(8,128)S(1)} collective-permute-done((f32[12,32,32]{2,1,0:T(8,128)S(1)}, f32[12,32,32]{2,1,0:T(8,128)S(1)}, u32[]{:S(2)}, u32[]{:S(2)}) %collective-permute-start.78) | collective-permute-done | bytes 49184 | tf_op jit(solution)/shard_map/ppermute | solution.py:1417
  508.1 2.6 collective-permute-start.80
  512.6 2.3 last_add.6
  514.8 8.3 %collective-permute-done.81 = f32[12,32,32]{2,1,0:T(8,128)S(1)} collective-permute-done((f32[12,32,32]{2,1,0:T(8,128)S(1)}, f32[12,32,32]{2,1,0:T(8,128)S(1)}, u32[]{:S(2)}, u32[]{:S(2)}) %collective-permute-start.81) | collective-permute-done | bytes 49184 | tf_op jit(solution)/shard_map/ppermute | solution.py:1438
  526.2 2.2 copy-done.8
  (435 shorter events, 121.9 us)
Async XLA Ops:
  3.8 27.7 %collective-permute-start.4 = (bf16[512,1024]{1,0:T(8,128)(2,1)S(1)}, bf16[512,1024]{1,0:T(8,128)(2,1)S(1)}, u32[]{:S(2)}, u32[]{:S(2)}) collective-permute-start(bf16[512,1024]{1,0:T(8,128)(2,1)S(1)} %cast_far.2), channel_id=1, source_target_pairs={{0,1},{1,0},{2,3},{3,2},{4,5},{5,4},{6,7},{7,6},{8,9},{9,8},{10,11... | collective-permute-start | bytes 3145736 | tf_op jit(solution)/shard_map/ppermute | solution.py:1417
  5.8 21.0 %collective-permute-start.2 = (bf16[32,4224]{1,0:T(8,128)(2,1)S(1)}, bf16[32,4224]{1,0:T(8,128)(2,1)S(1)}, u32[]{:S(2)}, u32[]{:S(2)}) collective-permute-start(bf16[32,4224]{1,0:T(8,128)(2,1)S(1)} %constant_dynamic-update-slice_fusion.refs_0_), channel_id=1, source_target_pairs={{0,24},{2,26},{4,28},{6,30},{8,0},{10,2},{12,4},{14,6},{16,8},{18,... | collective-permute-start | bytes 811016 | tf_op jit(solution)/shard_map/ppermute | solution.py:1438
  6.3 20.5 %collective-permute-start.1 = (bf16[32,4224]{1,0:T(8,128)(2,1)S(1)}, bf16[32,4224]{1,0:T(8,128)(2,1)S(1)}, u32[]{:S(2)}, u32[]{:S(2)}) collective-permute-start(bf16[32,4224]{1,0:T(8,128)(2,1)S(1)} %constant_dynamic-update-slice_fusion.refs_0_), channel_id=1, source_target_pairs={{0,16},{2,18},{4,20},{6,22},{8,24},{10,26},{12,28},{14,30},{16,0},... | collective-permute-start | bytes 811016 | tf_op jit(solution)/shard_map/ppermute | solution.py:1438
  8.9 22.6 %collective-permute-start = (bf16[32,4224]{1,0:T(8,128)(2,1)S(1)}, bf16[32,4224]{1,0:T(8,128)(2,1)S(1)}, u32[]{:S(2)}, u32[]{:S(2)}) collective-permute-start(bf16[32,4224]{1,0:T(8,128)(2,1)S(1)} %constant_dynamic-update-slice_fusion.refs_0_), channel_id=1, source_target_pairs={{0,8},{2,10},{4,12},{6,14},{8,16},{10,18},{12,20},{14,22},{16,24},... | collective-permute-start | bytes 811016 | tf_op jit(solution)/shard_map/ppermute | solution.py:1438
  32.9 28.1 %collective-permute-start.7 = (bf16[4,32,2176]{2,1,0:T(8,128)(2,1)S(1)}, bf16[4,32,2176]{2,1,0:T(8,128)(2,1)S(1)}, u32[]{:S(2)}, u32[]{:S(2)}) collective-permute-start(bf16[4,32,2176]{2,1,0:T(8,128)(2,1)S(1)} %get-tuple-element.393.refs_0_.refs_8_), channel_id=1, source_target_pairs={{0,4},{2,6},{4,0},{6,2},{8,12},{10,14},{12,8},{14,10},{16,20},{18,... | collective-permute-start | bytes 1671176 | tf_op jit(solution)/shard_map/ppermute | solution.py:1417
  34.9 26.1 %collective-permute-start.6 = (bf16[4,32,2048]{2,1,0:T(8,128)(2,1)}, bf16[4,32,2048]{2,1,0:T(8,128)(2,1)}, u32[]{:S(2)}, u32[]{:S(2)}) collective-permute-start(bf16[4,32,2048]{2,1,0:T(8,128)(2,1)} %get-tuple-element.405.refs_0_), channel_id=1, source_target_pairs={{0,1},{1,0},{2,3},{3,2},{4,5},{5,4},{6,7},{7,6},{8,9},{9,8},{10,11... | collective-permute-start | bytes 1572872 | tf_op jit(solution)/shard_map/ppermute | solution.py:1417
  36.5 22.0 %collective-permute-start.11 = (bf16[128,1024]{1,0:T(8,128)(2,1)S(1)}, bf16[128,1024]{1,0:T(8,128)(2,1)S(1)}, u32[]{:S(2)}, u32[]{:S(2)}) collective-permute-start(bf16[128,1024]{1,0:T(8,128)(2,1)S(1)} %collective-permute-done.3.refs_1_), channel_id=1, source_target_pairs={{0,1},{1,0},{2,3},{3,2},{4,5},{5,4},{6,7},{7,6},{8,9},{9,8},{10,11... | collective-permute-start | bytes 786440 | tf_op jit(solution)/shard_map/ppermute | solution.py:1417
  37.0 22.7 %collective-permute-start.9 = (bf16[32,4096]{1,0:T(8,128)(2,1)S(1)}, bf16[32,4096]{1,0:T(8,128)(2,1)S(1)}, u32[]{:S(2)}, u32[]{:S(2)}) collective-permute-start(bf16[32,4096]{1,0:T(8,128)(2,1)S(1)} %copy-done.61), channel_id=1, source_target_pairs={{0,24},{2,26},{4,28},{6,30},{8,0},{10,2},{12,4},{14,6},{16,8},{18,... | collective-permute-start | bytes 786440 | tf_op jit(solution)/shard_map/ppermute | solution.py:1438
  61.1 24.4 %collective-permute-start.14 = (bf16[4,32,2176]{2,1,0:T(8,128)(2,1)S(1)}, bf16[4,32,2176]{2,1,0:T(8,128)(2,1)}, u32[]{:S(2)}, u32[]{:S(2)}) collective-permute-start(bf16[4,32,2176]{2,1,0:T(8,128)(2,1)S(1)} %collective-permute-done.7.refs_4_.refs_12_), channel_id=1, source_target_pairs={{0,1},{1,0},{2,3},{3,2},{4,5},{5,4},{6,7},{7,6},{8,9},{9,8},{10,11... | collective-permute-start | bytes 1671176 | tf_op jit(solution)/shard_map/ppermute | solution.py:1417
  63.2 22.3 %collective-permute-start.12 = (bf16[4,32,2048]{2,1,0:T(8,128)(2,1)}, bf16[4,32,2048]{2,1,0:T(8,128)(2,1)}, u32[]{:S(2)}, u32[]{:S(2)}) collective-permute-start(bf16[4,32,2048]{2,1,0:T(8,128)(2,1)} %collective-permute-done.6.refs_1_), channel_id=1, source_target_pairs={{0,4},{2,6},{4,0},{6,2},{8,12},{10,14},{12,8},{14,10},{16,20},{18,... | collective-permute-start | bytes 1572872 | tf_op jit(solution)/shard_map/ppermute | solution.py:1417
  97.4 53.3 %collective-permute-start.28 = (bf16[4,32,4096]{2,1,0:T(8,128)(2,1)}, bf16[4,32,4096]{2,1,0:T(8,128)(2,1)S(1)}, u32[]{:S(2)}, u32[]{:S(2)}) collective-permute-start(bf16[4,32,4096]{2,1,0:T(8,128)(2,1)} %join_up.1.refs_0_), channel_id=1, source_target_pairs={{0,4},{2,6},{4,0},{6,2},{8,12},{10,14},{12,8},{14,10},{16,20},{18,... | collective-permute-start | bytes 3145736 | tf_op jit(solution)/shard_map/ppermute | solution.py:1417
  97.9 25.2 %collective-permute-start.25 = (bf16[4,32,4096]{2,1,0:T(8,128)(2,1)}, bf16[4,32,4096]{2,1,0:T(8,128)(2,1)}, u32[]{:S(2)}, u32[]{:S(2)}) collective-permute-start(bf16[4,32,4096]{2,1,0:T(8,128)(2,1)} %join_up.1.refs_0_), channel_id=1, source_target_pairs={{0,1},{1,0},{2,3},{3,2},{4,5},{5,4},{6,7},{7,6},{8,9},{9,8},{10,11... | collective-permute-start | bytes 3145736 | tf_op jit(solution)/shard_map/ppermute | solution.py:1417
  99.9 48.8 %collective-permute-start.27 = (bf16[2,2,128,1024]{3,2,1,0:T(8,128)(2,1)}, bf16[2,2,128,1024]{3,2,1,0:T(8,128)(2,1)}, u32[]{:S(2)}, u32[]{:S(2)}) collective-permute-start(bf16[2,2,128,1024]{3,2,1,0:T(8,128)(2,1)} %join_plane.1.refs_8_), channel_id=1, source_target_pairs={{0,24},{2,26},{4,28},{6,30},{8,0},{10,2},{12,4},{14,6},{16,8},{18,... | collective-permute-start | bytes 3145736 | tf_op jit(solution)/shard_map/ppermute | solution.py:1438
  99.9 48.8 %collective-permute-start.26 = (bf16[2,2,128,1024]{3,2,1,0:T(8,128)(2,1)}, bf16[2,2,128,1024]{3,2,1,0:T(8,128)(2,1)}, u32[]{:S(2)}, u32[]{:S(2)}) collective-permute-start(bf16[2,2,128,1024]{3,2,1,0:T(8,128)(2,1)} %join_plane.1.refs_8_), channel_id=1, source_target_pairs={{0,8},{2,10},{4,12},{6,14},{8,16},{10,18},{12,20},{14,22},{16,24},... | collective-permute-start | bytes 3145736 | tf_op jit(solution)/shard_map/ppermute | solution.py:1438
  123.2 28.5 %collective-permute-start.29 = (bf16[4,32,4096]{2,1,0:T(8,128)(2,1)}, bf16[4,32,4096]{2,1,0:T(8,128)(2,1)S(1)}, u32[]{:S(2)}, u32[]{:S(2)}) collective-permute-start(bf16[4,32,4096]{2,1,0:T(8,128)(2,1)} %collective-permute-done.25.refs_1_), channel_id=1, source_target_pairs={{0,4},{2,6},{4,0},{6,2},{8,12},{10,14},{12,8},{14,10},{16,20},{18,... | collective-permute-start | bytes 3145736 | tf_op jit(solution)/shard_map/ppermute | solution.py:1417
  148.7 34.7 %collective-permute-start.30 = (bf16[512,1024]{1,0:T(8,128)(2,1)}, bf16[512,1024]{1,0:T(8,128)(2,1)S(1)}, u32[]{:S(2)}, u32[]{:S(2)}) collective-permute-start(bf16[512,1024]{1,0:T(8,128)(2,1)} %cast_far.3), channel_id=1, source_target_pairs={{0,1},{1,0},{2,3},{3,2},{4,5},{5,4},{6,7},{7,6},{8,9},{9,8},{10,11... | collective-permute-start | bytes 3145736 | tf_op jit(solution)/shard_map/ppermute | solution.py:1417
  150.2 33.7 %collective-permute-start.31 = (bf16[4,32,4096]{2,1,0:T(8,128)(2,1)}, bf16[4,32,4096]{2,1,0:T(8,128)(2,1)}, u32[]{:S(2)}, u32[]{:S(2)}) collective-permute-start(bf16[4,32,4096]{2,1,0:T(8,128)(2,1)} %join_up.1.refs_0_), channel_id=1, source_target_pairs={{0,2},{2,0},{4,6},{6,4},{8,10},{10,8},{12,14},{14,12},{16,18},{18,... | collective-permute-start | bytes 3145736 | tf_op jit(solution)/shard_map/ppermute | solution.py:1417
  150.2 33.8 %collective-permute-start.32 = (bf16[4,32,4096]{2,1,0:T(8,128)(2,1)}, bf16[4,32,4096]{2,1,0:T(8,128)(2,1)}, u32[]{:S(2)}, u32[]{:S(2)}) collective-permute-start(bf16[4,32,4096]{2,1,0:T(8,128)(2,1)} %collective-permute-done.25.refs_1_), channel_id=1, source_target_pairs={{0,2},{2,0},{4,6},{6,4},{8,10},{10,8},{12,14},{14,12},{16,18},{18,... | collective-permute-start | bytes 3145736 | tf_op jit(solution)/shard_map/ppermute | solution.py:1417
  150.7 46.4 %collective-permute-start.37 = (bf16[2,2,128,1024]{3,2,1,0:T(8,128)(2,1)}, bf16[2,2,128,1024]{3,2,1,0:T(8,128)(2,1)}, u32[]{:S(2)}, u32[]{:S(2)}) collective-permute-start(bf16[2,2,128,1024]{3,2,1,0:T(8,128)(2,1)} %join_plane.1.refs_8_), channel_id=1, source_target_pairs={{0,16},{2,18},{4,20},{6,22},{8,24},{10,26},{12,28},{14,30},{16,0},... | collective-permute-start | bytes 3145736 | tf_op jit(solution)/shard_map/ppermute | solution.py:1438
  151.7 45.4 %collective-permute-start.36 = (bf16[2,2,128,1024]{3,2,1,0:T(8,128)(2,1)}, bf16[2,2,128,1024]{3,2,1,0:T(8,128)(2,1)}, u32[]{:S(2)}, u32[]{:S(2)}) collective-permute-start(bf16[2,2,128,1024]{3,2,1,0:T(8,128)(2,1)} %collective-permute-done.26.refs_10_), channel_id=1, source_target_pairs={{0,2},{2,0},{4,6},{6,4},{8,10},{10,8},{12,14},{14,12},{16,18},{18,... | collective-permute-start | bytes 3145736 | tf_op jit(solution)/shard_map/ppermute | solution.py:1417
  183.4 18.8 %collective-permute-start.35 = (bf16[2,2,128,1024]{3,2,1,0:T(8,128)(2,1)}, bf16[2,2,128,1024]{3,2,1,0:T(8,128)(2,1)S(1)}, u32[]{:S(2)}, u32[]{:S(2)}) collective-permute-start(bf16[2,2,128,1024]{3,2,1,0:T(8,128)(2,1)} %join_plane.1.refs_8_), channel_id=1, source_target_pairs={{0,2},{2,0},{4,6},{6,4},{8,10},{10,8},{12,14},{14,12},{16,18},{18,... | collective-permute-start | bytes 3145736 | tf_op jit(solution)/shard_map/ppermute | solution.py:1417
  246.6 27.8 %collective-permute-start.40 = (bf16[4,256,1024]{2,1,0:T(8,128)(2,1)}, bf16[4,256,1024]{2,1,0:T(8,128)(2,1)}, u32[]{:S(2)}, u32[]{:S(2)}) collective-permute-start(bf16[4,256,1024]{2,1,0:T(8,128)(2,1)} %get-tuple-element.446), channel_id=1, source_target_pairs={{0,2},{2,0},{4,6},{6,4},{8,10},{10,8},{12,14},{14,12},{16,18},{18,... | collective-permute-start | bytes 6291464 | tf_op jit(solution)/shard_map/ppermute | solution.py:1417
  246.7 27.7 %collective-permute-start.41 = (bf16[8,64,2048]{2,1,0:T(8,128)(2,1)}, bf16[8,64,2048]{2,1,0:T(8,128)(2,1)}, u32[]{:S(2)}, u32[]{:S(2)}) collective-permute-start(bf16[8,64,2048]{2,1,0:T(8,128)(2,1)} %get-tuple-element.452), channel_id=1, source_target_pairs={{0,2},{2,0},{4,6},{6,4},{8,10},{10,8},{12,14},{14,12},{16,18},{18,... | collective-permute-start | bytes 6291464 | tf_op jit(solution)/shard_map/ppermute | solution.py:1417
  274.3 42.2 %collective-permute-start.43 = (bf16[2,256,1024]{2,1,0:T(8,128)(2,1)}, bf16[2,256,1024]{2,1,0:T(8,128)(2,1)}, u32[]{:S(2)}, u32[]{:S(2)}) collective-permute-start(bf16[2,256,1024]{2,1,0:T(8,128)(2,1)} %get-tuple-element.467), channel_id=1, source_target_pairs={{0,2},{2,0},{4,6},{6,4},{8,10},{10,8},{12,14},{14,12},{16,18},{18,... | collective-permute-start | bytes 3145736 | tf_op jit(solution)/shard_map/ppermute | solution.py:1417
  285.8 30.7 %collective-permute-start.44 = (bf16[8,32,2048]{2,1,0:T(8,128)(2,1)}, bf16[8,32,2048]{2,1,0:T(8,128)(2,1)S(1)}, u32[]{:S(2)}, u32[]{:S(2)}) collective-permute-start(bf16[8,32,2048]{2,1,0:T(8,128)(2,1)} %get-tuple-element.469), channel_id=1, source_target_pairs={{0,1},{1,0},{2,3},{3,2},{4,5},{5,4},{6,7},{7,6},{8,9},{9,8},{10,11... | collective-permute-start | bytes 3145736 | tf_op jit(solution)/shard_map/ppermute | solution.py:1417
  287.0 29.4 %collective-permute-start.45 = (bf16[2,256,1024]{2,1,0:T(8,128)(2,1)}, bf16[2,256,1024]{2,1,0:T(8,128)(2,1)S(1)}, u32[]{:S(2)}, u32[]{:S(2)}) collective-permute-start(bf16[2,256,1024]{2,1,0:T(8,128)(2,1)} %get-tuple-element.471), channel_id=1, source_target_pairs={{0,4},{2,6},{4,0},{6,2},{8,12},{10,14},{12,8},{14,10},{16,20},{18,... | collective-permute-start | bytes 3145736 | tf_op jit(solution)/shard_map/ppermute | solution.py:1417
  315.9 29.1 %collective-permute-start.47 = (bf16[8,64,2048]{2,1,0:T(8,128)(2,1)}, bf16[8,64,2048]{2,1,0:T(8,128)(2,1)}, u32[]{:S(2)}, u32[]{:S(2)}) collective-permute-start(bf16[8,64,2048]{2,1,0:T(8,128)(2,1)} %get-tuple-element.495), channel_id=1, source_target_pairs={{0,2},{2,0},{4,6},{6,4},{8,10},{10,8},{12,14},{14,12},{16,18},{18,... | collective-permute-start | bytes 6291464 | tf_op jit(solution)/shard_map/ppermute | solution.py:1417
  315.9 26.5 %collective-permute-start.42 = (bf16[2,256,1024]{2,1,0:T(8,128)(2,1)}, bf16[2,256,1024]{2,1,0:T(8,128)(2,1)S(1)}, u32[]{:S(2)}, u32[]{:S(2)}) collective-permute-start(bf16[2,256,1024]{2,1,0:T(8,128)(2,1)} %copy-done.60), channel_id=1, source_target_pairs={{0,2},{2,0},{4,6},{6,4},{8,10},{10,8},{12,14},{14,12},{16,18},{18,... | collective-permute-start | bytes 3145736 | tf_op jit(solution)/shard_map/ppermute | solution.py:1417
  319.4 23.0 %collective-permute-start.46 = (bf16[1,256,1024]{2,1,0:T(8,128)(2,1)S(1)}, bf16[1,256,1024]{2,1,0:T(8,128)(2,1)S(1)}, u32[]{:S(2)}, u32[]{:S(2)}) collective-permute-start(bf16[1,256,1024]{2,1,0:T(8,128)(2,1)S(1)} %get-tuple-element.480), channel_id=1, source_target_pairs={{0,4},{2,6},{4,0},{6,2},{8,12},{10,14},{12,8},{14,10},{16,20},{18,... | collective-permute-start | bytes 1572872 | tf_op jit(solution)/shard_map/ppermute | solution.py:1417
  345.0 27.8 %collective-permute-start.48 = (bf16[512,1024]{1,0:T(8,128)(2,1)S(1)}, bf16[512,1024]{1,0:T(8,128)(2,1)S(1)}, u32[]{:S(2)}, u32[]{:S(2)}) collective-permute-start(bf16[512,1024]{1,0:T(8,128)(2,1)S(1)} %get-tuple-element.503), channel_id=1, source_target_pairs={{0,1},{1,0},{2,3},{3,2},{4,5},{5,4},{6,7},{7,6},{8,9},{9,8},{10,11... | collective-permute-start | bytes 3145736 | tf_op jit(solution)/shard_map/ppermute | solution.py:1417
  345.8 29.3 %collective-permute-start.51 = (bf16[8,64,1024]{2,1,0:T(8,128)(2,1)S(1)}, bf16[8,64,1024]{2,1,0:T(8,128)(2,1)S(1)}, u32[]{:S(2)}, u32[]{:S(2)}) collective-permute-start(bf16[8,64,1024]{2,1,0:T(8,128)(2,1)S(1)} %get-tuple-element.529), channel_id=1, source_target_pairs={{0,2},{2,0},{4,6},{6,4},{8,10},{10,8},{12,14},{14,12},{16,18},{18,... | collective-permute-start | bytes 3145736 | tf_op jit(solution)/shard_map/ppermute | solution.py:1417
  345.9 26.9 %collective-permute-start.50 = (bf16[4,32,2048]{2,1,0:T(8,128)(2,1)S(1)}, bf16[4,32,2048]{2,1,0:T(8,128)(2,1)S(1)}, u32[]{:S(2)}, u32[]{:S(2)}) collective-permute-start(bf16[4,32,2048]{2,1,0:T(8,128)(2,1)S(1)} %get-tuple-element.510), channel_id=1, source_target_pairs={{0,4},{2,6},{4,0},{6,2},{8,12},{10,14},{12,8},{14,10},{16,20},{18,... | collective-permute-start | bytes 1572872 | tf_op jit(solution)/shard_map/ppermute | solution.py:1417
  346.4 26.4 %collective-permute-start.49 = (bf16[1,256,1024]{2,1,0:T(8,128)(2,1)S(1)}, bf16[1,256,1024]{2,1,0:T(8,128)(2,1)S(1)}, u32[]{:S(2)}, u32[]{:S(2)}) collective-permute-start(bf16[1,256,1024]{2,1,0:T(8,128)(2,1)S(1)} %get-tuple-element.508), channel_id=1, source_target_pairs={{0,4},{2,6},{4,0},{6,2},{8,12},{10,14},{12,8},{14,10},{16,20},{18,... | collective-permute-start | bytes 1572872 | tf_op jit(solution)/shard_map/ppermute | solution.py:1417
  351.3 53.3 %collective-permute-start.52 = (bf16[4,64,2048]{2,1,0:T(8,128)(2,1)S(1)}, bf16[4,64,2048]{2,1,0:T(8,128)(2,1)S(1)}, u32[]{:S(2)}, u32[]{:S(2)}) collective-permute-start(bf16[4,64,2048]{2,1,0:T(8,128)(2,1)S(1)} %get-tuple-element.541), channel_id=1, source_target_pairs={{0,4},{2,6},{4,0},{6,2},{8,12},{10,14},{12,8},{14,10},{16,20},{18,... | collective-permute-start | bytes 3145736 | tf_op jit(solution)/shard_map/ppermute | solution.py:1417
  373.9 33.2 %collective-permute-start.56 = (bf16[4,128,1024]{2,1,0:T(8,128)(2,1)S(1)}, bf16[4,128,1024]{2,1,0:T(8,128)(2,1)S(1)}, u32[]{:S(2)}, u32[]{:S(2)}) collective-permute-start(bf16[4,128,1024]{2,1,0:T(8,128)(2,1)S(1)} %get-tuple-element.559), channel_id=1, source_target_pairs={{0,1},{1,0},{2,3},{3,2},{4,5},{5,4},{6,7},{7,6},{8,9},{9,8},{10,11... | collective-permute-start | bytes 3145736 | tf_op jit(solution)/shard_map/ppermute | solution.py:1417
  375.9 27.2 %collective-permute-start.53 = (bf16[32,2048]{1,0:T(8,128)(2,1)S(1)}, bf16[32,2048]{1,0:T(8,128)(2,1)S(1)}, u32[]{:S(2)}, u32[]{:S(2)}) collective-permute-start(bf16[32,2048]{1,0:T(8,128)(2,1)S(1)} %get-tuple-element.543), channel_id=1, source_target_pairs={{0,8},{2,10},{4,12},{6,14},{8,16},{10,18},{12,20},{14,22},{16,24},... | collective-permute-start | bytes 393224 | tf_op jit(solution)/shard_map/ppermute | solution.py:1438
  377.2 27.4 %collective-permute-start.54 = (bf16[32,2048]{1,0:T(8,128)(2,1)S(1)}, bf16[32,2048]{1,0:T(8,128)(2,1)S(1)}, u32[]{:S(2)}, u32[]{:S(2)}) collective-permute-start(bf16[32,2048]{1,0:T(8,128)(2,1)S(1)} %get-tuple-element.544), channel_id=1, source_target_pairs={{0,16},{2,18},{4,20},{6,22},{8,24},{10,26},{12,28},{14,30},{16,0},... | collective-permute-start | bytes 393224 | tf_op jit(solution)/shard_map/ppermute | solution.py:1438
  381.5 23.2 %collective-permute-start.55 = (bf16[32,2048]{1,0:T(8,128)(2,1)S(1)}, bf16[32,2048]{1,0:T(8,128)(2,1)S(1)}, u32[]{:S(2)}, u32[]{:S(2)}) collective-permute-start(bf16[32,2048]{1,0:T(8,128)(2,1)S(1)} %get-tuple-element.545), channel_id=1, source_target_pairs={{0,24},{2,26},{4,28},{6,30},{8,0},{10,2},{12,4},{14,6},{16,8},{18,... | collective-permute-start | bytes 393224 | tf_op jit(solution)/shard_map/ppermute | solution.py:1438
  424.6 26.2 %collective-permute-start.61 = (bf16[4,64,1536]{2,1,0:T(8,128)(2,1)}, bf16[4,64,1536]{2,1,0:T(8,128)(2,1)S(1)}, u32[]{:S(2)}, u32[]{:S(2)}) collective-permute-start(bf16[4,64,1536]{2,1,0:T(8,128)(2,1)} %get-tuple-element.618), channel_id=1, source_target_pairs={{0,4},{2,6},{4,0},{6,2},{8,12},{10,14},{12,8},{14,10},{16,20},{18,... | collective-permute-start | bytes 2359304 | tf_op jit(solution)/shard_map/ppermute | solution.py:1417
  426.2 25.8 %collective-permute-start.62 = (bf16[8,32,1536]{2,1,0:T(8,128)(2,1)S(1)}, bf16[8,32,1536]{2,1,0:T(8,128)(2,1)S(1)}, u32[]{:S(2)}, u32[]{:S(2)}) collective-permute-start(bf16[8,32,1536]{2,1,0:T(8,128)(2,1)S(1)} %get-tuple-element.624), channel_id=1, source_target_pairs={{0,1},{1,0},{2,3},{3,2},{4,5},{5,4},{6,7},{7,6},{8,9},{9,8},{10,11... | collective-permute-start | bytes 2359304 | tf_op jit(solution)/shard_map/ppermute | solution.py:1417
  426.8 28.8 %collective-permute-start.65 = (bf16[128,1024]{1,0:T(8,128)(2,1)}, bf16[128,1024]{1,0:T(8,128)(2,1)S(1)}, u32[]{:S(2)}, u32[]{:S(2)}) collective-permute-start(bf16[128,1024]{1,0:T(8,128)(2,1)} %get-tuple-element.644), channel_id=1, source_target_pairs={{0,8},{2,10},{4,12},{6,14},{8,16},{10,18},{12,20},{14,22},{16,24},... | collective-permute-start | bytes 786440 | tf_op jit(solution)/shard_map/ppermute | solution.py:1438
  428.8 26.8 %collective-permute-start.66 = (bf16[128,1024]{1,0:T(8,128)(2,1)}, bf16[128,1024]{1,0:T(8,128)(2,1)S(1)}, u32[]{:S(2)}, u32[]{:S(2)}) collective-permute-start(bf16[128,1024]{1,0:T(8,128)(2,1)} %get-tuple-element.645), channel_id=1, source_target_pairs={{0,16},{2,18},{4,20},{6,22},{8,24},{10,26},{12,28},{14,30},{16,0},... | collective-permute-start | bytes 786440 | tf_op jit(solution)/shard_map/ppermute | solution.py:1438
  430.6 22.8 %collective-permute-start.64 = (bf16[4,32,1024]{2,1,0:T(8,128)(2,1)}, bf16[4,32,1024]{2,1,0:T(8,128)(2,1)S(1)}, u32[]{:S(2)}, u32[]{:S(2)}) collective-permute-start(bf16[4,32,1024]{2,1,0:T(8,128)(2,1)} %get-tuple-element.637), channel_id=1, source_target_pairs={{0,1},{1,0},{2,3},{3,2},{4,5},{5,4},{6,7},{7,6},{8,9},{9,8},{10,11... | collective-permute-start | bytes 786440 | tf_op jit(solution)/shard_map/ppermute | solution.py:1417
  473.5 34.6 %collective-permute-start.70 = (bf16[32,3072]{1,0:T(8,128)(2,1)S(1)}, bf16[32,3072]{1,0:T(8,128)(2,1)S(1)}, u32[]{:S(2)}, u32[]{:S(2)}) collective-permute-start(bf16[32,3072]{1,0:T(8,128)(2,1)S(1)} %get-tuple-element.668), channel_id=1, source_target_pairs={{0,8},{2,10},{4,12},{6,14},{8,16},{10,18},{12,20},{14,22},{16,24},... | collective-permute-start | bytes 589832 | tf_op jit(solution)/shard_map/ppermute | solution.py:1438
  477.1 33.7 %collective-permute-start.71 = (bf16[32,3072]{1,0:T(8,128)(2,1)S(1)}, bf16[32,3072]{1,0:T(8,128)(2,1)}, u32[]{:S(2)}, u32[]{:S(2)}) collective-permute-start(bf16[32,3072]{1,0:T(8,128)(2,1)S(1)} %get-tuple-element.669), channel_id=1, source_target_pairs={{0,16},{2,18},{4,20},{6,22},{8,24},{10,26},{12,28},{14,30},{16,0},... | collective-permute-start | bytes 589832 | tf_op jit(solution)/shard_map/ppermute | solution.py:1438
  477.2 49.0 %collective-permute-start.69 = (bf16[512,1024]{1,0:T(8,128)(2,1)}, bf16[512,1024]{1,0:T(8,128)(2,1)S(1)}, u32[]{:S(2)}, u32[]{:S(2)}) collective-permute-start(bf16[512,1024]{1,0:T(8,128)(2,1)} %get-tuple-element.666), channel_id=1, source_target_pairs={{0,1},{1,0},{2,3},{3,2},{4,5},{5,4},{6,7},{7,6},{8,9},{9,8},{10,11... | collective-permute-start | bytes 3145736 | tf_op jit(solution)/shard_map/ppermute | solution.py:1417
  478.7 27.4 %collective-permute-start.78 = (f32[12,32,32]{2,1,0:T(8,128)S(1)}, f32[12,32,32]{2,1,0:T(8,128)S(1)}, u32[]{:S(2)}, u32[]{:S(2)}) collective-permute-start(f32[12,32,32]{2,1,0:T(8,128)S(1)} %add.110), channel_id=1, source_target_pairs={{0,1},{1,0},{2,3},{3,2},{4,5},{5,4},{6,7},{7,6},{8,9},{9,8},{10,11... | collective-permute-start | bytes 147464 | tf_op jit(solution)/shard_map/ppermute | solution.py:1417
  489.4 23.2 %collective-permute-start.72 = (bf16[32,3072]{1,0:T(8,128)(2,1)S(1)}, bf16[32,3072]{1,0:T(8,128)(2,1)S(1)}, u32[]{:S(2)}, u32[]{:S(2)}) collective-permute-start(bf16[32,3072]{1,0:T(8,128)(2,1)S(1)} %get-tuple-element.670), channel_id=1, source_target_pairs={{0,24},{2,26},{4,28},{6,30},{8,0},{10,2},{12,4},{14,6},{16,8},{18,... | collective-permute-start | bytes 589832 | tf_op jit(solution)/shard_map/ppermute | solution.py:1438
  (152 other events, 1680.7 us)

commit v2 on v1

--- a/solution.py
+++ b/solution.py
@@ -413,24 +413,26 @@
 TIMES = dict(
     cast_far=1,
     join_first=2,
+    join_beside=1,
     join_up=2,
     join_plane=2,
     small_vectors=2,
-    norm_project=2.2,
-    attn_forward=5,
-    out_norm=2,
-    join_low=2.5,
+    norm_project=0.3,
+    attn_forward=0.5,
+    out_norm=0.3,
+    join_low=0.3,
     feed_forward=9,
-    split_add=0.6,
-    merge_add=3,
+    split_add=0.1,
+    merge_add=0.3,
+    beside_add=0.3,
     middle_back=12,
     grad_wide=1.8,
     attn_backward=5,
-    split_depth=1.5,
-    input_back=4,
-    pack_vectors=3,
-    fill_far=1.5,
-    last_add=1.5,
+    split_depth=0.3,
+    input_back=0.25,
+    pack_vectors=0.3,
+    fill_far=0.05,
+    last_add=0.05,
 )
 COST = 0.3 * 1e9
 NEAR = tuple((dx, dc, dy) for dx in range(2) for dc in range(2) for dy in range(2))
@@ -577,6 +579,28 @@
         [shape_of(BF16, *shape) for shape in shapes],
         (place,) + tuple(blocks),
         vmem=10,
+    )
+
+
+def join_beside(place, blocks):
+    rows = blocks[0].shape[0]
+    widths = [block.shape[1] for block in blocks]
+
+    def body(place_ref, *refs):
+        start = 0
+        for ref, width in zip(refs, widths):
+            refs[-1][:, start : start + width] = ref[...]
+            start += width
+
+    return call(
+        body,
+        "join_beside",
+        (1,),
+        [held(*block.shape) for block in blocks],
+        held(rows, sum(widths)),
+        shape_of(BF16, rows, sum(widths)),
+        (place,) + tuple(blocks),
+        vmem=4,
     )
 
 
@@ -820,20 +844,20 @@
     rows = down_parts[0].shape[-2]
     group = width // (2 * depth)
     last = first + count == depth
-    sub = 256
     columns, offset, before = wide
     offset = offset // step
-
-    def body(place_ref, normed_ref, grad_ref, bias_ref, far_ref, out_in, back_in, *refs):
+    lines = up_parts[0].shape[1]
+    beside = (up_parts[0].shape[-1] - hidden_width) // width
+    rows = rows + beside * lines
+
+    def body(place_ref, bias_ref, normed_in, grad_in, far_in, out_in, back_in, *refs):
         up_refs, down_refs = refs[:8], refs[8 : 8 + 2 * depth]
         refs = refs[8 + 2 * depth + len(before) :]
-        tall_mine, tall_other, wide_mine, wide_other, sum_ref, back_ref = refs[:6]
-        if last:
-            out_ref, delta_ref = refs[6:8]
-            total, refs = refs[8], refs[9:]
-        else:
-            total, refs = refs[6], refs[7:]
-        up, down, up_sems, down_sems, hidden, before_low, tall_sums, wide_sums = refs
+        tall_mine, tall_other, wide_mine, wide_other, sum_ref, back_out = refs[:6]
+        outs = refs[6:8] if last else refs[6:7]
+        refs = refs[6 + len(outs) :]
+        normed_ref, grad_ref, far_ref, total, back, delta = refs[:6]
+        up, down, up_sems, down_sems, beside_sems, state_sems, tall_sums, wide_sums = refs[6:]
         at = pl.program_id(0)
         slot = lax.rem(at, 2)
 
@@ -856,11 +880,29 @@
             return [
                 pltpu.make_async_copy(
                     down_refs[2 * turn + dc].at[x],
-                    down.at[into, flip(place_ref[2], dc)],
+                    down.at[into, flip(place_ref[2], dc), :, pl.ds(0, rows - beside * lines)],
                     down_sems.at[into, dc],
                 )
                 for dc in range(2)
             ]
+
+        def beside_copies(index, into, dx):
+            copies = []
+            for dc in range(2):
+                for dy in range(2):
+                    which = NEAR.index((dx, dc, dy))
+                    c, y = flip(place_ref[2], dc), flip(place_ref[3], dy)
+                    for part in range(beside):
+                        copies.append(
+                            pltpu.make_async_copy(
+                                up_refs[which].at[
+                                    first + index // 2, :, pl.ds(hidden_width + part * width, width)
+                                ],
+                                down.at[into, c, y, pl.ds(rows - (beside - part) * lines, lines)],
+                                beside_sems.at[into, len(copies)],
+                            )
+                        )
+            return copies
 
         def begin(index, into):
             for copy in up_copies(index, into):
@@ -871,86 +913,144 @@
                 def _():
                     for copy in down_copies(index, into, turn):
                         copy.start()
+            for dx in range(2):
+                @pl.when(flip(place_ref[1], dx) == lax.rem(index, 2))
+                def _():
+                    for copy in beside_copies(index, into, dx):
+                        copy.start()
+
+        normed_copy = pltpu.make_async_copy(normed_in, normed_ref, state_sems.at[0])
+        grad_copy = pltpu.make_async_copy(grad_in, grad_ref, state_sems.at[1])
+        out_copy = pltpu.make_async_copy(out_in, total, state_sems.at[2])
+        if first:
+            back_copy = pltpu.make_async_copy(back_in, back, state_sems.at[3])
+        back_away = pltpu.make_async_copy(back, back_out, state_sems.at[5])
+        if last:
+            far_copy = pltpu.make_async_copy(far_in, far_ref, state_sems.at[4])
+            away = [
+                pltpu.make_async_copy(
+                    total.at[pl.ds(0, half)], outs[0].at[place_ref[3]], state_sems.at[6]
+                ),
+                pltpu.make_async_copy(delta, outs[1], state_sems.at[7]),
+            ]
+        else:
+            away = [pltpu.make_async_copy(total, outs[0], state_sems.at[6])]
 
         @pl.when(at == 0)
         def _():
+            normed_copy.start()
             begin(0, 0)
-            total[...] = out_in[...]
-            back_ref[...] = back_in[...] if first else jnp.zeros((tokens, width), F32)
+            grad_copy.start()
+            out_copy.start()
+            if first:
+                back_copy.start()
+            else:
+                back[...] = jnp.zeros((tokens, width), F32)
+            if last:
+                far_copy.start()
+            normed_copy.wait()
 
         @pl.when(at + 1 < steps)
         def _():
             begin(at + 1, 1 - slot)
 
-        for copy in up_copies(at, slot) + down_copies(at, slot, 0):
+        for copy in up_copies(at, slot):
             copy.wait()
-        up_part, down_part = flat(up[slot]), flat(down[slot])
-        bias_sum = jnp.zeros((1, step), F32)
-        for start in range(0, tokens, sub):
-            cut = slice(start, start + sub)
-            hidden_part, slope = gelu_both(contract(normed_ref[cut], up_part, 1, 0) + bias_ref[...])
-            hidden_low = hidden_part.astype(BF16)
-            hidden[cut] = hidden_low
-            total[cut] += contract(hidden_low, down_part, 1, 0)
-            low = (contract(grad_ref[cut], down_part, 1, 1) * slope).astype(BF16)
-            before_low[cut] = low
-            bias_sum += column(low.astype(F32))
-            back_ref[cut] += contract(low, up_part, 1, 1)
-        sum_ref[...] = bias_sum
-        tall_sums[...] = contract(hidden[...], grad_ref[...], 0, 0).reshape(tall_sums.shape)
-        tall_mine[0] = tall_sums[place_ref[2]].astype(BF16)
-        tall_other[0] = tall_sums[1 - place_ref[2]].astype(BF16)
-        wide_sums[...] = contract(normed_ref[...], before_low[...], 0, 0).reshape(wide_sums.shape)
-        wide_mine[...] = wide_sums[:, place_ref[2]].astype(BF16)
-        wide_other[...] = wide_sums[:, 1 - place_ref[2]].astype(BF16)
-
-        if last:
-            @pl.when(at == steps - 1)
-            def _():
-                out_ref[0] = total[:half]
-                delta_ref[...] = (total[half:] - far_ref[...].astype(F32)).astype(BF16)
-
-    full = held(tokens, width)
-    tall = pl.BlockSpec((1, 2 * rows, width), lambda i, _: (i, 0, 0))
-    broad = pl.BlockSpec((2 * depth, group // 2, step), lambda i, _: (0, 0, offset + i))
-    bias_spec = pl.BlockSpec((1, step), lambda i, _: (0, 2 * first + i))
-    out_specs = [tall, tall, broad, broad, pl.BlockSpec((1, step), lambda i, _: (0, i)), full]
+        up_part = flat(up[slot])
+        before_gelu = contract(normed_ref[...], up_part, 1, 0) + bias_ref[...]
+        hidden, slope = gelu_both(before_gelu)
+        hidden = hidden.astype(BF16)
+
+        @pl.when(at == 0)
+        def _():
+            grad_copy.wait()
+
+        tall = contract(hidden, grad_ref[...], 0, 0).astype(BF16)
+        tall_sums[...] = tall.reshape(tall_sums.shape)
+        tall_mine[0] = tall_sums[place_ref[2]]
+        tall_other[0] = tall_sums[1 - place_ref[2]]
+
+        for copy in down_copies(at, slot, 0) + beside_copies(at, slot, 0):
+            copy.wait()
+
+        @pl.when(at == 0)
+        def _():
+            out_copy.wait()
+            if first:
+                back_copy.wait()
+            if last:
+                far_copy.wait()
+
+        down_part = flat(down[slot])
+        total[...] += contract(hidden, down_part, 1, 0)
+
+        @pl.when(at == steps - 1)
+        def _():
+            if last:
+                delta[...] = (total[half:] - far_ref[...].astype(F32)).astype(BF16)
+            for copy in away:
+                copy.start()
+
+        low = (contract(grad_ref[...], down_part, 1, 1) * slope).astype(BF16)
+        back[...] += contract(low, up_part, 1, 1)
+
+        @pl.when(at == steps - 1)
+        def _():
+            back_away.start()
+
+        sum_ref[...] = column(low.astype(F32))
+        broad = contract(normed_ref[...], low, 0, 0).astype(BF16)
+        wide_sums[...] = broad.reshape(wide_sums.shape)
+        wide_mine[...] = wide_sums[:, place_ref[2]]
+        wide_other[...] = wide_sums[:, 1 - place_ref[2]]
+
+        @pl.when(at == steps - 1)
+        def _():
+            for copy in away + [back_away]:
+                copy.wait()
+
+    tall_spec = pl.BlockSpec((1, 2 * rows, width), lambda i, _: (i, 0, 0))
+    broad_spec = pl.BlockSpec((2 * depth, group // 2, step), lambda i, _: (0, 0, offset + i))
+    sum_spec = pl.BlockSpec((1, step), lambda i, _: (0, i))
+    out_specs = [tall_spec, tall_spec, broad_spec, broad_spec, sum_spec, whole_ref()]
     out_shape = [shape_of(BF16, steps, 2 * rows, width)] * 2
     out_shape += [shape_of(BF16, 2 * depth, group // 2, columns)] * 2
     out_shape += [shape_of(F32, 1, steps * step), shape_of(F32, tokens, width)]
+    if last:
+        out_specs += [whole_ref()] * 2
+        out_shape += [shape_of(F32, 2, half, width), shape_of(BF16, half, width)]
+    else:
+        out_specs += [whole_ref()]
+        out_shape += [shape_of(F32, tokens, width)]
     scratch = [
+        pltpu.VMEM((tokens, width), BF16),
+        pltpu.VMEM((tokens, width), BF16),
+        pltpu.VMEM((half, width), BF16),
+        pltpu.VMEM((tokens, width), F32),
+        pltpu.VMEM((tokens, width), F32),
+        pltpu.VMEM((half, width), BF16),
         pltpu.VMEM((2, depth, 2, 2, 2, group // 4, step), BF16),
         pltpu.VMEM((2, 2, 2, rows, width), BF16),
         pltpu.SemaphoreType.DMA((2, 8)),
         pltpu.SemaphoreType.DMA((2, 2)),
-        pltpu.VMEM((tokens, step), BF16),
-        pltpu.VMEM((tokens, step), BF16),
-        pltpu.VMEM((2, 2 * rows, width), F32),
-        pltpu.VMEM((2 * depth, 2, group // 2, step), F32),
+        pltpu.SemaphoreType.DMA((2, 4 * beside)),
+        pltpu.SemaphoreType.DMA((8,)),
+        pltpu.VMEM((2, 2 * rows, width), BF16),
+        pltpu.VMEM((2 * depth, 2, group // 2, step), BF16),
     ]
-    if last:
-        out_specs += [
-            pl.BlockSpec((1, half, width), lambda i, p: (p[3], 0, 0), pipeline_mode=pl.Buffered(1)),
-            held(half, width),
-        ]
-        out_shape += [shape_of(F32, 2, half, width), shape_of(BF16, half, width)]
-        scratch = [pltpu.VMEM((tokens, width), F32)] + scratch
-    else:
-        out_specs += [full]
-        out_shape += [shape_of(F32, tokens, width)]
-    args = (place, normed, grad_low, up_bias, far) + tuple(state) + tuple(up_parts) + tuple(down_parts)
+    args = (place, up_bias, normed, grad_low, far) + tuple(state) + tuple(up_parts) + tuple(down_parts)
     alias = {len(args) + i: 2 + i for i in range(len(before))}
     return call(
         body,
         "feed_forward",
         (steps,),
-        [full, full, bias_spec, held(half, width), full, full]
-        + [whole_ref()] * (8 + 2 * depth + len(before)),
+        [pl.BlockSpec((1, step), lambda i, _: (0, 2 * first + i))]
+        + [whole_ref()] * (5 + 8 + 2 * depth + len(before)),
         out_specs,
         out_shape,
         args + tuple(before),
         scratch=scratch,
-        vmem=50,
+        vmem=56,
         alias=alias,
     )
 
@@ -1009,7 +1109,7 @@
         + [shape_of(F32, 1, width)] * 3,
         (place, grad_normed, middle, gain, grad_out, far) + tuple(right),
         scratch=[weight_scratch(right[0], width), pltpu.SemaphoreType.DMA((1, 8))],
-        vmem=24,
+        vmem=56,
     )
 
 
@@ -1116,18 +1216,20 @@
     )
 
 
-def split_depth(place, pairs):
-    depth, rows = pairs[0][0].shape[:2]
-    widths = [mine.shape[2] for mine, _ in pairs]
-    total = sum(widths)
+def split_depth(place, pairs, rows):
+    depth = pairs[0][0].shape[0]
+    layout = [(which, part) for which, (mine, _) in enumerate(pairs) for part in range(mine.shape[1] // rows)]
+    total = sum(pairs[which][0].shape[2] for which, _ in layout)
 
     def body(place_ref, *refs):
         outs = refs[2 * len(pairs) :]
         for step, ref in enumerate(outs):
             at = lax.rem(place_ref[0] + step, depth)
             start = 0
-            for which, width in enumerate(widths):
-                value = refs[2 * which][at].astype(F32) + refs[2 * which + 1][at].astype(F32)
+            for which, part in layout:
+                width = pairs[which][0].shape[2]
+                cut = pl.ds(part * rows, rows)
+                value = refs[2 * which][at, cut].astype(F32) + refs[2 * which + 1][at, cut].astype(F32)
                 ref[:, start : start + width] = value.astype(ref.dtype)
                 start += width
 
@@ -1135,33 +1237,38 @@
         body,
         "split_depth",
         (1,),
-        [held(depth, rows, width) for width in widths for _ in range(2)],
+        [held(*mine.shape) for mine, _ in pairs for _ in range(2)],
         [held(rows, total)] * depth,
         [shape_of(F32, rows, total)] + [shape_of(BF16, rows, total)] * (depth - 1),
         (place,) + tuple(value for pair in pairs for value in pair),
-        vmem=8,
-    )
-
-
-def last_add(place, own, came, cuts):
+        vmem=12,
+    )
+
+
+def last_add(place, own, came, shapes):
     rows, total = own.shape
+    layout = [(which, part) for which, shape in enumerate(shapes) for part in range(shape[0] // rows)]
 
     def body(place_ref, own_ref, *refs):
-        value = own_ref[...]
-        for ref in refs[: len(came)]:
-            value = value + ref[...].astype(F32)
-        for ref, (start, stop) in zip(refs[len(came) :], cuts):
-            ref[...] = value[:, start:stop]
+        outs = refs[len(came) :]
+        start = 0
+        for which, part in layout:
+            width = shapes[which][1]
+            value = own_ref[:, start : start + width]
+            for ref in refs[: len(came)]:
+                value = value + ref[:, start : start + width].astype(F32)
+            outs[which][part * rows : (part + 1) * rows] = value
+            start += width
 
     return call(
         body,
         "last_add",
         (1,),
         [held(rows, total)] * (1 + len(came)),
-        [held(rows, stop - start) for start, stop in cuts],
-        [shape_of(F32, rows, stop - start) for start, stop in cuts],
+        [held(*shape) for shape in shapes],
+        [shape_of(F32, *shape) for shape in shapes],
         (place, own) + tuple(came),
-        vmem=6,
+        vmem=12,
     )
 
 
@@ -1212,37 +1319,6 @@
     )
 
 
-def pack_vectors(place, vectors, sizes, per):
-    count = vectors[0].shape[1] // (sizes[0] * per)
-
-    def body(place_ref, *refs):
-        out = refs[-1]
-        at = 0
-        for ref, size in zip(refs[:-1], sizes):
-            chosen = chosen_rows(count, size * per)
-            wide = jnp.where(chosen, jnp.broadcast_to(ref[...], (count, count * size * per)), 0.0)
-            for row in range(size):
-                out[at + row] = lax.dot_general(
-                    wide,
-                    spread_rows(count, per, size, row),
-                    (((1,), (1,)), ((), ())),
-                    precision=lax.Precision.HIGHEST,
-                    preferred_element_type=F32,
-                )
-            at += size
-
-    return call(
-        body,
-        "pack_vectors",
-        (1,),
-        [held(*vector.shape) for vector in vectors],
-        held(sum(sizes), count, per),
-        shape_of(F32, sum(sizes), count, per),
-        (place,) + tuple(vectors),
-        vmem=12,
-    )
-
-
 def merge_add(place, mine, came, spot):
     counts = [part.shape[0] for part in mine]
     _, _, rows, columns = mine[0].shape
@@ -1260,6 +1336,32 @@
     return call(
         body,
         "merge_add",
+        (1,),
+        [held(*part.shape) for part in mine + came],
+        [held(*shape)] * 2,
+        [shape_of(BF16, *shape)] * 2,
+        (place,) + tuple(mine) + tuple(came),
+        vmem=12,
+    )
+
+
+def beside_add(place, mine, came, spot):
+    groups, _, rows, _ = mine[0].shape
+    widths = [part.shape[-1] for part in mine]
+
+    def body(place_ref, *refs):
+        sent_ref, kept_ref = refs[2 * len(mine) :]
+        for ref, at in ((sent_ref, 1 - place_ref[spot]), (kept_ref, place_ref[spot])):
+            start = 0
+            for which, width in enumerate(widths):
+                total = refs[which][:, at].astype(F32) + refs[len(mine) + which][:, at].astype(F32)
+                ref[:, :, start : start + width] = total.astype(BF16)
+                start += width
+
+    shape = (groups, rows, sum(widths))
+    return call(
+        body,
+        "beside_add",
         (1,),
         [held(*part.shape) for part in mine + came],
         [held(*shape)] * 2,
@@ -1287,7 +1389,7 @@
         k_ext = jnp.where(own, k, bias).astype(jnp.bfloat16)
         v_ext = jnp.where(own, v, 1.0).astype(jnp.bfloat16)
         sides.append((q_ext, k_ext, v_ext))
-    rows = 256
+    rows = min(512, tokens)
     low_lane = lax.broadcasted_iota(jnp.int32, (rows, lanes), 1) < half
     for start in range(0, tokens, rows):
         sums = []
@@ -1442,12 +1544,13 @@
     return lax.optimization_barrier(values)
 
 
-def sum_all(values):
-    depth = lax.axis_size("dp") // 4
-    for swap in (swap_core, swap_x, swap_y):
-        values = values + swap(values)
+def swap_core_sum(values):
+    return values + swap_core(values)
+
+
+def sum_depth(values):
     total = values
-    for step in range(1, depth):
+    for step in range(1, lax.axis_size("dp") // 4):
         total = total + ring_z(values, step)
     return total
 
@@ -1469,27 +1572,30 @@
         sent, kept = split_add(self.place, self.mine.reshape(shape), self.came.reshape(shape), spot)
         self.mine, self.came = kept, swap(sent)
 
-    def second(self, *others):
+    def second(self, *others, beside=False):
         spot, swap = (3, swap_y) if self.x_first else (1, swap_x)
         mine, came = [], []
         for part in (self,) + others:
             shape = (-1, 2, self.rows, part.mine.shape[-1])
             mine.append(part.mine.reshape(shape))
             came.append(part.came.reshape(shape))
-        if others:
+        if beside:
+            sent, kept = beside_add(self.place, mine, came, spot)
+        elif others:
             sent, kept = merge_add(self.place, mine, came, spot)
         else:
             sent, kept = split_add(self.place, mine[0], came[0], spot)
         self.mine, self.came = kept, swap(sent)
 
     def third(self, *others):
-        pairs = [(self.mine, self.came)] + [(other.mine, other.came) for other in others]
-        own, *sent = split_depth(self.place, pairs)
+        parts = (self,) + others
+        rows = min(part.rows for part in parts)
+        own, *sent = split_depth(self.place, [(part.mine, part.came) for part in parts], rows)
         self.mine = own
         self.came = [ring_z(block, step + 1) for step, block in enumerate(sent)]
 
-    def last(self, cuts=None):
-        return last_add(self.place, self.mine, self.came, cuts or [(0, self.mine.shape[1])])
+    def last(self, *shapes):
+        return last_add(self.place, self.mine, self.came, shapes)
 
     def hold(self, *others):
         self.mine, self.came, others = tie(self.mine, self.came, others)
@@ -1538,38 +1644,48 @@
     pairs = width // PAIR
     ring = range(1, depth)
 
+    sizes = [vector.shape[0] // rows for vector in vectors]
     small = jnp.concatenate([vector.reshape(-1, rows) for vector in vectors])
     small = jnp.pad(small, ((0, rows - small.shape[0]), (0, PAIR - rows)))
-    shard = jnp.concatenate([w_query, w_key, w_value, w_out, small], axis=1)
+    shard = join_beside(place, [w_query, w_key, w_value, w_out, small])
     turned = [shard] + [ring_z(shard, step) for step in ring]
-    down_x = swap_x(w_down)
+    tall_half = tall_rows // 2
+    down_near, down_own = w_down[tall_half:], w_down[:tall_half]
+    down_x = swap_x(down_own)
     far_rows = swap_y(cast_far(place, inputs))
-    far_grad_low = cast_far(place, grad_out)
-    turned, down_x, far_rows, w_up, w_down, random_blocks = tie(
-        turned, down_x, far_rows, w_up, w_down, random_blocks
+    up_shard = join_beside(
+        place, [w_up] + [down_near[start : start + rows] for start in range(0, tall_half, rows)]
+    )
+    turned, down_x, far_rows, up_shard, down_own, random_blocks, grad_out = tie(
+        turned, down_x, far_rows, up_shard, down_own, random_blocks, grad_out
     )
     cut = 2 * width
     left, right = join_depth(place, turned, [(0, cut), (cut, shard.shape[1])], "join_first")
     left_y, right_x = swap_y(left), swap_x(right)
-    up_turned = {1: ring_z(w_up, 1), depth - 1: ring_z(w_up, depth - 1)}
-    down_y, down_xy = swap_y(w_down), swap_y(down_x)
-    left_y, right_x, up_turned, down_y, down_xy, down_x = tie(
-        left_y, right_x, up_turned, down_y, down_xy, down_x
+    up_turned = {1: ring_z(up_shard, 1), depth - 1: ring_z(up_shard, depth - 1)}
+    down_y, down_xy = swap_y(down_own), swap_y(down_x)
+    random_far = swap_y(pick(random_blocks, 1 - y, 0))
+    far_grad_low = cast_far(place, grad_out)
+    left_y, right_x, up_turned, down_own, down_x, down_y, down_xy, far_grad_low, random_far = tie(
+        left_y, right_x, up_turned, down_own, down_x, down_y, down_xy, far_grad_low, random_far
     )
     left_x, left_xy = swap_x(left), swap_x(left_y)
     right_y, right_xy = swap_y(right), swap_y(right_x)
     for step in ring:
         if step not in up_turned:
-            up_turned[step] = ring_z(w_up, step)
-    left_x, left_xy, right_y, right_xy, up_turned, left_y, right_x, down_x, random_blocks = tie(
-        left_x, left_xy, right_y, right_xy, up_turned, left_y, right_x, down_x, random_blocks
-    )
-    (up_own,) = join_depth(place, [w_up] + [up_turned[step] for step in ring], [(0, hidden_width)], "join_up")
-    plane = join_plane(place, [w_down, down_x, down_y, down_xy])
-    up_own, plane, left, left_x, left_y, left_xy, right, right_x, right_y, right_xy = tie(
-        up_own, plane, left, left_x, left_y, left_xy, right, right_x, right_y, right_xy
-    )
-    up_y = swap_y(up_own)
+            up_turned[step] = ring_z(up_shard, step)
+    plane = join_plane(place, [down_own, down_x, down_y, down_xy])
+    local_blocks = half // BLOCK
+    ids = jnp.arange(2 * local_blocks, dtype=jnp.int32)
+    block_ids = (ids + y * local_blocks) % (2 * local_blocks)
+    random_ids = jnp.concatenate([pick(random_blocks, y, 0), random_far], axis=1)
+    bias = key_bias(random_ids, block_ids)
+    left_x, left_xy, right_y, right_xy, up_turned, left_y, right_x, plane, bias = tie(
+        left_x, left_xy, right_y, right_xy, up_turned, left_y, right_x, plane, bias
+    )
+    (up_own,) = join_depth(
+        place, [up_shard] + [up_turned[step] for step in ring], [(0, up_shard.shape[1])], "join_up"
+    )
     left_core = {
         (0, 0): swap_core(left), (0, 1): swap_core(left_y),
         (1, 0): swap_core(left_x), (1, 1): swap_core(left_xy),
@@ -1578,18 +1694,13 @@
         (0, 0): swap_core(right), (0, 1): swap_core(right_y),
         (1, 0): swap_core(right_x), (1, 1): swap_core(right_xy),
     }
-    random_far = swap_y(pick(random_blocks, 1 - y, 0))
     left_parts = near_parts(left, left_x, left_y, left_xy, left_core)
     right_parts = near_parts(right, right_x, right_y, right_xy, right_core)
-    sizes = [vector.shape[0] // rows for vector in vectors]
-    local_blocks = half // BLOCK
-    ids = jnp.arange(2 * local_blocks, dtype=jnp.int32)
-    block_ids = (ids + y * local_blocks) % (2 * local_blocks)
-    random_ids = jnp.concatenate([pick(random_blocks, y, 0), random_far], axis=1)
-    bias = key_bias(random_ids, block_ids)
-    left_parts, right_parts, plane, bias = tie(left_parts, right_parts, plane, bias)
-
+    left_parts, right_parts, plane, up_own = tie(left_parts, right_parts, plane, up_own)
+
+    up_y, up_x = swap_y(up_own), swap_x(up_own)
     planes = {0: plane, 1: ring_z(plane, 1), depth - 1: ring_z(plane, depth - 1)}
+    up_core = {(0, 0): swap_core(up_own)}
     spans = small_vectors(place, right_parts, cut, sizes, rows)
     (
         ln1_gain,
@@ -1606,26 +1717,33 @@
     normed_low, qkv = norm_project(
         place, inputs, far_rows, ln1_gain, ln1_bias, left_parts, right_parts, qkv_bias
     )
-    qkv, up_y = tie(qkv, up_y)
-    up_x, up_xy = swap_x(up_own), swap_x(up_y)
     attended = attn_forward(place, qkv, bias, 0, pairs // 2)
-    attended, planes, far_grad_low = tie(attended, planes, far_grad_low)
+    attended, up_y, up_x, planes, up_core, far_grad_low = tie(
+        attended, up_y, up_x, planes, up_core, far_grad_low
+    )
+    up_xy = swap_x(up_y)
+    up_core[0, 1] = swap_core(up_y)
+    up_core[1, 0] = swap_core(up_x)
+    far_grad = swap_y(far_grad_low)
     for step in ring:
         if step not in planes:
             planes[step] = ring_z(planes[0], step)
-    far_grad = swap_y(far_grad_low)
-    prob, mixed_low, totals = attn_forward(place, qkv, bias, pairs // 2, pairs - pairs // 2, attended)
+    prob, mixed_low, totals = attn_forward(
+        place, qkv, bias, pairs // 2, pairs - pairs // 2, attended
+    )
+    mixed_low, far_grad, planes, up_core = tie(mixed_low, far_grad, planes, up_core)
+    plane_core = {0: swap_core(planes[0])}
+    for step in ring:
+        plane_core[step] = swap_core(planes[step])
+    grad_ff_low, grad_down_bias = join_low(place, grad_out, far_grad)
+    mixed_low, grad_ff_low = tie(mixed_low, grad_ff_low)
     middle, normed_two_low, start_out = out_norm(
         place, mixed_low, right_parts, out_bias, inputs, far_rows, ln2_gain, ln2_bias, down_bias
     )
-    normed_two_low, up_x, up_xy, far_grad = tie(normed_two_low, up_x, up_xy, far_grad)
-    up_core = {
-        (0, 0): swap_core(up_own), (0, 1): swap_core(up_y),
-        (1, 0): swap_core(up_x), (1, 1): swap_core(up_xy),
-    }
+    normed_two_low, up_xy, plane_core = tie(normed_two_low, up_xy, plane_core)
+    up_core[1, 1] = swap_core(up_xy)
     up_parts = near_parts(up_own, up_x, up_y, up_xy, up_core)
-    down_parts = [part for step in range(depth) for part in (planes[step], swap_core(planes[step]))]
-    grad_ff_low, grad_down_bias = join_low(place, grad_out, far_grad)
+    down_parts = [part for step in range(depth) for part in (planes[step], plane_core[step])]
 
     down_sums = [Reduce(place, tall_rows, True) for _ in range(3)]
     near_sum = Reduce(place, rows, False)
@@ -1688,6 +1806,7 @@
     (grads,) = down_sums[2].hold(grads)
     (grads,) = out_sum.hold(grads)
     wide_sum.first()
+    out_sum.first()
     near_sum.third()
     down_sums[0].second(*down_sums[1:])
     down_sum = down_sums[0]
@@ -1700,46 +1819,38 @@
     (grads,) = near_sum.hold(grads)
     (grads,) = wide_sum.hold(grads)
     (grads,) = down_sum.hold(grads)
-    out_sum.first()
     wide_sum.second()
-    down_sum.third()
-    out_sum.mine, wide_sum.mine, down_sum.mine, grads = tie(
-        out_sum.mine, wide_sum.mine, down_sum.mine, grads
-    )
+    wide_sum.mine, grads = tie(wide_sum.mine, grads)
     wide = grad_wide(place, normed_low, grads, rows, 2)
+    (wide,) = wide_sum.hold(wide)
     (wide,) = out_sum.hold(wide)
-    (wide,) = wide_sum.hold(wide)
+    out_sum.second()
+    out_sum.mine, wide = tie(out_sum.mine, wide)
     left_sum.begin(*wide[:2])
     right_sum.begin(*wide[2:])
-    out_sum.second()
-    (grad_up_near,) = near_sum.last()
-    left_sum.mine, grads, grad_up_near, out_sum.mine = tie(left_sum.mine, grads, grad_up_near, out_sum.mine)
+    (grad_up_near,) = near_sum.last((rows, near_width))
+    left_sum.mine, grads, grad_up_near = tie(left_sum.mine, grads, grad_up_near)
+    (grads,) = out_sum.hold(grads)
     (grads,) = left_sum.hold(grads)
     left_sum.first()
     (grads,) = right_sum.hold(grads)
     right_sum.first()
-    left_sum.mine, right_sum.mine, grads = tie(left_sum.mine, right_sum.mine, grads)
+    down_sum.third()
+    left_sum.mine, right_sum.mine, down_sum.mine, grads = tie(
+        left_sum.mine, right_sum.mine, down_sum.mine, grads
+    )
     in_part, in_delta, grad_ln1_gain, grad_ln1_bias, grad_query_bias, grad_value_bias = input_back(
         place, grads, left_parts, right_parts, inputs, far_rows, ln1_gain, grad_middle, far_grad
     )
+    (in_delta,) = down_sum.hold(in_delta)
     (in_delta,) = left_sum.hold(in_delta)
     left_sum.second()
     (in_delta,) = right_sum.hold(in_delta)
     right_sum.second()
-    left_sum.mine, right_sum.mine, in_delta, grad_ln1_gain, wide_sum.mine = tie(
-        left_sum.mine, right_sum.mine, in_delta, grad_ln1_gain, wide_sum.mine
-    )
-    (grad_ln1_gain,) = out_sum.hold(grad_ln1_gain)
-    (grad_ln1_gain,) = down_sum.hold(grad_ln1_gain)
     wide_sum.third(out_sum)
-    (grad_w_down,) = down_sum.last()
-    wide_sum.mine, in_delta, grad_ln1_gain, grad_w_down = tie(
-        wide_sum.mine, in_delta, grad_ln1_gain, grad_w_down
-    )
-    in_delta, grad_ln1_gain = left_sum.hold(in_delta, grad_ln1_gain)
-    in_delta, grad_ln1_gain = right_sum.hold(in_delta, grad_ln1_gain)
-    left_sum.third(right_sum)
-    left_sum.mine, in_delta, grad_ln1_gain = tie(left_sum.mine, in_delta, grad_ln1_gain)
+    left_sum.mine, right_sum.mine, wide_sum.mine, in_delta, grad_ln1_gain = tie(
+        left_sum.mine, right_sum.mine, wide_sum.mine, in_delta, grad_ln1_gain
+    )
     grad_vectors = (
         grad_ln1_gain,
         grad_ln1_bias,
@@ -1751,22 +1862,37 @@
         grad_up_bias,
         grad_down_bias,
     )
+    packed = jnp.concatenate(grad_vectors, axis=1)
     in_far = swap_y(in_delta)
-    packed = pick(sum_all(pack_vectors(place, grad_vectors, sizes, rows)), dp * 2 + y, 1)
+    packed = swap_core_sum(packed.reshape(-1, PAIR))
+    (packed,) = wide_sum.hold(packed)
+    (packed,) = left_sum.hold(packed)
+    (packed,) = right_sum.hold(packed)
+    packed = sum_depth(packed)
+    left_sum.third(right_sum)
+    left_sum.mine, packed = tie(left_sum.mine, packed)
+    packed = packed + swap_x(packed)
+    packed = (packed + swap_y(packed)).reshape(-1)
+    (grad_w_down,) = down_sum.last(w_down.shape)
+    grad_up_far, grad_w_out = wide_sum.last((rows, near_width), w_out.shape)
+    packed, out_far, grad_w_down, grad_up_far, in_far = tie(
+        packed, out_far, grad_w_down, grad_up_far, in_far
+    )
+    left_sum.came, in_far, out_far = tie(left_sum.came, in_far, out_far)
     result = fill_far(place, out_part, inputs, out_far)
-    grad_up_far, grad_w_out = wide_sum.last([(0, near_width), (near_width, near_width + width)])
+    grad_in = fill_far(place, in_part, grad_out, in_far)
     grad_w_up = jnp.concatenate([grad_up_near, grad_up_far], axis=1)
-    grad_in = fill_far(place, in_part, grad_out, in_far)
+    square, part = (rows, width), (rows, width // 2)
+    grad_left_q, grad_left_k, grad_right_k, grad_right_v = left_sum.last(square, part, part, square)
     out_vectors = []
     at = 0
-    for size in sizes:
-        out_vectors.append(packed[at : at + size].reshape(-1))
-        at += size
-    qkv_cuts = [(part * width, (part + 1) * width) for part in range(3)]
+    for vector in vectors:
+        count = vector.shape[0]
+        out_vectors.append(lax.dynamic_slice_in_dim(packed, at + (dp * 2 + y) * count, count))
+        at += count * depth * 8
+    grad_w_key = jnp.concatenate([grad_left_k, grad_right_k], axis=1)
     return (
-        (result, grad_in)
-        + tuple(left_sum.last(qkv_cuts))
-        + (grad_w_out, grad_w_up, grad_w_down)
+        (result, grad_in, grad_left_q, grad_w_key, grad_right_v, grad_w_out, grad_w_up, grad_w_down)
         + tuple(out_vectors)
     )
 

time: 538 us -> 485 us (0.901)
  Pallas kernels: 297 us -> 275 us
  waiting for transfers between devices: 111 us -> 93.1 us
  local copies, waits for them, and re-layouts: 41.2 us -> 31.6 us
    ppermute x58, waiting for transfers between devices: 60.7 us -> 36.3 us  [pair_swap(): return lax.ppermute(value, axis, [(i, i ^ bit) for i in range(size)])]
    pallas_call x45 -> x46, Pallas kernels: 297 us -> 275 us  [call(): pl.pallas_call(body, grid_spec=spec, out_shape=out_shape, name=name, inpu...]
    unnamed x241 -> x243, local copies, waits for them, and re-layouts: 38.9 us -> 29.8 us
    ppermute x24, waiting for transfers between devices: 50.7 us -> 56.9 us  [ring_z(): lax.ppermute(value, 'dp', [(i, (i + 4 * step) % size) for i in range(size)])]
  transfers between devices with their start and end apart: 82 -> 82, of which waited for: 21 -> 23; matrix products, arithmetic and copies ran while one was open for 1% -> 0% of each run, Pallas kernels for 47% -> 47%
where the time goes in v2:
time: 485 us; the launch traced here: 480 us
  Pallas kernels  275 us (57%)
  waiting for transfers between devices  93.1 us (19%)
  starting transfers between devices  75.7 us (16%)
  local copies, waits for them, and re-layouts  31.6 us (7%)
    pallas_call x46, Pallas kernels, call(): pl.pallas_call(body, grid_spec=spec, out_shape=out_shape, name=name, inpu...  275 us
    ppermute x24, waiting for transfers between devices, ring_z(): lax.ppermute(value, 'dp', [(i, (i + 4 * step) % size) for i in range(size)])  56.9 us
    ppermute x58, starting transfers between devices, pair_swap(): return lax.ppermute(value, axis, [(i, i ^ bit) for i in range(size)])  41.9 us
    ppermute x58, waiting for transfers between devices, pair_swap(): return lax.ppermute(value, axis, [(i, i ^ bit) for i in range(size)])  36.3 us
    ppermute x24, starting transfers between devices, ring_z(): lax.ppermute(value, 'dp', [(i, (i + 4 * step) % size) for i in range(size)])  33.8 us
    unnamed x243, local copies, waits for them, and re-layouts  29.8 us
  transfers between devices with their start and end apart: 82, of which 23 were waited for; matrix products, arithmetic and copies ran while one was open for 0% of the time, Pallas kernels for 47%

profile of v2, /device:TPU:8, one launch (start us, length us, event | category | flops | bytes accessed | tf_op | source)
XLA Modules:
  0.0 480.4 jit_solution(4934301964366138754)
XLA Ops:
  0.8 2.2 copy-done.1
  13.9 2.1 collective-permute-done.3.refs_1_
  16.0 10.4 %collective-permute-done.refs_1_ = bf16[32,4224]{1,0:T(8,128)(2,1)S(1)} collective-permute-done((bf16[32,4224]{1,0:T(8,128)(2,1)S(1)}, bf16[32,4224]{1,0:T(8,128)(2,1)S(1)}, u32[]{:S(2)}, u32[]{:S(2)}) %collective-permute-start) | collective-permute-done | bytes 270368 | tf_op jit(solution)/shard_map/ppermute | solution.py:1540
  26.5 4.3 collective-permute-done.1.refs_2_
  36.9 2.0 collective-permute-start.9
  38.9 9.8 %collective-permute-done.12 = s32[16,8,3]{0,1,2:T(8,128)S(1)} collective-permute-done((s32[16,8,3]{0,1,2:T(8,128)S(1)}, s32[16,8,3]{0,1,2:T(8,128)S(1)}, u32[]{:S(2)}, u32[]{:S(2)}) %collective-permute-start.12) | collective-permute-done | bytes 1568 | tf_op jit(solution)/shard_map/ppermute | solution.py:1519
  49.2 4.4 collective-permute-done.10.refs_2_
  54.2 2.2 copy-done.8
  61.6 2.2 collective-permute-start.16
  68.3 8.0 %collective-permute-done.16.refs_2_ = bf16[32,6144]{1,0:T(8,128)(2,1)S(1)} collective-permute-done((bf16[32,6144]{1,0:T(8,128)(2,1)}, bf16[32,6144]{1,0:T(8,128)(2,1)S(1)}, u32[]{:S(2)}, u32[]{:S(2)}) %collective-permute-start.16) | collective-permute-done | bytes 393248 | tf_op jit(solution)/shard_map/ppermute | solution.py:1540
  78.3 4.7 collective-permute-done.13.refs_5_
  90.6 2.2 collective-permute-start.28
  92.8 2.0 small_vectors.1
  95.6 13.9 %norm_project.1 = (bf16[1024,1024]{1,0:T(8,128)(2,1)}, bf16[1024,3072]{1,0:T(8,128)(2,1)}) custom-call(s32[4]{0:T(128)} %copy-done.40, f32[2,512,1024]{2,1,0:T(8,128)} %base_ref.1, bf16[512,1024]{1,0:T(8,128)(2,1)} %collective-permute-done.4.far_ref.far_in, f32[1,1024]{1,0:T(1,128)} %copy-done.63, f32[1,1024]{1,0:T(1,128)} %copy-done.64, ...), custom_call_target="tpu_custom_call" | custom-call | flops 540000000 | bytes 1 | tf_op jit(solution)/shard_map/norm_project/pallas_call | solution.py:464
  109.5 2.8 copy-done
  112.3 17.0 %attn_forward.2 = (bf16[16,1024,1024]{2,1,0:T(8,128)(2,1)}, bf16[1024,1024]{1,0:T(8,128)(2,1)S(1)}, f32[1024,1024]{1,0:T(8,128)S(1)}) custom-call(s32[4]{0:T(128)S(1)} %copy-done.41, bf16[1024,3072]{1,0:T(8,128)(2,1)S(1)} %copy-done, bf16[1024,3072]{1,0:T(8,128)(2,1)S(1)} %copy-done, bf16[1024,3072]{1,0:T(8,128)(2,1)S(1)} %copy-done, f32[16,16,128]{2,1,0:T(8,128)S(1)} %bitcast.77), custom_call_target="tpu_custom_call" | custom-call | flops 600000000 | bytes 1 | tf_op jit(solution)/shard_map/attn_forward/pallas_call | solution.py:464
  132.9 17.0 %attn_forward.3 = (bf16[16,1024,1024]{2,1,0:T(8,128)(2,1)}, bf16[1024,1024]{1,0:T(8,128)(2,1)S(1)}, f32[1024,1024]{1,0:T(8,128)S(1)}) custom-call(s32[4]{0:T(128)S(1)} %copy-done.41, bf16[1024,3072]{1,0:T(8,128)(2,1)S(1)} %copy-done, bf16[1024,3072]{1,0:T(8,128)(2,1)S(1)} %copy-done, ...), custom_call_target="tpu_custom_call", output_to_operand_aliasing={{0}: (5, {}), {1}: (6, {}), {2}: (7, {})} | custom-call | flops 600000000 | bytes 1 | tf_op jit(solution)/shard_map/attn_forward/pallas_call | solution.py:464
  150.0 2.1 copy-done.6
  152.0 3.3 collective-permute-done.31.refs_12_
  158.9 10.7 %out_norm.1 = (f32[1024,1024]{1,0:T(8,128)}, bf16[1024,1024]{1,0:T(8,128)(2,1)}, f32[1024,1024]{1,0:T(8,128)}) custom-call(s32[4]{0:T(128)} %copy-done.40, bf16[1024,1024]{1,0:T(8,128)(2,1)} %copy-done.3, f32[1,1024]{1,0:T(1,128)} %copy-done.66, f32[2,512,1024]{2,1,0:T(8,128)} %base_ref.1, bf16[512,1024]{1,0:T(8,128)(2,1)} %collective-permute-done.4.far_ref.far_in, ...), custom_call_target="tpu_custom_call" | custom-call | flops 360000000 | bytes 1 | tf_op jit(solution)/shard_map/out_norm/pallas_call | solution.py:464
  169.8 3.6 collective-permute-done.39.refs_7_
  174.5 38.5 %feed_forward.3 = (bf16[4,256,1024]{2,1,0:T(8,128)(2,1)}, bf16[4,256,1024]{2,1,0:T(8,128)(2,1)}, bf16[8,64,2048]{2,1,0:T(8,128)(2,1)}, bf16[8,64,2048]{2,1,0:T(8...) custom-call(s32[4]{0:T(128)} %copy-done.40, f32[1,4096]{1,0:T(1,128)} %copy-done.62, ...), custom_call_target="tpu_custom_call" | custom-call | flops 10800000000 | bytes 1 | tf_op jit(solution)/shard_map/feed_forward/pallas_call | solution.py:464
  213.6 22.1 %feed_forward.4 = (bf16[2,256,1024]{2,1,0:T(8,128)(2,1)}, bf16[2,256,1024]{2,1,0:T(8,128)(2,1)}, bf16[8,64,2048]{2,1,0:T(8,128)(2,1)}, bf16[8,64,2048]{2,1,0:T(8...) custom-call(s32[4]{0:T(128)} %copy-done.40, f32[1,4096]{1,0:T(1,128)} %copy-done.62, ...), custom_call_target="tpu_custom_call" | custom-call | flops 5400000000 | bytes 1 | tf_op jit(solution)/shard_map/feed_forward/pallas_call | solution.py:464
  235.9 3.4 split_add.14
  243.4 23.5 %feed_forward.5 = (bf16[2,256,1024]{2,1,0:T(8,128)(2,1)}, bf16[2,256,1024]{2,1,0:T(8,128)(2,1)}, bf16[8,64,2048]{2,1,0:T(8,128)(2,1)}, bf16[8,64,2048]{2,1,0:T(8...) custom-call(s32[4]{0:T(128)} %copy-done.40, ...), custom_call_target="tpu_custom_call", output_to_operand_aliasing={{2}: (23, {}), {3}: (24, {})} | custom-call | flops 5400000000 | bytes 1 | tf_op jit(solution)/shard_map/feed_forward/pallas_call | solution.py:464
  268.6 2.7 split_add.15
  271.9 11.8 %middle_back.1 = (f32[1024,1024]{1,0:T(8,128)}, bf16[1024,1024]{1,0:T(8,128)(2,1)}, bf16[1024,1024]{1,0:T(8,128)(2,1)}, f32[1,1024]{1,0:T(1,128)}, f32[1,1024]{1,0:T(1,128)}, /*index=5*/f32[1,1024]{1,0:T(1,128)}) custom-call(s32[4]{0:T(128)} %copy-done.40, f32[1024,1024]{1,0:T(8,128)} %get-tuple-element.508.grad_ref, ...), custom_call_target="tpu_custom_call" | custom-call | flops 14400000000 | bytes 1 | tf_op jit(solution)/shard_map/middle_back/pallas_call | solution.py:464
  286.9 3.7 grad_wide.2
  290.6 2.8 split_add.17
  293.5 2.3 split_add.16
  299.0 3.2 split_add.18
  303.5 20.9 %attn_backward.2 = (bf16[1024,1024]{1,0:T(8,128)(2,1)S(1)}, bf16[1024,1024]{1,0:T(8,128)(2,1)S(1)}, bf16[1024,1024]{1,0:T(8,128)(2,1)S(1)}) custom-call(s32[4]{0:T(128)S(1)} %copy-done.44, bf16[1024,3072]{1,0:T(8,128)(2,1)S(1)} %bitcast.67, bf16[1024,3072]{1,0:T(8,128)(2,1)S(1)} %bitcast.67, bf16[1024,3072]{1,0:T(8,128)(2,1)S(1)} %bitcast.67, ...), custom_call_target="tpu_custom_call" | custom-call | flops 6000000000 | bytes 1 | tf_op jit(solution)/shard_map/attn_backward/pallas_call | solution.py:464
  325.4 2.1 merge_add.1
  330.8 4.2 collective-permute-start.55
  335.0 20.7 %attn_backward.3 = (bf16[1024,1024]{1,0:T(8,128)(2,1)S(1)}, bf16[1024,1024]{1,0:T(8,128)(2,1)S(1)}, bf16[1024,1024]{1,0:T(8,128)(2,1)S(1)}) custom-call(s32[4]{0:T(128)S(1)} %copy-done.44, bf16[1024,3072]{1,0:T(8,128)(2,1)S(1)} %bitcast.67, bf16[1024,3072]{1,0:T(8,128)(2,1)S(1)} %bitcast.67, ...), custom_call_target="tpu_custom_call", output_to_operand_aliasing={{0}: (8, {}), {1}: (9, {}), {2}: (10, {})} | custom-call | flops 6000000000 | bytes 1 | tf_op jit(solution)/shard_map/attn_backward/pallas_call | solution.py:464
  359.1 10.3 %grad_wide.3 = (bf16[8,64,1536]{2,1,0:T(8,128)(2,1)S(1)}, bf16[8,64,1536]{2,1,0:T(8,128)(2,1)S(1)}, bf16[8,64,1536]{2,1,0:T(8,128)(2,1)S(1)}, bf16[8,64,1536]{2,1,0:T(8,128)(2,1)S(1)}) custom-call(s32[4]{0:T(128)S(1)} %copy-done.44, bf16[1024,1024]{1,0:T(8,128)(2,1)S(1)} %copy-done.69, bf16[1024,1024]{1,0:T(8,128)(2,1)S(1)} %get-tuple-element.655.refs_0_.query_ref, ...), custom_call_target="tpu_custom_call" | custom-call | flops 3240000000 | bytes 1 | tf_op jit(solution)/shard_map/grad_wide/pallas_call | solution.py:464
  373.0 6.6 %collective-permute-done.60.refs_3_ = bf16[4,32,1024]{2,1,0:T(8,128)(2,1)S(1)} collective-permute-done((bf16[4,32,1024]{2,1,0:T(8,128)(2,1)S(1)}, bf16[4,32,1024]{2,1,0:T(8,128)(2,1)S(1)}, u32[]{:S(2)}, u32[]{:S(2)}) %collective-permute-start.60) | collective-permute-done | bytes 262176 | tf_op jit(solution)/shard_map/ppermute | solution.py:1519
  386.8 2.1 collective-permute-start.64
  390.3 18.9 %input_back.1 = (f32[2,512,1024]{2,1,0:T(8,128)}, bf16[512,1024]{1,0:T(8,128)(2,1)}, f32[1,1024]{1,0:T(1,128)}, f32[1,1024]{1,0:T(1,128)}, f32[1,1024]{1,0:T(1,128)}, /*index=5*/f32[1,1024]{1,0:T(1,128)}) custom-call(s32[4]{0:T(128)} %copy-done.40, bf16[1024,1024]{1,0:T(8,128)(2,1)} %copy-done.20, bf16[1024,1024]{1,0:T(8,128)(2,1)} %copy-done.21, ...), custom_call_target="tpu_custom_call" | custom-call | flops 300000000 | bytes 1 | tf_op jit(solution)/shard_map/input_back/pallas_call | solution.py:464
  409.4 2.1 collective-permute-start.68
  416.3 2.6 collective-permute-start.69
  419.5 10.7 %collective-permute-done.69.refs_1_ = bf16[32,3072]{1,0:T(8,128)(2,1)S(1)} collective-permute-done((bf16[32,3072]{1,0:T(8,128)(2,1)S(1)}, bf16[32,3072]{1,0:T(8,128)(2,1)S(1)}, u32[]{:S(2)}, u32[]{:S(2)}) %collective-permute-start.69) | collective-permute-done | bytes 196640 | tf_op jit(solution)/shard_map/ppermute | solution.py:1540
  432.1 2.2 collective-permute-start.77
  440.8 2.5 collective-permute-done.79
  452.4 3.0 collective-permute-start.74
  456.0 10.0 %collective-permute-done.73.refs_0_ = bf16[32,3072]{1,0:T(8,128)(2,1)S(1)} collective-permute-done((bf16[32,3072]{1,0:T(8,128)(2,1)}, bf16[32,3072]{1,0:T(8,128)(2,1)S(1)}, u32[]{:S(2)}, u32[]{:S(2)}) %collective-permute-start.73) | collective-permute-done | bytes 196640 | tf_op jit(solution)/shard_map/ppermute | solution.py:1540
  466.0 2.1 collective-permute-done.74.refs_1_
  468.1 2.8 collective-permute-done.75.refs_2_
  (440 shorter events, 113.1 us)
Async XLA Ops:
  3.8 28.8 %collective-permute-start.4 = (bf16[512,1024]{1,0:T(8,128)(2,1)S(1)}, bf16[512,1024]{1,0:T(8,128)(2,1)}, u32[]{:S(2)}, u32[]{:S(2)}) collective-permute-start(bf16[512,1024]{1,0:T(8,128)(2,1)S(1)} %cast_far.2), channel_id=1, source_target_pairs={{0,1},{1,0},{2,3},{3,2},{4,5},{5,4},{6,7},{7,6},{8,9},{9,8},{10,11... | collective-permute-start | bytes 3145736 | tf_op jit(solution)/shard_map/ppermute | solution.py:1519
  6.3 20.1 %collective-permute-start = (bf16[32,4224]{1,0:T(8,128)(2,1)S(1)}, bf16[32,4224]{1,0:T(8,128)(2,1)S(1)}, u32[]{:S(2)}, u32[]{:S(2)}) collective-permute-start(bf16[32,4224]{1,0:T(8,128)(2,1)S(1)} %join_beside.2.refs_0_), channel_id=1, source_target_pairs={{0,8},{2,10},{4,12},{6,14},{8,16},{10,18},{12,20},{14,22},{16,24},... | collective-permute-start | bytes 811016 | tf_op jit(solution)/shard_map/ppermute | solution.py:1540
  8.0 22.8 %collective-permute-start.1 = (bf16[32,4224]{1,0:T(8,128)(2,1)S(1)}, bf16[32,4224]{1,0:T(8,128)(2,1)S(1)}, u32[]{:S(2)}, u32[]{:S(2)}) collective-permute-start(bf16[32,4224]{1,0:T(8,128)(2,1)S(1)} %join_beside.2.refs_0_), channel_id=1, source_target_pairs={{0,16},{2,18},{4,20},{6,22},{8,24},{10,26},{12,28},{14,30},{16,0},... | collective-permute-start | bytes 811016 | tf_op jit(solution)/shard_map/ppermute | solution.py:1540
  9.2 23.4 %collective-permute-start.2 = (bf16[32,4224]{1,0:T(8,128)(2,1)S(1)}, bf16[32,4224]{1,0:T(8,128)(2,1)S(1)}, u32[]{:S(2)}, u32[]{:S(2)}) collective-permute-start(bf16[32,4224]{1,0:T(8,128)(2,1)S(1)} %join_beside.2.refs_0_), channel_id=1, source_target_pairs={{0,24},{2,26},{4,28},{6,30},{8,0},{10,2},{12,4},{14,6},{16,8},{18,... | collective-permute-start | bytes 811016 | tf_op jit(solution)/shard_map/ppermute | solution.py:1540
  33.2 30.6 %collective-permute-start.7 = (bf16[4,32,2176]{2,1,0:T(8,128)(2,1)S(1)}, bf16[4,32,2176]{2,1,0:T(8,128)(2,1)S(1)}, u32[]{:S(2)}, u32[]{:S(2)}) collective-permute-start(bf16[4,32,2176]{2,1,0:T(8,128)(2,1)S(1)} %get-tuple-element.407.refs_0_.refs_8_), channel_id=1, source_target_pairs={{0,4},{2,6},{4,0},{6,2},{8,12},{10,14},{12,8},{14,10},{16,20},{18,... | collective-permute-start | bytes 1671176 | tf_op jit(solution)/shard_map/ppermute | solution.py:1519
  34.8 29.0 %collective-permute-start.6 = (bf16[4,32,2048]{2,1,0:T(8,128)(2,1)S(1)}, bf16[4,32,2048]{2,1,0:T(8,128)(2,1)S(1)}, u32[]{:S(2)}, u32[]{:S(2)}) collective-permute-start(bf16[4,32,2048]{2,1,0:T(8,128)(2,1)S(1)} %get-tuple-element.421.refs_0_), channel_id=1, source_target_pairs={{0,1},{1,0},{2,3},{3,2},{4,5},{5,4},{6,7},{7,6},{8,9},{9,8},{10,11... | collective-permute-start | bytes 1572872 | tf_op jit(solution)/shard_map/ppermute | solution.py:1519
  36.8 22.7 %collective-permute-start.8 = (bf16[32,6144]{1,0:T(8,128)(2,1)}, bf16[32,6144]{1,0:T(8,128)(2,1)S(1)}, u32[]{:S(2)}, u32[]{:S(2)}) collective-permute-start(bf16[32,6144]{1,0:T(8,128)(2,1)} %join_beside.3.refs_0_), channel_id=1, source_target_pairs={{0,8},{2,10},{4,12},{6,14},{8,16},{10,18},{12,20},{14,22},{16,24},... | collective-permute-start | bytes 1179656 | tf_op jit(solution)/shard_map/ppermute | solution.py:1540
  36.9 24.0 %collective-permute-start.9 = (bf16[32,6144]{1,0:T(8,128)(2,1)}, bf16[32,6144]{1,0:T(8,128)(2,1)S(1)}, u32[]{:S(2)}, u32[]{:S(2)}) collective-permute-start(bf16[32,6144]{1,0:T(8,128)(2,1)} %join_beside.3.refs_0_), channel_id=1, source_target_pairs={{0,24},{2,26},{4,28},{6,30},{8,0},{10,2},{12,4},{14,6},{16,8},{18,... | collective-permute-start | bytes 1179656 | tf_op jit(solution)/shard_map/ppermute | solution.py:1540
  58.7 19.5 %collective-permute-start.14 = (bf16[4,32,2176]{2,1,0:T(8,128)(2,1)S(1)}, bf16[4,32,2176]{2,1,0:T(8,128)(2,1)S(1)}, u32[]{:S(2)}, u32[]{:S(2)}) collective-permute-start(bf16[4,32,2176]{2,1,0:T(8,128)(2,1)S(1)} %get-tuple-element.407.refs_0_.refs_8_), channel_id=1, source_target_pairs={{0,1},{1,0},{2,3},{3,2},{4,5},{5,4},{6,7},{7,6},{8,9},{9,8},{10,11... | collective-permute-start | bytes 1671176 | tf_op jit(solution)/shard_map/ppermute | solution.py:1519
  60.3 16.0 %collective-permute-start.5 = (bf16[4,32,2048]{2,1,0:T(8,128)(2,1)S(1)}, bf16[4,32,2048]{2,1,0:T(8,128)(2,1)}, u32[]{:S(2)}, u32[]{:S(2)}) collective-permute-start(bf16[4,32,2048]{2,1,0:T(8,128)(2,1)S(1)} %get-tuple-element.421.refs_0_), channel_id=1, source_target_pairs={{0,4},{2,6},{4,0},{6,2},{8,12},{10,14},{12,8},{14,10},{16,20},{18,... | collective-permute-start | bytes 1572872 | tf_op jit(solution)/shard_map/ppermute | solution.py:1519
  65.0 18.0 %collective-permute-start.15 = (bf16[4,32,2176]{2,1,0:T(8,128)(2,1)S(1)}, bf16[4,32,2176]{2,1,0:T(8,128)(2,1)}, u32[]{:S(2)}, u32[]{:S(2)}) collective-permute-start(bf16[4,32,2176]{2,1,0:T(8,128)(2,1)S(1)} %collective-permute-done.7.refs_4_.refs_12_), channel_id=1, source_target_pairs={{0,1},{1,0},{2,3},{3,2},{4,5},{5,4},{6,7},{7,6},{8,9},{9,8},{10,11... | collective-permute-start | bytes 1671176 | tf_op jit(solution)/shard_map/ppermute | solution.py:1519
  66.6 16.4 %collective-permute-start.13 = (bf16[4,32,2048]{2,1,0:T(8,128)(2,1)}, bf16[4,32,2048]{2,1,0:T(8,128)(2,1)}, u32[]{:S(2)}, u32[]{:S(2)}) collective-permute-start(bf16[4,32,2048]{2,1,0:T(8,128)(2,1)} %copy-done.82), channel_id=1, source_target_pairs={{0,4},{2,6},{4,0},{6,2},{8,12},{10,14},{12,8},{14,10},{16,20},{18,... | collective-permute-start | bytes 1572872 | tf_op jit(solution)/shard_map/ppermute | solution.py:1519
  89.0 40.3 %collective-permute-start.25 = (bf16[4,32,6144]{2,1,0:T(8,128)(2,1)S(1)}, bf16[4,32,6144]{2,1,0:T(8,128)(2,1)}, u32[]{:S(2)}, u32[]{:S(2)}) collective-permute-start(bf16[4,32,6144]{2,1,0:T(8,128)(2,1)S(1)} %join_up.1.refs_0_), channel_id=1, source_target_pairs={{0,1},{1,0},{2,3},{3,2},{4,5},{5,4},{6,7},{7,6},{8,9},{9,8},{10,11... | collective-permute-start | bytes 4718600 | tf_op jit(solution)/shard_map/ppermute | solution.py:1519
  90.0 39.4 %collective-permute-start.26 = (bf16[4,32,6144]{2,1,0:T(8,128)(2,1)S(1)}, bf16[4,32,6144]{2,1,0:T(8,128)(2,1)}, u32[]{:S(2)}, u32[]{:S(2)}) collective-permute-start(bf16[4,32,6144]{2,1,0:T(8,128)(2,1)S(1)} %join_up.1.refs_0_), channel_id=1, source_target_pairs={{0,4},{2,6},{4,0},{6,2},{8,12},{10,14},{12,8},{14,10},{16,20},{18,... | collective-permute-start | bytes 4718600 | tf_op jit(solution)/shard_map/ppermute | solution.py:1519
  90.5 38.8 %collective-permute-start.29 = (bf16[4,32,6144]{2,1,0:T(8,128)(2,1)S(1)}, bf16[4,32,6144]{2,1,0:T(8,128)(2,1)}, u32[]{:S(2)}, u32[]{:S(2)}) collective-permute-start(bf16[4,32,6144]{2,1,0:T(8,128)(2,1)S(1)} %join_up.1.refs_0_), channel_id=1, source_target_pairs={{0,2},{2,0},{4,6},{6,4},{8,10},{10,8},{12,14},{14,12},{16,18},{18,... | collective-permute-start | bytes 4718600 | tf_op jit(solution)/shard_map/ppermute | solution.py:1519
  90.5 38.8 %collective-permute-start.27 = (bf16[2,2,64,1024]{3,2,1,0:T(8,128)(2,1)}, bf16[2,2,64,1024]{3,2,1,0:T(8,128)(2,1)S(1)}, u32[]{:S(2)}, u32[]{:S(2)}) collective-permute-start(bf16[2,2,64,1024]{3,2,1,0:T(8,128)(2,1)} %join_plane.1.refs_8_), channel_id=1, source_target_pairs={{0,8},{2,10},{4,12},{6,14},{8,16},{10,18},{12,20},{14,22},{16,24},... | collective-permute-start | bytes 1572872 | tf_op jit(solution)/shard_map/ppermute | solution.py:1540
  90.6 38.7 %collective-permute-start.28 = (bf16[2,2,64,1024]{3,2,1,0:T(8,128)(2,1)}, bf16[2,2,64,1024]{3,2,1,0:T(8,128)(2,1)}, u32[]{:S(2)}, u32[]{:S(2)}) collective-permute-start(bf16[2,2,64,1024]{3,2,1,0:T(8,128)(2,1)} %join_plane.1.refs_8_), channel_id=1, source_target_pairs={{0,24},{2,26},{4,28},{6,30},{8,0},{10,2},{12,4},{14,6},{16,8},{18,... | collective-permute-start | bytes 1572872 | tf_op jit(solution)/shard_map/ppermute | solution.py:1540
  129.4 26.0 %collective-permute-start.32 = (bf16[4,32,6144]{2,1,0:T(8,128)(2,1)}, bf16[4,32,6144]{2,1,0:T(8,128)(2,1)S(1)}, u32[]{:S(2)}, u32[]{:S(2)}) collective-permute-start(bf16[4,32,6144]{2,1,0:T(8,128)(2,1)} %collective-permute-done.25.refs_1_), channel_id=1, source_target_pairs={{0,2},{2,0},{4,6},{6,4},{8,10},{10,8},{12,14},{14,12},{16,18},{18,... | collective-permute-start | bytes 4718600 | tf_op jit(solution)/shard_map/ppermute | solution.py:1519
  129.4 25.9 %collective-permute-start.33 = (bf16[4,32,6144]{2,1,0:T(8,128)(2,1)}, bf16[4,32,6144]{2,1,0:T(8,128)(2,1)S(1)}, u32[]{:S(2)}, u32[]{:S(2)}) collective-permute-start(bf16[4,32,6144]{2,1,0:T(8,128)(2,1)} %collective-permute-done.26.refs_4_), channel_id=1, source_target_pairs={{0,2},{2,0},{4,6},{6,4},{8,10},{10,8},{12,14},{14,12},{16,18},{18,... | collective-permute-start | bytes 4718600 | tf_op jit(solution)/shard_map/ppermute | solution.py:1519
  129.9 25.4 %collective-permute-start.30 = (bf16[512,1024]{1,0:T(8,128)(2,1)S(1)}, bf16[512,1024]{1,0:T(8,128)(2,1)S(1)}, u32[]{:S(2)}, u32[]{:S(2)}) collective-permute-start(bf16[512,1024]{1,0:T(8,128)(2,1)S(1)} %copy-done.37), channel_id=1, source_target_pairs={{0,1},{1,0},{2,3},{3,2},{4,5},{5,4},{6,7},{7,6},{8,9},{9,8},{10,11... | collective-permute-start | bytes 3145736 | tf_op jit(solution)/shard_map/ppermute | solution.py:1519
  131.0 38.5 %collective-permute-start.34 = (bf16[4,32,6144]{2,1,0:T(8,128)(2,1)}, bf16[4,32,6144]{2,1,0:T(8,128)(2,1)}, u32[]{:S(2)}, u32[]{:S(2)}) collective-permute-start(bf16[4,32,6144]{2,1,0:T(8,128)(2,1)} %collective-permute-done.25.refs_1_), channel_id=1, source_target_pairs={{0,4},{2,6},{4,0},{6,2},{8,12},{10,14},{12,8},{14,10},{16,20},{18,... | collective-permute-start | bytes 4718600 | tf_op jit(solution)/shard_map/ppermute | solution.py:1519
  132.5 22.8 %collective-permute-start.31 = (bf16[2,2,64,1024]{3,2,1,0:T(8,128)(2,1)}, bf16[2,2,64,1024]{3,2,1,0:T(8,128)(2,1)S(1)}, u32[]{:S(2)}, u32[]{:S(2)}) collective-permute-start(bf16[2,2,64,1024]{3,2,1,0:T(8,128)(2,1)} %join_plane.1.refs_8_), channel_id=1, source_target_pairs={{0,16},{2,18},{4,20},{6,22},{8,24},{10,26},{12,28},{14,30},{16,0},... | collective-permute-start | bytes 1572872 | tf_op jit(solution)/shard_map/ppermute | solution.py:1540
  213.0 22.9 %collective-permute-start.40 = (bf16[4,256,1024]{2,1,0:T(8,128)(2,1)}, bf16[4,256,1024]{2,1,0:T(8,128)(2,1)S(1)}, u32[]{:S(2)}, u32[]{:S(2)}) collective-permute-start(bf16[4,256,1024]{2,1,0:T(8,128)(2,1)} %get-tuple-element.476), channel_id=1, source_target_pairs={{0,2},{2,0},{4,6},{6,4},{8,10},{10,8},{12,14},{14,12},{16,18},{18,... | collective-permute-start | bytes 6291464 | tf_op jit(solution)/shard_map/ppermute | solution.py:1519
  213.2 22.7 %collective-permute-start.41 = (bf16[8,64,2048]{2,1,0:T(8,128)(2,1)}, bf16[8,64,2048]{2,1,0:T(8,128)(2,1)S(1)}, u32[]{:S(2)}, u32[]{:S(2)}) collective-permute-start(bf16[8,64,2048]{2,1,0:T(8,128)(2,1)} %get-tuple-element.482), channel_id=1, source_target_pairs={{0,2},{2,0},{4,6},{6,4},{8,10},{10,8},{12,14},{14,12},{16,18},{18,... | collective-permute-start | bytes 6291464 | tf_op jit(solution)/shard_map/ppermute | solution.py:1519
  235.7 32.9 %collective-permute-start.43 = (bf16[2,256,1024]{2,1,0:T(8,128)(2,1)}, bf16[2,256,1024]{2,1,0:T(8,128)(2,1)}, u32[]{:S(2)}, u32[]{:S(2)}) collective-permute-start(bf16[2,256,1024]{2,1,0:T(8,128)(2,1)} %get-tuple-element.497), channel_id=1, source_target_pairs={{0,2},{2,0},{4,6},{6,4},{8,10},{10,8},{12,14},{14,12},{16,18},{18,... | collective-permute-start | bytes 3145736 | tf_op jit(solution)/shard_map/ppermute | solution.py:1519
  241.1 26.5 %collective-permute-start.42 = (bf16[2,256,1024]{2,1,0:T(8,128)(2,1)}, bf16[2,256,1024]{2,1,0:T(8,128)(2,1)S(1)}, u32[]{:S(2)}, u32[]{:S(2)}) collective-permute-start(bf16[2,256,1024]{2,1,0:T(8,128)(2,1)} %get-tuple-element.493), channel_id=1, source_target_pairs={{0,4},{2,6},{4,0},{6,2},{8,12},{10,14},{12,8},{14,10},{16,20},{18,... | collective-permute-start | bytes 3145736 | tf_op jit(solution)/shard_map/ppermute | solution.py:1519
  242.3 26.3 %collective-permute-start.44 = (bf16[8,32,2048]{2,1,0:T(8,128)(2,1)}, bf16[8,32,2048]{2,1,0:T(8,128)(2,1)}, u32[]{:S(2)}, u32[]{:S(2)}) collective-permute-start(bf16[8,32,2048]{2,1,0:T(8,128)(2,1)} %get-tuple-element.499), channel_id=1, source_target_pairs={{0,1},{1,0},{2,3},{3,2},{4,5},{5,4},{6,7},{7,6},{8,9},{9,8},{10,11... | collective-permute-start | bytes 3145736 | tf_op jit(solution)/shard_map/ppermute | solution.py:1519
  267.0 28.8 %collective-permute-start.47 = (bf16[8,64,2048]{2,1,0:T(8,128)(2,1)}, bf16[8,64,2048]{2,1,0:T(8,128)(2,1)}, u32[]{:S(2)}, u32[]{:S(2)}) collective-permute-start(bf16[8,64,2048]{2,1,0:T(8,128)(2,1)} %get-tuple-element.525), channel_id=1, source_target_pairs={{0,2},{2,0},{4,6},{6,4},{8,10},{10,8},{12,14},{14,12},{16,18},{18,... | collective-permute-start | bytes 6291464 | tf_op jit(solution)/shard_map/ppermute | solution.py:1519
  267.1 26.4 %collective-permute-start.46 = (bf16[2,256,1024]{2,1,0:T(8,128)(2,1)}, bf16[2,256,1024]{2,1,0:T(8,128)(2,1)}, u32[]{:S(2)}, u32[]{:S(2)}) collective-permute-start(bf16[2,256,1024]{2,1,0:T(8,128)(2,1)} %get-tuple-element.516), channel_id=1, source_target_pairs={{0,2},{2,0},{4,6},{6,4},{8,10},{10,8},{12,14},{14,12},{16,18},{18,... | collective-permute-start | bytes 3145736 | tf_op jit(solution)/shard_map/ppermute | solution.py:1519
  271.3 22.1 %collective-permute-start.45 = (bf16[1,256,1024]{2,1,0:T(8,128)(2,1)}, bf16[1,256,1024]{2,1,0:T(8,128)(2,1)}, u32[]{:S(2)}, u32[]{:S(2)}) collective-permute-start(bf16[1,256,1024]{2,1,0:T(8,128)(2,1)} %get-tuple-element.507), channel_id=1, source_target_pairs={{0,4},{2,6},{4,0},{6,2},{8,12},{10,14},{12,8},{14,10},{16,20},{18,... | collective-permute-start | bytes 1572872 | tf_op jit(solution)/shard_map/ppermute | solution.py:1519
  295.7 28.6 %collective-permute-start.50 = (bf16[512,1024]{1,0:T(8,128)(2,1)}, bf16[512,1024]{1,0:T(8,128)(2,1)S(1)}, u32[]{:S(2)}, u32[]{:S(2)}) collective-permute-start(bf16[512,1024]{1,0:T(8,128)(2,1)} %get-tuple-element.539), channel_id=1, source_target_pairs={{0,1},{1,0},{2,3},{3,2},{4,5},{5,4},{6,7},{7,6},{8,9},{9,8},{10,11... | collective-permute-start | bytes 3145736 | tf_op jit(solution)/shard_map/ppermute | solution.py:1519
  297.0 31.7 %collective-permute-start.51 = (bf16[8,64,1024]{2,1,0:T(8,128)(2,1)S(1)}, bf16[8,64,1024]{2,1,0:T(8,128)(2,1)S(1)}, u32[]{:S(2)}, u32[]{:S(2)}) collective-permute-start(bf16[8,64,1024]{2,1,0:T(8,128)(2,1)S(1)} %get-tuple-element.558), channel_id=1, source_target_pairs={{0,2},{2,0},{4,6},{6,4},{8,10},{10,8},{12,14},{14,12},{16,18},{18,... | collective-permute-start | bytes 3145736 | tf_op jit(solution)/shard_map/ppermute | solution.py:1519
  297.0 28.4 %collective-permute-start.49 = (bf16[4,32,2048]{2,1,0:T(8,128)(2,1)S(1)}, bf16[4,32,2048]{2,1,0:T(8,128)(2,1)S(1)}, u32[]{:S(2)}, u32[]{:S(2)}) collective-permute-start(bf16[4,32,2048]{2,1,0:T(8,128)(2,1)S(1)} %get-tuple-element.532), channel_id=1, source_target_pairs={{0,4},{2,6},{4,0},{6,2},{8,12},{10,14},{12,8},{14,10},{16,20},{18,... | collective-permute-start | bytes 1572872 | tf_op jit(solution)/shard_map/ppermute | solution.py:1519
  298.2 27.2 %collective-permute-start.48 = (bf16[1,256,1024]{2,1,0:T(8,128)(2,1)S(1)}, bf16[1,256,1024]{2,1,0:T(8,128)(2,1)S(1)}, u32[]{:S(2)}, u32[]{:S(2)}) collective-permute-start(bf16[1,256,1024]{2,1,0:T(8,128)(2,1)S(1)} %get-tuple-element.530), channel_id=1, source_target_pairs={{0,4},{2,6},{4,0},{6,2},{8,12},{10,14},{12,8},{14,10},{16,20},{18,... | collective-permute-start | bytes 1572872 | tf_op jit(solution)/shard_map/ppermute | solution.py:1519
  302.2 53.6 %collective-permute-start.53 = (bf16[4,64,2048]{2,1,0:T(8,128)(2,1)S(1)}, bf16[4,64,2048]{2,1,0:T(8,128)(2,1)S(1)}, u32[]{:S(2)}, u32[]{:S(2)}) collective-permute-start(bf16[4,64,2048]{2,1,0:T(8,128)(2,1)S(1)} %get-tuple-element.571), channel_id=1, source_target_pairs={{0,4},{2,6},{4,0},{6,2},{8,12},{10,14},{12,8},{14,10},{16,20},{18,... | collective-permute-start | bytes 3145736 | tf_op jit(solution)/shard_map/ppermute | solution.py:1519
  327.5 31.6 %collective-permute-start.57 = (bf16[4,128,1024]{2,1,0:T(8,128)(2,1)S(1)}, bf16[4,128,1024]{2,1,0:T(8,128)(2,1)S(1)}, u32[]{:S(2)}, u32[]{:S(2)}) collective-permute-start(bf16[4,128,1024]{2,1,0:T(8,128)(2,1)S(1)} %get-tuple-element.589), channel_id=1, source_target_pairs={{0,1},{1,0},{2,3},{3,2},{4,5},{5,4},{6,7},{7,6},{8,9},{9,8},{10,11... | collective-permute-start | bytes 3145736 | tf_op jit(solution)/shard_map/ppermute | solution.py:1519
  330.2 25.5 %collective-permute-start.54 = (bf16[32,2048]{1,0:T(8,128)(2,1)S(1)}, bf16[32,2048]{1,0:T(8,128)(2,1)S(1)}, u32[]{:S(2)}, u32[]{:S(2)}) collective-permute-start(bf16[32,2048]{1,0:T(8,128)(2,1)S(1)} %get-tuple-element.573), channel_id=1, source_target_pairs={{0,8},{2,10},{4,12},{6,14},{8,16},{10,18},{12,20},{14,22},{16,24},... | collective-permute-start | bytes 393224 | tf_op jit(solution)/shard_map/ppermute | solution.py:1540
  330.8 25.0 %collective-permute-start.55 = (bf16[32,2048]{1,0:T(8,128)(2,1)S(1)}, bf16[32,2048]{1,0:T(8,128)(2,1)S(1)}, u32[]{:S(2)}, u32[]{:S(2)}) collective-permute-start(bf16[32,2048]{1,0:T(8,128)(2,1)S(1)} %get-tuple-element.574), channel_id=1, source_target_pairs={{0,16},{2,18},{4,20},{6,22},{8,24},{10,26},{12,28},{14,30},{16,0},... | collective-permute-start | bytes 393224 | tf_op jit(solution)/shard_map/ppermute | solution.py:1540
  335.0 20.8 %collective-permute-start.56 = (bf16[32,2048]{1,0:T(8,128)(2,1)S(1)}, bf16[32,2048]{1,0:T(8,128)(2,1)S(1)}, u32[]{:S(2)}, u32[]{:S(2)}) collective-permute-start(bf16[32,2048]{1,0:T(8,128)(2,1)S(1)} %get-tuple-element.575), channel_id=1, source_target_pairs={{0,24},{2,26},{4,28},{6,30},{8,0},{10,2},{12,4},{14,6},{16,8},{18,... | collective-permute-start | bytes 393224 | tf_op jit(solution)/shard_map/ppermute | solution.py:1540
  380.6 30.9 %collective-permute-start.62 = (bf16[4,64,1536]{2,1,0:T(8,128)(2,1)S(1)}, bf16[4,64,1536]{2,1,0:T(8,128)(2,1)S(1)}, u32[]{:S(2)}, u32[]{:S(2)}) collective-permute-start(bf16[4,64,1536]{2,1,0:T(8,128)(2,1)S(1)} %get-tuple-element.650), channel_id=1, source_target_pairs={{0,4},{2,6},{4,0},{6,2},{8,12},{10,14},{12,8},{14,10},{16,20},{18,... | collective-permute-start | bytes 2359304 | tf_op jit(solution)/shard_map/ppermute | solution.py:1519
  383.2 28.3 %collective-permute-start.66 = (bf16[8,32,1536]{2,1,0:T(8,128)(2,1)S(1)}, bf16[8,32,1536]{2,1,0:T(8,128)(2,1)S(1)}, u32[]{:S(2)}, u32[]{:S(2)}) collective-permute-start(bf16[8,32,1536]{2,1,0:T(8,128)(2,1)S(1)} %get-tuple-element.665), channel_id=1, source_target_pairs={{0,1},{1,0},{2,3},{3,2},{4,5},{5,4},{6,7},{7,6},{8,9},{9,8},{10,11... | collective-permute-start | bytes 2359304 | tf_op jit(solution)/shard_map/ppermute | solution.py:1519
  385.0 24.3 %collective-permute-start.63 = (bf16[128,1024]{1,0:T(8,128)(2,1)S(1)}, bf16[128,1024]{1,0:T(8,128)(2,1)S(1)}, u32[]{:S(2)}, u32[]{:S(2)}) collective-permute-start(bf16[128,1024]{1,0:T(8,128)(2,1)S(1)} %get-tuple-element.652), channel_id=1, source_target_pairs={{0,8},{2,10},{4,12},{6,14},{8,16},{10,18},{12,20},{14,22},{16,24},... | collective-permute-start | bytes 786440 | tf_op jit(solution)/shard_map/ppermute | solution.py:1540
  386.8 24.6 %collective-permute-start.64 = (bf16[128,1024]{1,0:T(8,128)(2,1)S(1)}, bf16[128,1024]{1,0:T(8,128)(2,1)S(1)}, u32[]{:S(2)}, u32[]{:S(2)}) collective-permute-start(bf16[128,1024]{1,0:T(8,128)(2,1)S(1)} %get-tuple-element.653), channel_id=1, source_target_pairs={{0,16},{2,18},{4,20},{6,22},{8,24},{10,26},{12,28},{14,30},{16,0},... | collective-permute-start | bytes 786440 | tf_op jit(solution)/shard_map/ppermute | solution.py:1540
  388.9 22.6 %collective-permute-start.65 = (bf16[128,1024]{1,0:T(8,128)(2,1)S(1)}, bf16[128,1024]{1,0:T(8,128)(2,1)S(1)}, u32[]{:S(2)}, u32[]{:S(2)}) collective-permute-start(bf16[128,1024]{1,0:T(8,128)(2,1)S(1)} %get-tuple-element.654), channel_id=1, source_target_pairs={{0,24},{2,26},{4,28},{6,30},{8,0},{10,2},{12,4},{14,6},{16,8},{18,... | collective-permute-start | bytes 786440 | tf_op jit(solution)/shard_map/ppermute | solution.py:1540
  413.2 19.0 %collective-permute-start.67 = (bf16[4,32,1536]{2,1,0:T(8,128)(2,1)S(1)}, bf16[4,32,1536]{2,1,0:T(8,128)(2,1)S(1)}, u32[]{:S(2)}, u32[]{:S(2)}) collective-permute-start(bf16[4,32,1536]{2,1,0:T(8,128)(2,1)S(1)} %get-tuple-element.678), channel_id=1, source_target_pairs={{0,1},{1,0},{2,3},{3,2},{4,5},{5,4},{6,7},{7,6},{8,9},{9,8},{10,11... | collective-permute-start | bytes 1179656 | tf_op jit(solution)/shard_map/ppermute | solution.py:1519
  414.3 17.9 %collective-permute-start.72 = (bf16[4,32,1536]{2,1,0:T(8,128)(2,1)S(1)}, bf16[4,32,1536]{2,1,0:T(8,128)(2,1)S(1)}, u32[]{:S(2)}, u32[]{:S(2)}) collective-permute-start(bf16[4,32,1536]{2,1,0:T(8,128)(2,1)S(1)} %get-tuple-element.698), channel_id=1, source_target_pairs={{0,4},{2,6},{4,0},{6,2},{8,12},{10,14},{12,8},{14,10},{16,20},{18,... | collective-permute-start | bytes 1179656 | tf_op jit(solution)/shard_map/ppermute | solution.py:1519
  415.1 40.8 %collective-permute-start.81 = (bf16[512,1024]{1,0:T(8,128)(2,1)}, bf16[512,1024]{1,0:T(8,128)(2,1)S(1)}, u32[]{:S(2)}, u32[]{:S(2)}) collective-permute-start(bf16[512,1024]{1,0:T(8,128)(2,1)} %get-tuple-element.718), channel_id=1, source_target_pairs={{0,1},{1,0},{2,3},{3,2},{4,5},{5,4},{6,7},{7,6},{8,9},{9,8},{10,11... | collective-permute-start | bytes 3145736 | tf_op jit(solution)/shard_map/ppermute | solution.py:1519
  452.4 15.7 %collective-permute-start.74 = (bf16[32,3072]{1,0:T(8,128)(2,1)}, bf16[32,3072]{1,0:T(8,128)(2,1)S(1)}, u32[]{:S(2)}, u32[]{:S(2)}) collective-permute-start(bf16[32,3072]{1,0:T(8,128)(2,1)} %copy-done.72), channel_id=1, source_target_pairs={{0,16},{2,18},{4,20},{6,22},{8,24},{10,26},{12,28},{14,30},{16,0},... | collective-permute-start | bytes 589832 | tf_op jit(solution)/shard_map/ppermute | solution.py:1540
  (150 other events, 1360.1 us)

commit v3 on v2

--- a/solution.py
+++ b/solution.py
@@ -710,7 +710,7 @@
     )
 
 
-def out_norm(place, mixed, right, bias, inputs, far, gain, shift, down_bias):
+def out_norm(place, mixed, up_parts, at_out, bias, inputs, far, gain, shift, down_bias):
     half, width = far.shape
     step = 256
     parts = half // step
@@ -721,7 +721,7 @@
 
         @pl.when(pl.program_id(0) == 0)
         def _():
-            copies = parts_copies(place_ref, right_refs, weight, sems, width, width, 0, 0)
+            copies = parts_copies(place_ref, right_refs, weight, sems, at_out, width, 0, 0)
             for copy in copies:
                 copy.start()
             for copy in copies:
@@ -752,8 +752,8 @@
         + [whole_ref()] * 8,
         [here, here, here],
         [shape_of(F32, 2 * half, width), shape_of(BF16, 2 * half, width), shape_of(F32, 2 * half, width)],
-        (place, mixed, bias, inputs, far, gain, shift, down_bias) + tuple(right),
-        scratch=[weight_scratch(right[0], width), pltpu.SemaphoreType.DMA((1, 8))],
+        (place, mixed, bias, inputs, far, gain, shift, down_bias) + tuple(up_parts),
+        scratch=[weight_scratch(up_parts[0], width), pltpu.SemaphoreType.DMA((1, 8))],
         vmem=56,
     )
 
@@ -779,59 +779,54 @@
     )
 
 
-def grad_wide(place, left, rights, rows, pieces, before=()):
+def grad_wide(place, left, rights, rows, span, pieces=1):
     tokens, tall = left.shape
     width = rights[0].shape[1]
     step = 512
     each = width // step
-    steps = each * len(rights)
+    first, stop = span
+    steps = stop - first
+    per = steps // pieces
     group = 4 * rows
-    per = steps // pieces
-    total = width * len(rights)
+    used = sorted({at // each for at in range(first, stop)})
 
     def body(place_ref, left_ref, *refs):
-        right_refs = refs[: len(rights)]
-        outs = refs[len(rights) + len(before) : -1]
-        sums = refs[-1]
+        right_refs = refs[: len(used)]
+        outs, sums = refs[len(used) : -1], refs[-1]
         at = pl.program_id(0)
-        for which, right_ref in enumerate(right_refs):
-            @pl.when(at // each == which)
+        for which, right_ref in zip(used, right_refs):
+            @pl.when((at + first) // each == which)
             def _():
-                result = contract(left_ref[...], right_ref[...], 0, 0)
+                result = contract(left_ref[...], right_ref[...], 0, 0).astype(BF16)
                 sums[...] = result.reshape(tall // group, 2, group // 2, step)
 
         for piece in range(pieces):
             @pl.when(at // per == piece)
             def _():
-                outs[2 * piece][...] = sums[:, place_ref[2]].astype(BF16)
-                outs[2 * piece + 1][...] = sums[:, 1 - place_ref[2]].astype(BF16)
+                outs[2 * piece][...] = sums[:, place_ref[2]]
+                outs[2 * piece + 1][...] = sums[:, 1 - place_ref[2]]
 
     def right_at(which):
-        return lambda i, _: (0, jnp.clip(i - which * each, 0, each - 1))
-
-    wide_total = before[0].shape[-1] if before else total // pieces
-    start = (wide_total - total // pieces) // step
+        low, high = max(first - which * each, 0), min(stop - which * each, each) - 1
+        return lambda i, _: (0, jnp.clip(i + first - which * each, low, high))
 
     def out_at(piece):
-        return lambda i, _: (0, 0, start + jnp.clip(i - piece * per, 0, per - 1))
+        return lambda i, _: (0, 0, jnp.clip(i - piece * per, 0, per - 1))
 
     return call(
         body,
         "grad_wide",
         (steps,),
-        [held(tokens, tall)]
-        + [pl.BlockSpec((tokens, step), right_at(i)) for i in range(len(rights))]
-        + [whole_ref()] * len(before),
+        [held(tokens, tall)] + [pl.BlockSpec((tokens, step), right_at(which)) for which in used],
         [
             pl.BlockSpec((tall // group, group // 2, step), out_at(piece))
             for piece in range(pieces)
             for _ in range(2)
         ],
-        [shape_of(BF16, tall // group, group // 2, wide_total)] * (2 * pieces),
-        (place, left) + tuple(rights) + tuple(before),
-        scratch=[pltpu.VMEM((tall // group, 2, group // 2, step), F32)],
+        [shape_of(BF16, tall // group, group // 2, per * step)] * (2 * pieces),
+        (place, left) + tuple(rights[which] for which in used),
+        scratch=[pltpu.VMEM((tall // group, 2, group // 2, step), BF16)],
         vmem=20,
-        alias={2 + len(rights) + i: i for i in range(len(before))},
     )
 
 
@@ -1055,7 +1050,7 @@
     )
 
 
-def middle_back(place, grad_normed, middle, gain, grad_out, far, right):
+def middle_back(place, grad_normed, middle, gain, grad_out, far, up_parts, at_out):
     half, width = far.shape
     step = 256
     parts = half // step
@@ -1068,7 +1063,7 @@
         at = pl.program_id(0)
 
         def copies():
-            return parts_copies(place_ref, right_refs, weight, sems, width, width, 0, 0)
+            return parts_copies(place_ref, right_refs, weight, sems, at_out, width, 0, 0)
 
         @pl.when(at == 0)
         def _():
@@ -1107,14 +1102,15 @@
         [here, here, here, vector, vector, vector],
         [shape_of(F32, tokens, width), shape_of(BF16, tokens, width), shape_of(BF16, tokens, width)]
         + [shape_of(F32, 1, width)] * 3,
-        (place, grad_normed, middle, gain, grad_out, far) + tuple(right),
-        scratch=[weight_scratch(right[0], width), pltpu.SemaphoreType.DMA((1, 8))],
+        (place, grad_normed, middle, gain, grad_out, far) + tuple(up_parts),
+        scratch=[weight_scratch(up_parts[0], width), pltpu.SemaphoreType.DMA((1, 8))],
         vmem=56,
     )
 
 
 def input_back(place, grads, left, right, inputs, far, gain, middle_grad, far_grad):
     half, width = far.shape
+    cut = left[0].shape[-1]
     step = 256
     parts = half // step
 
@@ -1130,9 +1126,10 @@
 
         def copies():
             result = []
-            for chunk, part_refs in enumerate((left_refs, left_refs, right_refs)):
+            for chunk, part_refs in enumerate((left_refs, right_refs)):
+                size = (cut, 3 * width - cut)[chunk]
                 result += parts_copies(
-                    place_ref, part_refs, weight, sems, (chunk % 2) * width, width, chunk * width, chunk
+                    place_ref, part_refs, weight, sems, 0, size, chunk * cut, chunk
                 )
             return result
 
@@ -1190,7 +1187,7 @@
         [own_spec(step, width, parts), far_spec(step, width, parts), vector, vector, vector, vector],
         [shape_of(F32, 2, half, width), shape_of(BF16, half, width)] + [shape_of(F32, 1, width)] * 4,
         (place,) + tuple(grads) + (inputs, far, gain, middle_grad, far_grad) + tuple(left) + tuple(right),
-        scratch=[weight_scratch(left[0], 3 * width), pltpu.SemaphoreType.DMA((3, 8))],
+        scratch=[weight_scratch(left[0], 3 * width), pltpu.SemaphoreType.DMA((2, 8))],
         vmem=56,
     )
 
@@ -1216,13 +1213,16 @@
     )
 
 
-def split_depth(place, pairs, rows):
+def split_depth(place, pairs, rows, vectors=None, sizes=()):
     depth = pairs[0][0].shape[0]
     layout = [(which, part) for which, (mine, _) in enumerate(pairs) for part in range(mine.shape[1] // rows)]
     total = sum(pairs[which][0].shape[2] for which, _ in layout)
+    extra = () if vectors is None else (vectors,)
+    wide = total + PAIR * len(extra)
+    count = depth * 8
 
     def body(place_ref, *refs):
-        outs = refs[2 * len(pairs) :]
+        outs = refs[2 * len(pairs) + len(extra) :]
         for step, ref in enumerate(outs):
             at = lax.rem(place_ref[0] + step, depth)
             start = 0
@@ -1232,15 +1232,25 @@
                 value = refs[2 * which][at, cut].astype(F32) + refs[2 * which + 1][at, cut].astype(F32)
                 ref[:, start : start + width] = value.astype(ref.dtype)
                 start += width
+            if extra:
+                device = ((at * 2 + place_ref[1]) * 2 + place_ref[2]) * 2 + place_ref[3]
+                line = lax.broadcasted_iota(jnp.int32, (rows, PAIR), 0)
+                block = jnp.zeros((rows, PAIR), F32)
+                base = 0
+                for index, size in enumerate(sizes):
+                    values = refs[2 * len(pairs)][pl.ds(base + device * size * rows // PAIR, 1), :]
+                    block = jnp.where(line == index, values, block)
+                    base += count * size * rows // PAIR
+                ref[:, total:] = block.astype(ref.dtype)
 
     return call(
         body,
         "split_depth",
         (1,),
-        [held(*mine.shape) for mine, _ in pairs for _ in range(2)],
-        [held(rows, total)] * depth,
-        [shape_of(F32, rows, total)] + [shape_of(BF16, rows, total)] * (depth - 1),
-        (place,) + tuple(value for pair in pairs for value in pair),
+        [held(*mine.shape) for mine, _ in pairs for _ in range(2)] + [held(*value.shape) for value in extra],
+        [held(rows, wide)] * depth,
+        [shape_of(F32, rows, wide)] + [shape_of(BF16, rows, wide)] * (depth - 1),
+        (place,) + tuple(value for pair in pairs for value in pair) + extra,
         vmem=12,
     )
 
@@ -1535,6 +1545,11 @@
     return pair_swap(value, "seq", 1)
 
 
+def swap_xy(value):
+    pairs = 2 * lax.axis_size("dp")
+    return lax.ppermute(value, BOTH, [(i, i ^ 5) for i in range(pairs)])
+
+
 def ring_z(value, step):
     size = lax.axis_size("dp")
     return lax.ppermute(value, "dp", [(i, (i + 4 * step) % size) for i in range(size)])
@@ -1542,17 +1557,6 @@
 
 def tie(*values):
     return lax.optimization_barrier(values)
-
-
-def swap_core_sum(values):
-    return values + swap_core(values)
-
-
-def sum_depth(values):
-    total = values
-    for step in range(1, lax.axis_size("dp") // 4):
-        total = total + ring_z(values, step)
-    return total
 
 
 class Reduce:
@@ -1587,10 +1591,11 @@
             sent, kept = split_add(self.place, mine[0], came[0], spot)
         self.mine, self.came = kept, swap(sent)
 
-    def third(self, *others):
+    def third(self, *others, vectors=None, sizes=()):
         parts = (self,) + others
         rows = min(part.rows for part in parts)
-        own, *sent = split_depth(self.place, [(part.mine, part.came) for part in parts], rows)
+        pairs = [(part.mine, part.came) for part in parts]
+        own, *sent = split_depth(self.place, pairs, rows, vectors, sizes)
         self.mine = own
         self.came = [ring_z(block, step + 1) for step, block in enumerate(sent)]
 
@@ -1649,22 +1654,24 @@
     small = jnp.pad(small, ((0, rows - small.shape[0]), (0, PAIR - rows)))
     shard = join_beside(place, [w_query, w_key, w_value, w_out, small])
     turned = [shard] + [ring_z(shard, step) for step in ring]
-    tall_half = tall_rows // 2
-    down_near, down_own = w_down[tall_half:], w_down[:tall_half]
+    tall_cut = tall_rows // 2
+    down_near, down_own = w_down[tall_cut:], w_down[:tall_cut]
     down_x = swap_x(down_own)
-    far_rows = swap_y(cast_far(place, inputs))
+    random_far = swap_y(pick(random_blocks, 1 - y, 0))
+    random_far, far_rows = tie(random_far, cast_far(place, inputs))
+    far_rows = swap_y(far_rows)
     up_shard = join_beside(
-        place, [w_up] + [down_near[start : start + rows] for start in range(0, tall_half, rows)]
-    )
-    turned, down_x, far_rows, up_shard, down_own, random_blocks, grad_out = tie(
-        turned, down_x, far_rows, up_shard, down_own, random_blocks, grad_out
+        place, [w_up] + [down_near[start : start + rows] for start in range(0, tall_cut, rows)]
+    )
+    at_out = width
+    turned, down_x, far_rows, up_shard, down_own, random_far, grad_out = tie(
+        turned, down_x, far_rows, up_shard, down_own, random_far, grad_out
     )
     cut = 2 * width
     left, right = join_depth(place, turned, [(0, cut), (cut, shard.shape[1])], "join_first")
     left_y, right_x = swap_y(left), swap_x(right)
     up_turned = {1: ring_z(up_shard, 1), depth - 1: ring_z(up_shard, depth - 1)}
     down_y, down_xy = swap_y(down_own), swap_y(down_x)
-    random_far = swap_y(pick(random_blocks, 1 - y, 0))
     far_grad_low = cast_far(place, grad_out)
     left_y, right_x, up_turned, down_own, down_x, down_y, down_xy, far_grad_low, random_far = tie(
         left_y, right_x, up_turned, down_own, down_x, down_y, down_xy, far_grad_low, random_far
@@ -1686,6 +1693,10 @@
     (up_own,) = join_depth(
         place, [up_shard] + [up_turned[step] for step in ring], [(0, up_shard.shape[1])], "join_up"
     )
+    up_own, left, left_x, left_y, left_xy, right, right_x, right_y, right_xy = tie(
+        up_own, left, left_x, left_y, left_xy, right, right_x, right_y, right_xy
+    )
+    up_y, up_x = swap_y(up_own), swap_x(up_own)
     left_core = {
         (0, 0): swap_core(left), (0, 1): swap_core(left_y),
         (1, 0): swap_core(left_x), (1, 1): swap_core(left_xy),
@@ -1696,11 +1707,9 @@
     }
     left_parts = near_parts(left, left_x, left_y, left_xy, left_core)
     right_parts = near_parts(right, right_x, right_y, right_xy, right_core)
-    left_parts, right_parts, plane, up_own = tie(left_parts, right_parts, plane, up_own)
-
-    up_y, up_x = swap_y(up_own), swap_x(up_own)
+    left_parts, right_parts, up_own = tie(left_parts, right_parts, up_own)
+
     planes = {0: plane, 1: ring_z(plane, 1), depth - 1: ring_z(plane, depth - 1)}
-    up_core = {(0, 0): swap_core(up_own)}
     spans = small_vectors(place, right_parts, cut, sizes, rows)
     (
         ln1_gain,
@@ -1717,31 +1726,33 @@
     normed_low, qkv = norm_project(
         place, inputs, far_rows, ln1_gain, ln1_bias, left_parts, right_parts, qkv_bias
     )
-    attended = attn_forward(place, qkv, bias, 0, pairs // 2)
-    attended, up_y, up_x, planes, up_core, far_grad_low = tie(
-        attended, up_y, up_x, planes, up_core, far_grad_low
-    )
+    near_pairs = 3 * pairs // 8
+    attended = attn_forward(place, qkv, bias, 0, near_pairs)
+    attended, up_y, up_x, planes, far_grad_low = tie(attended, up_y, up_x, planes, far_grad_low)
     up_xy = swap_x(up_y)
-    up_core[0, 1] = swap_core(up_y)
-    up_core[1, 0] = swap_core(up_x)
+    up_core = {(0, 0): swap_core(up_own), (0, 1): swap_core(up_y)}
     far_grad = swap_y(far_grad_low)
     for step in ring:
         if step not in planes:
             planes[step] = ring_z(planes[0], step)
     prob, mixed_low, totals = attn_forward(
-        place, qkv, bias, pairs // 2, pairs - pairs // 2, attended
-    )
-    mixed_low, far_grad, planes, up_core = tie(mixed_low, far_grad, planes, up_core)
-    plane_core = {0: swap_core(planes[0])}
-    for step in ring:
-        plane_core[step] = swap_core(planes[step])
+        place, qkv, bias, near_pairs, pairs - near_pairs, attended
+    )
+    mixed_low, far_grad, up_core, up_x, planes = tie(mixed_low, far_grad, up_core, up_x, planes)
+    up_core[1, 0] = swap_core(up_x)
+    plane_core = {step: swap_core(planes[step]) for step in (0, 1, depth - 1)}
     grad_ff_low, grad_down_bias = join_low(place, grad_out, far_grad)
     mixed_low, grad_ff_low = tie(mixed_low, grad_ff_low)
     middle, normed_two_low, start_out = out_norm(
-        place, mixed_low, right_parts, out_bias, inputs, far_rows, ln2_gain, ln2_bias, down_bias
-    )
-    normed_two_low, up_xy, plane_core = tie(normed_two_low, up_xy, plane_core)
+        place, mixed_low, right_parts, at_out, out_bias, inputs, far_rows, ln2_gain, ln2_bias, down_bias
+    )
+    normed_two_low, up_xy, plane_core, up_core, planes = tie(
+        normed_two_low, up_xy, plane_core, up_core, planes
+    )
     up_core[1, 1] = swap_core(up_xy)
+    for step in ring:
+        if step not in plane_core:
+            plane_core[step] = swap_core(planes[step])
     up_parts = near_parts(up_own, up_x, up_y, up_xy, up_core)
     down_parts = [part for step in range(depth) for part in (planes[step], plane_core[step])]
 
@@ -1787,9 +1798,9 @@
     down_sums[1].mine, back = tie(down_sums[1].mine, back)
     grad_up_bias = jnp.concatenate([bias_0, bias_1, bias_2], axis=1)
     grad_middle, grad_attn_low, grad_mixed_low, grad_ln2_gain, grad_ln2_bias, grad_out_bias = middle_back(
-        place, back, middle, ln2_gain, grad_out, far_grad, right_parts
-    )
-    out_sum.begin(*grad_wide(place, mixed_low, (grad_attn_low,), rows, 1))
+        place, back, middle, ln2_gain, grad_out, far_grad, right_parts, at_out
+    )
+    out_sum.begin(*grad_wide(place, mixed_low, (grad_attn_low,), rows, (0, 2)))
     out_sum.mine, grad_mixed_low = tie(out_sum.mine, grad_mixed_low)
     (grad_mixed_low,) = down_sums[1].hold(grad_mixed_low)
     (grad_mixed_low,) = down_sums[2].hold(grad_mixed_low)
@@ -1821,7 +1832,7 @@
     (grads,) = down_sum.hold(grads)
     wide_sum.second()
     wide_sum.mine, grads = tie(wide_sum.mine, grads)
-    wide = grad_wide(place, normed_low, grads, rows, 2)
+    wide = grad_wide(place, normed_low, grads, rows, (0, 6), 2)
     (wide,) = wide_sum.hold(wide)
     (wide,) = out_sum.hold(wide)
     out_sum.second()
@@ -1835,21 +1846,19 @@
     left_sum.first()
     (grads,) = right_sum.hold(grads)
     right_sum.first()
-    down_sum.third()
+    down_sum.third(wide_sum, out_sum)
     left_sum.mine, right_sum.mine, down_sum.mine, grads = tie(
         left_sum.mine, right_sum.mine, down_sum.mine, grads
     )
     in_part, in_delta, grad_ln1_gain, grad_ln1_bias, grad_query_bias, grad_value_bias = input_back(
         place, grads, left_parts, right_parts, inputs, far_rows, ln1_gain, grad_middle, far_grad
     )
-    (in_delta,) = down_sum.hold(in_delta)
     (in_delta,) = left_sum.hold(in_delta)
     left_sum.second()
     (in_delta,) = right_sum.hold(in_delta)
     right_sum.second()
-    wide_sum.third(out_sum)
-    left_sum.mine, right_sum.mine, wide_sum.mine, in_delta, grad_ln1_gain = tie(
-        left_sum.mine, right_sum.mine, wide_sum.mine, in_delta, grad_ln1_gain
+    left_sum.mine, right_sum.mine, in_delta, grad_ln1_gain = tie(
+        left_sum.mine, right_sum.mine, in_delta, grad_ln1_gain
     )
     grad_vectors = (
         grad_ln1_gain,
@@ -1862,34 +1871,32 @@
         grad_up_bias,
         grad_down_bias,
     )
-    packed = jnp.concatenate(grad_vectors, axis=1)
+    packed = jnp.concatenate(grad_vectors, axis=1).reshape(-1, PAIR)
+    packed = packed + swap_core(packed)
+    packed = packed + swap_x(packed) + swap_y(packed) + swap_xy(packed)
+    (in_delta,) = down_sum.hold(in_delta)
+    (in_delta,) = left_sum.hold(in_delta)
+    (in_delta,) = right_sum.hold(in_delta)
+    packed, in_delta = tie(packed, in_delta)
     in_far = swap_y(in_delta)
-    packed = swap_core_sum(packed.reshape(-1, PAIR))
-    (packed,) = wide_sum.hold(packed)
-    (packed,) = left_sum.hold(packed)
-    (packed,) = right_sum.hold(packed)
-    packed = sum_depth(packed)
-    left_sum.third(right_sum)
-    left_sum.mine, packed = tie(left_sum.mine, packed)
-    packed = packed + swap_x(packed)
-    packed = (packed + swap_y(packed)).reshape(-1)
-    (grad_w_down,) = down_sum.last(w_down.shape)
-    grad_up_far, grad_w_out = wide_sum.last((rows, near_width), w_out.shape)
-    packed, out_far, grad_w_down, grad_up_far, in_far = tie(
-        packed, out_far, grad_w_down, grad_up_far, in_far
-    )
-    left_sum.came, in_far, out_far = tie(left_sum.came, in_far, out_far)
+    left_sum.third(right_sum, vectors=packed, sizes=sizes)
+    left_sum.mine, out_far, down_sum.mine = tie(left_sum.mine, out_far, down_sum.mine)
+    grad_w_down, grad_up_far, grad_w_out = down_sum.last(w_down.shape, (rows, near_width), w_out.shape)
     result = fill_far(place, out_part, inputs, out_far)
+    result, in_far, grad_up_far = tie(result, in_far, grad_up_far)
     grad_in = fill_far(place, in_part, grad_out, in_far)
+    left_sum.came, grad_in = tie(left_sum.came, grad_in)
     grad_w_up = jnp.concatenate([grad_up_near, grad_up_far], axis=1)
     square, part = (rows, width), (rows, width // 2)
-    grad_left_q, grad_left_k, grad_right_k, grad_right_v = left_sum.last(square, part, part, square)
+    grad_left_q, grad_left_k, grad_right_k, grad_right_v, packed = left_sum.last(
+        square, part, part, square, (rows, PAIR)
+    )
+    packed = packed.reshape(-1)
     out_vectors = []
-    at = 0
-    for vector in vectors:
-        count = vector.shape[0]
-        out_vectors.append(lax.dynamic_slice_in_dim(packed, at + (dp * 2 + y) * count, count))
-        at += count * depth * 8
+    for index, size in enumerate(sizes):
+        count = size * rows
+        lane = (dp * 2 + y) * count % PAIR
+        out_vectors.append(lax.dynamic_slice_in_dim(packed, index * PAIR + lane, count))
     grad_w_key = jnp.concatenate([grad_left_k, grad_right_k], axis=1)
     return (
         (result, grad_in, grad_left_q, grad_w_key, grad_right_v, grad_w_out, grad_w_up, grad_w_down)

time: 485 us -> 468 us (0.965)
  starting transfers between devices: 75.7 us -> 64.9 us
  waiting for transfers between devices: 93.1 us -> 84.6 us
    ppermute x24 -> x18, waiting for transfers between devices: 56.9 us -> 38.4 us  [ring_z(): lax.ppermute(value, 'dp', [(i, (i + 4 * step) % size) for i in range(size)])]
    ppermute x24 -> x18, starting transfers between devices: 33.8 us -> 22.9 us  [ring_z(): lax.ppermute(value, 'dp', [(i, (i + 4 * step) % size) for i in range(size)])]
    ppermute x58, waiting for transfers between devices: 36.3 us -> 43.3 us  [pair_swap(): return lax.ppermute(value, axis, [(i, i ^ bit) for i in range(size)])]
    unnamed x243 -> x233, local copies, waits for them, and re-layouts: 29.8 us -> 31.2 us
    pallas_call x46 -> x44, Pallas kernels: 275 us -> 275 us  [call(): pl.pallas_call(body, grid_spec=spec, out_shape=out_shape, name=name, inpu...]
  transfers between devices with their start and end apart: 82 -> 77, of which waited for: 23 -> 23; matrix products, arithmetic and copies ran while one was open for 0% -> 0% of each run, Pallas kernels for 47% -> 50%
where the time goes in v3:
time: 468 us; the launch traced here: 463 us
  Pallas kernels  275 us (59%)
  waiting for transfers between devices  84.6 us (18%)
  starting transfers between devices  64.9 us (14%)
  local copies, waits for them, and re-layouts  33.7 us (7%)
    pallas_call x44, Pallas kernels, call(): pl.pallas_call(body, grid_spec=spec, out_shape=out_shape, name=name, inpu...  275 us
    ppermute x58, waiting for transfers between devices, pair_swap(): return lax.ppermute(value, axis, [(i, i ^ bit) for i in range(size)])  43.3 us
    ppermute x58, starting transfers between devices, pair_swap(): return lax.ppermute(value, axis, [(i, i ^ bit) for i in range(size)])  40.6 us
    ppermute x18, waiting for transfers between devices, ring_z(): lax.ppermute(value, 'dp', [(i, (i + 4 * step) % size) for i in range(size)])  38.4 us
    unnamed x233, local copies, waits for them, and re-layouts  31.2 us
    ppermute x18, starting transfers between devices, ring_z(): lax.ppermute(value, 'dp', [(i, (i + 4 * step) % size) for i in range(size)])  22.9 us
  transfers between devices with their start and end apart: 77, of which 23 were waited for; matrix products, arithmetic and copies ran while one was open for 0% of the time, Pallas kernels for 50%

profile of v3, /device:TPU:8, one launch (start us, length us, event | category | flops | bytes accessed | tf_op | source)
XLA Modules:
  0.0 463.1 jit_solution(7263140078212579428)
XLA Ops:
  3.0 2.2 copy-done.1
  10.4 1.8 collective-permute-start.2
  15.1 2.1 collective-permute-done.3.refs_1_
  17.2 10.4 %collective-permute-done.refs_1_ = bf16[32,4224]{1,0:T(8,128)(2,1)S(1)} collective-permute-done((bf16[32,4224]{1,0:T(8,128)(2,1)S(1)}, bf16[32,4224]{1,0:T(8,128)(2,1)S(1)}, u32[]{:S(2)}, u32[]{:S(2)}) %collective-permute-start) | collective-permute-done | bytes 270368 | tf_op jit(solution)/shard_map/ppermute | solution.py:1555
  27.7 4.0 collective-permute-done.1.refs_2_
  31.7 1.8 collective-permute-done.2.refs_3_
  37.3 2.0 collective-permute-start.9
  39.8 12.3 %collective-permute-done.11.refs_2_ = bf16[64,1024]{1,0:T(8,128)(2,1)S(1)} collective-permute-done((bf16[64,1024]{1,0:T(8,128)(2,1)S(1)}, bf16[64,1024]{1,0:T(8,128)(2,1)S(1)}, u32[]{:S(2)}, u32[]{:S(2)}) %collective-permute-start.11) | collective-permute-done | bytes 131104 | tf_op jit(solution)/shard_map/ppermute | solution.py:1529
  53.7 2.2 copy-done.8
  65.3 10.4 %collective-permute-done.16.refs_2_ = bf16[32,6144]{1,0:T(8,128)(2,1)S(1)} collective-permute-done((bf16[32,6144]{1,0:T(8,128)(2,1)}, bf16[32,6144]{1,0:T(8,128)(2,1)S(1)}, u32[]{:S(2)}, u32[]{:S(2)}) %collective-permute-start.16) | collective-permute-done | bytes 393248 | tf_op jit(solution)/shard_map/ppermute | solution.py:1555
  76.4 5.7 %collective-permute-done.13.refs_5_ = bf16[4,32,2048]{2,1,0:T(8,128)(2,1)S(1)} collective-permute-done((bf16[4,32,2048]{2,1,0:T(8,128)(2,1)}, bf16[4,32,2048]{2,1,0:T(8,128)(2,1)S(1)}, u32[]{:S(2)}, u32[]{:S(2)}) %collective-permute-start.13) | collective-permute-done | bytes 524320 | tf_op jit(solution)/shard_map/ppermute | solution.py:1529
  96.8 14.1 %norm_project.1 = (bf16[1024,1024]{1,0:T(8,128)(2,1)}, bf16[1024,3072]{1,0:T(8,128)(2,1)}) custom-call(s32[4]{0:T(128)} %copy-done.41, f32[2,512,1024]{2,1,0:T(8,128)} %base_ref.1, bf16[512,1024]{1,0:T(8,128)(2,1)} %collective-permute-done.5.far_ref.far_in, f32[1,1024]{1,0:T(1,128)} %copy-done.62, f32[1,1024]{1,0:T(1,128)} %copy-done.63, ...), custom_call_target="tpu_custom_call" | custom-call | flops 540000000 | bytes 1 | tf_op jit(solution)/shard_map/norm_project/pallas_call | solution.py:464
  110.9 2.8 copy-done
  113.7 13.3 %attn_forward.2 = (bf16[16,1024,1024]{2,1,0:T(8,128)(2,1)}, bf16[1024,1024]{1,0:T(8,128)(2,1)S(1)}, f32[1024,1024]{1,0:T(8,128)S(1)}) custom-call(s32[4]{0:T(128)S(1)} %copy-done.42, bf16[1024,3072]{1,0:T(8,128)(2,1)S(1)} %copy-done, bf16[1024,3072]{1,0:T(8,128)(2,1)S(1)} %copy-done, bf16[1024,3072]{1,0:T(8,128)(2,1)S(1)} %copy-done, f32[16,16,128]{2,1,0:T(8,128)S(1)} %bitcast.76), custom_call_target="tpu_custom_call" | custom-call | flops 450000000 | bytes 1 | tf_op jit(solution)/shard_map/attn_forward/pallas_call | solution.py:464
  129.4 20.6 %attn_forward.3 = (bf16[16,1024,1024]{2,1,0:T(8,128)(2,1)}, bf16[1024,1024]{1,0:T(8,128)(2,1)S(1)}, f32[1024,1024]{1,0:T(8,128)S(1)}) custom-call(s32[4]{0:T(128)S(1)} %copy-done.42, bf16[1024,3072]{1,0:T(8,128)(2,1)S(1)} %copy-done, bf16[1024,3072]{1,0:T(8,128)(2,1)S(1)} %copy-done, ...), custom_call_target="tpu_custom_call", output_to_operand_aliasing={{0}: (5, {}), {1}: (6, {}), {2}: (7, {})} | custom-call | flops 750000000 | bytes 1 | tf_op jit(solution)/shard_map/attn_forward/pallas_call | solution.py:464
  150.1 2.1 copy-done.6
  156.5 10.8 %out_norm.1 = (f32[1024,1024]{1,0:T(8,128)}, bf16[1024,1024]{1,0:T(8,128)(2,1)}, f32[1024,1024]{1,0:T(8,128)}) custom-call(s32[4]{0:T(128)} %copy-done.41, bf16[1024,1024]{1,0:T(8,128)(2,1)} %copy-done.3, f32[1,1024]{1,0:T(1,128)} %copy-done.65, f32[2,512,1024]{2,1,0:T(8,128)} %base_ref.1, bf16[512,1024]{1,0:T(8,128)(2,1)} %collective-permute-done.5.far_ref.far_in, ...), custom_call_target="tpu_custom_call" | custom-call | flops 360000000 | bytes 1 | tf_op jit(solution)/shard_map/out_norm/pallas_call | solution.py:464
  167.9 3.3 collective-permute-done.39.refs_13_
  173.0 38.5 %feed_forward.3 = (bf16[4,256,1024]{2,1,0:T(8,128)(2,1)}, bf16[4,256,1024]{2,1,0:T(8,128)(2,1)}, bf16[8,64,2048]{2,1,0:T(8,128)(2,1)}, bf16[8,64,2048]{2,1,0:T(8...) custom-call(s32[4]{0:T(128)} %copy-done.41, f32[1,4096]{1,0:T(1,128)} %copy-done.61, ...), custom_call_target="tpu_custom_call" | custom-call | flops 10800000000 | bytes 1 | tf_op jit(solution)/shard_map/feed_forward/pallas_call | solution.py:464
  212.1 22.1 %feed_forward.4 = (bf16[2,256,1024]{2,1,0:T(8,128)(2,1)}, bf16[2,256,1024]{2,1,0:T(8,128)(2,1)}, bf16[8,64,2048]{2,1,0:T(8,128)(2,1)}, bf16[8,64,2048]{2,1,0:T(8...) custom-call(s32[4]{0:T(128)} %copy-done.41, f32[1,4096]{1,0:T(1,128)} %copy-done.61, ...), custom_call_target="tpu_custom_call" | custom-call | flops 5400000000 | bytes 1 | tf_op jit(solution)/shard_map/feed_forward/pallas_call | solution.py:464
  234.5 3.4 split_add.14
  237.9 1.8 split_add.13
  242.0 23.6 %feed_forward.5 = (bf16[2,256,1024]{2,1,0:T(8,128)(2,1)}, bf16[2,256,1024]{2,1,0:T(8,128)(2,1)}, bf16[8,64,2048]{2,1,0:T(8,128)(2,1)}, bf16[8,64,2048]{2,1,0:T(8...) custom-call(s32[4]{0:T(128)} %copy-done.41, ...), custom_call_target="tpu_custom_call", output_to_operand_aliasing={{2}: (23, {}), {3}: (24, {})} | custom-call | flops 5400000000 | bytes 1 | tf_op jit(solution)/shard_map/feed_forward/pallas_call | solution.py:464
  267.2 2.7 split_add.15
  270.7 11.7 %middle_back.1 = (f32[1024,1024]{1,0:T(8,128)}, bf16[1024,1024]{1,0:T(8,128)(2,1)}, bf16[1024,1024]{1,0:T(8,128)(2,1)}, f32[1,1024]{1,0:T(1,128)}, f32[1,1024]{1,0:T(1,128)}, /*index=5*/f32[1,1024]{1,0:T(1,128)}) custom-call(s32[4]{0:T(128)} %copy-done.41, f32[1024,1024]{1,0:T(8,128)} %get-tuple-element.530.grad_ref, ...), custom_call_target="tpu_custom_call" | custom-call | flops 14400000000 | bytes 1 | tf_op jit(solution)/shard_map/middle_back/pallas_call | solution.py:464
  285.6 3.7 grad_wide.2
  289.3 2.8 split_add.17
  292.2 2.3 split_add.16
  297.5 3.2 split_add.18
  302.3 20.9 %attn_backward.2 = (bf16[1024,1024]{1,0:T(8,128)(2,1)S(1)}, bf16[1024,1024]{1,0:T(8,128)(2,1)S(1)}, bf16[1024,1024]{1,0:T(8,128)(2,1)S(1)}) custom-call(s32[4]{0:T(128)S(1)} %copy-done.45, bf16[1024,3072]{1,0:T(8,128)(2,1)S(1)} %bitcast.66, bf16[1024,3072]{1,0:T(8,128)(2,1)S(1)} %bitcast.66, bf16[1024,3072]{1,0:T(8,128)(2,1)S(1)} %bitcast.66, ...), custom_call_target="tpu_custom_call" | custom-call | flops 6000000000 | bytes 1 | tf_op jit(solution)/shard_map/attn_backward/pallas_call | solution.py:464
  324.2 2.1 merge_add.1
  330.4 3.0 collective-permute-start.55
  333.8 20.7 %attn_backward.3 = (bf16[1024,1024]{1,0:T(8,128)(2,1)S(1)}, bf16[1024,1024]{1,0:T(8,128)(2,1)S(1)}, bf16[1024,1024]{1,0:T(8,128)(2,1)S(1)}) custom-call(s32[4]{0:T(128)S(1)} %copy-done.45, bf16[1024,3072]{1,0:T(8,128)(2,1)S(1)} %bitcast.66, bf16[1024,3072]{1,0:T(8,128)(2,1)S(1)} %bitcast.66, ...), custom_call_target="tpu_custom_call", output_to_operand_aliasing={{0}: (8, {}), {1}: (9, {}), {2}: (10, {})} | custom-call | flops 6000000000 | bytes 1 | tf_op jit(solution)/shard_map/attn_backward/pallas_call | solution.py:464
  357.7 10.3 %grad_wide.3 = (bf16[8,64,1536]{2,1,0:T(8,128)(2,1)S(1)}, bf16[8,64,1536]{2,1,0:T(8,128)(2,1)S(1)}, bf16[8,64,1536]{2,1,0:T(8,128)(2,1)S(1)}, bf16[8,64,1536]{2,1,0:T(8,128)(2,1)S(1)}) custom-call(s32[4]{0:T(128)S(1)} %copy-done.45, bf16[1024,1024]{1,0:T(8,128)(2,1)S(1)} %copy-done.68, bf16[1024,1024]{1,0:T(8,128)(2,1)S(1)} %get-tuple-element.677.refs_0_.query_ref, ...), custom_call_target="tpu_custom_call" | custom-call | flops 3240000000 | bytes 1 | tf_op jit(solution)/shard_map/grad_wide/pallas_call | solution.py:464
  371.5 6.9 %collective-permute-done.60.refs_5_ = bf16[4,32,1024]{2,1,0:T(8,128)(2,1)S(1)} collective-permute-done((bf16[4,32,1024]{2,1,0:T(8,128)(2,1)S(1)}, bf16[4,32,1024]{2,1,0:T(8,128)(2,1)S(1)}, u32[]{:S(2)}, u32[]{:S(2)}) %collective-permute-start.60) | collective-permute-done | bytes 262176 | tf_op jit(solution)/shard_map/ppermute | solution.py:1529
  382.5 1.9 split_depth.4
  386.1 2.1 collective-permute-start.66
  388.2 18.8 %input_back.1 = (f32[2,512,1024]{2,1,0:T(8,128)}, bf16[512,1024]{1,0:T(8,128)(2,1)}, f32[1,1024]{1,0:T(1,128)}, f32[1,1024]{1,0:T(1,128)}, f32[1,1024]{1,0:T(1,128)}, /*index=5*/f32[1,1024]{1,0:T(1,128)}) custom-call(s32[4]{0:T(128)} %copy-done.41, bf16[1024,1024]{1,0:T(8,128)(2,1)} %copy-done.21, bf16[1024,1024]{1,0:T(8,128)(2,1)} %copy-done.22, ...), custom_call_target="tpu_custom_call" | custom-call | flops 300000000 | bytes 1 | tf_op jit(solution)/shard_map/input_back/pallas_call | solution.py:464
  411.3 5.8 %collective-permute-done.65.refs_0_ = bf16[32,7168]{1,0:T(8,128)(2,1)S(1)} collective-permute-done((bf16[32,7168]{1,0:T(8,128)(2,1)}, bf16[32,7168]{1,0:T(8,128)(2,1)S(1)}, u32[]{:S(2)}, u32[]{:S(2)}) %collective-permute-start.65) | collective-permute-done | bytes 458784 | tf_op jit(solution)/shard_map/ppermute | solution.py:1555
  418.7 5.8 %collective-permute-done.66.refs_1_ = bf16[32,7168]{1,0:T(8,128)(2,1)S(1)} collective-permute-done((bf16[32,7168]{1,0:T(8,128)(2,1)}, bf16[32,7168]{1,0:T(8,128)(2,1)S(1)}, u32[]{:S(2)}, u32[]{:S(2)}) %collective-permute-start.66) | collective-permute-done | bytes 458784 | tf_op jit(solution)/shard_map/ppermute | solution.py:1555
  429.4 2.9 collective-permute-done.72
  435.8 3.1 collective-permute-start.75
  438.9 2.0 collective-permute-start.76
  445.4 2.2 copy-done.2
  447.6 2.0 fill_far.2
  449.6 6.2 %collective-permute-done.73.delta_ref = bf16[512,1024]{1,0:T(8,128)(2,1)S(1)} collective-permute-done((bf16[512,1024]{1,0:T(8,128)(2,1)}, bf16[512,1024]{1,0:T(8,128)(2,1)S(1)}, u32[]{:S(2)}, u32[]{:S(2)}) %collective-permute-start.73) | collective-permute-done | bytes 1048608 | tf_op jit(solution)/shard_map/ppermute | solution.py:1529
  455.8 2.0 fill_far.3
  458.6 2.3 last_add.5
  (416 shorter events, 101.9 us)
Async XLA Ops:
  6.1 27.5 %collective-permute-start.5 = (bf16[512,1024]{1,0:T(8,128)(2,1)S(1)}, bf16[512,1024]{1,0:T(8,128)(2,1)}, u32[]{:S(2)}, u32[]{:S(2)}) collective-permute-start(bf16[512,1024]{1,0:T(8,128)(2,1)S(1)} %cast_far.2), channel_id=1, source_target_pairs={{0,1},{1,0},{2,3},{3,2},{4,5},{5,4},{6,7},{7,6},{8,9},{9,8},{10,11... | collective-permute-start | bytes 3145736 | tf_op jit(solution)/shard_map/ppermute | solution.py:1529
  7.5 20.2 %collective-permute-start = (bf16[32,4224]{1,0:T(8,128)(2,1)S(1)}, bf16[32,4224]{1,0:T(8,128)(2,1)S(1)}, u32[]{:S(2)}, u32[]{:S(2)}) collective-permute-start(bf16[32,4224]{1,0:T(8,128)(2,1)S(1)} %join_beside.2.refs_0_), channel_id=1, source_target_pairs={{0,8},{2,10},{4,12},{6,14},{8,16},{10,18},{12,20},{14,22},{16,24},... | collective-permute-start | bytes 811016 | tf_op jit(solution)/shard_map/ppermute | solution.py:1555
  9.2 22.6 %collective-permute-start.1 = (bf16[32,4224]{1,0:T(8,128)(2,1)S(1)}, bf16[32,4224]{1,0:T(8,128)(2,1)S(1)}, u32[]{:S(2)}, u32[]{:S(2)}) collective-permute-start(bf16[32,4224]{1,0:T(8,128)(2,1)S(1)} %join_beside.2.refs_0_), channel_id=1, source_target_pairs={{0,16},{2,18},{4,20},{6,22},{8,24},{10,26},{12,28},{14,30},{16,0},... | collective-permute-start | bytes 811016 | tf_op jit(solution)/shard_map/ppermute | solution.py:1555
  10.4 23.1 %collective-permute-start.2 = (bf16[32,4224]{1,0:T(8,128)(2,1)S(1)}, bf16[32,4224]{1,0:T(8,128)(2,1)S(1)}, u32[]{:S(2)}, u32[]{:S(2)}) collective-permute-start(bf16[32,4224]{1,0:T(8,128)(2,1)S(1)} %join_beside.2.refs_0_), channel_id=1, source_target_pairs={{0,24},{2,26},{4,28},{6,30},{8,0},{10,2},{12,4},{14,6},{16,8},{18,... | collective-permute-start | bytes 811016 | tf_op jit(solution)/shard_map/ppermute | solution.py:1555
  34.2 27.5 %collective-permute-start.8 = (bf16[4,32,2176]{2,1,0:T(8,128)(2,1)S(1)}, bf16[4,32,2176]{2,1,0:T(8,128)(2,1)S(1)}, u32[]{:S(2)}, u32[]{:S(2)}) collective-permute-start(bf16[4,32,2176]{2,1,0:T(8,128)(2,1)S(1)} %get-tuple-element.424.refs_0_.refs_8_), channel_id=1, source_target_pairs={{0,4},{2,6},{4,0},{6,2},{8,12},{10,14},{12,8},{14,10},{16,20},{18,... | collective-permute-start | bytes 1671176 | tf_op jit(solution)/shard_map/ppermute | solution.py:1529
  35.7 25.9 %collective-permute-start.7 = (bf16[4,32,2048]{2,1,0:T(8,128)(2,1)S(1)}, bf16[4,32,2048]{2,1,0:T(8,128)(2,1)}, u32[]{:S(2)}, u32[]{:S(2)}) collective-permute-start(bf16[4,32,2048]{2,1,0:T(8,128)(2,1)S(1)} %get-tuple-element.438.refs_0_), channel_id=1, source_target_pairs={{0,1},{1,0},{2,3},{3,2},{4,5},{5,4},{6,7},{7,6},{8,9},{9,8},{10,11... | collective-permute-start | bytes 1572872 | tf_op jit(solution)/shard_map/ppermute | solution.py:1529
  37.3 21.3 %collective-permute-start.10 = (bf16[32,6144]{1,0:T(8,128)(2,1)}, bf16[32,6144]{1,0:T(8,128)(2,1)S(1)}, u32[]{:S(2)}, u32[]{:S(2)}) collective-permute-start(bf16[32,6144]{1,0:T(8,128)(2,1)} %join_beside.3.refs_0_), channel_id=1, source_target_pairs={{0,24},{2,26},{4,28},{6,30},{8,0},{10,2},{12,4},{14,6},{16,8},{18,... | collective-permute-start | bytes 1179656 | tf_op jit(solution)/shard_map/ppermute | solution.py:1555
  37.3 22.6 %collective-permute-start.9 = (bf16[32,6144]{1,0:T(8,128)(2,1)}, bf16[32,6144]{1,0:T(8,128)(2,1)S(1)}, u32[]{:S(2)}, u32[]{:S(2)}) collective-permute-start(bf16[32,6144]{1,0:T(8,128)(2,1)} %join_beside.3.refs_0_), channel_id=1, source_target_pairs={{0,8},{2,10},{4,12},{6,14},{8,16},{10,18},{12,20},{14,22},{16,24},... | collective-permute-start | bytes 1179656 | tf_op jit(solution)/shard_map/ppermute | solution.py:1555
  57.6 18.9 %collective-permute-start.14 = (bf16[4,32,2176]{2,1,0:T(8,128)(2,1)S(1)}, bf16[4,32,2176]{2,1,0:T(8,128)(2,1)S(1)}, u32[]{:S(2)}, u32[]{:S(2)}) collective-permute-start(bf16[4,32,2176]{2,1,0:T(8,128)(2,1)S(1)} %get-tuple-element.424.refs_0_.refs_8_), channel_id=1, source_target_pairs={{0,1},{1,0},{2,3},{3,2},{4,5},{5,4},{6,7},{7,6},{8,9},{9,8},{10,11... | collective-permute-start | bytes 1671176 | tf_op jit(solution)/shard_map/ppermute | solution.py:1529
  62.2 20.4 %collective-permute-start.15 = (bf16[4,32,2176]{2,1,0:T(8,128)(2,1)S(1)}, bf16[4,32,2176]{2,1,0:T(8,128)(2,1)S(1)}, u32[]{:S(2)}, u32[]{:S(2)}) collective-permute-start(bf16[4,32,2176]{2,1,0:T(8,128)(2,1)S(1)} %collective-permute-done.8.refs_4_.refs_12_), channel_id=1, source_target_pairs={{0,1},{1,0},{2,3},{3,2},{4,5},{5,4},{6,7},{7,6},{8,9},{9,8},{10,11... | collective-permute-start | bytes 1671176 | tf_op jit(solution)/shard_map/ppermute | solution.py:1529
  62.2 19.9 %collective-permute-start.13 = (bf16[4,32,2048]{2,1,0:T(8,128)(2,1)}, bf16[4,32,2048]{2,1,0:T(8,128)(2,1)S(1)}, u32[]{:S(2)}, u32[]{:S(2)}) collective-permute-start(bf16[4,32,2048]{2,1,0:T(8,128)(2,1)} %collective-permute-done.7.refs_1_), channel_id=1, source_target_pairs={{0,4},{2,6},{4,0},{6,2},{8,12},{10,14},{12,8},{14,10},{16,20},{18,... | collective-permute-start | bytes 1572872 | tf_op jit(solution)/shard_map/ppermute | solution.py:1529
  87.5 39.6 %collective-permute-start.25 = (bf16[4,32,6144]{2,1,0:T(8,128)(2,1)S(1)}, bf16[4,32,6144]{2,1,0:T(8,128)(2,1)}, u32[]{:S(2)}, u32[]{:S(2)}) collective-permute-start(bf16[4,32,6144]{2,1,0:T(8,128)(2,1)S(1)} %join_up.1.refs_0_), channel_id=1, source_target_pairs={{0,1},{1,0},{2,3},{3,2},{4,5},{5,4},{6,7},{7,6},{8,9},{9,8},{10,11... | collective-permute-start | bytes 4718600 | tf_op jit(solution)/shard_map/ppermute | solution.py:1529
  89.2 37.9 %collective-permute-start.26 = (bf16[4,32,6144]{2,1,0:T(8,128)(2,1)S(1)}, bf16[4,32,6144]{2,1,0:T(8,128)(2,1)}, u32[]{:S(2)}, u32[]{:S(2)}) collective-permute-start(bf16[4,32,6144]{2,1,0:T(8,128)(2,1)S(1)} %join_up.1.refs_0_), channel_id=1, source_target_pairs={{0,4},{2,6},{4,0},{6,2},{8,12},{10,14},{12,8},{14,10},{16,20},{18,... | collective-permute-start | bytes 4718600 | tf_op jit(solution)/shard_map/ppermute | solution.py:1529
  92.6 34.4 %collective-permute-start.27 = (bf16[2,2,64,1024]{3,2,1,0:T(8,128)(2,1)}, bf16[2,2,64,1024]{3,2,1,0:T(8,128)(2,1)S(1)}, u32[]{:S(2)}, u32[]{:S(2)}) collective-permute-start(bf16[2,2,64,1024]{3,2,1,0:T(8,128)(2,1)} %join_plane.1.refs_8_), channel_id=1, source_target_pairs={{0,8},{2,10},{4,12},{6,14},{8,16},{10,18},{12,20},{14,22},{16,24},... | collective-permute-start | bytes 1572872 | tf_op jit(solution)/shard_map/ppermute | solution.py:1555
  93.4 33.6 %collective-permute-start.28 = (bf16[2,2,64,1024]{3,2,1,0:T(8,128)(2,1)}, bf16[2,2,64,1024]{3,2,1,0:T(8,128)(2,1)}, u32[]{:S(2)}, u32[]{:S(2)}) collective-permute-start(bf16[2,2,64,1024]{3,2,1,0:T(8,128)(2,1)} %join_plane.1.refs_8_), channel_id=1, source_target_pairs={{0,24},{2,26},{4,28},{6,30},{8,0},{10,2},{12,4},{14,6},{16,8},{18,... | collective-permute-start | bytes 1572872 | tf_op jit(solution)/shard_map/ppermute | solution.py:1555
  94.7 57.5 %collective-permute-start.30 = (bf16[4,32,6144]{2,1,0:T(8,128)(2,1)S(1)}, bf16[4,32,6144]{2,1,0:T(8,128)(2,1)}, u32[]{:S(2)}, u32[]{:S(2)}) collective-permute-start(bf16[4,32,6144]{2,1,0:T(8,128)(2,1)S(1)} %join_up.1.refs_0_), channel_id=1, source_target_pairs={{0,2},{2,0},{4,6},{6,4},{8,10},{10,8},{12,14},{14,12},{16,18},{18,... | collective-permute-start | bytes 4718600 | tf_op jit(solution)/shard_map/ppermute | solution.py:1529
  127.0 25.7 %collective-permute-start.31 = (bf16[4,32,6144]{2,1,0:T(8,128)(2,1)}, bf16[4,32,6144]{2,1,0:T(8,128)(2,1)S(1)}, u32[]{:S(2)}, u32[]{:S(2)}) collective-permute-start(bf16[4,32,6144]{2,1,0:T(8,128)(2,1)} %collective-permute-done.25.refs_1_), channel_id=1, source_target_pairs={{0,2},{2,0},{4,6},{6,4},{8,10},{10,8},{12,14},{14,12},{16,18},{18,... | collective-permute-start | bytes 4718600 | tf_op jit(solution)/shard_map/ppermute | solution.py:1529
  127.6 25.1 %collective-permute-start.29 = (bf16[512,1024]{1,0:T(8,128)(2,1)S(1)}, bf16[512,1024]{1,0:T(8,128)(2,1)S(1)}, u32[]{:S(2)}, u32[]{:S(2)}) collective-permute-start(bf16[512,1024]{1,0:T(8,128)(2,1)S(1)} %copy-done.38), channel_id=1, source_target_pairs={{0,1},{1,0},{2,3},{3,2},{4,5},{5,4},{6,7},{7,6},{8,9},{9,8},{10,11... | collective-permute-start | bytes 3145736 | tf_op jit(solution)/shard_map/ppermute | solution.py:1529
  128.8 23.3 %collective-permute-start.32 = (bf16[2,2,64,1024]{3,2,1,0:T(8,128)(2,1)}, bf16[2,2,64,1024]{3,2,1,0:T(8,128)(2,1)S(1)}, u32[]{:S(2)}, u32[]{:S(2)}) collective-permute-start(bf16[2,2,64,1024]{3,2,1,0:T(8,128)(2,1)} %join_plane.1.refs_8_), channel_id=1, source_target_pairs={{0,16},{2,18},{4,20},{6,22},{8,24},{10,26},{12,28},{14,30},{16,0},... | collective-permute-start | bytes 1572872 | tf_op jit(solution)/shard_map/ppermute | solution.py:1555
  128.8 38.4 %collective-permute-start.33 = (bf16[4,32,6144]{2,1,0:T(8,128)(2,1)}, bf16[4,32,6144]{2,1,0:T(8,128)(2,1)}, u32[]{:S(2)}, u32[]{:S(2)}) collective-permute-start(bf16[4,32,6144]{2,1,0:T(8,128)(2,1)} %collective-permute-done.25.refs_1_), channel_id=1, source_target_pairs={{0,4},{2,6},{4,0},{6,2},{8,12},{10,14},{12,8},{14,10},{16,20},{18,... | collective-permute-start | bytes 4718600 | tf_op jit(solution)/shard_map/ppermute | solution.py:1529
  211.5 22.9 %collective-permute-start.40 = (bf16[4,256,1024]{2,1,0:T(8,128)(2,1)}, bf16[4,256,1024]{2,1,0:T(8,128)(2,1)S(1)}, u32[]{:S(2)}, u32[]{:S(2)}) collective-permute-start(bf16[4,256,1024]{2,1,0:T(8,128)(2,1)} %get-tuple-element.498), channel_id=1, source_target_pairs={{0,2},{2,0},{4,6},{6,4},{8,10},{10,8},{12,14},{14,12},{16,18},{18,... | collective-permute-start | bytes 6291464 | tf_op jit(solution)/shard_map/ppermute | solution.py:1529
  211.7 22.7 %collective-permute-start.41 = (bf16[8,64,2048]{2,1,0:T(8,128)(2,1)}, bf16[8,64,2048]{2,1,0:T(8,128)(2,1)S(1)}, u32[]{:S(2)}, u32[]{:S(2)}) collective-permute-start(bf16[8,64,2048]{2,1,0:T(8,128)(2,1)} %get-tuple-element.504), channel_id=1, source_target_pairs={{0,2},{2,0},{4,6},{6,4},{8,10},{10,8},{12,14},{14,12},{16,18},{18,... | collective-permute-start | bytes 6291464 | tf_op jit(solution)/shard_map/ppermute | solution.py:1529
  234.2 33.0 %collective-permute-start.43 = (bf16[2,256,1024]{2,1,0:T(8,128)(2,1)}, bf16[2,256,1024]{2,1,0:T(8,128)(2,1)}, u32[]{:S(2)}, u32[]{:S(2)}) collective-permute-start(bf16[2,256,1024]{2,1,0:T(8,128)(2,1)} %get-tuple-element.519), channel_id=1, source_target_pairs={{0,2},{2,0},{4,6},{6,4},{8,10},{10,8},{12,14},{14,12},{16,18},{18,... | collective-permute-start | bytes 3145736 | tf_op jit(solution)/shard_map/ppermute | solution.py:1529
  239.6 26.6 %collective-permute-start.42 = (bf16[2,256,1024]{2,1,0:T(8,128)(2,1)}, bf16[2,256,1024]{2,1,0:T(8,128)(2,1)S(1)}, u32[]{:S(2)}, u32[]{:S(2)}) collective-permute-start(bf16[2,256,1024]{2,1,0:T(8,128)(2,1)} %get-tuple-element.515), channel_id=1, source_target_pairs={{0,4},{2,6},{4,0},{6,2},{8,12},{10,14},{12,8},{14,10},{16,20},{18,... | collective-permute-start | bytes 3145736 | tf_op jit(solution)/shard_map/ppermute | solution.py:1529
  241.1 26.1 %collective-permute-start.44 = (bf16[8,32,2048]{2,1,0:T(8,128)(2,1)}, bf16[8,32,2048]{2,1,0:T(8,128)(2,1)}, u32[]{:S(2)}, u32[]{:S(2)}) collective-permute-start(bf16[8,32,2048]{2,1,0:T(8,128)(2,1)} %get-tuple-element.521), channel_id=1, source_target_pairs={{0,1},{1,0},{2,3},{3,2},{4,5},{5,4},{6,7},{7,6},{8,9},{9,8},{10,11... | collective-permute-start | bytes 3145736 | tf_op jit(solution)/shard_map/ppermute | solution.py:1529
  265.6 28.8 %collective-permute-start.47 = (bf16[8,64,2048]{2,1,0:T(8,128)(2,1)}, bf16[8,64,2048]{2,1,0:T(8,128)(2,1)}, u32[]{:S(2)}, u32[]{:S(2)}) collective-permute-start(bf16[8,64,2048]{2,1,0:T(8,128)(2,1)} %get-tuple-element.547), channel_id=1, source_target_pairs={{0,2},{2,0},{4,6},{6,4},{8,10},{10,8},{12,14},{14,12},{16,18},{18,... | collective-permute-start | bytes 6291464 | tf_op jit(solution)/shard_map/ppermute | solution.py:1529
  265.7 26.4 %collective-permute-start.46 = (bf16[2,256,1024]{2,1,0:T(8,128)(2,1)}, bf16[2,256,1024]{2,1,0:T(8,128)(2,1)}, u32[]{:S(2)}, u32[]{:S(2)}) collective-permute-start(bf16[2,256,1024]{2,1,0:T(8,128)(2,1)} %get-tuple-element.538), channel_id=1, source_target_pairs={{0,2},{2,0},{4,6},{6,4},{8,10},{10,8},{12,14},{14,12},{16,18},{18,... | collective-permute-start | bytes 3145736 | tf_op jit(solution)/shard_map/ppermute | solution.py:1529
  269.9 22.2 %collective-permute-start.45 = (bf16[1,256,1024]{2,1,0:T(8,128)(2,1)}, bf16[1,256,1024]{2,1,0:T(8,128)(2,1)}, u32[]{:S(2)}, u32[]{:S(2)}) collective-permute-start(bf16[1,256,1024]{2,1,0:T(8,128)(2,1)} %get-tuple-element.529), channel_id=1, source_target_pairs={{0,4},{2,6},{4,0},{6,2},{8,12},{10,14},{12,8},{14,10},{16,20},{18,... | collective-permute-start | bytes 1572872 | tf_op jit(solution)/shard_map/ppermute | solution.py:1529
  294.4 28.7 %collective-permute-start.50 = (bf16[512,1024]{1,0:T(8,128)(2,1)}, bf16[512,1024]{1,0:T(8,128)(2,1)S(1)}, u32[]{:S(2)}, u32[]{:S(2)}) collective-permute-start(bf16[512,1024]{1,0:T(8,128)(2,1)} %get-tuple-element.561), channel_id=1, source_target_pairs={{0,1},{1,0},{2,3},{3,2},{4,5},{5,4},{6,7},{7,6},{8,9},{9,8},{10,11... | collective-permute-start | bytes 3145736 | tf_op jit(solution)/shard_map/ppermute | solution.py:1529
  295.5 31.7 %collective-permute-start.51 = (bf16[8,64,1024]{2,1,0:T(8,128)(2,1)S(1)}, bf16[8,64,1024]{2,1,0:T(8,128)(2,1)S(1)}, u32[]{:S(2)}, u32[]{:S(2)}) collective-permute-start(bf16[8,64,1024]{2,1,0:T(8,128)(2,1)S(1)} %get-tuple-element.580), channel_id=1, source_target_pairs={{0,2},{2,0},{4,6},{6,4},{8,10},{10,8},{12,14},{14,12},{16,18},{18,... | collective-permute-start | bytes 3145736 | tf_op jit(solution)/shard_map/ppermute | solution.py:1529
  295.5 28.7 %collective-permute-start.49 = (bf16[4,32,2048]{2,1,0:T(8,128)(2,1)S(1)}, bf16[4,32,2048]{2,1,0:T(8,128)(2,1)S(1)}, u32[]{:S(2)}, u32[]{:S(2)}) collective-permute-start(bf16[4,32,2048]{2,1,0:T(8,128)(2,1)S(1)} %get-tuple-element.554), channel_id=1, source_target_pairs={{0,4},{2,6},{4,0},{6,2},{8,12},{10,14},{12,8},{14,10},{16,20},{18,... | collective-permute-start | bytes 1572872 | tf_op jit(solution)/shard_map/ppermute | solution.py:1529
  297.0 27.3 %collective-permute-start.48 = (bf16[1,256,1024]{2,1,0:T(8,128)(2,1)S(1)}, bf16[1,256,1024]{2,1,0:T(8,128)(2,1)S(1)}, u32[]{:S(2)}, u32[]{:S(2)}) collective-permute-start(bf16[1,256,1024]{2,1,0:T(8,128)(2,1)S(1)} %get-tuple-element.552), channel_id=1, source_target_pairs={{0,4},{2,6},{4,0},{6,2},{8,12},{10,14},{12,8},{14,10},{16,20},{18,... | collective-permute-start | bytes 1572872 | tf_op jit(solution)/shard_map/ppermute | solution.py:1529
  300.7 53.8 %collective-permute-start.53 = (bf16[4,64,2048]{2,1,0:T(8,128)(2,1)S(1)}, bf16[4,64,2048]{2,1,0:T(8,128)(2,1)S(1)}, u32[]{:S(2)}, u32[]{:S(2)}) collective-permute-start(bf16[4,64,2048]{2,1,0:T(8,128)(2,1)S(1)} %get-tuple-element.593), channel_id=1, source_target_pairs={{0,4},{2,6},{4,0},{6,2},{8,12},{10,14},{12,8},{14,10},{16,20},{18,... | collective-permute-start | bytes 3145736 | tf_op jit(solution)/shard_map/ppermute | solution.py:1529
  326.3 31.2 %collective-permute-start.57 = (bf16[4,128,1024]{2,1,0:T(8,128)(2,1)S(1)}, bf16[4,128,1024]{2,1,0:T(8,128)(2,1)S(1)}, u32[]{:S(2)}, u32[]{:S(2)}) collective-permute-start(bf16[4,128,1024]{2,1,0:T(8,128)(2,1)S(1)} %get-tuple-element.611), channel_id=1, source_target_pairs={{0,1},{1,0},{2,3},{3,2},{4,5},{5,4},{6,7},{7,6},{8,9},{9,8},{10,11... | collective-permute-start | bytes 3145736 | tf_op jit(solution)/shard_map/ppermute | solution.py:1529
  328.8 25.7 %collective-permute-start.54 = (bf16[32,2048]{1,0:T(8,128)(2,1)S(1)}, bf16[32,2048]{1,0:T(8,128)(2,1)S(1)}, u32[]{:S(2)}, u32[]{:S(2)}) collective-permute-start(bf16[32,2048]{1,0:T(8,128)(2,1)S(1)} %get-tuple-element.595), channel_id=1, source_target_pairs={{0,8},{2,10},{4,12},{6,14},{8,16},{10,18},{12,20},{14,22},{16,24},... | collective-permute-start | bytes 393224 | tf_op jit(solution)/shard_map/ppermute | solution.py:1555
  330.4 24.1 %collective-permute-start.55 = (bf16[32,2048]{1,0:T(8,128)(2,1)S(1)}, bf16[32,2048]{1,0:T(8,128)(2,1)S(1)}, u32[]{:S(2)}, u32[]{:S(2)}) collective-permute-start(bf16[32,2048]{1,0:T(8,128)(2,1)S(1)} %get-tuple-element.596), channel_id=1, source_target_pairs={{0,16},{2,18},{4,20},{6,22},{8,24},{10,26},{12,28},{14,30},{16,0},... | collective-permute-start | bytes 393224 | tf_op jit(solution)/shard_map/ppermute | solution.py:1555
  333.5 21.1 %collective-permute-start.56 = (bf16[32,2048]{1,0:T(8,128)(2,1)S(1)}, bf16[32,2048]{1,0:T(8,128)(2,1)S(1)}, u32[]{:S(2)}, u32[]{:S(2)}) collective-permute-start(bf16[32,2048]{1,0:T(8,128)(2,1)S(1)} %get-tuple-element.597), channel_id=1, source_target_pairs={{0,24},{2,26},{4,28},{6,30},{8,0},{10,2},{12,4},{14,6},{16,8},{18,... | collective-permute-start | bytes 393224 | tf_op jit(solution)/shard_map/ppermute | solution.py:1555
  379.4 27.8 %collective-permute-start.62 = (bf16[4,64,1536]{2,1,0:T(8,128)(2,1)S(1)}, bf16[4,64,1536]{2,1,0:T(8,128)(2,1)S(1)}, u32[]{:S(2)}, u32[]{:S(2)}) collective-permute-start(bf16[4,64,1536]{2,1,0:T(8,128)(2,1)S(1)} %get-tuple-element.676), channel_id=1, source_target_pairs={{0,4},{2,6},{4,0},{6,2},{8,12},{10,14},{12,8},{14,10},{16,20},{18,... | collective-permute-start | bytes 2359304 | tf_op jit(solution)/shard_map/ppermute | solution.py:1529
  381.7 25.5 %collective-permute-start.63 = (bf16[8,32,1536]{2,1,0:T(8,128)(2,1)S(1)}, bf16[8,32,1536]{2,1,0:T(8,128)(2,1)S(1)}, u32[]{:S(2)}, u32[]{:S(2)}) collective-permute-start(bf16[8,32,1536]{2,1,0:T(8,128)(2,1)S(1)} %get-tuple-element.686), channel_id=1, source_target_pairs={{0,1},{1,0},{2,3},{3,2},{4,5},{5,4},{6,7},{7,6},{8,9},{9,8},{10,11... | collective-permute-start | bytes 2359304 | tf_op jit(solution)/shard_map/ppermute | solution.py:1529
  384.4 32.7 %collective-permute-start.65 = (bf16[32,7168]{1,0:T(8,128)(2,1)}, bf16[32,7168]{1,0:T(8,128)(2,1)S(1)}, u32[]{:S(2)}, u32[]{:S(2)}) collective-permute-start(bf16[32,7168]{1,0:T(8,128)(2,1)} %get-tuple-element.696), channel_id=1, source_target_pairs={{0,8},{2,10},{4,12},{6,14},{8,16},{10,18},{12,20},{14,22},{16,24},... | collective-permute-start | bytes 1376264 | tf_op jit(solution)/shard_map/ppermute | solution.py:1555
  386.1 38.4 %collective-permute-start.66 = (bf16[32,7168]{1,0:T(8,128)(2,1)}, bf16[32,7168]{1,0:T(8,128)(2,1)S(1)}, u32[]{:S(2)}, u32[]{:S(2)}) collective-permute-start(bf16[32,7168]{1,0:T(8,128)(2,1)} %get-tuple-element.697), channel_id=1, source_target_pairs={{0,16},{2,18},{4,20},{6,22},{8,24},{10,26},{12,28},{14,30},{16,0},... | collective-permute-start | bytes 1376264 | tf_op jit(solution)/shard_map/ppermute | solution.py:1555
  388.2 38.3 %collective-permute-start.67 = (bf16[32,7168]{1,0:T(8,128)(2,1)S(1)}, bf16[32,7168]{1,0:T(8,128)(2,1)S(1)}, u32[]{:S(2)}, u32[]{:S(2)}) collective-permute-start(bf16[32,7168]{1,0:T(8,128)(2,1)S(1)} %get-tuple-element.698), channel_id=1, source_target_pairs={{0,24},{2,26},{4,28},{6,30},{8,0},{10,2},{12,4},{14,6},{16,8},{18,... | collective-permute-start | bytes 1376264 | tf_op jit(solution)/shard_map/ppermute | solution.py:1555
  409.1 23.2 %collective-permute-start.64 = (bf16[4,32,1536]{2,1,0:T(8,128)(2,1)S(1)}, bf16[4,32,1536]{2,1,0:T(8,128)(2,1)S(1)}, u32[]{:S(2)}, u32[]{:S(2)}) collective-permute-start(bf16[4,32,1536]{2,1,0:T(8,128)(2,1)S(1)} %get-tuple-element.694), channel_id=1, source_target_pairs={{0,1},{1,0},{2,3},{3,2},{4,5},{5,4},{6,7},{7,6},{8,9},{9,8},{10,11... | collective-permute-start | bytes 1179656 | tf_op jit(solution)/shard_map/ppermute | solution.py:1529
  410.4 21.9 %collective-permute-start.68 = (bf16[4,32,1536]{2,1,0:T(8,128)(2,1)S(1)}, bf16[4,32,1536]{2,1,0:T(8,128)(2,1)S(1)}, u32[]{:S(2)}, u32[]{:S(2)}) collective-permute-start(bf16[4,32,1536]{2,1,0:T(8,128)(2,1)S(1)} %get-tuple-element.704), channel_id=1, source_target_pairs={{0,4},{2,6},{4,0},{6,2},{8,12},{10,14},{12,8},{14,10},{16,20},{18,... | collective-permute-start | bytes 1179656 | tf_op jit(solution)/shard_map/ppermute | solution.py:1529
  432.4 23.4 %collective-permute-start.73 = (bf16[512,1024]{1,0:T(8,128)(2,1)}, bf16[512,1024]{1,0:T(8,128)(2,1)S(1)}, u32[]{:S(2)}, u32[]{:S(2)}) collective-permute-start(bf16[512,1024]{1,0:T(8,128)(2,1)} %get-tuple-element.725), channel_id=1, source_target_pairs={{0,1},{1,0},{2,3},{3,2},{4,5},{5,4},{6,7},{7,6},{8,9},{9,8},{10,11... | collective-permute-start | bytes 3145736 | tf_op jit(solution)/shard_map/ppermute | solution.py:1529
  435.8 22.0 %collective-permute-start.74 = (bf16[32,3200]{1,0:T(8,128)(2,1)}, bf16[32,3200]{1,0:T(8,128)(2,1)S(1)}, u32[]{:S(2)}, u32[]{:S(2)}) collective-permute-start(bf16[32,3200]{1,0:T(8,128)(2,1)} %get-tuple-element.732), channel_id=1, source_target_pairs={{0,8},{2,10},{4,12},{6,14},{8,16},{10,18},{12,20},{14,22},{16,24},... | collective-permute-start | bytes 614408 | tf_op jit(solution)/shard_map/ppermute | solution.py:1555
  435.8 22.0 %collective-permute-start.75 = (bf16[32,3200]{1,0:T(8,128)(2,1)}, bf16[32,3200]{1,0:T(8,128)(2,1)}, u32[]{:S(2)}, u32[]{:S(2)}) collective-permute-start(bf16[32,3200]{1,0:T(8,128)(2,1)} %get-tuple-element.733), channel_id=1, source_target_pairs={{0,16},{2,18},{4,20},{6,22},{8,24},{10,26},{12,28},{14,30},{16,0},... | collective-permute-start | bytes 614408 | tf_op jit(solution)/shard_map/ppermute | solution.py:1555
  438.9 18.9 %collective-permute-start.76 = (bf16[32,3200]{1,0:T(8,128)(2,1)}, bf16[32,3200]{1,0:T(8,128)(2,1)}, u32[]{:S(2)}, u32[]{:S(2)}) collective-permute-start(bf16[32,3200]{1,0:T(8,128)(2,1)} %get-tuple-element.734), channel_id=1, source_target_pairs={{0,24},{2,26},{4,28},{6,30},{8,0},{10,2},{12,4},{14,6},{16,8},{18,... | collective-permute-start | bytes 614408 | tf_op jit(solution)/shard_map/ppermute | solution.py:1555
  (140 other events, 1176.5 us)

commit v4 on v3

--- a/solution.py
+++ b/solution.py
@@ -417,19 +417,19 @@
     join_up=2,
     join_plane=2,
     small_vectors=2,
-    norm_project=0.3,
+    norm_project=4,
     attn_forward=0.5,
-    out_norm=0.3,
+    out_norm=1,
     join_low=0.3,
     feed_forward=9,
     split_add=0.1,
     merge_add=0.3,
     beside_add=0.3,
-    middle_back=12,
+    middle_back=40,
     grad_wide=1.8,
     attn_backward=5,
     split_depth=0.3,
-    input_back=0.25,
+    input_back=1,
     pack_vectors=0.3,
     fill_far=0.05,
     last_add=0.05,
@@ -647,113 +647,161 @@
     )
 
 
+class Transfers:
+    def __init__(self, sems):
+        self.sems, self.count = sems, 0
+
+    def start(self, source, target):
+        copy = pltpu.make_async_copy(source, target, self.sems.at[self.count])
+        self.count += 1
+        copy.start()
+        return copy
+
+
+def wait_all(copies):
+    for copy in copies:
+        copy.wait()
+
+
+def start_parts(moves, place_ref, part_refs, weight, start, size, into):
+    copies = []
+    for part_ref, (dx, dc, dy) in zip(part_refs, NEAR):
+        x, c, y = flip(place_ref[1], dx), flip(place_ref[2], dc), flip(place_ref[3], dy)
+        copies.append(
+            moves.start(
+                part_ref.at[:, :, pl.ds(start, size)],
+                weight.at[:, x, c, y, :, pl.ds(into, size)],
+            )
+        )
+    return copies
+
+
+def start_rows(moves, place_ref, whole_in, far_in, own, far, cuts):
+    half = own.shape[0]
+    copies = []
+    for cut in cuts:
+        if cut.start < half:
+            copies.append(moves.start(whole_in.at[place_ref[3], cut], own.at[cut]))
+        else:
+            back = pl.ds(cut.start - half, cut.size)
+            copies.append(moves.start(far_in.at[back], far.at[back]))
+    return copies
+
+
+def rows_at(own, far, cut):
+    half = own.shape[0]
+    if cut.start < half:
+        return own[cut]
+    return far[pl.ds(cut.start - half, cut.size)].astype(F32)
+
+
+def row_cuts(tokens, step):
+    return [pl.ds(start, step) for start in range(0, tokens, step)]
+
+
 def norm_project(place, inputs, far, gain, shift, left, right, bias):
     half, width = far.shape
+    tokens = 2 * half
     columns = bias.shape[1]
     step = 512
     left_steps = left[0].shape[-1] // step
     steps = columns // step
-    sub = 256
-
-    def body(place_ref, own_ref, far_ref, gain_ref, shift_ref, bias_ref, *refs):
+    cuts = row_cuts(tokens, 256)
+
+    def body(place_ref, gain_ref, shift_ref, bias_ref, inputs_in, far_in, *refs):
         left_refs, right_refs = refs[:8], refs[8:16]
-        normed_ref, out_ref, weight, sems = refs[16:]
-        at = pl.program_id(0)
-
-        def copies(chunk):
+        normed_out, out_ref, own, far_rows, normed, weight, result, sems = refs[16:]
+        moves = Transfers(sems)
+
+        def weights(chunk):
             refs, start = (left_refs, chunk) if chunk < left_steps else (right_refs, chunk - left_steps)
-            return parts_copies(place_ref, refs, weight, sems, start * step, step, chunk * step, chunk)
-
-        @pl.when(at == 0)
-        def _():
-            for chunk in range(steps):
-                for copy in copies(chunk):
-                    copy.start()
-            for start, rows in ((0, own_ref[0]), (half, far_ref[...])):
-                unit, _ = norm_parts(rows.astype(F32))
-                normed_ref[start : start + half, :] = (
-                    unit * gain_ref[...] + shift_ref[...]
-                ).astype(BF16)
-
+            return start_parts(moves, place_ref, refs, weight, start * step, step, chunk * step)
+
+        rows = start_rows(moves, place_ref, inputs_in, far_in, own, far_rows, cuts)
+        parts = [weights(chunk) for chunk in range(steps)]
+        away = []
+        wait_all(rows)
         for chunk in range(steps):
-            @pl.when(at == chunk)
-            def _():
-                for copy in copies(chunk):
-                    copy.wait()
-
-        cut = pl.ds(pl.multiple_of(at * step, step), step)
-        part = flat(weight[:, :, :, :, :, cut])
-        for start in range(0, 2 * half, sub):
-            result = contract(normed_ref[start : start + sub], part, 1, 0) + bias_ref[...]
-            out_ref[start : start + sub] = result.astype(BF16)
+            span = pl.ds(chunk * step, step)
+            wait_all(parts[chunk])
+            part = flat(weight[:, :, :, :, :, span])
+            for cut in cuts:
+                if chunk == 0:
+                    unit, _ = norm_parts(rows_at(own, far_rows, cut))
+                    low = (unit * gain_ref[...] + shift_ref[...]).astype(BF16)
+                    normed[cut] = low
+                else:
+                    low = normed[cut]
+                value = contract(low, part, 1, 0) + bias_ref[:, span]
+                result[chunk, cut] = value.astype(BF16)
+            if chunk == 0:
+                away.append(moves.start(normed, normed_out))
+            away.append(moves.start(result.at[chunk], out_ref.at[:, span]))
+        wait_all(away)
 
     return call(
         body,
         "norm_project",
-        (steps,),
-        [
-            pl.BlockSpec((1, half, width), lambda i, p: (p[3], 0, 0), pipeline_mode=pl.Buffered(1)),
-            held(half, width),
-            held(1, width),
-            held(1, width),
-            pl.BlockSpec((1, step), lambda i, _: (0, i)),
-        ]
-        + [whole_ref()] * 16,
-        [
-            pl.BlockSpec((2 * half, width), lambda i, _: (0, 0)),
-            pl.BlockSpec((2 * half, step), lambda i, _: (0, i)),
+        (1,),
+        [held(1, width), held(1, width), held(1, columns)] + [whole_ref()] * 18,
+        [whole_ref(), whole_ref()],
+        [shape_of(BF16, tokens, width), shape_of(BF16, tokens, columns)],
+        (place, gain, shift, bias, inputs, far) + tuple(left) + tuple(right),
+        scratch=[
+            pltpu.VMEM((half, width), F32),
+            pltpu.VMEM((half, width), BF16),
+            pltpu.VMEM((tokens, width), BF16),
+            weight_scratch(left[0], columns),
+            pltpu.VMEM((steps, tokens, step), BF16),
+            pltpu.SemaphoreType.DMA((2 * len(cuts) + 9 * steps,)),
         ],
-        [shape_of(BF16, 2 * half, width), shape_of(BF16, 2 * half, columns)],
-        (place, inputs, far, gain, shift, bias) + tuple(left) + tuple(right),
-        scratch=[weight_scratch(left[0], columns), pltpu.SemaphoreType.DMA((steps, 8))],
         vmem=56,
     )
 
 
-def out_norm(place, mixed, up_parts, at_out, bias, inputs, far, gain, shift, down_bias):
+def out_norm(place, mixed, up_parts, at_out, bias, inputs, far, gain, shift):
     half, width = far.shape
-    step = 256
-    parts = half // step
-
-    def body(place_ref, mixed_ref, bias_ref, own_ref, far_ref, gain_ref, shift_ref, down_ref, *refs):
-        right_refs = refs[:8]
-        middle_ref, normed_ref, start_ref, weight, sems = refs[8:]
-
-        @pl.when(pl.program_id(0) == 0)
-        def _():
-            copies = parts_copies(place_ref, right_refs, weight, sems, at_out, width, 0, 0)
-            for copy in copies:
-                copy.start()
-            for copy in copies:
-                copy.wait()
-
-        near = pl.program_id(0) < parts
-        rows = jnp.where(near, own_ref[0], far_ref[...].astype(F32))
-        middle = rows + (contract(mixed_ref[...], flat(weight[...]), 1, 0) + bias_ref[...])
-        middle_ref[...] = middle
-        start_ref[...] = middle + down_ref[...]
-        unit, _ = norm_parts(middle)
-        normed_ref[...] = (unit * gain_ref[...] + shift_ref[...]).astype(BF16)
-
-    here = pl.BlockSpec((step, width), lambda i, _: (i, 0))
+    tokens = 2 * half
+    cuts = row_cuts(tokens, 256)
+
+    def body(place_ref, bias_ref, gain_ref, shift_ref, mixed_in, inputs_in, far_in, *refs):
+        part_refs = refs[:8]
+        middle_out, normed_out, mixed_rows, own, far_rows, middle, normed, weight, sems = refs[8:]
+        moves = Transfers(sems)
+        parts = start_parts(moves, place_ref, part_refs, weight, at_out, width, 0)
+        mixes = [moves.start(mixed_in.at[cut], mixed_rows.at[cut]) for cut in cuts]
+        rows = start_rows(moves, place_ref, inputs_in, far_in, own, far_rows, cuts)
+        wait_all(parts)
+        away = []
+        for at, cut in enumerate(cuts):
+            mixes[at].wait()
+            product = contract(mixed_rows[cut], flat(weight[...]), 1, 0) + bias_ref[...]
+            rows[at].wait()
+            value = rows_at(own, far_rows, cut) + product
+            middle[cut] = value
+            away.append(moves.start(middle.at[cut], middle_out.at[cut]))
+            unit, _ = norm_parts(value)
+            normed[cut] = (unit * gain_ref[...] + shift_ref[...]).astype(BF16)
+            away.append(moves.start(normed.at[cut], normed_out.at[cut]))
+        wait_all(away)
+
     return call(
         body,
         "out_norm",
-        (2 * parts,),
-        [
-            here,
-            held(1, width),
-            own_spec(step, width, parts),
-            far_spec(step, width, parts),
-            held(1, width),
-            held(1, width),
-            held(1, width),
-        ]
-        + [whole_ref()] * 8,
-        [here, here, here],
-        [shape_of(F32, 2 * half, width), shape_of(BF16, 2 * half, width), shape_of(F32, 2 * half, width)],
-        (place, mixed, bias, inputs, far, gain, shift, down_bias) + tuple(up_parts),
-        scratch=[weight_scratch(up_parts[0], width), pltpu.SemaphoreType.DMA((1, 8))],
+        (1,),
+        [held(1, width)] * 3 + [whole_ref()] * 11,
+        [whole_ref(), whole_ref()],
+        [shape_of(F32, tokens, width), shape_of(BF16, tokens, width)],
+        (place, bias, gain, shift, mixed, inputs, far) + tuple(up_parts),
+        scratch=[
+            pltpu.VMEM((tokens, width), BF16),
+            pltpu.VMEM((half, width), F32),
+            pltpu.VMEM((half, width), BF16),
+            pltpu.VMEM((tokens, width), F32),
+            pltpu.VMEM((tokens, width), BF16),
+            weight_scratch(up_parts[0], width),
+            pltpu.SemaphoreType.DMA((8 + 4 * len(cuts),)),
+        ],
         vmem=56,
     )
 
@@ -830,7 +878,7 @@
     )
 
 
-def feed_forward(place, first, count, depth, normed, grad_low, up_parts, down_parts, up_bias, far, state, wide):
+def feed_forward(place, first, count, depth, normed, grad_low, up_parts, down_parts, up_bias, down_bias, far, state, wide):
     tokens, width = normed.shape
     half = tokens // 2
     hidden_width = up_bias.shape[1]
@@ -845,7 +893,7 @@
     beside = (up_parts[0].shape[-1] - hidden_width) // width
     rows = rows + beside * lines
 
-    def body(place_ref, bias_ref, normed_in, grad_in, far_in, out_in, back_in, *refs):
+    def body(place_ref, bias_ref, down_ref, normed_in, grad_in, far_in, out_in, back_in, *refs):
         up_refs, down_refs = refs[:8], refs[8 : 8 + 2 * depth]
         refs = refs[8 + 2 * depth + len(before) :]
         tall_mine, tall_other, wide_mine, wide_other, sum_ref, back_out = refs[:6]
@@ -982,6 +1030,7 @@
         @pl.when(at == steps - 1)
         def _():
             if last:
+                total[...] += down_ref[...]
                 delta[...] = (total[half:] - far_ref[...].astype(F32)).astype(BF16)
             for copy in away:
                 copy.start()
@@ -1033,162 +1082,169 @@
         pltpu.VMEM((2, 2 * rows, width), BF16),
         pltpu.VMEM((2 * depth, 2, group // 2, step), BF16),
     ]
-    args = (place, up_bias, normed, grad_low, far) + tuple(state) + tuple(up_parts) + tuple(down_parts)
+    args = (place, up_bias, down_bias, normed, grad_low, far) + tuple(state) + tuple(up_parts) + tuple(down_parts)
     alias = {len(args) + i: 2 + i for i in range(len(before))}
     return call(
         body,
         "feed_forward",
         (steps,),
-        [pl.BlockSpec((1, step), lambda i, _: (0, 2 * first + i))]
+        [pl.BlockSpec((1, step), lambda i, _: (0, 2 * first + i)), held(1, width)]
         + [whole_ref()] * (5 + 8 + 2 * depth + len(before)),
         out_specs,
         out_shape,
         args + tuple(before),
         scratch=scratch,
-        vmem=56,
+        vmem=46,
         alias=alias,
     )
 
 
 def middle_back(place, grad_normed, middle, gain, grad_out, far, up_parts, at_out):
     half, width = far.shape
-    step = 256
-    parts = half // step
-
-    def body(place_ref, grad_ref, middle_ref, gain_ref, own_ref, far_ref, *refs):
-        right_refs = refs[:8]
-        total_ref, low_ref, mixed_ref = refs[8:11]
-        sums = refs[11:14]
-        weight, sems = refs[14:]
-        at = pl.program_id(0)
-
-        def copies():
-            return parts_copies(place_ref, right_refs, weight, sems, at_out, width, 0, 0)
-
-        @pl.when(at == 0)
-        def _():
-            for copy in copies():
-                copy.start()
-            for ref in sums:
-                ref[...] = jnp.zeros_like(ref)
-
-        grad_normed = grad_ref[...]
-        unit, scale = norm_parts(middle_ref[...])
-        out_grad = jnp.where(at < parts, own_ref[0], far_ref[...].astype(F32))
-        total = out_grad + norm_back(unit, scale, gain_ref[...], grad_normed)
-        total_ref[...] = total
-        low = total.astype(BF16)
-        low_ref[...] = low
-        sums[0][...] += column(grad_normed * unit)
-        sums[1][...] += column(grad_normed)
-        sums[2][...] += column(low.astype(F32))
-
-        @pl.when(at == 0)
-        def _():
-            for copy in copies():
-                copy.wait()
-
-        mixed_ref[...] = contract(low, flat(weight[...]), 1, 1).astype(BF16)
-
-    here = pl.BlockSpec((step, width), lambda i, _: (i, 0))
-    vector = pl.BlockSpec((1, width), lambda i, _: (0, 0))
     tokens = 2 * half
+    cuts = row_cuts(tokens, 256)
+
+    def body(place_ref, gain_ref, grad_in, middle_in, grad_out_in, far_in, *refs):
+        part_refs = refs[:8]
+        total_out, low_out, mixed_out = refs[8:11]
+        sum_refs = refs[11:14]
+        grads, middles, own, far_rows, total, low, mixed, weight, sems = refs[14:]
+        moves = Transfers(sems)
+        pairs = []
+        for at, cut in enumerate(cuts):
+            pairs.append(
+                [
+                    moves.start(grad_in.at[cut], grads.at[cut]),
+                    moves.start(middle_in.at[cut], middles.at[cut]),
+                ]
+                + start_rows(moves, place_ref, grad_out_in, far_in, own, far_rows, [cut])
+            )
+            if at == 0:
+                parts = start_parts(moves, place_ref, part_refs, weight, at_out, width, 0)
+        sums = [jnp.zeros((1, width), F32) for _ in range(3)]
+        away = []
+        for at, cut in enumerate(cuts):
+            wait_all(pairs[at])
+            grad = grads[cut]
+            unit, scale = norm_parts(middles[cut])
+            value = rows_at(own, far_rows, cut) + norm_back(unit, scale, gain_ref[...], grad)
+            total[cut] = value
+            away.append(moves.start(total.at[cut], total_out.at[cut]))
+            value_low = value.astype(BF16)
+            low[cut] = value_low
+            away.append(moves.start(low.at[cut], low_out.at[cut]))
+            sums[0] += column(grad * unit)
+            sums[1] += column(grad)
+            sums[2] += column(value_low.astype(F32))
+            if at == 0:
+                wait_all(parts)
+            mixed[cut] = contract(value_low, flat(weight[...]), 1, 1).astype(BF16)
+            away.append(moves.start(mixed.at[cut], mixed_out.at[cut]))
+        for ref, value in zip(sum_refs, sums):
+            ref[...] = value
+        wait_all(away)
+
+    vector = held(1, width)
     return call(
         body,
         "middle_back",
-        (2 * parts,),
-        [here, here, held(1, width), own_spec(step, width, parts), far_spec(step, width, parts)]
-        + [whole_ref()] * 8,
-        [here, here, here, vector, vector, vector],
+        (1,),
+        [vector] + [whole_ref()] * 12,
+        [whole_ref()] * 3 + [vector] * 3,
         [shape_of(F32, tokens, width), shape_of(BF16, tokens, width), shape_of(BF16, tokens, width)]
         + [shape_of(F32, 1, width)] * 3,
-        (place, grad_normed, middle, gain, grad_out, far) + tuple(up_parts),
-        scratch=[weight_scratch(up_parts[0], width), pltpu.SemaphoreType.DMA((1, 8))],
+        (place, gain, grad_normed, middle, grad_out, far) + tuple(up_parts),
+        scratch=[
+            pltpu.VMEM((tokens, width), F32),
+            pltpu.VMEM((tokens, width), F32),
+            pltpu.VMEM((half, width), F32),
+            pltpu.VMEM((half, width), BF16),
+            pltpu.VMEM((tokens, width), F32),
+            pltpu.VMEM((tokens, width), BF16),
+            pltpu.VMEM((tokens, width), BF16),
+            weight_scratch(up_parts[0], width),
+            pltpu.SemaphoreType.DMA((8 + 6 * len(cuts),)),
+        ],
         vmem=56,
     )
 
 
 def input_back(place, grads, left, right, inputs, far, gain, middle_grad, far_grad):
     half, width = far.shape
-    cut = left[0].shape[-1]
-    step = 256
-    parts = half // step
-
-    def body(
-        place_ref, query_ref, key_ref, value_ref, own_ref, far_ref, gain_ref, middle_ref, far_grad_ref, *refs
-    ):
+    tokens = 2 * half
+    split = left[0].shape[-1]
+    cuts = row_cuts(tokens, 256)
+
+    def body(place_ref, gain_ref, query_in, key_in, value_in, inputs_in, far_in, middle_in, far_grad_in, *refs):
         left_refs, right_refs = refs[:8], refs[8:16]
-        out_ref, delta_ref = refs[16:18]
-        sums = refs[18:22]
-        gain_sum_ref, shift_sum_ref, query_sum_ref, value_sum_ref = sums
-        weight, sems = refs[22:]
-        at = pl.program_id(0)
-
-        def copies():
-            result = []
-            for chunk, part_refs in enumerate((left_refs, right_refs)):
-                size = (cut, 3 * width - cut)[chunk]
-                result += parts_copies(
-                    place_ref, part_refs, weight, sems, 0, size, chunk * cut, chunk
-                )
-            return result
-
-        @pl.when(at == 0)
-        def _():
-            for copy in copies():
-                copy.start()
-            for ref in sums:
-                ref[...] = jnp.zeros_like(ref)
-
-        @pl.when(at == 0)
-        def _():
-            for copy in copies():
-                copy.wait()
+        out_ref, delta_out = refs[16:18]
+        sum_refs = refs[18:22]
+        query, key, value, own, far_rows, middle, far_grads, result, delta, weight, sems = refs[22:]
+        moves = Transfers(sems)
+        first = start_parts(moves, place_ref, left_refs, weight, 0, split, 0)
+        pairs, lates = [], []
+        for at, cut in enumerate(cuts):
+            pairs.append([moves.start(query_in.at[cut], query.at[cut]), moves.start(key_in.at[cut], key.at[cut])])
+            late = [moves.start(value_in.at[cut], value.at[cut])]
+            if at == 0:
+                late += start_parts(moves, place_ref, right_refs, weight, 0, 3 * width - split, split)
+            late += start_rows(moves, place_ref, inputs_in, far_in, own, far_rows, [cut])
+            late.append(moves.start(middle_in.at[cut], middle.at[cut]))
+            if cut.start >= half:
+                back = pl.ds(cut.start - half, cut.size)
+                late.append(moves.start(far_grad_in.at[back], far_grads.at[back]))
+            lates.append(late)
 
         def part(chunk):
             return flat(weight[:, :, :, :, :, chunk * width : (chunk + 1) * width])
 
-        grad_normed = contract(query_ref[...], part(0), 1, 1)
-        grad_normed += contract(key_ref[...], part(1), 1, 1)
-        grad_normed += contract(value_ref[...], part(2), 1, 1)
-        rows = jnp.where(at < parts, own_ref[0], far_ref[...].astype(F32))
-        unit, scale = norm_parts(rows)
-        gain_sum_ref[...] += column(grad_normed * unit)
-        shift_sum_ref[...] += column(grad_normed)
-        query_sum_ref[...] += column(query_ref[...].astype(F32))
-        value_sum_ref[...] += column(value_ref[...].astype(F32))
-        result = middle_ref[...] + norm_back(unit, scale, gain_ref[...], grad_normed)
-
-        @pl.when(at < parts)
-        def _():
-            out_ref[0] = result
-
-        @pl.when(at >= parts)
-        def _():
-            delta_ref[...] = (result - far_grad_ref[...].astype(F32)).astype(BF16)
-
-    here = pl.BlockSpec((step, width), lambda i, _: (i, 0))
-    vector = pl.BlockSpec((1, width), lambda i, _: (0, 0))
+        sums = [jnp.zeros((1, width), F32) for _ in range(4)]
+        away = []
+        for at, cut in enumerate(cuts):
+            wait_all(pairs[at])
+            if at == 0:
+                wait_all(first)
+            grad = contract(query[cut], part(0), 1, 1) + contract(key[cut], part(1), 1, 1)
+            wait_all(lates[at])
+            grad += contract(value[cut], part(2), 1, 1)
+            unit, scale = norm_parts(rows_at(own, far_rows, cut))
+            sums[0] += column(grad * unit)
+            sums[1] += column(grad)
+            sums[2] += column(query[cut].astype(F32))
+            sums[3] += column(value[cut].astype(F32))
+            total = middle[cut] + norm_back(unit, scale, gain_ref[...], grad)
+            if cut.start < half:
+                result[cut] = total
+                away.append(moves.start(result.at[cut], out_ref.at[place_ref[3], cut]))
+            else:
+                back = pl.ds(cut.start - half, cut.size)
+                delta[back] = (total - far_grads[back].astype(F32)).astype(BF16)
+                away.append(moves.start(delta.at[back], delta_out.at[back]))
+        for ref, total in zip(sum_refs, sums):
+            ref[...] = total
+        wait_all(away)
+
+    vector = held(1, width)
     return call(
         body,
         "input_back",
-        (2 * parts,),
-        [
-            here,
-            here,
-            here,
-            own_spec(step, width, parts),
-            far_spec(step, width, parts),
-            held(1, width),
-            here,
-            far_spec(step, width, parts),
-        ]
-        + [whole_ref()] * 16,
-        [own_spec(step, width, parts), far_spec(step, width, parts), vector, vector, vector, vector],
+        (1,),
+        [vector] + [whole_ref()] * 23,
+        [whole_ref()] * 2 + [vector] * 4,
         [shape_of(F32, 2, half, width), shape_of(BF16, half, width)] + [shape_of(F32, 1, width)] * 4,
-        (place,) + tuple(grads) + (inputs, far, gain, middle_grad, far_grad) + tuple(left) + tuple(right),
-        scratch=[weight_scratch(left[0], 3 * width), pltpu.SemaphoreType.DMA((2, 8))],
-        vmem=56,
+        (place, gain) + tuple(grads) + (inputs, far, middle_grad, far_grad) + tuple(left) + tuple(right),
+        scratch=[pltpu.VMEM((tokens, width), BF16)] * 3
+        + [
+            pltpu.VMEM((half, width), F32),
+            pltpu.VMEM((half, width), BF16),
+            pltpu.VMEM((tokens, width), F32),
+            pltpu.VMEM((half, width), BF16),
+            pltpu.VMEM((half, width), F32),
+            pltpu.VMEM((half, width), BF16),
+            weight_scratch(left[0], 3 * width),
+            pltpu.SemaphoreType.DMA((16 + 8 * len(cuts),)),
+        ],
+        vmem=34,
     )
 
 
@@ -1255,29 +1311,35 @@
     )
 
 
-def last_add(place, own, came, shapes):
+def last_add(place, own, came, shapes, before):
     rows, total = own.shape
     layout = [(which, part) for which, shape in enumerate(shapes) for part in range(shape[0] // rows)]
+    offsets = [before[which].shape[1] if which in before else 0 for which in range(len(shapes))]
+    extra = sorted(before)
 
     def body(place_ref, own_ref, *refs):
-        outs = refs[len(came) :]
+        outs = refs[len(came) + len(extra) :]
+        for which, ref in zip(extra, refs[len(came) :]):
+            outs[which][:, : offsets[which]] = ref[...]
         start = 0
         for which, part in layout:
             width = shapes[which][1]
             value = own_ref[:, start : start + width]
             for ref in refs[: len(came)]:
                 value = value + ref[:, start : start + width].astype(F32)
-            outs[which][part * rows : (part + 1) * rows] = value
+            first = offsets[which]
+            outs[which][part * rows : (part + 1) * rows, first : first + width] = value
             start += width
 
+    wholes = [(shape[0], shape[1] + offset) for shape, offset in zip(shapes, offsets)]
     return call(
         body,
         "last_add",
         (1,),
-        [held(rows, total)] * (1 + len(came)),
-        [held(*shape) for shape in shapes],
-        [shape_of(F32, *shape) for shape in shapes],
-        (place, own) + tuple(came),
+        [held(rows, total)] * (1 + len(came)) + [held(*before[which].shape) for which in extra],
+        [held(*shape) for shape in wholes],
+        [shape_of(F32, *shape) for shape in wholes],
+        (place, own) + tuple(came) + tuple(before[which] for which in extra),
         vmem=12,
     )
 
@@ -1480,7 +1542,7 @@
             shape_of(F32, tokens, width),
         ],
         (place, qkv, qkv, qkv, bias) + tuple(before),
-        vmem=28,
+        vmem=56,
         alias={5 + i: i for i in range(len(before))},
     )
 
@@ -1599,8 +1661,8 @@
         self.mine = own
         self.came = [ring_z(block, step + 1) for step, block in enumerate(sent)]
 
-    def last(self, *shapes):
-        return last_add(self.place, self.mine, self.came, shapes)
+    def last(self, *shapes, before={}):
+        return last_add(self.place, self.mine, self.came, shapes, before)
 
     def hold(self, *others):
         self.mine, self.came, others = tie(self.mine, self.came, others)
@@ -1743,8 +1805,8 @@
     plane_core = {step: swap_core(planes[step]) for step in (0, 1, depth - 1)}
     grad_ff_low, grad_down_bias = join_low(place, grad_out, far_grad)
     mixed_low, grad_ff_low = tie(mixed_low, grad_ff_low)
-    middle, normed_two_low, start_out = out_norm(
-        place, mixed_low, right_parts, at_out, out_bias, inputs, far_rows, ln2_gain, ln2_bias, down_bias
+    middle, normed_two_low = out_norm(
+        place, mixed_low, right_parts, at_out, out_bias, inputs, far_rows, ln2_gain, ln2_bias
     )
     normed_two_low, up_xy, plane_core, up_core, planes = tie(
         normed_two_low, up_xy, plane_core, up_core, planes
@@ -1766,14 +1828,14 @@
     def feed(first, count, state, wide):
         return feed_forward(
             place, first, count, depth, normed_two_low, grad_ff_low, up_parts, down_parts, up_bias,
-            far_rows, state, wide,
+            down_bias, far_rows, state, wide,
         )
 
     near = depth // 2
     near_width = hidden_width // 2
     each = hidden_width // depth
     mine, other, up_mine, up_other, bias_0, back, total = feed(
-        0, near, (start_out, start_out), (near_width, 0, ())
+        0, near, (middle, middle), (near_width, 0, ())
     )
     down_sums[0].begin(mine, other)
     near_sum.begin(up_mine, up_other)
@@ -1881,15 +1943,16 @@
     in_far = swap_y(in_delta)
     left_sum.third(right_sum, vectors=packed, sizes=sizes)
     left_sum.mine, out_far, down_sum.mine = tie(left_sum.mine, out_far, down_sum.mine)
-    grad_w_down, grad_up_far, grad_w_out = down_sum.last(w_down.shape, (rows, near_width), w_out.shape)
+    grad_w_down, grad_w_up, grad_w_out = down_sum.last(
+        w_down.shape, (rows, near_width), w_out.shape, before={1: grad_up_near}
+    )
     result = fill_far(place, out_part, inputs, out_far)
-    result, in_far, grad_up_far = tie(result, in_far, grad_up_far)
+    result, in_far, grad_w_up = tie(result, in_far, grad_w_up)
     grad_in = fill_far(place, in_part, grad_out, in_far)
     left_sum.came, grad_in = tie(left_sum.came, grad_in)
-    grad_w_up = jnp.concatenate([grad_up_near, grad_up_far], axis=1)
-    square, part = (rows, width), (rows, width // 2)
-    grad_left_q, grad_left_k, grad_right_k, grad_right_v, packed = left_sum.last(
-        square, part, part, square, (rows, PAIR)
+    square = (rows, width)
+    grad_w_query, grad_w_key, grad_w_value, packed = left_sum.last(
+        square, square, square, (rows, PAIR)
     )
     packed = packed.reshape(-1)
     out_vectors = []
@@ -1897,9 +1960,8 @@
         count = size * rows
         lane = (dp * 2 + y) * count % PAIR
         out_vectors.append(lax.dynamic_slice_in_dim(packed, index * PAIR + lane, count))
-    grad_w_key = jnp.concatenate([grad_left_k, grad_right_k], axis=1)
     return (
-        (result, grad_in, grad_left_q, grad_w_key, grad_right_v, grad_w_out, grad_w_up, grad_w_down)
+        (result, grad_in, grad_w_query, grad_w_key, grad_w_value, grad_w_out, grad_w_up, grad_w_down)
         + tuple(out_vectors)
     )
 

time: 468 us -> 465 us (level)
  Pallas kernels: 275 us -> 265 us
  local copies, waits for them, and re-layouts: 33.7 us -> 42.5 us
    pallas_call x44, Pallas kernels: 275 us -> 265 us  [call(): pl.pallas_call(body, grid_spec=spec, out_shape=out_shape, name=name, inpu...]
    unnamed x233 -> x251, local copies, waits for them, and re-layouts: 31.2 us -> 34.3 us
  transfers between devices with their start and end apart: 77 -> 77, of which waited for: 23 -> 25; matrix products, arithmetic and copies ran while one was open for 0% -> 2% of each run, Pallas kernels for 50% -> 48%
where the time goes in v4:
time: 465 us; the launch traced here: 460 us
  Pallas kernels  265 us (57%)
  waiting for transfers between devices  84.3 us (18%)
  starting transfers between devices  64 us (14%)
  local copies, waits for them, and re-layouts  42.5 us (9%)
    pallas_call x44, Pallas kernels, call(): pl.pallas_call(body, grid_spec=spec, out_shape=out_shape, name=name, inpu...  265 us
    ppermute x58, waiting for transfers between devices, pair_swap(): return lax.ppermute(value, axis, [(i, i ^ bit) for i in range(size)])  43.6 us
    ppermute x58, starting transfers between devices, pair_swap(): return lax.ppermute(value, axis, [(i, i ^ bit) for i in range(size)])  41 us
    ppermute x18, waiting for transfers between devices, ring_z(): lax.ppermute(value, 'dp', [(i, (i + 4 * step) % size) for i in range(size)])  37.6 us
    unnamed x251, local copies, waits for them, and re-layouts  34.3 us
    ppermute x18, starting transfers between devices, ring_z(): lax.ppermute(value, 'dp', [(i, (i + 4 * step) % size) for i in range(size)])  21.7 us
  transfers between devices with their start and end apart: 77, of which 25 were waited for; matrix products, arithmetic and copies ran while one was open for 2% of the time, Pallas kernels for 48%

profile of v4, /device:TPU:8, one launch (start us, length us, event | category | flops | bytes accessed | tf_op | source)
XLA Modules:
  0.0 459.8 jit_solution(12710448125684260864)
XLA Ops:
  3.0 2.2 copy-done
  10.4 1.8 collective-permute-start.2
  18.2 9.4 %collective-permute-done.refs_1_ = bf16[32,4224]{1,0:T(8,128)(2,1)S(1)} collective-permute-done((bf16[32,4224]{1,0:T(8,128)(2,1)S(1)}, bf16[32,4224]{1,0:T(8,128)(2,1)S(1)}, u32[]{:S(2)}, u32[]{:S(2)}) %collective-permute-start) | collective-permute-done | bytes 270368 | tf_op jit(solution)/shard_map/ppermute | solution.py:1617
  28.4 3.3 collective-permute-done.1.refs_2_
  31.7 1.9 collective-permute-done.2.refs_3_
  35.5 1.7 join_first.1
  40.3 2.0 collective-permute-start.9
  42.9 12.3 %collective-permute-done.11.refs_2_ = bf16[64,1024]{1,0:T(8,128)(2,1)S(1)} collective-permute-done((bf16[64,1024]{1,0:T(8,128)(2,1)S(1)}, bf16[64,1024]{1,0:T(8,128)(2,1)S(1)}, u32[]{:S(2)}, u32[]{:S(2)}) %collective-permute-start.11) | collective-permute-done | bytes 131104 | tf_op jit(solution)/shard_map/ppermute | solution.py:1591
  56.7 2.2 copy-done.5
  65.8 1.7 copy.51
  72.9 2.3 join_plane.1.refs_8_
  75.2 4.0 collective-permute-done.16.refs_2_
  79.2 6.8 %collective-permute-done.13.refs_5_ = bf16[4,32,2048]{2,1,0:T(8,128)(2,1)S(1)} collective-permute-done((bf16[4,32,2048]{2,1,0:T(8,128)(2,1)}, bf16[4,32,2048]{2,1,0:T(8,128)(2,1)S(1)}, u32[]{:S(2)}, u32[]{:S(2)}) %collective-permute-start.13) | collective-permute-done | bytes 524320 | tf_op jit(solution)/shard_map/ppermute | solution.py:1591
  86.2 1.6 join_up.1.refs_0_
  101.6 13.5 %norm_project.1 = (bf16[1024,1024]{1,0:T(8,128)(2,1)}, bf16[1024,3072]{1,0:T(8,128)(2,1)}) custom-call(s32[4]{0:T(128)} %copy-done.68, f32[1,1024]{1,0:T(1,128)} %copy-done.86, f32[1,1024]{1,0:T(1,128)} %copy-done.88, f32[1,3072]{1,0:T(1,128)} %pad_maximum_fusion.1.bias_ref, f32[2,512,1024]{2,1,0:T(8,128)} %base_ref.1, bf16[512,1024]{1,0:T(8,128)(2,1)} %copy-done.8, ...), custom_call_target="tpu_custom_call" | custom-call | flops 1200000000 | bytes 1 | tf_op jit(solution)/shard_map/norm_project/pallas_call | solution.py:464
  115.1 13.9 %attn_forward.2 = (bf16[16,1024,1024]{2,1,0:T(8,128)(2,1)}, bf16[1024,1024]{1,0:T(8,128)(2,1)}, f32[1024,1024]{1,0:T(8,128)}) custom-call(s32[4]{0:T(128)} %copy-done.68, bf16[1024,3072]{1,0:T(8,128)(2,1)} %get-tuple-element.448.refs_0_.refs_1_.refs_2_, bf16[1024,3072]{1,0:T(8,128)(2,1)} %get-tuple-element.448.refs_0_.refs_1_.refs_2_, ...), custom_call_target="tpu_custom_call" | custom-call | flops 450000000 | bytes 1 | tf_op jit(solution)/shard_map/attn_forward/pallas_call | solution.py:464
  131.4 20.8 %attn_forward.3 = (bf16[16,1024,1024]{2,1,0:T(8,128)(2,1)}, bf16[1024,1024]{1,0:T(8,128)(2,1)}, f32[1024,1024]{1,0:T(8,128)}) custom-call(s32[4]{0:T(128)} %copy-done.68, bf16[1024,3072]{1,0:T(8,128)(2,1)} %get-tuple-element.448.refs_0_.refs_1_.refs_2_, ...), custom_call_target="tpu_custom_call", output_to_operand_aliasing={{0}: (5, {}), {1}: (6, {}), {2}: (7, {})} | custom-call | flops 750000000 | bytes 1 | tf_op jit(solution)/shard_map/attn_forward/pallas_call | solution.py:464
  158.3 8.9 %out_norm.1 = (f32[1024,1024]{1,0:T(8,128)}, bf16[1024,1024]{1,0:T(8,128)(2,1)}) custom-call(s32[4]{0:T(128)} %copy-done.68, f32[1,1024]{1,0:T(1,128)} %copy-done.90, f32[1,1024]{1,0:T(1,128)} %copy-done.89, f32[1,1024]{1,0:T(1,128)} %copy-done.91, bf16[1024,1024]{1,0:T(8,128)(2,1)} %get-tuple-element.469.mixed_in.left_ref.refs_4_, ...), custom_call_target="tpu_custom_call" | custom-call | flops 300000000 | bytes 1 | tf_op jit(solution)/shard_map/out_norm/pallas_call | solution.py:464
  167.8 3.3 collective-permute-done.39.refs_13_
  172.8 38.2 %feed_forward.3 = (bf16[4,256,1024]{2,1,0:T(8,128)(2,1)}, bf16[4,256,1024]{2,1,0:T(8,128)(2,1)}, bf16[8,64,2048]{2,1,0:T(8,128)(2,1)}, bf16[8,64,2048]{2,1,0:T(8...) custom-call(s32[4]{0:T(128)S(1)} %copy-done.70, ...), custom_call_target="tpu_custom_call" | custom-call | flops 10800000000 | bytes 1 | tf_op jit(solution)/shard_map/feed_forward/pallas_call | solution.py:464
  211.7 21.2 %feed_forward.4 = (bf16[2,256,1024]{2,1,0:T(8,128)(2,1)S(1)}, bf16[2,256,1024]{2,1,0:T(8,128)(2,1)}, bf16[8,64,2048]{2,1,0:T(8,128)(2,1)}, bf16[8,64,2048]{2,1,0...) custom-call(s32[4]{0:T(128)S(1)} %copy-done.70, ...), custom_call_target="tpu_custom_call" | custom-call | flops 5400000000 | bytes 1 | tf_op jit(solution)/shard_map/feed_forward/pallas_call | solution.py:464
  233.1 3.4 split_add.14
  237.4 1.9 split_add.13
  241.1 23.1 %feed_forward.5 = (bf16[2,256,1024]{2,1,0:T(8,128)(2,1)S(1)}, bf16[2,256,1024]{2,1,0:T(8,128)(2,1)}, bf16[8,64,2048]{2,1,0:T(8,128)(2,1)}, bf16[8,64,2048]{2,1,0...) custom-call(s32[4]{0:T(128)S(1)} %copy-done.70, ...), custom_call_target="tpu_custom_call", output_to_operand_aliasing={{2}: (24, {}), {3}: (25, {})} | custom-call | flops 5400000000 | bytes 1 | tf_op jit(solution)/shard_map/feed_forward/pallas_call | solution.py:464
  267.7 2.8 split_add.15
  271.9 10.8 %middle_back.1 = (f32[1024,1024]{1,0:T(8,128)}, bf16[1024,1024]{1,0:T(8,128)(2,1)}, bf16[1024,1024]{1,0:T(8,128)(2,1)}, f32[1,1024]{1,0:T(1,128)}, f32[1,1024]{1,0:T(1,128)}, /*index=5*/f32[1,1024]{1,0:T(1,128)}) custom-call(s32[4]{0:T(128)} %copy-done.68, f32[1,1024]{1,0:T(1,128)} %copy-done.89, f32[1024,1024]{1,0:T(8,128)} %get-tuple-element.528.grad_in, ...), custom_call_target="tpu_custom_call" | custom-call | flops 12000000000 | bytes 1 | tf_op jit(solution)/shard_map/middle_back/pallas_call | solution.py:464
  285.9 3.7 grad_wide.2
  291.7 2.2 split_add.16
  296.9 3.2 split_add.18
  300.9 21.1 %attn_backward.2 = (bf16[1024,1024]{1,0:T(8,128)(2,1)S(1)}, bf16[1024,1024]{1,0:T(8,128)(2,1)S(1)}, bf16[1024,1024]{1,0:T(8,128)(2,1)S(1)}) custom-call(s32[4]{0:T(128)S(1)} %copy-done.71, bf16[1024,3072]{1,0:T(8,128)(2,1)S(1)} %bitcast.66, bf16[1024,3072]{1,0:T(8,128)(2,1)S(1)} %bitcast.66, bf16[1024,3072]{1,0:T(8,128)(2,1)S(1)} %bitcast.66, ...), custom_call_target="tpu_custom_call" | custom-call | flops 6000000000 | bytes 1 | tf_op jit(solution)/shard_map/attn_backward/pallas_call | solution.py:464
  322.1 2.1 merge_add.1
  329.1 2.9 collective-permute-start.55
  332.5 20.9 %attn_backward.3 = (bf16[1024,1024]{1,0:T(8,128)(2,1)S(1)}, bf16[1024,1024]{1,0:T(8,128)(2,1)S(1)}, bf16[1024,1024]{1,0:T(8,128)(2,1)S(1)}) custom-call(s32[4]{0:T(128)S(1)} %copy-done.71, bf16[1024,3072]{1,0:T(8,128)(2,1)S(1)} %bitcast.66, bf16[1024,3072]{1,0:T(8,128)(2,1)S(1)} %bitcast.66, ...), custom_call_target="tpu_custom_call", output_to_operand_aliasing={{0}: (8, {}), {1}: (9, {}), {2}: (10, {})} | custom-call | flops 6000000000 | bytes 1 | tf_op jit(solution)/shard_map/attn_backward/pallas_call | solution.py:464
  356.8 10.3 %grad_wide.3 = (bf16[8,64,1536]{2,1,0:T(8,128)(2,1)S(1)}, bf16[8,64,1536]{2,1,0:T(8,128)(2,1)S(1)}, bf16[8,64,1536]{2,1,0:T(8,128)(2,1)S(1)}, bf16[8,64,1536]{2,1,0:T(8,128)(2,1)S(1)}) custom-call(s32[4]{0:T(128)S(1)} %copy-done.71, bf16[1024,1024]{1,0:T(8,128)(2,1)S(1)} %copy-done.92, bf16[1024,1024]{1,0:T(8,128)(2,1)S(1)} %get-tuple-element.674.refs_0_.query_in, ...), custom_call_target="tpu_custom_call" | custom-call | flops 3240000000 | bytes 1 | tf_op jit(solution)/shard_map/grad_wide/pallas_call | solution.py:464
  370.5 6.7 %collective-permute-done.60.refs_5_ = bf16[4,32,1024]{2,1,0:T(8,128)(2,1)S(1)} collective-permute-done((bf16[4,32,1024]{2,1,0:T(8,128)(2,1)S(1)}, bf16[4,32,1024]{2,1,0:T(8,128)(2,1)S(1)}, u32[]{:S(2)}, u32[]{:S(2)}) %collective-permute-start.60) | collective-permute-done | bytes 262176 | tf_op jit(solution)/shard_map/ppermute | solution.py:1591
  384.2 2.1 collective-permute-start.66
  386.5 13.4 %input_back.1 = (f32[2,512,1024]{2,1,0:T(8,128)}, bf16[512,1024]{1,0:T(8,128)(2,1)}, f32[1,1024]{1,0:T(1,128)S(1)}, f32[1,1024]{1,0:T(1,128)S(1)}, f32[1,1024]{1,0:T(1,128)S(1)}, /*index=5*/f32[1,1024]{1,0:T(1,128)S(1)}) custom-call(s32[4]{0:T(128)S(1)} %copy-done.71, f32[1,1024]{1,0:T(1,128)S(1)} %copy-done.87, ...), custom_call_target="tpu_custom_call" | custom-call | flops 300000000 | bytes 1 | tf_op jit(solution)/shard_map/input_back/pallas_call | solution.py:464
  403.7 11.1 %collective-permute-done.65.refs_0_ = bf16[32,7168]{1,0:T(8,128)(2,1)S(1)} collective-permute-done((bf16[32,7168]{1,0:T(8,128)(2,1)S(1)}, bf16[32,7168]{1,0:T(8,128)(2,1)S(1)}, u32[]{:S(2)}, u32[]{:S(2)}) %collective-permute-start.65) | collective-permute-done | bytes 458784 | tf_op jit(solution)/shard_map/ppermute | solution.py:1617
  416.4 6.0 %collective-permute-done.66.refs_1_ = bf16[32,7168]{1,0:T(8,128)(2,1)S(1)} collective-permute-done((bf16[32,7168]{1,0:T(8,128)(2,1)S(1)}, bf16[32,7168]{1,0:T(8,128)(2,1)S(1)}, u32[]{:S(2)}, u32[]{:S(2)}) %collective-permute-start.66) | collective-permute-done | bytes 458784 | tf_op jit(solution)/shard_map/ppermute | solution.py:1617
  427.2 3.1 collective-permute-done.72
  433.7 3.0 collective-permute-start.75
  436.7 2.0 collective-permute-start.76
  441.8 1.7 last_add.4
  443.5 2.2 copy-done.1
  445.7 2.0 fill_far.2
  447.7 6.4 %collective-permute-done.73.delta_ref = bf16[512,1024]{1,0:T(8,128)(2,1)S(1)} collective-permute-done((bf16[512,1024]{1,0:T(8,128)(2,1)}, bf16[512,1024]{1,0:T(8,128)(2,1)S(1)}, u32[]{:S(2)}, u32[]{:S(2)}) %collective-permute-start.73) | collective-permute-done | bytes 1048608 | tf_op jit(solution)/shard_map/ppermute | solution.py:1591
  454.0 2.0 fill_far.3
  456.0 2.3 last_add.5
  (432 shorter events, 112.3 us)
Async XLA Ops:
  6.0 27.6 %collective-permute-start.5 = (bf16[512,1024]{1,0:T(8,128)(2,1)S(1)}, bf16[512,1024]{1,0:T(8,128)(2,1)S(1)}, u32[]{:S(2)}, u32[]{:S(2)}) collective-permute-start(bf16[512,1024]{1,0:T(8,128)(2,1)S(1)} %cast_far.2), channel_id=1, source_target_pairs={{0,1},{1,0},{2,3},{3,2},{4,5},{5,4},{6,7},{7,6},{8,9},{9,8},{10,11... | collective-permute-start | bytes 3145736 | tf_op jit(solution)/shard_map/ppermute | solution.py:1591
  7.5 20.2 %collective-permute-start = (bf16[32,4224]{1,0:T(8,128)(2,1)S(1)}, bf16[32,4224]{1,0:T(8,128)(2,1)S(1)}, u32[]{:S(2)}, u32[]{:S(2)}) collective-permute-start(bf16[32,4224]{1,0:T(8,128)(2,1)S(1)} %join_beside.2.refs_0_), channel_id=1, source_target_pairs={{0,8},{2,10},{4,12},{6,14},{8,16},{10,18},{12,20},{14,22},{16,24},... | collective-permute-start | bytes 811016 | tf_op jit(solution)/shard_map/ppermute | solution.py:1617
  9.2 22.6 %collective-permute-start.1 = (bf16[32,4224]{1,0:T(8,128)(2,1)S(1)}, bf16[32,4224]{1,0:T(8,128)(2,1)}, u32[]{:S(2)}, u32[]{:S(2)}) collective-permute-start(bf16[32,4224]{1,0:T(8,128)(2,1)S(1)} %join_beside.2.refs_0_), channel_id=1, source_target_pairs={{0,16},{2,18},{4,20},{6,22},{8,24},{10,26},{12,28},{14,30},{16,0},... | collective-permute-start | bytes 811016 | tf_op jit(solution)/shard_map/ppermute | solution.py:1617
  10.4 23.2 %collective-permute-start.2 = (bf16[32,4224]{1,0:T(8,128)(2,1)S(1)}, bf16[32,4224]{1,0:T(8,128)(2,1)}, u32[]{:S(2)}, u32[]{:S(2)}) collective-permute-start(bf16[32,4224]{1,0:T(8,128)(2,1)S(1)} %join_beside.2.refs_0_), channel_id=1, source_target_pairs={{0,24},{2,26},{4,28},{6,30},{8,0},{10,2},{12,4},{14,6},{16,8},{18,... | collective-permute-start | bytes 811016 | tf_op jit(solution)/shard_map/ppermute | solution.py:1617
  37.2 27.6 %collective-permute-start.8 = (bf16[4,32,2176]{2,1,0:T(8,128)(2,1)S(1)}, bf16[4,32,2176]{2,1,0:T(8,128)(2,1)S(1)}, u32[]{:S(2)}, u32[]{:S(2)}) collective-permute-start(bf16[4,32,2176]{2,1,0:T(8,128)(2,1)S(1)} %get-tuple-element.422.refs_0_.refs_8_), channel_id=1, source_target_pairs={{0,4},{2,6},{4,0},{6,2},{8,12},{10,14},{12,8},{14,10},{16,20},{18,... | collective-permute-start | bytes 1671176 | tf_op jit(solution)/shard_map/ppermute | solution.py:1591
  38.8 26.0 %collective-permute-start.7 = (bf16[4,32,2048]{2,1,0:T(8,128)(2,1)S(1)}, bf16[4,32,2048]{2,1,0:T(8,128)(2,1)}, u32[]{:S(2)}, u32[]{:S(2)}) collective-permute-start(bf16[4,32,2048]{2,1,0:T(8,128)(2,1)S(1)} %get-tuple-element.440.refs_0_), channel_id=1, source_target_pairs={{0,1},{1,0},{2,3},{3,2},{4,5},{5,4},{6,7},{7,6},{8,9},{9,8},{10,11... | collective-permute-start | bytes 1572872 | tf_op jit(solution)/shard_map/ppermute | solution.py:1591
  40.3 22.2 %collective-permute-start.10 = (bf16[32,6144]{1,0:T(8,128)(2,1)S(1)}, bf16[32,6144]{1,0:T(8,128)(2,1)S(1)}, u32[]{:S(2)}, u32[]{:S(2)}) collective-permute-start(bf16[32,6144]{1,0:T(8,128)(2,1)S(1)} %join_beside.3.refs_0_), channel_id=1, source_target_pairs={{0,24},{2,26},{4,28},{6,30},{8,0},{10,2},{12,4},{14,6},{16,8},{18,... | collective-permute-start | bytes 1179656 | tf_op jit(solution)/shard_map/ppermute | solution.py:1617
  40.3 23.5 %collective-permute-start.9 = (bf16[32,6144]{1,0:T(8,128)(2,1)S(1)}, bf16[32,6144]{1,0:T(8,128)(2,1)S(1)}, u32[]{:S(2)}, u32[]{:S(2)}) collective-permute-start(bf16[32,6144]{1,0:T(8,128)(2,1)S(1)} %join_beside.3.refs_0_), channel_id=1, source_target_pairs={{0,8},{2,10},{4,12},{6,14},{8,16},{10,18},{12,20},{14,22},{16,24},... | collective-permute-start | bytes 1179656 | tf_op jit(solution)/shard_map/ppermute | solution.py:1617
  61.2 18.0 %collective-permute-start.14 = (bf16[4,32,2176]{2,1,0:T(8,128)(2,1)S(1)}, bf16[4,32,2176]{2,1,0:T(8,128)(2,1)S(1)}, u32[]{:S(2)}, u32[]{:S(2)}) collective-permute-start(bf16[4,32,2176]{2,1,0:T(8,128)(2,1)S(1)} %get-tuple-element.422.refs_0_.refs_8_), channel_id=1, source_target_pairs={{0,1},{1,0},{2,3},{3,2},{4,5},{5,4},{6,7},{7,6},{8,9},{9,8},{10,11... | collective-permute-start | bytes 1671176 | tf_op jit(solution)/shard_map/ppermute | solution.py:1591
  68.4 17.8 %collective-permute-start.15 = (bf16[4,32,2176]{2,1,0:T(8,128)(2,1)S(1)}, bf16[4,32,2176]{2,1,0:T(8,128)(2,1)S(1)}, u32[]{:S(2)}, u32[]{:S(2)}) collective-permute-start(bf16[4,32,2176]{2,1,0:T(8,128)(2,1)S(1)} %collective-permute-done.8.refs_4_.refs_12_), channel_id=1, source_target_pairs={{0,1},{1,0},{2,3},{3,2},{4,5},{5,4},{6,7},{7,6},{8,9},{9,8},{10,11... | collective-permute-start | bytes 1671176 | tf_op jit(solution)/shard_map/ppermute | solution.py:1591
  68.9 17.1 %collective-permute-start.13 = (bf16[4,32,2048]{2,1,0:T(8,128)(2,1)}, bf16[4,32,2048]{2,1,0:T(8,128)(2,1)S(1)}, u32[]{:S(2)}, u32[]{:S(2)}) collective-permute-start(bf16[4,32,2048]{2,1,0:T(8,128)(2,1)} %collective-permute-done.7.refs_1_), channel_id=1, source_target_pairs={{0,4},{2,6},{4,0},{6,2},{8,12},{10,14},{12,8},{14,10},{16,20},{18,... | collective-permute-start | bytes 1572872 | tf_op jit(solution)/shard_map/ppermute | solution.py:1591
  89.9 39.2 %collective-permute-start.25 = (bf16[4,32,6144]{2,1,0:T(8,128)(2,1)S(1)}, bf16[4,32,6144]{2,1,0:T(8,128)(2,1)}, u32[]{:S(2)}, u32[]{:S(2)}) collective-permute-start(bf16[4,32,6144]{2,1,0:T(8,128)(2,1)S(1)} %join_up.1.refs_0_), channel_id=1, source_target_pairs={{0,1},{1,0},{2,3},{3,2},{4,5},{5,4},{6,7},{7,6},{8,9},{9,8},{10,11... | collective-permute-start | bytes 4718600 | tf_op jit(solution)/shard_map/ppermute | solution.py:1591
  91.6 37.5 %collective-permute-start.26 = (bf16[4,32,6144]{2,1,0:T(8,128)(2,1)S(1)}, bf16[4,32,6144]{2,1,0:T(8,128)(2,1)}, u32[]{:S(2)}, u32[]{:S(2)}) collective-permute-start(bf16[4,32,6144]{2,1,0:T(8,128)(2,1)S(1)} %join_up.1.refs_0_), channel_id=1, source_target_pairs={{0,4},{2,6},{4,0},{6,2},{8,12},{10,14},{12,8},{14,10},{16,20},{18,... | collective-permute-start | bytes 4718600 | tf_op jit(solution)/shard_map/ppermute | solution.py:1591
  95.1 34.0 %collective-permute-start.27 = (bf16[2,2,64,1024]{3,2,1,0:T(8,128)(2,1)}, bf16[2,2,64,1024]{3,2,1,0:T(8,128)(2,1)S(1)}, u32[]{:S(2)}, u32[]{:S(2)}) collective-permute-start(bf16[2,2,64,1024]{3,2,1,0:T(8,128)(2,1)} %join_plane.1.refs_8_), channel_id=1, source_target_pairs={{0,8},{2,10},{4,12},{6,14},{8,16},{10,18},{12,20},{14,22},{16,24},... | collective-permute-start | bytes 1572872 | tf_op jit(solution)/shard_map/ppermute | solution.py:1617
  95.9 33.2 %collective-permute-start.28 = (bf16[2,2,64,1024]{3,2,1,0:T(8,128)(2,1)}, bf16[2,2,64,1024]{3,2,1,0:T(8,128)(2,1)}, u32[]{:S(2)}, u32[]{:S(2)}) collective-permute-start(bf16[2,2,64,1024]{3,2,1,0:T(8,128)(2,1)} %join_plane.1.refs_8_), channel_id=1, source_target_pairs={{0,24},{2,26},{4,28},{6,30},{8,0},{10,2},{12,4},{14,6},{16,8},{18,... | collective-permute-start | bytes 1572872 | tf_op jit(solution)/shard_map/ppermute | solution.py:1617
  97.3 56.5 %collective-permute-start.30 = (bf16[4,32,6144]{2,1,0:T(8,128)(2,1)S(1)}, bf16[4,32,6144]{2,1,0:T(8,128)(2,1)}, u32[]{:S(2)}, u32[]{:S(2)}) collective-permute-start(bf16[4,32,6144]{2,1,0:T(8,128)(2,1)S(1)} %join_up.1.refs_0_), channel_id=1, source_target_pairs={{0,2},{2,0},{4,6},{6,4},{8,10},{10,8},{12,14},{14,12},{16,18},{18,... | collective-permute-start | bytes 4718600 | tf_op jit(solution)/shard_map/ppermute | solution.py:1591
  129.1 25.9 %collective-permute-start.31 = (bf16[4,32,6144]{2,1,0:T(8,128)(2,1)}, bf16[4,32,6144]{2,1,0:T(8,128)(2,1)}, u32[]{:S(2)}, u32[]{:S(2)}) collective-permute-start(bf16[4,32,6144]{2,1,0:T(8,128)(2,1)} %collective-permute-done.25.refs_1_), channel_id=1, source_target_pairs={{0,2},{2,0},{4,6},{6,4},{8,10},{10,8},{12,14},{14,12},{16,18},{18,... | collective-permute-start | bytes 4718600 | tf_op jit(solution)/shard_map/ppermute | solution.py:1591
  129.6 25.4 %collective-permute-start.29 = (bf16[512,1024]{1,0:T(8,128)(2,1)}, bf16[512,1024]{1,0:T(8,128)(2,1)S(1)}, u32[]{:S(2)}, u32[]{:S(2)}) collective-permute-start(bf16[512,1024]{1,0:T(8,128)(2,1)} %cast_far.3), channel_id=1, source_target_pairs={{0,1},{1,0},{2,3},{3,2},{4,5},{5,4},{6,7},{7,6},{8,9},{9,8},{10,11... | collective-permute-start | bytes 3145736 | tf_op jit(solution)/shard_map/ppermute | solution.py:1591
  130.8 23.0 %collective-permute-start.32 = (bf16[2,2,64,1024]{3,2,1,0:T(8,128)(2,1)}, bf16[2,2,64,1024]{3,2,1,0:T(8,128)(2,1)S(1)}, u32[]{:S(2)}, u32[]{:S(2)}) collective-permute-start(bf16[2,2,64,1024]{3,2,1,0:T(8,128)(2,1)} %join_plane.1.refs_8_), channel_id=1, source_target_pairs={{0,16},{2,18},{4,20},{6,22},{8,24},{10,26},{12,28},{14,30},{16,0},... | collective-permute-start | bytes 1572872 | tf_op jit(solution)/shard_map/ppermute | solution.py:1617
  130.8 36.4 %collective-permute-start.33 = (bf16[4,32,6144]{2,1,0:T(8,128)(2,1)}, bf16[4,32,6144]{2,1,0:T(8,128)(2,1)}, u32[]{:S(2)}, u32[]{:S(2)}) collective-permute-start(bf16[4,32,6144]{2,1,0:T(8,128)(2,1)} %collective-permute-done.25.refs_1_), channel_id=1, source_target_pairs={{0,4},{2,6},{4,0},{6,2},{8,12},{10,14},{12,8},{14,10},{16,20},{18,... | collective-permute-start | bytes 4718600 | tf_op jit(solution)/shard_map/ppermute | solution.py:1591
  211.1 22.0 %collective-permute-start.40 = (bf16[4,256,1024]{2,1,0:T(8,128)(2,1)}, bf16[4,256,1024]{2,1,0:T(8,128)(2,1)S(1)}, u32[]{:S(2)}, u32[]{:S(2)}) collective-permute-start(bf16[4,256,1024]{2,1,0:T(8,128)(2,1)} %get-tuple-element.496), channel_id=1, source_target_pairs={{0,2},{2,0},{4,6},{6,4},{8,10},{10,8},{12,14},{14,12},{16,18},{18,... | collective-permute-start | bytes 6291464 | tf_op jit(solution)/shard_map/ppermute | solution.py:1591
  211.3 21.8 %collective-permute-start.41 = (bf16[8,64,2048]{2,1,0:T(8,128)(2,1)}, bf16[8,64,2048]{2,1,0:T(8,128)(2,1)S(1)}, u32[]{:S(2)}, u32[]{:S(2)}) collective-permute-start(bf16[8,64,2048]{2,1,0:T(8,128)(2,1)} %get-tuple-element.502), channel_id=1, source_target_pairs={{0,2},{2,0},{4,6},{6,4},{8,10},{10,8},{12,14},{14,12},{16,18},{18,... | collective-permute-start | bytes 6291464 | tf_op jit(solution)/shard_map/ppermute | solution.py:1591
  232.9 34.8 %collective-permute-start.43 = (bf16[2,256,1024]{2,1,0:T(8,128)(2,1)}, bf16[2,256,1024]{2,1,0:T(8,128)(2,1)}, u32[]{:S(2)}, u32[]{:S(2)}) collective-permute-start(bf16[2,256,1024]{2,1,0:T(8,128)(2,1)} %get-tuple-element.517), channel_id=1, source_target_pairs={{0,2},{2,0},{4,6},{6,4},{8,10},{10,8},{12,14},{14,12},{16,18},{18,... | collective-permute-start | bytes 3145736 | tf_op jit(solution)/shard_map/ppermute | solution.py:1591
  239.3 27.4 %collective-permute-start.42 = (bf16[2,256,1024]{2,1,0:T(8,128)(2,1)}, bf16[2,256,1024]{2,1,0:T(8,128)(2,1)S(1)}, u32[]{:S(2)}, u32[]{:S(2)}) collective-permute-start(bf16[2,256,1024]{2,1,0:T(8,128)(2,1)} %get-tuple-element.513), channel_id=1, source_target_pairs={{0,4},{2,6},{4,0},{6,2},{8,12},{10,14},{12,8},{14,10},{16,20},{18,... | collective-permute-start | bytes 3145736 | tf_op jit(solution)/shard_map/ppermute | solution.py:1591
  240.0 27.7 %collective-permute-start.44 = (bf16[8,32,2048]{2,1,0:T(8,128)(2,1)}, bf16[8,32,2048]{2,1,0:T(8,128)(2,1)S(1)}, u32[]{:S(2)}, u32[]{:S(2)}) collective-permute-start(bf16[8,32,2048]{2,1,0:T(8,128)(2,1)} %get-tuple-element.519), channel_id=1, source_target_pairs={{0,1},{1,0},{2,3},{3,2},{4,5},{5,4},{6,7},{7,6},{8,9},{9,8},{10,11... | collective-permute-start | bytes 3145736 | tf_op jit(solution)/shard_map/ppermute | solution.py:1591
  266.1 27.8 %collective-permute-start.47 = (bf16[8,64,2048]{2,1,0:T(8,128)(2,1)}, bf16[8,64,2048]{2,1,0:T(8,128)(2,1)}, u32[]{:S(2)}, u32[]{:S(2)}) collective-permute-start(bf16[8,64,2048]{2,1,0:T(8,128)(2,1)} %get-tuple-element.544), channel_id=1, source_target_pairs={{0,2},{2,0},{4,6},{6,4},{8,10},{10,8},{12,14},{14,12},{16,18},{18,... | collective-permute-start | bytes 6291464 | tf_op jit(solution)/shard_map/ppermute | solution.py:1591
  266.2 25.5 %collective-permute-start.46 = (bf16[2,256,1024]{2,1,0:T(8,128)(2,1)}, bf16[2,256,1024]{2,1,0:T(8,128)(2,1)}, u32[]{:S(2)}, u32[]{:S(2)}) collective-permute-start(bf16[2,256,1024]{2,1,0:T(8,128)(2,1)} %get-tuple-element.535), channel_id=1, source_target_pairs={{0,2},{2,0},{4,6},{6,4},{8,10},{10,8},{12,14},{14,12},{16,18},{18,... | collective-permute-start | bytes 3145736 | tf_op jit(solution)/shard_map/ppermute | solution.py:1591
  270.4 21.2 %collective-permute-start.45 = (bf16[1,256,1024]{2,1,0:T(8,128)(2,1)}, bf16[1,256,1024]{2,1,0:T(8,128)(2,1)}, u32[]{:S(2)}, u32[]{:S(2)}) collective-permute-start(bf16[1,256,1024]{2,1,0:T(8,128)(2,1)} %get-tuple-element.527), channel_id=1, source_target_pairs={{0,4},{2,6},{4,0},{6,2},{8,12},{10,14},{12,8},{14,10},{16,20},{18,... | collective-permute-start | bytes 1572872 | tf_op jit(solution)/shard_map/ppermute | solution.py:1591
  294.0 28.1 %collective-permute-start.50 = (bf16[512,1024]{1,0:T(8,128)(2,1)}, bf16[512,1024]{1,0:T(8,128)(2,1)S(1)}, u32[]{:S(2)}, u32[]{:S(2)}) collective-permute-start(bf16[512,1024]{1,0:T(8,128)(2,1)} %copy-done.93), channel_id=1, source_target_pairs={{0,1},{1,0},{2,3},{3,2},{4,5},{5,4},{6,7},{7,6},{8,9},{9,8},{10,11... | collective-permute-start | bytes 3145736 | tf_op jit(solution)/shard_map/ppermute | solution.py:1591
  294.9 31.5 %collective-permute-start.51 = (bf16[8,64,1024]{2,1,0:T(8,128)(2,1)S(1)}, bf16[8,64,1024]{2,1,0:T(8,128)(2,1)S(1)}, u32[]{:S(2)}, u32[]{:S(2)}) collective-permute-start(bf16[8,64,1024]{2,1,0:T(8,128)(2,1)S(1)} %get-tuple-element.577), channel_id=1, source_target_pairs={{0,2},{2,0},{4,6},{6,4},{8,10},{10,8},{12,14},{14,12},{16,18},{18,... | collective-permute-start | bytes 3145736 | tf_op jit(solution)/shard_map/ppermute | solution.py:1591
  294.9 27.1 %collective-permute-start.49 = (bf16[4,32,2048]{2,1,0:T(8,128)(2,1)S(1)}, bf16[4,32,2048]{2,1,0:T(8,128)(2,1)S(1)}, u32[]{:S(2)}, u32[]{:S(2)}) collective-permute-start(bf16[4,32,2048]{2,1,0:T(8,128)(2,1)S(1)} %get-tuple-element.551), channel_id=1, source_target_pairs={{0,4},{2,6},{4,0},{6,2},{8,12},{10,14},{12,8},{14,10},{16,20},{18,... | collective-permute-start | bytes 1572872 | tf_op jit(solution)/shard_map/ppermute | solution.py:1591
  295.6 26.5 %collective-permute-start.48 = (bf16[1,256,1024]{2,1,0:T(8,128)(2,1)S(1)}, bf16[1,256,1024]{2,1,0:T(8,128)(2,1)S(1)}, u32[]{:S(2)}, u32[]{:S(2)}) collective-permute-start(bf16[1,256,1024]{2,1,0:T(8,128)(2,1)S(1)} %get-tuple-element.549), channel_id=1, source_target_pairs={{0,4},{2,6},{4,0},{6,2},{8,12},{10,14},{12,8},{14,10},{16,20},{18,... | collective-permute-start | bytes 1572872 | tf_op jit(solution)/shard_map/ppermute | solution.py:1591
  300.1 53.3 %collective-permute-start.53 = (bf16[4,64,2048]{2,1,0:T(8,128)(2,1)S(1)}, bf16[4,64,2048]{2,1,0:T(8,128)(2,1)S(1)}, u32[]{:S(2)}, u32[]{:S(2)}) collective-permute-start(bf16[4,64,2048]{2,1,0:T(8,128)(2,1)S(1)} %get-tuple-element.590), channel_id=1, source_target_pairs={{0,4},{2,6},{4,0},{6,2},{8,12},{10,14},{12,8},{14,10},{16,20},{18,... | collective-permute-start | bytes 3145736 | tf_op jit(solution)/shard_map/ppermute | solution.py:1591
  325.1 31.7 %collective-permute-start.57 = (bf16[4,128,1024]{2,1,0:T(8,128)(2,1)S(1)}, bf16[4,128,1024]{2,1,0:T(8,128)(2,1)S(1)}, u32[]{:S(2)}, u32[]{:S(2)}) collective-permute-start(bf16[4,128,1024]{2,1,0:T(8,128)(2,1)S(1)} %get-tuple-element.608), channel_id=1, source_target_pairs={{0,1},{1,0},{2,3},{3,2},{4,5},{5,4},{6,7},{7,6},{8,9},{9,8},{10,11... | collective-permute-start | bytes 3145736 | tf_op jit(solution)/shard_map/ppermute | solution.py:1591
  327.9 25.5 %collective-permute-start.54 = (bf16[32,2048]{1,0:T(8,128)(2,1)S(1)}, bf16[32,2048]{1,0:T(8,128)(2,1)S(1)}, u32[]{:S(2)}, u32[]{:S(2)}) collective-permute-start(bf16[32,2048]{1,0:T(8,128)(2,1)S(1)} %get-tuple-element.592), channel_id=1, source_target_pairs={{0,8},{2,10},{4,12},{6,14},{8,16},{10,18},{12,20},{14,22},{16,24},... | collective-permute-start | bytes 393224 | tf_op jit(solution)/shard_map/ppermute | solution.py:1617
  329.1 24.3 %collective-permute-start.55 = (bf16[32,2048]{1,0:T(8,128)(2,1)S(1)}, bf16[32,2048]{1,0:T(8,128)(2,1)S(1)}, u32[]{:S(2)}, u32[]{:S(2)}) collective-permute-start(bf16[32,2048]{1,0:T(8,128)(2,1)S(1)} %get-tuple-element.593), channel_id=1, source_target_pairs={{0,16},{2,18},{4,20},{6,22},{8,24},{10,26},{12,28},{14,30},{16,0},... | collective-permute-start | bytes 393224 | tf_op jit(solution)/shard_map/ppermute | solution.py:1617
  332.0 21.4 %collective-permute-start.56 = (bf16[32,2048]{1,0:T(8,128)(2,1)S(1)}, bf16[32,2048]{1,0:T(8,128)(2,1)S(1)}, u32[]{:S(2)}, u32[]{:S(2)}) collective-permute-start(bf16[32,2048]{1,0:T(8,128)(2,1)S(1)} %get-tuple-element.594), channel_id=1, source_target_pairs={{0,24},{2,26},{4,28},{6,30},{8,0},{10,2},{12,4},{14,6},{16,8},{18,... | collective-permute-start | bytes 393224 | tf_op jit(solution)/shard_map/ppermute | solution.py:1617
  378.2 21.7 %collective-permute-start.62 = (bf16[4,64,1536]{2,1,0:T(8,128)(2,1)S(1)}, bf16[4,64,1536]{2,1,0:T(8,128)(2,1)S(1)}, u32[]{:S(2)}, u32[]{:S(2)}) collective-permute-start(bf16[4,64,1536]{2,1,0:T(8,128)(2,1)S(1)} %get-tuple-element.673), channel_id=1, source_target_pairs={{0,4},{2,6},{4,0},{6,2},{8,12},{10,14},{12,8},{14,10},{16,20},{18,... | collective-permute-start | bytes 2359304 | tf_op jit(solution)/shard_map/ppermute | solution.py:1591
  380.7 19.2 %collective-permute-start.63 = (bf16[8,32,1536]{2,1,0:T(8,128)(2,1)S(1)}, bf16[8,32,1536]{2,1,0:T(8,128)(2,1)S(1)}, u32[]{:S(2)}, u32[]{:S(2)}) collective-permute-start(bf16[8,32,1536]{2,1,0:T(8,128)(2,1)S(1)} %get-tuple-element.683), channel_id=1, source_target_pairs={{0,1},{1,0},{2,3},{3,2},{4,5},{5,4},{6,7},{7,6},{8,9},{9,8},{10,11... | collective-permute-start | bytes 2359304 | tf_op jit(solution)/shard_map/ppermute | solution.py:1591
  382.6 32.2 %collective-permute-start.65 = (bf16[32,7168]{1,0:T(8,128)(2,1)S(1)}, bf16[32,7168]{1,0:T(8,128)(2,1)S(1)}, u32[]{:S(2)}, u32[]{:S(2)}) collective-permute-start(bf16[32,7168]{1,0:T(8,128)(2,1)S(1)} %get-tuple-element.693), channel_id=1, source_target_pairs={{0,8},{2,10},{4,12},{6,14},{8,16},{10,18},{12,20},{14,22},{16,24},... | collective-permute-start | bytes 1376264 | tf_op jit(solution)/shard_map/ppermute | solution.py:1617
  384.2 38.1 %collective-permute-start.66 = (bf16[32,7168]{1,0:T(8,128)(2,1)S(1)}, bf16[32,7168]{1,0:T(8,128)(2,1)S(1)}, u32[]{:S(2)}, u32[]{:S(2)}) collective-permute-start(bf16[32,7168]{1,0:T(8,128)(2,1)S(1)} %get-tuple-element.694), channel_id=1, source_target_pairs={{0,16},{2,18},{4,20},{6,22},{8,24},{10,26},{12,28},{14,30},{16,0},... | collective-permute-start | bytes 1376264 | tf_op jit(solution)/shard_map/ppermute | solution.py:1617
  386.3 38.2 %collective-permute-start.67 = (bf16[32,7168]{1,0:T(8,128)(2,1)S(1)}, bf16[32,7168]{1,0:T(8,128)(2,1)S(1)}, u32[]{:S(2)}, u32[]{:S(2)}) collective-permute-start(bf16[32,7168]{1,0:T(8,128)(2,1)S(1)} %get-tuple-element.695), channel_id=1, source_target_pairs={{0,24},{2,26},{4,28},{6,30},{8,0},{10,2},{12,4},{14,6},{16,8},{18,... | collective-permute-start | bytes 1376264 | tf_op jit(solution)/shard_map/ppermute | solution.py:1617
  401.8 28.5 %collective-permute-start.64 = (bf16[4,32,1536]{2,1,0:T(8,128)(2,1)S(1)}, bf16[4,32,1536]{2,1,0:T(8,128)(2,1)S(1)}, u32[]{:S(2)}, u32[]{:S(2)}) collective-permute-start(bf16[4,32,1536]{2,1,0:T(8,128)(2,1)S(1)} %get-tuple-element.691), channel_id=1, source_target_pairs={{0,1},{1,0},{2,3},{3,2},{4,5},{5,4},{6,7},{7,6},{8,9},{9,8},{10,11... | collective-permute-start | bytes 1179656 | tf_op jit(solution)/shard_map/ppermute | solution.py:1591
  403.0 27.3 %collective-permute-start.68 = (bf16[4,32,1536]{2,1,0:T(8,128)(2,1)S(1)}, bf16[4,32,1536]{2,1,0:T(8,128)(2,1)S(1)}, u32[]{:S(2)}, u32[]{:S(2)}) collective-permute-start(bf16[4,32,1536]{2,1,0:T(8,128)(2,1)S(1)} %get-tuple-element.701), channel_id=1, source_target_pairs={{0,4},{2,6},{4,0},{6,2},{8,12},{10,14},{12,8},{14,10},{16,20},{18,... | collective-permute-start | bytes 1179656 | tf_op jit(solution)/shard_map/ppermute | solution.py:1591
  430.3 23.7 %collective-permute-start.73 = (bf16[512,1024]{1,0:T(8,128)(2,1)}, bf16[512,1024]{1,0:T(8,128)(2,1)S(1)}, u32[]{:S(2)}, u32[]{:S(2)}) collective-permute-start(bf16[512,1024]{1,0:T(8,128)(2,1)} %get-tuple-element.722), channel_id=1, source_target_pairs={{0,1},{1,0},{2,3},{3,2},{4,5},{5,4},{6,7},{7,6},{8,9},{9,8},{10,11... | collective-permute-start | bytes 3145736 | tf_op jit(solution)/shard_map/ppermute | solution.py:1591
  433.7 22.3 %collective-permute-start.74 = (bf16[32,3200]{1,0:T(8,128)(2,1)}, bf16[32,3200]{1,0:T(8,128)(2,1)S(1)}, u32[]{:S(2)}, u32[]{:S(2)}) collective-permute-start(bf16[32,3200]{1,0:T(8,128)(2,1)} %get-tuple-element.730), channel_id=1, source_target_pairs={{0,8},{2,10},{4,12},{6,14},{8,16},{10,18},{12,20},{14,22},{16,24},... | collective-permute-start | bytes 614408 | tf_op jit(solution)/shard_map/ppermute | solution.py:1617
  433.7 22.3 %collective-permute-start.75 = (bf16[32,3200]{1,0:T(8,128)(2,1)}, bf16[32,3200]{1,0:T(8,128)(2,1)}, u32[]{:S(2)}, u32[]{:S(2)}) collective-permute-start(bf16[32,3200]{1,0:T(8,128)(2,1)} %get-tuple-element.731), channel_id=1, source_target_pairs={{0,16},{2,18},{4,20},{6,22},{8,24},{10,26},{12,28},{14,30},{16,0},... | collective-permute-start | bytes 614408 | tf_op jit(solution)/shard_map/ppermute | solution.py:1617
  436.7 19.3 %collective-permute-start.76 = (bf16[32,3200]{1,0:T(8,128)(2,1)}, bf16[32,3200]{1,0:T(8,128)(2,1)}, u32[]{:S(2)}, u32[]{:S(2)}) collective-permute-start(bf16[32,3200]{1,0:T(8,128)(2,1)} %get-tuple-element.732), channel_id=1, source_target_pairs={{0,24},{2,26},{4,28},{6,30},{8,0},{10,2},{12,4},{14,6},{16,8},{18,... | collective-permute-start | bytes 614408 | tf_op jit(solution)/shard_map/ppermute | solution.py:1617
  (149 other events, 1335.8 us)

commit v5 on v4

--- a/solution.py
+++ b/solution.py
@@ -1607,11 +1607,6 @@
     return pair_swap(value, "seq", 1)
 
 
-def swap_xy(value):
-    pairs = 2 * lax.axis_size("dp")
-    return lax.ppermute(value, BOTH, [(i, i ^ 5) for i in range(pairs)])
-
-
 def ring_z(value, step):
     size = lax.axis_size("dp")
     return lax.ppermute(value, "dp", [(i, (i + 4 * step) % size) for i in range(size)])
@@ -1788,7 +1783,7 @@
     normed_low, qkv = norm_project(
         place, inputs, far_rows, ln1_gain, ln1_bias, left_parts, right_parts, qkv_bias
     )
-    near_pairs = 3 * pairs // 8
+    near_pairs = 2 * pairs // 8
     attended = attn_forward(place, qkv, bias, 0, near_pairs)
     attended, up_y, up_x, planes, far_grad_low = tie(attended, up_y, up_x, planes, far_grad_low)
     up_xy = swap_x(up_y)
@@ -1935,12 +1930,13 @@
     )
     packed = jnp.concatenate(grad_vectors, axis=1).reshape(-1, PAIR)
     packed = packed + swap_core(packed)
-    packed = packed + swap_x(packed) + swap_y(packed) + swap_xy(packed)
+    packed = packed + swap_y(packed)
     (in_delta,) = down_sum.hold(in_delta)
     (in_delta,) = left_sum.hold(in_delta)
     (in_delta,) = right_sum.hold(in_delta)
     packed, in_delta = tie(packed, in_delta)
     in_far = swap_y(in_delta)
+    packed = packed + swap_x(packed)
     left_sum.third(right_sum, vectors=packed, sizes=sizes)
     left_sum.mine, out_far, down_sum.mine = tie(left_sum.mine, out_far, down_sum.mine)
     grad_w_down, grad_w_up, grad_w_out = down_sum.last(

time: 465 us -> 460 us (0.989)
  transfers between devices with their start and end apart: 77 -> 76, of which waited for: 25 -> 27; matrix products, arithmetic and copies ran while one was open for 2% -> 2% of each run, Pallas kernels for 48% -> 48%
where the time goes in v5:
time: 460 us; the launch traced here: 456 us
  Pallas kernels  265 us (58%)
  waiting for transfers between devices  83.6 us (18%)
  starting transfers between devices  60.1 us (13%)
  local copies, waits for them, and re-layouts  42.5 us (9%)
    pallas_call x44, Pallas kernels, call(): pl.pallas_call(body, grid_spec=spec, out_shape=out_shape, name=name, inpu...  265 us
    ppermute x58, waiting for transfers between devices, pair_swap(): return lax.ppermute(value, axis, [(i, i ^ bit) for i in range(size)])  47.2 us
    ppermute x58, starting transfers between devices, pair_swap(): return lax.ppermute(value, axis, [(i, i ^ bit) for i in range(size)])  40.5 us
    ppermute x18, waiting for transfers between devices, ring_z(): lax.ppermute(value, 'dp', [(i, (i + 4 * step) % size) for i in range(size)])  36.4 us
    unnamed x251, local copies, waits for them, and re-layouts  34.3 us
    ppermute x18, starting transfers between devices, ring_z(): lax.ppermute(value, 'dp', [(i, (i + 4 * step) % size) for i in range(size)])  19.6 us
  transfers between devices with their start and end apart: 76, of which 27 were waited for; matrix products, arithmetic and copies ran while one was open for 2% of the time, Pallas kernels for 48%

profile of v5, /device:TPU:8, one launch (start us, length us, event | category | flops | bytes accessed | tf_op | source)
XLA Modules:
  0.0 455.5 jit_solution(9617818270127839717)
XLA Ops:
  3.0 2.2 copy-done
  10.4 1.8 collective-permute-start.2
  18.2 9.4 %collective-permute-done.refs_1_ = bf16[32,4224]{1,0:T(8,128)(2,1)S(1)} collective-permute-done((bf16[32,4224]{1,0:T(8,128)(2,1)S(1)}, bf16[32,4224]{1,0:T(8,128)(2,1)S(1)}, u32[]{:S(2)}, u32[]{:S(2)}) %collective-permute-start) | collective-permute-done | bytes 270368 | tf_op jit(solution)/shard_map/ppermute | solution.py:1612
  28.4 3.3 collective-permute-done.1.refs_2_
  31.7 1.9 collective-permute-done.2.refs_3_
  40.3 2.0 collective-permute-start.9
  42.9 12.3 %collective-permute-done.11.refs_2_ = bf16[64,1024]{1,0:T(8,128)(2,1)S(1)} collective-permute-done((bf16[64,1024]{1,0:T(8,128)(2,1)S(1)}, bf16[64,1024]{1,0:T(8,128)(2,1)S(1)}, u32[]{:S(2)}, u32[]{:S(2)}) %collective-permute-start.11) | collective-permute-done | bytes 131104 | tf_op jit(solution)/shard_map/ppermute | solution.py:1591
  56.7 2.2 copy-done.5
  65.8 1.7 copy.51
  72.9 2.3 join_plane.1.refs_8_
  75.2 4.0 collective-permute-done.16.refs_2_
  79.2 6.8 %collective-permute-done.13.refs_5_ = bf16[4,32,2048]{2,1,0:T(8,128)(2,1)S(1)} collective-permute-done((bf16[4,32,2048]{2,1,0:T(8,128)(2,1)}, bf16[4,32,2048]{2,1,0:T(8,128)(2,1)S(1)}, u32[]{:S(2)}, u32[]{:S(2)}) %collective-permute-start.13) | collective-permute-done | bytes 524320 | tf_op jit(solution)/shard_map/ppermute | solution.py:1591
  101.6 13.5 %norm_project.1 = (bf16[1024,1024]{1,0:T(8,128)(2,1)}, bf16[1024,3072]{1,0:T(8,128)(2,1)}) custom-call(s32[4]{0:T(128)} %copy-done.68, f32[1,1024]{1,0:T(1,128)} %copy-done.86, f32[1,1024]{1,0:T(1,128)} %copy-done.88, f32[1,3072]{1,0:T(1,128)} %pad_maximum_fusion.1.bias_ref, f32[2,512,1024]{2,1,0:T(8,128)} %base_ref.1, bf16[512,1024]{1,0:T(8,128)(2,1)} %copy-done.8, ...), custom_call_target="tpu_custom_call" | custom-call | flops 1200000000 | bytes 1 | tf_op jit(solution)/shard_map/norm_project/pallas_call | solution.py:464
  115.1 10.5 %attn_forward.2 = (bf16[16,1024,1024]{2,1,0:T(8,128)(2,1)}, bf16[1024,1024]{1,0:T(8,128)(2,1)}, f32[1024,1024]{1,0:T(8,128)}) custom-call(s32[4]{0:T(128)} %copy-done.68, bf16[1024,3072]{1,0:T(8,128)(2,1)} %get-tuple-element.448.refs_0_.refs_1_.refs_2_, bf16[1024,3072]{1,0:T(8,128)(2,1)} %get-tuple-element.448.refs_0_.refs_1_.refs_2_, ...), custom_call_target="tpu_custom_call" | custom-call | flops 300000000 | bytes 1 | tf_op jit(solution)/shard_map/attn_forward/pallas_call | solution.py:464
  126.4 1.7 collective-permute-done.26.refs_4_
  129.8 24.2 %attn_forward.3 = (bf16[16,1024,1024]{2,1,0:T(8,128)(2,1)}, bf16[1024,1024]{1,0:T(8,128)(2,1)}, f32[1024,1024]{1,0:T(8,128)}) custom-call(s32[4]{0:T(128)} %copy-done.68, bf16[1024,3072]{1,0:T(8,128)(2,1)} %get-tuple-element.448.refs_0_.refs_1_.refs_2_, ...), custom_call_target="tpu_custom_call", output_to_operand_aliasing={{0}: (5, {}), {1}: (6, {}), {2}: (7, {})} | custom-call | flops 900000000 | bytes 1 | tf_op jit(solution)/shard_map/attn_forward/pallas_call | solution.py:464
  157.5 8.8 %out_norm.1 = (f32[1024,1024]{1,0:T(8,128)}, bf16[1024,1024]{1,0:T(8,128)(2,1)}) custom-call(s32[4]{0:T(128)} %copy-done.68, f32[1,1024]{1,0:T(1,128)} %copy-done.90, f32[1,1024]{1,0:T(1,128)} %copy-done.89, f32[1,1024]{1,0:T(1,128)} %copy-done.91, bf16[1024,1024]{1,0:T(8,128)(2,1)} %get-tuple-element.469.mixed_in.left_ref.refs_4_, ...), custom_call_target="tpu_custom_call" | custom-call | flops 300000000 | bytes 1 | tf_op jit(solution)/shard_map/out_norm/pallas_call | solution.py:464
  167.0 3.4 collective-permute-done.39.refs_13_
  172.0 38.2 %feed_forward.3 = (bf16[4,256,1024]{2,1,0:T(8,128)(2,1)}, bf16[4,256,1024]{2,1,0:T(8,128)(2,1)}, bf16[8,64,2048]{2,1,0:T(8,128)(2,1)}, bf16[8,64,2048]{2,1,0:T(8...) custom-call(s32[4]{0:T(128)S(1)} %copy-done.70, ...), custom_call_target="tpu_custom_call" | custom-call | flops 10800000000 | bytes 1 | tf_op jit(solution)/shard_map/feed_forward/pallas_call | solution.py:464
  210.8 21.2 %feed_forward.4 = (bf16[2,256,1024]{2,1,0:T(8,128)(2,1)S(1)}, bf16[2,256,1024]{2,1,0:T(8,128)(2,1)}, bf16[8,64,2048]{2,1,0:T(8,128)(2,1)}, bf16[8,64,2048]{2,1,0...) custom-call(s32[4]{0:T(128)S(1)} %copy-done.70, ...), custom_call_target="tpu_custom_call" | custom-call | flops 5400000000 | bytes 1 | tf_op jit(solution)/shard_map/feed_forward/pallas_call | solution.py:464
  232.2 3.4 split_add.14
  236.6 1.9 split_add.13
  240.9 23.1 %feed_forward.5 = (bf16[2,256,1024]{2,1,0:T(8,128)(2,1)S(1)}, bf16[2,256,1024]{2,1,0:T(8,128)(2,1)}, bf16[8,64,2048]{2,1,0:T(8,128)(2,1)}, bf16[8,64,2048]{2,1,0...) custom-call(s32[4]{0:T(128)S(1)} %copy-done.70, ...), custom_call_target="tpu_custom_call", output_to_operand_aliasing={{2}: (24, {}), {3}: (25, {})} | custom-call | flops 5400000000 | bytes 1 | tf_op jit(solution)/shard_map/feed_forward/pallas_call | solution.py:464
  267.5 2.8 split_add.15
  270.9 10.9 %middle_back.1 = (f32[1024,1024]{1,0:T(8,128)}, bf16[1024,1024]{1,0:T(8,128)(2,1)}, bf16[1024,1024]{1,0:T(8,128)(2,1)}, f32[1,1024]{1,0:T(1,128)}, f32[1,1024]{1,0:T(1,128)}, /*index=5*/f32[1,1024]{1,0:T(1,128)}) custom-call(s32[4]{0:T(128)} %copy-done.68, f32[1,1024]{1,0:T(1,128)} %copy-done.89, f32[1024,1024]{1,0:T(8,128)} %get-tuple-element.528.grad_in, ...), custom_call_target="tpu_custom_call" | custom-call | flops 12000000000 | bytes 1 | tf_op jit(solution)/shard_map/middle_back/pallas_call | solution.py:464
  285.0 3.7 grad_wide.2
  290.9 2.2 split_add.16
  296.3 3.2 split_add.18
  301.0 21.1 %attn_backward.2 = (bf16[1024,1024]{1,0:T(8,128)(2,1)S(1)}, bf16[1024,1024]{1,0:T(8,128)(2,1)S(1)}, bf16[1024,1024]{1,0:T(8,128)(2,1)S(1)}) custom-call(s32[4]{0:T(128)S(1)} %copy-done.71, bf16[1024,3072]{1,0:T(8,128)(2,1)S(1)} %bitcast.66, bf16[1024,3072]{1,0:T(8,128)(2,1)S(1)} %bitcast.66, bf16[1024,3072]{1,0:T(8,128)(2,1)S(1)} %bitcast.66, ...), custom_call_target="tpu_custom_call" | custom-call | flops 6000000000 | bytes 1 | tf_op jit(solution)/shard_map/attn_backward/pallas_call | solution.py:464
  322.1 2.1 merge_add.1
  327.7 3.2 collective-permute-start.55
  330.9 1.8 collective-permute-start.56
  332.8 20.9 %attn_backward.3 = (bf16[1024,1024]{1,0:T(8,128)(2,1)S(1)}, bf16[1024,1024]{1,0:T(8,128)(2,1)S(1)}, bf16[1024,1024]{1,0:T(8,128)(2,1)S(1)}) custom-call(s32[4]{0:T(128)S(1)} %copy-done.71, bf16[1024,3072]{1,0:T(8,128)(2,1)S(1)} %bitcast.66, bf16[1024,3072]{1,0:T(8,128)(2,1)S(1)} %bitcast.66, ...), custom_call_target="tpu_custom_call", output_to_operand_aliasing={{0}: (8, {}), {1}: (9, {}), {2}: (10, {})} | custom-call | flops 6000000000 | bytes 1 | tf_op jit(solution)/shard_map/attn_backward/pallas_call | solution.py:464
  356.4 10.3 %grad_wide.3 = (bf16[8,64,1536]{2,1,0:T(8,128)(2,1)S(1)}, bf16[8,64,1536]{2,1,0:T(8,128)(2,1)S(1)}, bf16[8,64,1536]{2,1,0:T(8,128)(2,1)S(1)}, bf16[8,64,1536]{2,1,0:T(8,128)(2,1)S(1)}) custom-call(s32[4]{0:T(128)S(1)} %copy-done.71, bf16[1024,1024]{1,0:T(8,128)(2,1)S(1)} %copy-done.92, bf16[1024,1024]{1,0:T(8,128)(2,1)S(1)} %get-tuple-element.674.refs_0_.query_in, ...), custom_call_target="tpu_custom_call" | custom-call | flops 3240000000 | bytes 1 | tf_op jit(solution)/shard_map/grad_wide/pallas_call | solution.py:464
  370.7 6.7 %collective-permute-done.60.refs_5_ = bf16[4,32,1024]{2,1,0:T(8,128)(2,1)S(1)} collective-permute-done((bf16[4,32,1024]{2,1,0:T(8,128)(2,1)S(1)}, bf16[4,32,1024]{2,1,0:T(8,128)(2,1)S(1)}, u32[]{:S(2)}, u32[]{:S(2)}) %collective-permute-start.60) | collective-permute-done | bytes 262176 | tf_op jit(solution)/shard_map/ppermute | solution.py:1591
  382.7 2.3 collective-permute-start.66
  385.1 13.4 %input_back.1 = (f32[2,512,1024]{2,1,0:T(8,128)}, bf16[512,1024]{1,0:T(8,128)(2,1)}, f32[1,1024]{1,0:T(1,128)S(1)}, f32[1,1024]{1,0:T(1,128)S(1)}, f32[1,1024]{1,0:T(1,128)S(1)}, /*index=5*/f32[1,1024]{1,0:T(1,128)S(1)}) custom-call(s32[4]{0:T(128)S(1)} %copy-done.71, f32[1,1024]{1,0:T(1,128)S(1)} %copy-done.87, ...), custom_call_target="tpu_custom_call" | custom-call | flops 300000000 | bytes 1 | tf_op jit(solution)/shard_map/input_back/pallas_call | solution.py:464
  403.3 10.1 %collective-permute-done.65.refs_0_ = bf16[32,7168]{1,0:T(8,128)(2,1)S(1)} collective-permute-done((bf16[32,7168]{1,0:T(8,128)(2,1)S(1)}, bf16[32,7168]{1,0:T(8,128)(2,1)S(1)}, u32[]{:S(2)}, u32[]{:S(2)}) %collective-permute-start.65) | collective-permute-done | bytes 458784 | tf_op jit(solution)/shard_map/ppermute | solution.py:1612
  415.2 5.6 %collective-permute-done.66.refs_1_ = bf16[32,7168]{1,0:T(8,128)(2,1)S(1)} collective-permute-done((bf16[32,7168]{1,0:T(8,128)(2,1)S(1)}, bf16[32,7168]{1,0:T(8,128)(2,1)S(1)}, u32[]{:S(2)}, u32[]{:S(2)}) %collective-permute-start.66) | collective-permute-done | bytes 458784 | tf_op jit(solution)/shard_map/ppermute | solution.py:1612
  421.6 2.0 collective-permute-done.67.refs_2_
  426.9 2.7 collective-permute-done.71
  433.3 2.0 collective-permute-start.75
  438.4 1.7 last_add.4
  440.0 2.2 copy-done.1
  442.2 2.0 fill_far.2
  444.2 5.5 %collective-permute-done.72.delta_ref = bf16[512,1024]{1,0:T(8,128)(2,1)S(1)} collective-permute-done((bf16[512,1024]{1,0:T(8,128)(2,1)}, bf16[512,1024]{1,0:T(8,128)(2,1)S(1)}, u32[]{:S(2)}, u32[]{:S(2)}) %collective-permute-start.72) | collective-permute-done | bytes 1048608 | tf_op jit(solution)/shard_map/ppermute | solution.py:1591
  449.8 2.0 fill_far.3
  451.8 2.3 last_add.5
  (431 shorter events, 110.7 us)
Async XLA Ops:
  6.0 27.6 %collective-permute-start.5 = (bf16[512,1024]{1,0:T(8,128)(2,1)S(1)}, bf16[512,1024]{1,0:T(8,128)(2,1)S(1)}, u32[]{:S(2)}, u32[]{:S(2)}) collective-permute-start(bf16[512,1024]{1,0:T(8,128)(2,1)S(1)} %cast_far.2), channel_id=1, source_target_pairs={{0,1},{1,0},{2,3},{3,2},{4,5},{5,4},{6,7},{7,6},{8,9},{9,8},{10,11... | collective-permute-start | bytes 3145736 | tf_op jit(solution)/shard_map/ppermute | solution.py:1591
  7.5 20.2 %collective-permute-start = (bf16[32,4224]{1,0:T(8,128)(2,1)S(1)}, bf16[32,4224]{1,0:T(8,128)(2,1)S(1)}, u32[]{:S(2)}, u32[]{:S(2)}) collective-permute-start(bf16[32,4224]{1,0:T(8,128)(2,1)S(1)} %join_beside.2.refs_0_), channel_id=1, source_target_pairs={{0,8},{2,10},{4,12},{6,14},{8,16},{10,18},{12,20},{14,22},{16,24},... | collective-permute-start | bytes 811016 | tf_op jit(solution)/shard_map/ppermute | solution.py:1612
  9.2 22.6 %collective-permute-start.1 = (bf16[32,4224]{1,0:T(8,128)(2,1)S(1)}, bf16[32,4224]{1,0:T(8,128)(2,1)}, u32[]{:S(2)}, u32[]{:S(2)}) collective-permute-start(bf16[32,4224]{1,0:T(8,128)(2,1)S(1)} %join_beside.2.refs_0_), channel_id=1, source_target_pairs={{0,16},{2,18},{4,20},{6,22},{8,24},{10,26},{12,28},{14,30},{16,0},... | collective-permute-start | bytes 811016 | tf_op jit(solution)/shard_map/ppermute | solution.py:1612
  10.4 23.2 %collective-permute-start.2 = (bf16[32,4224]{1,0:T(8,128)(2,1)S(1)}, bf16[32,4224]{1,0:T(8,128)(2,1)}, u32[]{:S(2)}, u32[]{:S(2)}) collective-permute-start(bf16[32,4224]{1,0:T(8,128)(2,1)S(1)} %join_beside.2.refs_0_), channel_id=1, source_target_pairs={{0,24},{2,26},{4,28},{6,30},{8,0},{10,2},{12,4},{14,6},{16,8},{18,... | collective-permute-start | bytes 811016 | tf_op jit(solution)/shard_map/ppermute | solution.py:1612
  37.2 27.6 %collective-permute-start.8 = (bf16[4,32,2176]{2,1,0:T(8,128)(2,1)S(1)}, bf16[4,32,2176]{2,1,0:T(8,128)(2,1)S(1)}, u32[]{:S(2)}, u32[]{:S(2)}) collective-permute-start(bf16[4,32,2176]{2,1,0:T(8,128)(2,1)S(1)} %get-tuple-element.422.refs_0_.refs_8_), channel_id=1, source_target_pairs={{0,4},{2,6},{4,0},{6,2},{8,12},{10,14},{12,8},{14,10},{16,20},{18,... | collective-permute-start | bytes 1671176 | tf_op jit(solution)/shard_map/ppermute | solution.py:1591
  38.8 26.0 %collective-permute-start.7 = (bf16[4,32,2048]{2,1,0:T(8,128)(2,1)S(1)}, bf16[4,32,2048]{2,1,0:T(8,128)(2,1)}, u32[]{:S(2)}, u32[]{:S(2)}) collective-permute-start(bf16[4,32,2048]{2,1,0:T(8,128)(2,1)S(1)} %get-tuple-element.440.refs_0_), channel_id=1, source_target_pairs={{0,1},{1,0},{2,3},{3,2},{4,5},{5,4},{6,7},{7,6},{8,9},{9,8},{10,11... | collective-permute-start | bytes 1572872 | tf_op jit(solution)/shard_map/ppermute | solution.py:1591
  40.3 22.2 %collective-permute-start.10 = (bf16[32,6144]{1,0:T(8,128)(2,1)S(1)}, bf16[32,6144]{1,0:T(8,128)(2,1)S(1)}, u32[]{:S(2)}, u32[]{:S(2)}) collective-permute-start(bf16[32,6144]{1,0:T(8,128)(2,1)S(1)} %join_beside.3.refs_0_), channel_id=1, source_target_pairs={{0,24},{2,26},{4,28},{6,30},{8,0},{10,2},{12,4},{14,6},{16,8},{18,... | collective-permute-start | bytes 1179656 | tf_op jit(solution)/shard_map/ppermute | solution.py:1612
  40.3 23.5 %collective-permute-start.9 = (bf16[32,6144]{1,0:T(8,128)(2,1)S(1)}, bf16[32,6144]{1,0:T(8,128)(2,1)S(1)}, u32[]{:S(2)}, u32[]{:S(2)}) collective-permute-start(bf16[32,6144]{1,0:T(8,128)(2,1)S(1)} %join_beside.3.refs_0_), channel_id=1, source_target_pairs={{0,8},{2,10},{4,12},{6,14},{8,16},{10,18},{12,20},{14,22},{16,24},... | collective-permute-start | bytes 1179656 | tf_op jit(solution)/shard_map/ppermute | solution.py:1612
  61.2 18.0 %collective-permute-start.14 = (bf16[4,32,2176]{2,1,0:T(8,128)(2,1)S(1)}, bf16[4,32,2176]{2,1,0:T(8,128)(2,1)S(1)}, u32[]{:S(2)}, u32[]{:S(2)}) collective-permute-start(bf16[4,32,2176]{2,1,0:T(8,128)(2,1)S(1)} %get-tuple-element.422.refs_0_.refs_8_), channel_id=1, source_target_pairs={{0,1},{1,0},{2,3},{3,2},{4,5},{5,4},{6,7},{7,6},{8,9},{9,8},{10,11... | collective-permute-start | bytes 1671176 | tf_op jit(solution)/shard_map/ppermute | solution.py:1591
  68.4 17.8 %collective-permute-start.15 = (bf16[4,32,2176]{2,1,0:T(8,128)(2,1)S(1)}, bf16[4,32,2176]{2,1,0:T(8,128)(2,1)S(1)}, u32[]{:S(2)}, u32[]{:S(2)}) collective-permute-start(bf16[4,32,2176]{2,1,0:T(8,128)(2,1)S(1)} %collective-permute-done.8.refs_4_.refs_12_), channel_id=1, source_target_pairs={{0,1},{1,0},{2,3},{3,2},{4,5},{5,4},{6,7},{7,6},{8,9},{9,8},{10,11... | collective-permute-start | bytes 1671176 | tf_op jit(solution)/shard_map/ppermute | solution.py:1591
  68.9 17.1 %collective-permute-start.13 = (bf16[4,32,2048]{2,1,0:T(8,128)(2,1)}, bf16[4,32,2048]{2,1,0:T(8,128)(2,1)S(1)}, u32[]{:S(2)}, u32[]{:S(2)}) collective-permute-start(bf16[4,32,2048]{2,1,0:T(8,128)(2,1)} %collective-permute-done.7.refs_1_), channel_id=1, source_target_pairs={{0,4},{2,6},{4,0},{6,2},{8,12},{10,14},{12,8},{14,10},{16,20},{18,... | collective-permute-start | bytes 1572872 | tf_op jit(solution)/shard_map/ppermute | solution.py:1591
  89.9 36.5 %collective-permute-start.25 = (bf16[4,32,6144]{2,1,0:T(8,128)(2,1)S(1)}, bf16[4,32,6144]{2,1,0:T(8,128)(2,1)}, u32[]{:S(2)}, u32[]{:S(2)}) collective-permute-start(bf16[4,32,6144]{2,1,0:T(8,128)(2,1)S(1)} %join_up.1.refs_0_), channel_id=1, source_target_pairs={{0,1},{1,0},{2,3},{3,2},{4,5},{5,4},{6,7},{7,6},{8,9},{9,8},{10,11... | collective-permute-start | bytes 4718600 | tf_op jit(solution)/shard_map/ppermute | solution.py:1591
  91.6 36.5 %collective-permute-start.26 = (bf16[4,32,6144]{2,1,0:T(8,128)(2,1)S(1)}, bf16[4,32,6144]{2,1,0:T(8,128)(2,1)}, u32[]{:S(2)}, u32[]{:S(2)}) collective-permute-start(bf16[4,32,6144]{2,1,0:T(8,128)(2,1)S(1)} %join_up.1.refs_0_), channel_id=1, source_target_pairs={{0,4},{2,6},{4,0},{6,2},{8,12},{10,14},{12,8},{14,10},{16,20},{18,... | collective-permute-start | bytes 4718600 | tf_op jit(solution)/shard_map/ppermute | solution.py:1591
  95.1 30.6 %collective-permute-start.27 = (bf16[2,2,64,1024]{3,2,1,0:T(8,128)(2,1)}, bf16[2,2,64,1024]{3,2,1,0:T(8,128)(2,1)S(1)}, u32[]{:S(2)}, u32[]{:S(2)}) collective-permute-start(bf16[2,2,64,1024]{3,2,1,0:T(8,128)(2,1)} %join_plane.1.refs_8_), channel_id=1, source_target_pairs={{0,8},{2,10},{4,12},{6,14},{8,16},{10,18},{12,20},{14,22},{16,24},... | collective-permute-start | bytes 1572872 | tf_op jit(solution)/shard_map/ppermute | solution.py:1612
  95.9 29.8 %collective-permute-start.28 = (bf16[2,2,64,1024]{3,2,1,0:T(8,128)(2,1)}, bf16[2,2,64,1024]{3,2,1,0:T(8,128)(2,1)}, u32[]{:S(2)}, u32[]{:S(2)}) collective-permute-start(bf16[2,2,64,1024]{3,2,1,0:T(8,128)(2,1)} %join_plane.1.refs_8_), channel_id=1, source_target_pairs={{0,24},{2,26},{4,28},{6,30},{8,0},{10,2},{12,4},{14,6},{16,8},{18,... | collective-permute-start | bytes 1572872 | tf_op jit(solution)/shard_map/ppermute | solution.py:1612
  97.3 56.7 %collective-permute-start.30 = (bf16[4,32,6144]{2,1,0:T(8,128)(2,1)S(1)}, bf16[4,32,6144]{2,1,0:T(8,128)(2,1)}, u32[]{:S(2)}, u32[]{:S(2)}) collective-permute-start(bf16[4,32,6144]{2,1,0:T(8,128)(2,1)S(1)} %join_up.1.refs_0_), channel_id=1, source_target_pairs={{0,2},{2,0},{4,6},{6,4},{8,10},{10,8},{12,14},{14,12},{16,18},{18,... | collective-permute-start | bytes 4718600 | tf_op jit(solution)/shard_map/ppermute | solution.py:1591
  128.1 25.9 %collective-permute-start.31 = (bf16[4,32,6144]{2,1,0:T(8,128)(2,1)}, bf16[4,32,6144]{2,1,0:T(8,128)(2,1)}, u32[]{:S(2)}, u32[]{:S(2)}) collective-permute-start(bf16[4,32,6144]{2,1,0:T(8,128)(2,1)} %collective-permute-done.25.refs_1_), channel_id=1, source_target_pairs={{0,2},{2,0},{4,6},{6,4},{8,10},{10,8},{12,14},{14,12},{16,18},{18,... | collective-permute-start | bytes 4718600 | tf_op jit(solution)/shard_map/ppermute | solution.py:1591
  128.1 25.9 %collective-permute-start.29 = (bf16[512,1024]{1,0:T(8,128)(2,1)}, bf16[512,1024]{1,0:T(8,128)(2,1)S(1)}, u32[]{:S(2)}, u32[]{:S(2)}) collective-permute-start(bf16[512,1024]{1,0:T(8,128)(2,1)} %cast_far.3), channel_id=1, source_target_pairs={{0,1},{1,0},{2,3},{3,2},{4,5},{5,4},{6,7},{7,6},{8,9},{9,8},{10,11... | collective-permute-start | bytes 3145736 | tf_op jit(solution)/shard_map/ppermute | solution.py:1591
  129.3 24.7 %collective-permute-start.32 = (bf16[2,2,64,1024]{3,2,1,0:T(8,128)(2,1)}, bf16[2,2,64,1024]{3,2,1,0:T(8,128)(2,1)S(1)}, u32[]{:S(2)}, u32[]{:S(2)}) collective-permute-start(bf16[2,2,64,1024]{3,2,1,0:T(8,128)(2,1)} %join_plane.1.refs_8_), channel_id=1, source_target_pairs={{0,16},{2,18},{4,20},{6,22},{8,24},{10,26},{12,28},{14,30},{16,0},... | collective-permute-start | bytes 1572872 | tf_op jit(solution)/shard_map/ppermute | solution.py:1612
  129.3 37.1 %collective-permute-start.33 = (bf16[4,32,6144]{2,1,0:T(8,128)(2,1)}, bf16[4,32,6144]{2,1,0:T(8,128)(2,1)}, u32[]{:S(2)}, u32[]{:S(2)}) collective-permute-start(bf16[4,32,6144]{2,1,0:T(8,128)(2,1)} %collective-permute-done.25.refs_1_), channel_id=1, source_target_pairs={{0,4},{2,6},{4,0},{6,2},{8,12},{10,14},{12,8},{14,10},{16,20},{18,... | collective-permute-start | bytes 4718600 | tf_op jit(solution)/shard_map/ppermute | solution.py:1591
  210.2 22.0 %collective-permute-start.40 = (bf16[4,256,1024]{2,1,0:T(8,128)(2,1)}, bf16[4,256,1024]{2,1,0:T(8,128)(2,1)S(1)}, u32[]{:S(2)}, u32[]{:S(2)}) collective-permute-start(bf16[4,256,1024]{2,1,0:T(8,128)(2,1)} %get-tuple-element.496), channel_id=1, source_target_pairs={{0,2},{2,0},{4,6},{6,4},{8,10},{10,8},{12,14},{14,12},{16,18},{18,... | collective-permute-start | bytes 6291464 | tf_op jit(solution)/shard_map/ppermute | solution.py:1591
  210.4 21.8 %collective-permute-start.41 = (bf16[8,64,2048]{2,1,0:T(8,128)(2,1)}, bf16[8,64,2048]{2,1,0:T(8,128)(2,1)S(1)}, u32[]{:S(2)}, u32[]{:S(2)}) collective-permute-start(bf16[8,64,2048]{2,1,0:T(8,128)(2,1)} %get-tuple-element.502), channel_id=1, source_target_pairs={{0,2},{2,0},{4,6},{6,4},{8,10},{10,8},{12,14},{14,12},{16,18},{18,... | collective-permute-start | bytes 6291464 | tf_op jit(solution)/shard_map/ppermute | solution.py:1591
  232.0 35.5 %collective-permute-start.43 = (bf16[2,256,1024]{2,1,0:T(8,128)(2,1)}, bf16[2,256,1024]{2,1,0:T(8,128)(2,1)}, u32[]{:S(2)}, u32[]{:S(2)}) collective-permute-start(bf16[2,256,1024]{2,1,0:T(8,128)(2,1)} %get-tuple-element.517), channel_id=1, source_target_pairs={{0,2},{2,0},{4,6},{6,4},{8,10},{10,8},{12,14},{14,12},{16,18},{18,... | collective-permute-start | bytes 3145736 | tf_op jit(solution)/shard_map/ppermute | solution.py:1591
  238.5 28.1 %collective-permute-start.42 = (bf16[2,256,1024]{2,1,0:T(8,128)(2,1)}, bf16[2,256,1024]{2,1,0:T(8,128)(2,1)S(1)}, u32[]{:S(2)}, u32[]{:S(2)}) collective-permute-start(bf16[2,256,1024]{2,1,0:T(8,128)(2,1)} %get-tuple-element.513), channel_id=1, source_target_pairs={{0,4},{2,6},{4,0},{6,2},{8,12},{10,14},{12,8},{14,10},{16,20},{18,... | collective-permute-start | bytes 3145736 | tf_op jit(solution)/shard_map/ppermute | solution.py:1591
  240.0 27.5 %collective-permute-start.44 = (bf16[8,32,2048]{2,1,0:T(8,128)(2,1)}, bf16[8,32,2048]{2,1,0:T(8,128)(2,1)S(1)}, u32[]{:S(2)}, u32[]{:S(2)}) collective-permute-start(bf16[8,32,2048]{2,1,0:T(8,128)(2,1)} %get-tuple-element.519), channel_id=1, source_target_pairs={{0,1},{1,0},{2,3},{3,2},{4,5},{5,4},{6,7},{7,6},{8,9},{9,8},{10,11... | collective-permute-start | bytes 3145736 | tf_op jit(solution)/shard_map/ppermute | solution.py:1591
  266.0 27.1 %collective-permute-start.47 = (bf16[8,64,2048]{2,1,0:T(8,128)(2,1)}, bf16[8,64,2048]{2,1,0:T(8,128)(2,1)}, u32[]{:S(2)}, u32[]{:S(2)}) collective-permute-start(bf16[8,64,2048]{2,1,0:T(8,128)(2,1)} %get-tuple-element.544), channel_id=1, source_target_pairs={{0,2},{2,0},{4,6},{6,4},{8,10},{10,8},{12,14},{14,12},{16,18},{18,... | collective-permute-start | bytes 6291464 | tf_op jit(solution)/shard_map/ppermute | solution.py:1591
  266.0 24.8 %collective-permute-start.46 = (bf16[2,256,1024]{2,1,0:T(8,128)(2,1)}, bf16[2,256,1024]{2,1,0:T(8,128)(2,1)}, u32[]{:S(2)}, u32[]{:S(2)}) collective-permute-start(bf16[2,256,1024]{2,1,0:T(8,128)(2,1)} %get-tuple-element.535), channel_id=1, source_target_pairs={{0,2},{2,0},{4,6},{6,4},{8,10},{10,8},{12,14},{14,12},{16,18},{18,... | collective-permute-start | bytes 3145736 | tf_op jit(solution)/shard_map/ppermute | solution.py:1591
  270.3 20.5 %collective-permute-start.45 = (bf16[1,256,1024]{2,1,0:T(8,128)(2,1)}, bf16[1,256,1024]{2,1,0:T(8,128)(2,1)}, u32[]{:S(2)}, u32[]{:S(2)}) collective-permute-start(bf16[1,256,1024]{2,1,0:T(8,128)(2,1)} %get-tuple-element.527), channel_id=1, source_target_pairs={{0,4},{2,6},{4,0},{6,2},{8,12},{10,14},{12,8},{14,10},{16,20},{18,... | collective-permute-start | bytes 1572872 | tf_op jit(solution)/shard_map/ppermute | solution.py:1591
  293.1 29.0 %collective-permute-start.50 = (bf16[512,1024]{1,0:T(8,128)(2,1)}, bf16[512,1024]{1,0:T(8,128)(2,1)S(1)}, u32[]{:S(2)}, u32[]{:S(2)}) collective-permute-start(bf16[512,1024]{1,0:T(8,128)(2,1)} %copy-done.93), channel_id=1, source_target_pairs={{0,1},{1,0},{2,3},{3,2},{4,5},{5,4},{6,7},{7,6},{8,9},{9,8},{10,11... | collective-permute-start | bytes 3145736 | tf_op jit(solution)/shard_map/ppermute | solution.py:1591
  294.3 31.8 %collective-permute-start.51 = (bf16[8,64,1024]{2,1,0:T(8,128)(2,1)S(1)}, bf16[8,64,1024]{2,1,0:T(8,128)(2,1)S(1)}, u32[]{:S(2)}, u32[]{:S(2)}) collective-permute-start(bf16[8,64,1024]{2,1,0:T(8,128)(2,1)S(1)} %get-tuple-element.577), channel_id=1, source_target_pairs={{0,2},{2,0},{4,6},{6,4},{8,10},{10,8},{12,14},{14,12},{16,18},{18,... | collective-permute-start | bytes 3145736 | tf_op jit(solution)/shard_map/ppermute | solution.py:1591
  294.3 27.9 %collective-permute-start.49 = (bf16[4,32,2048]{2,1,0:T(8,128)(2,1)S(1)}, bf16[4,32,2048]{2,1,0:T(8,128)(2,1)S(1)}, u32[]{:S(2)}, u32[]{:S(2)}) collective-permute-start(bf16[4,32,2048]{2,1,0:T(8,128)(2,1)S(1)} %get-tuple-element.551), channel_id=1, source_target_pairs={{0,4},{2,6},{4,0},{6,2},{8,12},{10,14},{12,8},{14,10},{16,20},{18,... | collective-permute-start | bytes 1572872 | tf_op jit(solution)/shard_map/ppermute | solution.py:1591
  295.6 26.5 %collective-permute-start.48 = (bf16[1,256,1024]{2,1,0:T(8,128)(2,1)S(1)}, bf16[1,256,1024]{2,1,0:T(8,128)(2,1)S(1)}, u32[]{:S(2)}, u32[]{:S(2)}) collective-permute-start(bf16[1,256,1024]{2,1,0:T(8,128)(2,1)S(1)} %get-tuple-element.549), channel_id=1, source_target_pairs={{0,4},{2,6},{4,0},{6,2},{8,12},{10,14},{12,8},{14,10},{16,20},{18,... | collective-permute-start | bytes 1572872 | tf_op jit(solution)/shard_map/ppermute | solution.py:1591
  299.5 54.2 %collective-permute-start.53 = (bf16[4,64,2048]{2,1,0:T(8,128)(2,1)S(1)}, bf16[4,64,2048]{2,1,0:T(8,128)(2,1)S(1)}, u32[]{:S(2)}, u32[]{:S(2)}) collective-permute-start(bf16[4,64,2048]{2,1,0:T(8,128)(2,1)S(1)} %get-tuple-element.590), channel_id=1, source_target_pairs={{0,4},{2,6},{4,0},{6,2},{8,12},{10,14},{12,8},{14,10},{16,20},{18,... | collective-permute-start | bytes 3145736 | tf_op jit(solution)/shard_map/ppermute | solution.py:1591
  325.2 31.2 %collective-permute-start.57 = (bf16[4,128,1024]{2,1,0:T(8,128)(2,1)S(1)}, bf16[4,128,1024]{2,1,0:T(8,128)(2,1)S(1)}, u32[]{:S(2)}, u32[]{:S(2)}) collective-permute-start(bf16[4,128,1024]{2,1,0:T(8,128)(2,1)S(1)} %get-tuple-element.608), channel_id=1, source_target_pairs={{0,1},{1,0},{2,3},{3,2},{4,5},{5,4},{6,7},{7,6},{8,9},{9,8},{10,11... | collective-permute-start | bytes 3145736 | tf_op jit(solution)/shard_map/ppermute | solution.py:1591
  327.6 26.0 %collective-permute-start.54 = (bf16[32,2048]{1,0:T(8,128)(2,1)S(1)}, bf16[32,2048]{1,0:T(8,128)(2,1)S(1)}, u32[]{:S(2)}, u32[]{:S(2)}) collective-permute-start(bf16[32,2048]{1,0:T(8,128)(2,1)S(1)} %get-tuple-element.592), channel_id=1, source_target_pairs={{0,8},{2,10},{4,12},{6,14},{8,16},{10,18},{12,20},{14,22},{16,24},... | collective-permute-start | bytes 393224 | tf_op jit(solution)/shard_map/ppermute | solution.py:1612
  327.7 26.0 %collective-permute-start.55 = (bf16[32,2048]{1,0:T(8,128)(2,1)S(1)}, bf16[32,2048]{1,0:T(8,128)(2,1)S(1)}, u32[]{:S(2)}, u32[]{:S(2)}) collective-permute-start(bf16[32,2048]{1,0:T(8,128)(2,1)S(1)} %get-tuple-element.593), channel_id=1, source_target_pairs={{0,16},{2,18},{4,20},{6,22},{8,24},{10,26},{12,28},{14,30},{16,0},... | collective-permute-start | bytes 393224 | tf_op jit(solution)/shard_map/ppermute | solution.py:1612
  330.9 22.7 %collective-permute-start.56 = (bf16[32,2048]{1,0:T(8,128)(2,1)S(1)}, bf16[32,2048]{1,0:T(8,128)(2,1)S(1)}, u32[]{:S(2)}, u32[]{:S(2)}) collective-permute-start(bf16[32,2048]{1,0:T(8,128)(2,1)S(1)} %get-tuple-element.594), channel_id=1, source_target_pairs={{0,24},{2,26},{4,28},{6,30},{8,0},{10,2},{12,4},{14,6},{16,8},{18,... | collective-permute-start | bytes 393224 | tf_op jit(solution)/shard_map/ppermute | solution.py:1612
  378.5 20.1 %collective-permute-start.62 = (bf16[4,64,1536]{2,1,0:T(8,128)(2,1)S(1)}, bf16[4,64,1536]{2,1,0:T(8,128)(2,1)S(1)}, u32[]{:S(2)}, u32[]{:S(2)}) collective-permute-start(bf16[4,64,1536]{2,1,0:T(8,128)(2,1)S(1)} %get-tuple-element.673), channel_id=1, source_target_pairs={{0,4},{2,6},{4,0},{6,2},{8,12},{10,14},{12,8},{14,10},{16,20},{18,... | collective-permute-start | bytes 2359304 | tf_op jit(solution)/shard_map/ppermute | solution.py:1591
  380.3 18.5 %collective-permute-start.63 = (bf16[8,32,1536]{2,1,0:T(8,128)(2,1)S(1)}, bf16[8,32,1536]{2,1,0:T(8,128)(2,1)S(1)}, u32[]{:S(2)}, u32[]{:S(2)}) collective-permute-start(bf16[8,32,1536]{2,1,0:T(8,128)(2,1)S(1)} %get-tuple-element.683), channel_id=1, source_target_pairs={{0,1},{1,0},{2,3},{3,2},{4,5},{5,4},{6,7},{7,6},{8,9},{9,8},{10,11... | collective-permute-start | bytes 2359304 | tf_op jit(solution)/shard_map/ppermute | solution.py:1591
  382.3 31.1 %collective-permute-start.65 = (bf16[32,7168]{1,0:T(8,128)(2,1)S(1)}, bf16[32,7168]{1,0:T(8,128)(2,1)S(1)}, u32[]{:S(2)}, u32[]{:S(2)}) collective-permute-start(bf16[32,7168]{1,0:T(8,128)(2,1)S(1)} %get-tuple-element.693), channel_id=1, source_target_pairs={{0,8},{2,10},{4,12},{6,14},{8,16},{10,18},{12,20},{14,22},{16,24},... | collective-permute-start | bytes 1376264 | tf_op jit(solution)/shard_map/ppermute | solution.py:1612
  382.7 38.1 %collective-permute-start.66 = (bf16[32,7168]{1,0:T(8,128)(2,1)S(1)}, bf16[32,7168]{1,0:T(8,128)(2,1)S(1)}, u32[]{:S(2)}, u32[]{:S(2)}) collective-permute-start(bf16[32,7168]{1,0:T(8,128)(2,1)S(1)} %get-tuple-element.694), channel_id=1, source_target_pairs={{0,16},{2,18},{4,20},{6,22},{8,24},{10,26},{12,28},{14,30},{16,0},... | collective-permute-start | bytes 1376264 | tf_op jit(solution)/shard_map/ppermute | solution.py:1612
  385.0 38.6 %collective-permute-start.67 = (bf16[32,7168]{1,0:T(8,128)(2,1)S(1)}, bf16[32,7168]{1,0:T(8,128)(2,1)S(1)}, u32[]{:S(2)}, u32[]{:S(2)}) collective-permute-start(bf16[32,7168]{1,0:T(8,128)(2,1)S(1)} %get-tuple-element.695), channel_id=1, source_target_pairs={{0,24},{2,26},{4,28},{6,30},{8,0},{10,2},{12,4},{14,6},{16,8},{18,... | collective-permute-start | bytes 1376264 | tf_op jit(solution)/shard_map/ppermute | solution.py:1612
  400.7 23.7 %collective-permute-start.64 = (bf16[4,32,1536]{2,1,0:T(8,128)(2,1)S(1)}, bf16[4,32,1536]{2,1,0:T(8,128)(2,1)S(1)}, u32[]{:S(2)}, u32[]{:S(2)}) collective-permute-start(bf16[4,32,1536]{2,1,0:T(8,128)(2,1)S(1)} %get-tuple-element.691), channel_id=1, source_target_pairs={{0,1},{1,0},{2,3},{3,2},{4,5},{5,4},{6,7},{7,6},{8,9},{9,8},{10,11... | collective-permute-start | bytes 1179656 | tf_op jit(solution)/shard_map/ppermute | solution.py:1591
  401.9 22.5 %collective-permute-start.68 = (bf16[4,32,1536]{2,1,0:T(8,128)(2,1)S(1)}, bf16[4,32,1536]{2,1,0:T(8,128)(2,1)S(1)}, u32[]{:S(2)}, u32[]{:S(2)}) collective-permute-start(bf16[4,32,1536]{2,1,0:T(8,128)(2,1)S(1)} %get-tuple-element.701), channel_id=1, source_target_pairs={{0,4},{2,6},{4,0},{6,2},{8,12},{10,14},{12,8},{14,10},{16,20},{18,... | collective-permute-start | bytes 1179656 | tf_op jit(solution)/shard_map/ppermute | solution.py:1591
  424.4 25.4 %collective-permute-start.72 = (bf16[512,1024]{1,0:T(8,128)(2,1)}, bf16[512,1024]{1,0:T(8,128)(2,1)S(1)}, u32[]{:S(2)}, u32[]{:S(2)}) collective-permute-start(bf16[512,1024]{1,0:T(8,128)(2,1)} %get-tuple-element.722), channel_id=1, source_target_pairs={{0,1},{1,0},{2,3},{3,2},{4,5},{5,4},{6,7},{7,6},{8,9},{9,8},{10,11... | collective-permute-start | bytes 3145736 | tf_op jit(solution)/shard_map/ppermute | solution.py:1591
  431.9 19.8 %collective-permute-start.73 = (bf16[32,3200]{1,0:T(8,128)(2,1)}, bf16[32,3200]{1,0:T(8,128)(2,1)S(1)}, u32[]{:S(2)}, u32[]{:S(2)}) collective-permute-start(bf16[32,3200]{1,0:T(8,128)(2,1)} %get-tuple-element.730), channel_id=1, source_target_pairs={{0,8},{2,10},{4,12},{6,14},{8,16},{10,18},{12,20},{14,22},{16,24},... | collective-permute-start | bytes 614408 | tf_op jit(solution)/shard_map/ppermute | solution.py:1612
  431.9 19.8 %collective-permute-start.74 = (bf16[32,3200]{1,0:T(8,128)(2,1)}, bf16[32,3200]{1,0:T(8,128)(2,1)}, u32[]{:S(2)}, u32[]{:S(2)}) collective-permute-start(bf16[32,3200]{1,0:T(8,128)(2,1)} %get-tuple-element.731), channel_id=1, source_target_pairs={{0,16},{2,18},{4,20},{6,22},{8,24},{10,26},{12,28},{14,30},{16,0},... | collective-permute-start | bytes 614408 | tf_op jit(solution)/shard_map/ppermute | solution.py:1612
  433.3 18.5 %collective-permute-start.75 = (bf16[32,3200]{1,0:T(8,128)(2,1)}, bf16[32,3200]{1,0:T(8,128)(2,1)}, u32[]{:S(2)}, u32[]{:S(2)}) collective-permute-start(bf16[32,3200]{1,0:T(8,128)(2,1)} %get-tuple-element.732), channel_id=1, source_target_pairs={{0,24},{2,26},{4,28},{6,30},{8,0},{10,2},{12,4},{14,6},{16,8},{18,... | collective-permute-start | bytes 614408 | tf_op jit(solution)/shard_map/ppermute | solution.py:1612
  (148 other events, 1309.6 us)
